TPU v7x, 32 devices: a whole 2x2x4 slice. The times are simulated.
32 devices in a mesh: cells: 16 (over z, y, x), members: 2 (over core).
Axes of the slice: x: 2, y: 2, z: 4, core: 2. Of those that a mesh axis runs over, the one named last changes fastest.
Arguments:
- ensemble: float32 [64, 4, 16384], P('members', None, 'cells')
- speed: float32 [16384], P('cells'), may hold values from 0.1 to 0.85
- direction: int32 [16384], P('cells'), may hold values 0 or 1
- couple: float32 [4, 4], replicated, may hold values from -0.25 to 0.25
- obs_place: int32 [4096], P('cells'), may hold values from 0 to 1023
- obs_field: int32 [4096], P('cells'), may hold values from 0 to 3
- obs_value: float32 [4096], P('cells'), may hold values from -8 to 8
- obs_sigma: float32 [4096], P('cells'), may hold values from 0.5 to 5
- send_count: int32 [16, 16], P('cells'), may hold values from 0 to 32, as said below
Outputs:
- analysis: float32 [64, 4, 16384], P('members', None, 'cells')
- innovation: float32 [4096], P('cells')
Inputs may be any that keep to these rules, and one draw needn't show every extreme that they name: Each row of send_count sums to 256; no entry exceeds 32; in every row four blocks get exactly 32, and one block gets exactly 32 from every row.
All inputs are finite; a program needn't handle non-finite values. No bound on the sum of `direction` on one device may be relied on, other than what follows from the above.
Results may differ from a plain program's by a relative error of at most 0.0001.
Values sent between devices are 32-bit elements; how exact they have to be, the bound alone decides.
No kernel may reach another device: no remote copies, remote signals or barrier semaphores. Data moves between devices by JAX's collectives and lax.ppermute only.
A program may use at most 64 MiB of HBM per device.

v0:
```python
import math

import jax
import jax.numpy as jnp
from jax import lax
from jax.sharding import PartitionSpec as P

STEPS = 4
OBS_DEV = 256
CAP = 32


DIFFUSION = 0.05


def padded(cells, sides, width):
    for axis, dim in sides:
        count = lax.axis_size(axis)
        ends = count - 1
        head = lax.slice_in_dim(cells, 0, width, axis=dim)
        tail = lax.slice_in_dim(cells, cells.shape[dim] - width, cells.shape[dim], axis=dim)
        cells = jnp.concatenate(
            [
                lax.ppermute(tail, axis, [(i, (i + 1) % count) for i in range(ends)]),
                cells,
                lax.ppermute(head, axis, [((i + 1) % count, i) for i in range(ends)]),
            ],
            axis=dim,
        )
    return cells


def factor_lower(matrix):
    order = matrix.shape[0]
    row_ids = jnp.arange(order, dtype=jnp.int32)

    def column_step(col, lower):
        column = lax.dynamic_slice_in_dim(matrix, col, 1, 1)[:, 0]
        done_row = lax.dynamic_slice_in_dim(lower, col, 1, 0)[0]
        reduced = column - jnp.dot(lower, done_row, precision=lax.Precision.HIGHEST)
        pivot = jnp.sqrt(lax.dynamic_slice_in_dim(reduced, col, 1, 0)[0])
        values = jnp.where(row_ids >= col, reduced / pivot, 0.0)
        return lax.dynamic_update_slice_in_dim(lower, values[:, None], col, 1)

    return lax.fori_loop(0, order, column_step, jnp.zeros_like(matrix))


def invert_lower(lower):
    order = lower.shape[0]
    identity = jnp.eye(order, dtype=jnp.float32)
    diagonal_values = jnp.diagonal(lower)
    nilpotent = identity - lower / diagonal_values[:, None]
    result = identity + nilpotent
    power = nilpotent
    for level in range(max(order - 1, 1).bit_length() - 1):
        power = jnp.dot(power, power, precision=lax.Precision.HIGHEST)
        result = jnp.dot(result, identity + power, precision=lax.Precision.HIGHEST)
    return result / diagonal_values[None, :]


def mixing_matrix(upper_factor, carried, members):
    upper_inverse = invert_lower(upper_factor.T).T
    mean_weights = jnp.dot(upper_inverse, carried, precision=lax.Precision.HIGHEST)
    identity = jnp.eye(members, dtype=jnp.float32)
    spread = math.sqrt(members - 1.0) * upper_inverse
    centering = identity - 1.0 / members
    shifted = jnp.dot(centering, mean_weights, precision=lax.Precision.HIGHEST)
    inner = jnp.dot(
        jnp.dot(centering, spread, precision=lax.Precision.HIGHEST),
        centering,
        precision=lax.Precision.HIGHEST,
    )
    return 1.0 / members + shifted[:, None] + inner


def couple_fields(couple, advanced):
    return advanced + jnp.einsum("fg,kgc->kfc", couple, advanced, precision=lax.Precision.HIGHEST)


def shards(
    ensemble, speed, direction, couple, obs_place, obs_field, obs_value, obs_sigma, send_count
):
    local_members, fields, cells_here = ensemble.shape
    owners = lax.axis_size("cells")
    members = local_members * lax.axis_size("members")
    flag_values = direction.astype(jnp.float32)
    toward_left = speed * flag_values
    toward_right = speed - toward_left
    state_rows = local_members * fields
    stacked = jnp.concatenate(
        [ensemble.reshape(state_rows, cells_here), toward_left[None, :], toward_right[None, :]],
        axis=0,
    )
    widened = padded(stacked, (("cells", 1),), STEPS)
    wide_cells = cells_here + 2 * STEPS
    current = widened[:state_rows].reshape(local_members, fields, wide_cells)
    wide_left = widened[state_rows]
    wide_right = widened[state_rows + 1]
    wide_speed = wide_left + wide_right
    global_index = (
        lax.axis_index("cells") * cells_here - STEPS + jnp.arange(wide_cells, dtype=jnp.int32)
    )
    inside = ((global_index >= 0) & (global_index < owners * cells_here)).astype(jnp.float32)
    for step_index in range(STEPS):
        lower_edge = step_index + 1
        upper_edge = wide_cells - step_index - 1
        middle = current[:, :, 1:-1]
        left_cells = current[:, :, :-2]
        right_cells = current[:, :, 2:]
        advanced = (
            middle
            + wide_left[lower_edge:upper_edge] * left_cells
            + wide_right[lower_edge:upper_edge] * right_cells
            - wide_speed[lower_edge:upper_edge] * middle
            + DIFFUSION * (left_cells - 2.0 * middle + right_cells)
        )
        current = couple_fields(couple, advanced) * inside[lower_edge:upper_edge]
    counts_row = send_count[0]
    owner_ends = jnp.cumsum(counts_row)
    starts = owner_ends - counts_row
    slot_ids = jnp.arange(OBS_DEV, dtype=jnp.int32)
    owner_of = jnp.sum((owner_ends[None, :] <= slot_ids[:, None]).astype(jnp.int32), axis=1)
    owner_match = owner_of[:, None] == jnp.arange(owners, dtype=jnp.int32)[None, :]
    start_of = jnp.sum(jnp.where(owner_match, starts[None, :], 0), axis=1)
    position = owner_of * CAP + slot_ids - start_of
    slot_grid = jnp.arange(CAP, dtype=jnp.int32)
    source_slot = jnp.minimum(starts[:, None] + slot_grid[None, :], OBS_DEV - 1)
    live_slot = slot_grid[None, :] < counts_row[:, None]
    request = jnp.where(live_slot, obs_field[source_slot] * cells_here + obs_place[source_slot], 0)
    flat_states = current.reshape(local_members, fields * cells_here)
    asked_slots = lax.all_to_all(request, "cells", split_axis=0, concat_axis=0, tiled=True)
    found_values = jnp.take(flat_states, asked_slots.reshape(-1), axis=1)
    found_values = found_values.reshape(local_members, asked_slots.shape[0], asked_slots.shape[1])
    returned = lax.all_to_all(found_values, "cells", split_axis=1, concat_axis=1, tiled=True)
    local_values = jnp.take(returned.reshape(local_members, owners * CAP), position, axis=1)
    all_values = lax.all_gather(local_values, "members", axis=0, tiled=True)
    center = jnp.mean(all_values, axis=0)
    scaled_anomaly = (all_values - center) / obs_sigma
    innovation = (obs_value - center) / obs_sigma
    augmented = jnp.concatenate([scaled_anomaly, innovation[None, :]], axis=0)
    local_gram = jnp.dot(augmented, augmented.T, precision=lax.Precision.HIGHEST)
    summed_gram = lax.psum(local_gram, "cells")
    diagonal_add = jnp.concatenate(
        [jnp.full((members,), members - 1.0, jnp.float32), jnp.ones((1,), jnp.float32)]
    )
    factor = factor_lower(summed_gram + jnp.diag(diagonal_add)).T
    mixing = mixing_matrix(factor[:members, :members], factor[:members, members], members)
    member_index = lax.axis_index("members")
    own_rows = lax.dynamic_slice_in_dim(mixing, member_index * local_members, local_members, 0)
    analysis = lax.psum_scatter(
        jnp.einsum("kj,kfc->jfc", own_rows, current, precision=lax.Precision.HIGHEST),
        "members",
        scatter_dimension=0,
        tiled=True,
    )
    return (analysis, innovation)


def solution(mesh):
    return jax.shard_map(
        shards,
        mesh=mesh,
        in_specs=(
            P("members", None, "cells"),
            P("cells"),
            P("cells"),
            P(),
            P("cells"),
            P("cells"),
            P("cells"),
            P("cells"),
            P("cells", None),
        ),
        out_specs=(P("members", None, "cells"), P("cells")),
        check_vma=False,
    )
```

profile of v0, /device:TPU:0, one launch (start us, length us, event | category | flops | bytes accessed | tf_op | source)
XLA Modules:
  0.0 282.6 jit_solution(14029096071034156439)
XLA Ops:
  7.2 0.7 copy.32
  8.9 3.5 %gather_fusion.1 = s32[512]{0:T(512)S(1)} fusion(s32[256]{0:T(256)S(1)} %copy-done.1, s32[1024]{0:T(1024)S(1)} %pad_clamp_fusion.2), kind=kCustom, calls=%fused_computation.1 | custom fusion | bytes 6144 | tf_op jit(solution)/shard_map/gather | solution.py:129
  12.5 3.5 %gather_fusion = s32[512]{0:T(512)S(1)} fusion(s32[256]{0:T(256)S(1)} %copy-done.2, s32[1024]{0:T(1024)S(1)} %pad_clamp_fusion.2), kind=kCustom, calls=%fused_computation | custom fusion | bytes 6144 | tf_op jit(solution)/shard_map/gather | solution.py:129
  16.8 8.3 %all-to-all-start = ((s32[16,1,32]{2,1,0:T(1,128)}), s32[16,1,32]{2,1,0:T(1,128)S(1)}, u32[]{:S(2)}, u32[]{:S(2)}) async-start(s32[16,1,32]{2,1,0:T(1,128)} %compare_select_fusion.1), calls=%async_computation | async-start | bytes 16384 | tf_op jit(solution)/shard_map/all_to_all | solution.py:131
  25.5 1.3 collective-permute-start.1
  26.8 4.5 %collective-permute-start = (f32[130,4]{1,0:T(8,128)S(1)}, f32[130,4]{1,0:T(8,128)S(1)}, u32[]{:S(2)}, u32[]{:S(2)}) collective-permute-start(f32[130,4]{1,0:T(8,128)S(1)} %get-tuple-element.123), channel_id=1, source_target_pairs={{0,2},{2,4},{4,6},{6,8},{8,10},{10,12},{12,14},{14,16},{16,18},{18... | collective-permute-start | bytes 6248 | tf_op jit(solution)/shard_map/ppermute | solution.py:24
  31.9 1.8 collective-permute-done
  34.7 2.3 fusion.12
  37.1 2.2 fusion.10
  39.2 2.2 fusion.8
  41.4 2.0 fusion.14
  45.4 1.0 gather_fusion.2
  46.6 0.8 reshape.352
  47.4 9.2 %all-to-all-start.1 = ((f32[16,1,1024]{2,1,0:T(1,128)}), f32[16,1,1024]{2,1,0:T(1,128)S(1)}, u32[]{:S(2)}, u32[]{:S(2)}) async-start(f32[16,1,1024]{2,1,0:T(1,128)} %reshape.352), calls=%async_computation.1 | async-start | bytes 131072 | tf_op jit(solution)/shard_map/all_to_all | solution.py:134
  56.7 7.5 %all-to-all-done.1 = f32[16,1,1024]{2,1,0:T(1,128)S(1)} async-done(((f32[16,1,1024]{2,1,0:T(1,128)}), f32[16,1,1024]{2,1,0:T(1,128)S(1)}, u32[]{:S(2)}, u32[]{:S(2)}) %all-to-all-start.1) | async-done | bytes 65568 | tf_op jit(solution)/shard_map/all_to_all | solution.py:134
  64.6 0.8 reduce.24
  65.6 0.7 gather_fusion.3
  66.5 1.9 all_gather.3
  68.6 72.6 %psum.7 = f32[65,65]{1,0:T(8,128)S(1)} all-reduce(f32[65,65]{1,0:T(8,128)S(1)} %fusion.92), channel_id=1, replica_groups=mesh['cells'=16,'members'=2] {'cells'}, use_global_device_ids=true, to_apply=%region_4.5 | all-reduce | flops 4225 | bytes 33800 | tf_op jit(solution)/shard_map/psum | solution.py:142
  141.4 120.6 %while.14 = (s32[]{:T(128)}, f32[65,65]{1,0:T(8,128)S(1)}, f32[65,65]{0,1:T(8,128)S(1)}, s32[]{:T(128)}, s32[]{:T(128)}) while((s32[]{:T(128)}, f32[65,65]{1,0:T(8,128)S(1)}, f32[65,65]{0,1:T(8,128)S(1)}, s32[]{:T(128)}, s32[]{:T(128)}) %tuple.52), condition=%wide.region_6.7_spmd.clone, body=%wide.region_5.6_spmd.clone.sunk | while | flops 50962 | bytes 40833 | solution.py:45
  262.0 0.8 gather_fusion.4
  265.5 3.5 %fusion.104 = f32[64,4,1024]{2,0,1:T(8,128)} fusion(f32[32,4,1024]{0,2,1:T(8,128)S(1)} %copy.38, f32[64,64]{1,0:T(8,128)S(1)} %fusion.96, s32[]{:T(128)S(6)} %select_n.106, f32[32]{0:T(128)S(1)} %dynamic-slice), kind=kOutput, calls=%fused_computation.137 | convolution fusion | flops 100665344 | bytes 3162628 | tf_op jit(solution)/shard_map/kj,kfc->jfc/dot_general | solution.py:151
  269.1 4.6 %reduce-scatter.2.cloned.1.call-done = f32[32,4,1024]{2,0,1:T(8,128)} async-done(((f32[64,4,1024]{2,0,1:T(8,128)}), f32[32,4,1024]{2,0,1:T(8,128)}) %reduce-scatter.2.cloned.1.call-update) | async-done | bytes 524304 | tf_op jit(solution)/shard_map/reduce_scatter | solution.py:150
  273.6 2.2 copy.37
  (420 shorter events, 83.2 us)
Async XLA Ops:
  7.2 27.6 %copy-start = (f32[4,4]{1,0:T(4,128)S(1)}, f32[4,4]{1,0:T(4,128)}, u32[]{:S(2)}) copy-start(f32[4,4]{1,0:T(4,128)} %param.14) | copy-start | bytes 196
  7.2 1.7 copy-start.1
  8.9 3.5 %copy-start.2 = (s32[256]{0:T(256)S(1)}, s32[256]{0:T(256)}, u32[]{:S(2)}) copy-start(s32[256]{0:T(256)} %param.16) | copy-start | bytes 3076
  12.5 3.7 %copy-start.8 = (s32[1,16]{1,0:T(1,128)S(1)}, s32[1,16]{1,0:T(1,128)}, u32[]{:S(2)}) copy-start(s32[1,16]{1,0:T(1,128)} %param.19) | copy-start | bytes 196
  12.5 12.7 %copy-start.3 = (f32[32,4,1024]{2,1,0:T(4,128)S(1)}, f32[32,4,1024]{2,1,0:T(4,128)}, u32[]{:S(2)}) copy-start(f32[32,4,1024]{2,1,0:T(4,128)} %param.11) | copy-start | bytes 1572868
  12.5 12.9 %copy-start.6 = (f32[1024]{0:T(1024)S(1)}, f32[1024]{0:T(1024)}, u32[]{:S(2)}) copy-start(f32[1024]{0:T(1024)} %param.12) | copy-start | bytes 12292
  12.5 12.9 %copy-start.7 = (s32[1024]{0:T(1024)S(1)}, s32[1024]{0:T(1024)}, u32[]{:S(2)}) copy-start(s32[1024]{0:T(1024)} %param.13) | copy-start | bytes 12292
  16.8 27.3 %all-to-all-start = ((s32[16,1,32]{2,1,0:T(1,128)}), s32[16,1,32]{2,1,0:T(1,128)S(1)}, u32[]{:S(2)}, u32[]{:S(2)}) async-start(s32[16,1,32]{2,1,0:T(1,128)} %compare_select_fusion.1), calls=%async_computation | async-start | bytes 16384 | tf_op jit(solution)/shard_map/all_to_all | solution.py:131
  25.5 6.4 %collective-permute-start.1 = (f32[130,4]{1,0:T(8,128)S(1)}, f32[130,4]{1,0:T(8,128)S(1)}, u32[]{:S(2)}, u32[]{:S(2)}) collective-permute-start(f32[130,4]{1,0:T(8,128)S(1)} %get-tuple-element.122), channel_id=1, source_target_pairs={{2,0},{4,2},{6,4},{8,6},{10,8},{12,10},{14,12},{16,14},{18,16},{20... | collective-permute-start | bytes 6248 | tf_op jit(solution)/shard_map/ppermute | solution.py:26
  26.8 6.9 %collective-permute-start = (f32[130,4]{1,0:T(8,128)S(1)}, f32[130,4]{1,0:T(8,128)S(1)}, u32[]{:S(2)}, u32[]{:S(2)}) collective-permute-start(f32[130,4]{1,0:T(8,128)S(1)} %get-tuple-element.123), channel_id=1, source_target_pairs={{0,2},{2,4},{4,6},{6,8},{8,10},{10,12},{12,14},{14,16},{16,18},{18... | collective-permute-start | bytes 6248 | tf_op jit(solution)/shard_map/ppermute | solution.py:24
  44.1 24.3 %copy-start.4 = (f32[256]{0:T(256)S(1)}, f32[256]{0:T(256)}, u32[]{:S(2)}) copy-start(f32[256]{0:T(256)} %param.18) | copy-start | bytes 3076
  44.1 24.3 %copy-start.9 = (f32[256]{0:T(256)S(1)}, f32[256]{0:T(256)}, u32[]{:S(2)}) copy-start(f32[256]{0:T(256)} %param.17) | copy-start | bytes 3076
  44.1 97.1 %copy-start.10 = (f32[65]{0:T(128)S(1)}, f32[65]{0:T(128)}, u32[]{:S(2)}) copy-start(f32[65]{0:T(128)} %constant.117.clone.1) | copy-start | bytes 784
  47.4 16.7 %all-to-all-start.1 = ((f32[16,1,1024]{2,1,0:T(1,128)}), f32[16,1,1024]{2,1,0:T(1,128)S(1)}, u32[]{:S(2)}, u32[]{:S(2)}) async-start(f32[16,1,1024]{2,1,0:T(1,128)} %reshape.352), calls=%async_computation.1 | async-start | bytes 131072 | tf_op jit(solution)/shard_map/all_to_all | solution.py:134
  56.6 217.0 %reduce-scatter.2.cloned.1.call-start = ((), (), s32[]{:S(2)}) async-start(), calls=%async_computation.3 | async-start | bytes 1572864 | tf_op jit(solution)/shard_map/reduce_scatter | solution.py:150
  68.4 200.7 %copy-start.5 = (f32[256]{0:T(256)}, f32[256]{0:T(256)S(1)}, u32[]{:S(2)}) copy-start(f32[256]{0:T(256)S(1)} %get-tuple-element.127) | copy-start | bytes 3076
Sparse Core Ops, SparseCore 0:
  269.2 4.4 reduce-scatter.1
where the time goes:
time: 288 us; the launch traced here: 283 us
  local copies, waits for them, and re-layouts  80.7 us (28%)
  blocking collectives  74.4 us (26%)
  loops' own time  47.1 us (16%)
  matrix products  24.5 us (9%)
  starting transfers between devices  23.4 us (8%)
  between operations  14.6 us (5%)
  waiting for transfers between devices  13.8 us (5%)
  other arithmetic  4.11 us (1%)
    psum x1, blocking collectives, shards(): summed_gram = lax.psum(local_gram, 'cells')  72.6 us
    another operation x1, loops' own time, factor_lower(): return lax.fori_loop(0, order, column_step, jnp.zeros_like(matrix))  47.1 us
    dynamic_slice x65, local copies, waits for them, and re-layouts, column_step(): pivot = jnp.sqrt(lax.dynamic_slice_in_dim(reduced, col, 1, 0)[0])  40.2 us
    dynamic_update_slice x65, local copies, waits for them, and re-layouts, column_step(): return lax.dynamic_update_slice_in_dim(lower, values[:, None], col, 1)  16.2 us
    dot_general x65, matrix products, column_step(): reduced = column - jnp.dot(lower, done_row, precision=lax.Precision.HIGHEST)  9.65 us
    all_to_all x1, starting transfers between devices, shards(): lax.all_to_all(found_values, 'cells', split_axis=1, concat_axis=1, tiled=...  9.2 us
    dot_general x4, matrix products, couple_fields(): jnp.einsum('fg,kgc->kfc', couple, advanced, precision=lax.Precision.HIGHEST)  8.64 us
    all_to_all x1, starting transfers between devices, shards(): lax.all_to_all(request, 'cells', split_axis=0, concat_axis=0, tiled=True)  8.31 us
  transfers between devices with their start and end apart: 5, of which 3 were waited for; matrix products, arithmetic and copies ran while one was open for 4% of the time, Pallas kernels for 0%

commit v1 on v0

v1 whole, which is shorter than its diff:
```python
import functools
import math

import jax
import jax.numpy as jnp
from jax import lax
from jax.experimental import pallas as pl
from jax.experimental.pallas import tpu as pltpu
from jax.sharding import PartitionSpec as P

STEPS = 4
DIFFUSION = 0.05
LANES = 128
BOTH = ("cells", "members")
EXACT = lax.Precision.HIGHEST
VMEM_BYTES = 48 * 1024 * 1024


def core_pairs(owners, place):
    pairs = []
    for block in range(owners):
        for core in range(2):
            to_block, to_core = place(block, core)
            pairs.append((block * 2 + core, to_block * 2 + to_core))
    return pairs


def stage_units(owners):
    units = []
    unit = 1
    while unit < owners:
        radix = 4 if unit * 4 <= owners else 2
        units.append((unit, radix))
        unit *= radix
    return units


def swap_cores(x, owners):
    return lax.ppermute(x, BOTH, core_pairs(owners, lambda block, core: (block, 1 - core)))


def exchange(x, owners, unit, radix):
    if radix == 2:
        return (lax.ppermute(x, BOTH, core_pairs(owners, lambda block, core: (block ^ unit, core))),)
    first = lax.ppermute(
        x, BOTH, core_pairs(owners, lambda block, core: (block ^ (unit * (1 + core)), core))
    )
    third = lax.ppermute(x, BOTH, core_pairs(owners, lambda block, core: (block ^ (unit * 3), core)))
    return first, swap_cores(first, owners), third


def stage_slot(units, block, target, core):
    distance = jnp.bitwise_xor(block, target)
    side = core
    place = jnp.zeros_like(target)
    for unit, radix in reversed(units):
        digit = lax.rem(lax.div(distance, jnp.int32(unit)), jnp.int32(radix))
        if radix == 4:
            middle = (digit == 1) | (digit == 2)
            own_side = digit == 1 + side
            slot = jnp.where(middle, jnp.where(own_side, 1, 2), digit)
            side = jnp.where(middle & ~own_side, 1 - side, side)
        else:
            slot = digit
        place = place + slot * unit
    return place


def pack_kernel(
    send_ref, mine_head, mine_tail, other_head, other_tail, speed_ref, flag_ref, place_ref, field_ref,
    value_ref, sigma_ref, which_ref, out_ref, *, cells, fields, rows,
):
    own_core = which_ref[1]
    members = mine_head.shape[0]
    for own, head, tail in ((True, mine_head, mine_tail), (False, other_head, other_tail)):
        head_rows = jnp.concatenate([head[:, f, :] for f in range(fields)], axis=0)
        tail_rows = jnp.concatenate([tail[:, f, :] for f in range(fields)], axis=0)
        first = jnp.transpose(head_rows)[:STEPS, :]
        last = jnp.transpose(tail_rows)[LANES - STEPS :, :]
        strip = jnp.concatenate([first, last], axis=0)
        core = own_core if own else 1 - own_core
        out_ref[pl.ds(pl.multiple_of(core * 8, 8), 8), :] = strip
    slots = (
        lax.broadcasted_iota(jnp.int32, (rows, LANES), 0) * LANES
        + lax.broadcasted_iota(jnp.int32, (rows, LANES), 1)
    )
    owner = jnp.zeros((rows, LANES), jnp.int32)
    end = jnp.int32(0)
    for d in range(send_ref.shape[1]):
        end = end + send_ref[0, d]
        owner = owner + jnp.where(slots >= end, 1, 0)
    ids = (owner * fields + field_ref[...]) * cells + place_ref[...]
    weight = 1.0 / (sigma_ref[...] * sigma_ref[...])
    base = 16
    out_ref[base : base + rows, :] = ids.astype(jnp.float32)
    out_ref[base + rows : base + 2 * rows, :] = weight
    out_ref[base + 2 * rows : base + 3 * rows, :] = weight * value_ref[...]
    tiles = speed_ref.shape[0]
    lane = lax.broadcasted_iota(jnp.int32, (1, LANES), 1)
    toward_left = speed_ref[...] * flag_ref[...].astype(jnp.float32)
    toward_right = speed_ref[...] - toward_left
    low = lane < LANES // 2
    base = base + 3 * rows
    out_ref[base : base + 1, :] = jnp.where(low, toward_left[:1], toward_left[tiles - 1 :])
    out_ref[base + 1 : base + 2, :] = jnp.where(low, toward_right[:1], toward_right[tiles - 1 :])


def pieces_of(x):
    high = x.astype(jnp.bfloat16).astype(jnp.float32)
    rest = x - high
    middle = rest.astype(jnp.bfloat16).astype(jnp.float32)
    return high, middle, rest - middle


def forecast_kernel(
    which_ref, couple_ref, mine_ref, other_ref, speed_ref, flag_ref, *refs, owners, parts, block_rows, obs_rows,
):
    gathered = refs[:parts]
    state_ref, sums_ref, halo_ref, work_ref, all_ref, mean_ref, onehot_ref, spread_ref, weighted_ref, plain_ref, found_ref = refs[parts:]
    block, core = which_ref[0], which_ref[1]
    left_slot = which_ref[2 + jnp.maximum(block - 1, 0)]
    right_slot = which_ref[2 + jnp.minimum(block + 1, owners - 1)]
    members, fields, cells = mine_ref.shape
    tiles = cells // LANES
    total = 2 * members
    places = fields * tiles
    part_rows = gathered[0].shape[0]
    for p in range(parts):
        all_ref[p * part_rows : (p + 1) * part_rows, :] = gathered[p][...]
    left_at = pl.multiple_of(left_slot * block_rows, 8)
    right_at = pl.multiple_of(right_slot * block_rows, 8)
    has_left = (block > 0).astype(jnp.float32)
    has_right = (block < owners - 1).astype(jnp.float32)
    sub = lax.broadcasted_iota(jnp.int32, (8, LANES), 0)
    lane = lax.broadcasted_iota(jnp.int32, (1, LANES), 1)

    strip_rows = fields * members
    for half in range(2):
        left = all_ref[pl.ds(left_at + 8 * half, 8), :]
        right = all_ref[pl.ds(right_at + 8 * half, 8), :]
        top = jnp.where(sub < STEPS, right * has_right, 0.0)
        bottom = jnp.where(sub >= 8 - STEPS, left * has_left, 0.0)
        tile = jnp.concatenate(
            [top, jnp.zeros((LANES - 16, LANES), jnp.float32), bottom], axis=0
        )
        halo_ref[half * strip_rows : (half + 1) * strip_rows, :] = jnp.transpose(tile)
    coef_at = block_rows - 8
    left_coef = all_ref[pl.ds(left_at + coef_at, 8), :]
    right_coef = all_ref[pl.ds(right_at + coef_at, 8), :]
    low = lane < LANES // 2
    inside = jnp.where(low, has_right, has_left)
    row = 16 + 3 * obs_rows - coef_at
    halo_left = jnp.where(low, right_coef[row : row + 1], left_coef[row : row + 1])
    halo_right = jnp.where(low, right_coef[row + 1 : row + 2], left_coef[row + 1 : row + 2])
    speed = speed_ref[...]
    toward_left = speed * flag_ref[...].astype(jnp.float32)
    toward_right = speed - toward_left
    from_left = [toward_left[t : t + 1] + DIFFUSION for t in range(tiles)]
    from_right = [toward_right[t : t + 1] + DIFFUSION for t in range(tiles)]
    stay = [1.0 - 2.0 * DIFFUSION - speed[t : t + 1] for t in range(tiles)]
    from_left.append((halo_left + DIFFUSION) * inside)
    from_right.append((halo_right + DIFFUSION) * inside)
    stay.append((1.0 - 2.0 * DIFFUSION - halo_left - halo_right) * inside)

    def wide(parts_of):
        return jnp.broadcast_to(jnp.concatenate(parts_of, axis=1), (8, LANES * (tiles + 1)))

    from_left, from_right, stay = wide(from_left), wide(from_right), wide(stay)
    width = LANES * (tiles + 1)

    mix = [[couple_ref[f, g] + (1.0 if f == g else 0.0) for g in range(fields)] for f in range(fields)]
    for _ in range(2):
        mix = [
            [sum(mix[f][h] * mix[h][g] for h in range(fields)) for g in range(fields)]
            for f in range(fields)
        ]

    mean_ref[...] = jnp.zeros_like(mean_ref)
    for half_of, source in ((core, mine_ref), (1 - core, other_ref)):

        def group(i, _, half_of=half_of, source=source):
            at = pl.multiple_of(i * 8, 8)
            for f in range(fields):
                halo_at = pl.multiple_of(half_of * strip_rows + f * members + at, 8)
                x = jnp.concatenate(
                    [source[pl.ds(at, 8), f, :], halo_ref[pl.ds(halo_at, 8), :]], axis=1
                )
                for _ in range(STEPS):
                    x = (
                        from_left * pltpu.roll(x, 1, 1)
                        + stay * x
                        + from_right * pltpu.roll(x, width - 1, 1)
                    )
                work_ref[f * 8 : (f + 1) * 8, :] = x[:, :cells]
            into = pl.multiple_of(half_of * members + at, 8)
            for t in range(tiles):
                lanes = slice(t * LANES, (t + 1) * LANES)
                moved = [work_ref[f * 8 : (f + 1) * 8, lanes] for f in range(fields)]
                for f in range(fields):
                    value = sum(mix[f][g] * moved[g] for g in range(fields))
                    state_ref[pl.ds(f * total + into, 8), lanes] = value
                    at_mean = (f * tiles + t) * 8
                    mean_ref[at_mean : at_mean + 8, :] += value
            return 0

        lax.fori_loop(0, members // 8, group, 0)

    mean = jnp.concatenate(
        [jnp.sum(mean_ref[p * 8 : (p + 1) * 8, :], axis=0, keepdims=True) for p in range(places)],
        axis=0,
    ) * (1.0 / total)

    place_ids = lax.broadcasted_iota(jnp.int32, (places, LANES), 0)
    lane_ids = lax.broadcasted_iota(jnp.int32, (LANES, LANES), 0)
    start = block * (fields * cells)

    def spread(i, _):
        at = i * block_rows + 16
        rows = all_ref[pl.ds(pl.multiple_of(at, 8), 8), :]
        for r in range(obs_rows):
            local = rows[r : r + 1].astype(jnp.int32) - start
            hit = place_ids == lax.shift_right_arithmetic(local, 7)
            onehot = (lane_ids == jnp.bitwise_and(local, LANES - 1)).astype(jnp.float32)
            lanes = pl.ds(pl.multiple_of((i * obs_rows + r) * LANES, LANES), LANES)
            onehot_ref[:, lanes] = onehot.astype(jnp.bfloat16)
            weight = rows[obs_rows + r : obs_rows + r + 1]
            pull = rows[2 * obs_rows + r : 2 * obs_rows + r + 1]
            stack = [jnp.where(hit, piece, 0.0) for piece in pieces_of(weight) + pieces_of(pull)]
            spread_ref[:, lanes] = jnp.concatenate(stack, axis=0).astype(jnp.bfloat16)
        return 0

    lax.fori_loop(0, owners, spread, 0)
    placed = lax.dot_general(
        spread_ref[...], onehot_ref[...], (((1,), (1,)), ((), ())), preferred_element_type=jnp.float32
    )
    placed = [placed[p * places : (p + 1) * places] for p in range(6)]
    weight = placed[0] + placed[1] + placed[2]
    pull = placed[3] + placed[4] + placed[5] - weight * mean

    for f in range(fields):
        for t in range(tiles):
            at = f * tiles + t
            lanes = slice(t * LANES, (t + 1) * LANES)
            into = slice(at * LANES, (at + 1) * LANES)
            anomaly = state_ref[f * total : (f + 1) * total, lanes] - mean[at : at + 1]
            plain_ref[:, into] = anomaly
            weighted_ref[:total, into] = anomaly * weight[at : at + 1]
            weighted_ref[total : total + 8, into] = jnp.where(sub == 0, pull[at : at + 1], 0.0)
    gram = lax.dot_general(
        weighted_ref[...], plain_ref[...], (((1,), (1,)), ((), ())),
        precision=EXACT, preferred_element_type=jnp.float32,
    )
    gram = jnp.concatenate([gram, jnp.zeros((total + 8, LANES - total), jnp.float32)], axis=1)
    sums_ref[:members, :] = gram[:members] + pltpu.roll(gram[members:total], total, 1)
    sums_ref[members : members + 8, :] = gram[total:]

    found = lax.dot_general(
        jnp.concatenate(pieces_of(mean), axis=0).astype(jnp.bfloat16), onehot_ref[...],
        (((1,), (0,)), ((), ())), preferred_element_type=jnp.float32,
    )
    found_ref[...] = found[:places] + found[places : 2 * places] + found[2 * places :]
    for i in range(owners):
        slot = which_ref[2 + i]
        rows = all_ref[pl.ds(pl.multiple_of(slot * block_rows + 16, 8), 8), :]
        for r in range(obs_rows):
            local = rows[r : r + 1].astype(jnp.int32) - start
            hit = place_ids == lax.shift_right_arithmetic(local, 7)
            lanes = pl.ds(pl.multiple_of((slot * obs_rows + r) * LANES, LANES), LANES)
            into = members + 8 + i * obs_rows + r
            sums_ref[into : into + 1, :] = jnp.sum(
                jnp.where(hit, found_ref[:, lanes], 0.0), axis=0, keepdims=True
            )


def spread_row(row):
    return jnp.broadcast_to(row, (8, LANES))


def eliminate(rows):
    count = len(rows)
    rows = list(rows)
    sub = lax.broadcasted_iota(jnp.int32, (8, LANES), 0)
    for b in range(count):
        columns = [
            [jnp.broadcast_to(rows[i][:, 8 * b + k : 8 * b + k + 1], (8, LANES)) for k in range(8)]
            for i in range(b, count)
        ]
        for j in range(8):
            scale = lax.rsqrt(spread_row(columns[0][j][j : j + 1, :]))
            upper = spread_row(rows[b][j : j + 1, :]) * scale
            lower = columns[0][j] * scale
            factors = [spread_row(lower[k : k + 1, :]) for k in range(8)]
            for i in range(b, count):
                here = lower if i == b else columns[i - b][j] * scale
                if i == b:
                    rows[b] = jnp.where(sub == j, upper, rows[b] - jnp.where(sub > j, here, 0.0) * upper)
                else:
                    rows[i] = rows[i] - here * upper
                for k in range(j + 1, 8):
                    columns[i - b][k] = columns[i - b][k] - here * factors[k]
    return rows


def analysis_kernel(which_ref, state_ref, value_ref, sigma_ref, *refs, parts, obs_rows):
    pieces = refs[:parts]
    analysis_ref, innovation_ref, mixing_ref, center_ref = refs[parts:]
    block, core = which_ref[0], which_ref[1]
    members, fields, cells = analysis_ref.shape
    total = 2 * members
    if parts == 4:
        sums = (pieces[0][...] + pieces[3][...]) + (pieces[1][...] + pieces[2][...])
    else:
        sums = pieces[0][...] + pieces[1][...]
    center_ref[...] = sums[members + 8 :]
    lane = lax.broadcasted_iota(jnp.int32, (8, LANES), 1)
    sub = lax.broadcasted_iota(jnp.int32, (8, LANES), 0)
    shifted = pltpu.roll(sums[:members], LANES - total, 1)
    rows = []
    for b in range(total // 8):
        at = 8 * b
        source = sums[at : at + 8] if at < members else shifted[at - members : at - members + 8]
        own = jnp.where(lane == sub + at, total - 1.0, 0.0)
        unit = jnp.where(lane == sub + at + total, 1.0, 0.0)
        rows.append(jnp.where(lane < total, source + own, unit))
    rows = eliminate(rows)
    cross = sums[members : members + 1]
    inverse = [jnp.where(lane < total, pltpu.roll(r, LANES - total, 1), 0.0) for r in rows]
    carried = [jnp.sum(r * cross, axis=1, keepdims=True) for r in inverse]
    weights = sum(jnp.sum(r * c, axis=0, keepdims=True) for r, c in zip(inverse, carried))
    row_means = [jnp.sum(r, axis=1, keepdims=True) * (1.0 / total) for r in inverse]
    column_mean = sum(jnp.sum(r, axis=0, keepdims=True) for r in inverse) * (1.0 / total)
    grand = jnp.sum(column_mean, axis=1, keepdims=True) * (1.0 / total)
    weights = weights - jnp.sum(weights, axis=1, keepdims=True) * (1.0 / total)
    root = math.sqrt(total - 1.0)
    add = weights + 1.0 / total - root * (column_mean - grand)
    for b in range(total // 8):
        mixing_ref[8 * b : 8 * b + 8, :] = root * (inverse[b] - row_means[b]) + add
    own_rows = mixing_ref[pl.ds(pl.multiple_of(core * members, 8), members), :][:, :total]
    for f in range(fields):
        analysis_ref[:, f, :] = jnp.dot(
            own_rows, state_ref[f * total : (f + 1) * total, :],
            precision=EXACT, preferred_element_type=jnp.float32,
        )
    for r in range(obs_rows):
        center = center_ref[pl.ds(block * obs_rows + r, 1), :]
        innovation_ref[r : r + 1, :] = (value_ref[r : r + 1, :] - center) / sigma_ref[r : r + 1, :]


def shards(
    ensemble, speed, direction, couple, obs_place, obs_field, obs_value, obs_sigma, send_count
):
    members, fields, cells = ensemble.shape
    owners = lax.axis_size("cells")
    total = members * lax.axis_size("members")
    obs = obs_place.shape[0]
    obs_rows = obs // LANES
    tiles = cells // LANES
    places = fields * tiles
    units = stage_units(owners)
    block = lax.axis_index("cells").astype(jnp.int32)
    core = lax.axis_index("members").astype(jnp.int32)
    slots = stage_slot(units, block, jnp.arange(owners, dtype=jnp.int32), core)
    which = jnp.concatenate([jnp.stack([block, core]), slots])
    speed = speed.reshape(tiles, LANES)
    direction = direction.reshape(tiles, LANES)
    obs_place, obs_field, obs_value, obs_sigma = (
        x.reshape(obs_rows, LANES) for x in (obs_place, obs_field, obs_value, obs_sigma)
    )
    whole = pl.BlockSpec(memory_space=pltpu.VMEM)
    scalars = pl.BlockSpec(memory_space=pltpu.SMEM)
    params = pltpu.CompilerParams(vmem_limit_bytes=VMEM_BYTES)

    other = swap_cores(ensemble, owners)

    block_rows = -(-(16 + 3 * obs_rows + 2) // 8) * 8
    head = pl.BlockSpec((members, fields, LANES), lambda i: (0, 0, 0))
    tail = pl.BlockSpec((members, fields, LANES), lambda i: (0, 0, tiles - 1))
    flat = lambda x: pl.BlockSpec(x.shape, lambda i: (0, 0))
    packed = pl.pallas_call(
        functools.partial(pack_kernel, cells=cells, fields=fields, rows=obs_rows),
        out_shape=jax.ShapeDtypeStruct((block_rows, LANES), jnp.float32),
        grid=(1,),
        in_specs=[scalars, head, tail, head, tail]
        + [flat(x) for x in (speed, direction, obs_place, obs_field, obs_value, obs_sigma)]
        + [scalars],
        out_specs=pl.BlockSpec((block_rows, LANES), lambda i: (0, 0)),
        compiler_params=params,
        name="pack",
    )(
        send_count, ensemble, ensemble, other, other, speed, direction, obs_place, obs_field,
        obs_value, obs_sigma, which,
    )

    pieces = (packed,)
    for unit, radix in units:
        packed = jnp.concatenate(pieces, axis=0) if len(pieces) > 1 else pieces[0]
        pieces = (packed,) + exchange(packed, owners, unit, radix)

    sums_rows = members + 8 + owners * obs_rows
    all_obs = owners * obs
    states, sums = pl.pallas_call(
        functools.partial(
            forecast_kernel, owners=owners, parts=len(pieces), block_rows=block_rows, obs_rows=obs_rows
        ),
        out_shape=(
            jax.ShapeDtypeStruct((fields * total, cells), jnp.float32),
            jax.ShapeDtypeStruct((sums_rows, LANES), jnp.float32),
        ),
        in_specs=[scalars, scalars] + [whole] * (4 + len(pieces)),
        out_specs=(whole, whole),
        scratch_shapes=[
            pltpu.VMEM((2 * fields * members, LANES), jnp.float32),
            pltpu.VMEM((fields * 8, cells), jnp.float32),
            pltpu.VMEM((owners * block_rows, LANES), jnp.float32),
            pltpu.VMEM((places * 8, LANES), jnp.float32),
            pltpu.VMEM((LANES, all_obs), jnp.bfloat16),
            pltpu.VMEM((6 * places, all_obs), jnp.bfloat16),
            pltpu.VMEM((total + 8, fields * cells), jnp.float32),
            pltpu.VMEM((total, fields * cells), jnp.float32),
            pltpu.VMEM((places, all_obs), jnp.float32),
        ],
        compiler_params=params,
        name="forecast",
    )(which, couple, ensemble, other, speed, direction, *pieces)

    pieces = (sums,)
    for unit, radix in units:
        if len(pieces) == 4:
            sums = (pieces[0] + pieces[3]) + (pieces[1] + pieces[2])
        elif len(pieces) == 2:
            sums = pieces[0] + pieces[1]
        pieces = (sums,) + exchange(sums, owners, unit, radix)

    analysis, innovation = pl.pallas_call(
        functools.partial(analysis_kernel, parts=len(pieces), obs_rows=obs_rows),
        out_shape=(
            jax.ShapeDtypeStruct((members, fields, cells), jnp.float32),
            jax.ShapeDtypeStruct((obs_rows, LANES), jnp.float32),
        ),
        in_specs=[scalars] + [whole] * (3 + len(pieces)),
        out_specs=(whole, whole),
        scratch_shapes=[
            pltpu.VMEM((total, LANES), jnp.float32),
            pltpu.VMEM((owners * obs_rows, LANES), jnp.float32),
        ],
        compiler_params=params,
        name="analysis",
    )(which, states, obs_value, obs_sigma, *pieces)
    return (analysis, innovation.reshape(obs))


def solution(mesh):
    return jax.shard_map(
        shards,
        mesh=mesh,
        in_specs=(
            P("members", None, "cells"),
            P("cells"),
            P("cells"),
            P(),
            P("cells"),
            P("cells"),
            P("cells"),
            P("cells"),
            P("cells", None),
        ),
        out_specs=(P("members", None, "cells"), P("cells")),
        check_vma=False,
    )
```

time: 288 us -> 45.5 us (0.16); the launches traced: 283 us -> 45.3 us
  local copies, waits for them, and re-layouts: 80.7 us -> 1.77 us
  blocking collectives: 74.4 us -> 0 us
  loops' own time: 47.1 us -> 0 us
  matrix products: 24.5 us -> 0 us
  between operations: 14.6 us -> 0.71 us
  Pallas kernels: 0 us -> 13.4 us
  starting transfers between devices: 23.4 us -> 14.6 us
  other arithmetic: 4.11 us -> 0.12 us
    psum x1 -> x0, blocking collectives: 72.6 us -> none  [shards(): summed_gram = lax.psum(local_gram, 'cells')]
    another operation x1 -> x0, loops' own time: 47.1 us -> none  [factor_lower(): return lax.fori_loop(0, order, column_step, jnp.zeros_like(matrix))]
    dynamic_slice x66 -> x0, local copies, waits for them, and re-layouts: 40.3 us -> none  [the longest x65 40.2 us: column_step(): pivot = jnp.sqrt(lax.dynamic_slice_in_dim(reduced, col, 1, 0)[0])]
    dot_general x85 -> x0, matrix products: 24.5 us -> none  [the longest x65 9.65 us: column_step(): reduced = column - jnp.dot(lower, done_row, precision=lax.Precision.HIGHEST)]
    all_to_all x2 -> x0, starting transfers between devices: 17.5 us -> none  [the longest x1 9.2 us: shards(): lax.all_to_all(found_values, 'cells', split_axis=1, concat_axis=1, tiled=...]
    dynamic_update_slice x65 -> x0, local copies, waits for them, and re-layouts: 16.2 us -> none  [column_step(): return lax.dynamic_update_slice_in_dim(lower, values[:, None], col, 1)]
    pallas_call x0 -> x3, Pallas kernels: none -> 13.4 us  [the longest x1 8.76 us: shards(): pl.pallas_call(functools.partial(forecast_kernel, owners=owners, parts=le...]
    ppermute x2 -> x13, waiting for transfers between devices: 1.8 us -> 14.7 us  [the longest x8 13 us: exchange(): lax.ppermute(x, BOTH, core_pairs(owners, lambda block, core: (block ^ uni...]
  transfers between devices with their start and end apart: 5 -> 13, of which waited for: 3 -> 8; matrix products, arithmetic and copies ran while one was open for 4% -> 0% of each run, Pallas kernels for 0% -> 0%
where the time goes in v1:
time: 45.5 us; the launch traced here: 45.3 us
  waiting for transfers between devices  14.7 us (32%)
  starting transfers between devices  14.6 us (32%)
  Pallas kernels  13.4 us (29%)
  local copies, waits for them, and re-layouts  1.77 us (4%)
  between operations  0.71 us (2%)
    ppermute x8, starting transfers between devices, exchange(): lax.ppermute(x, BOTH, core_pairs(owners, lambda block, core: (block ^ uni...  14.1 us
    ppermute x8, waiting for transfers between devices, exchange(): lax.ppermute(x, BOTH, core_pairs(owners, lambda block, core: (block ^ uni...  13 us
    pallas_call x1, Pallas kernels, shards(): pl.pallas_call(functools.partial(forecast_kernel, owners=owners, parts=le...  8.76 us
    pallas_call x1, Pallas kernels, shards(): pl.pallas_call(functools.partial(analysis_kernel, parts=len(pieces), obs_...  3.9 us
    unnamed x20, local copies, waits for them, and re-layouts  1.77 us
    ppermute x5, waiting for transfers between devices, swap_cores(): lax.ppermute(x, BOTH, core_pairs(owners, lambda block, core: (block, 1 -...  1.63 us
  transfers between devices with their start and end apart: 13, of which 8 were waited for; matrix products, arithmetic and copies ran while one was open for 0% of the time, Pallas kernels for 0%

profile of v1, /device:TPU:0, one launch (start us, length us, event | category | flops | bytes accessed | tf_op | source)
XLA Modules:
  0.0 45.3 jit_solution(14883123551001279217)
XLA Ops:
  0.6 0.5 %collective-permute-start = (f32[32,4,1024]{2,1,0:T(4,128)}, f32[32,4,1024]{2,1,0:T(4,128)S(1)}, u32[]{:S(2)}, u32[]{:S(2)}) collective-permute-start(f32[32,4,1024]{2,1,0:T(4,128)} %mine_ref.1), channel_id=1, source_target_pairs={{0,1},{1,0},{2,3},{3,2},{4,5},{5,4},{6,7},{7,6},{8,9},{9,8},{10,11... | collective-permute-start | bytes 1572872 | tf_op jit(solution)/shard_map/ppermute | solution.py:39
  1.2 0.1 pad_add_fusion.which_ref
  1.3 1.6 %collective-permute-done.other_head.other_tail.other_ref = f32[32,4,1024]{2,1,0:T(4,128)S(1)} collective-permute-done((f32[32,4,1024]{2,1,0:T(4,128)}, f32[32,4,1024]{2,1,0:T(4,128)S(1)}, u32[]{:S(2)}, u32[]{:S(2)}) %collective-permute-start) | collective-permute-done | bytes 524320 | tf_op jit(solution)/shard_map/ppermute | solution.py:39
  2.9 0.6 %copy-done.5 = f32[256]{0:T(256)S(1)} copy-done((f32[256]{0:T(256)S(1)}, f32[256]{0:T(256)}, u32[]{:S(2)}) %copy-start.5) | copy-done | bytes 1048
  3.6 1.0 %copy-done = f32[32,4,1024]{2,1,0:T(4,128)S(1)} copy-done((f32[32,4,1024]{2,1,0:T(4,128)S(1)}, f32[32,4,1024]{2,1,0:T(4,128)}, u32[]{:S(2)}) %copy-start) | copy-done | bytes 524312
  4.7 0.8 %pack.1 = f32[24,128]{1,0:T(8,128)S(1)} custom-call(s32[1,16]{1,0:T(1,128)S(1)} %copy-done.9, f32[32,4,1024]{2,1,0:T(4,128)S(1)} %copy-done, f32[32,4,1024]{2,1,0:T(4,128)S(1)} %copy-done, f32[32,4,1024]{2,1,0:T(4,128)S(1)} %collective-permute-done.other_head.other_tail.other_ref, f32[32,4,1024]{2,1,0:T(4,128)S(1)} %collective-permute-done.other_head.other_tail.other_ref, ...), custom_call_target="tpu_custom_call" | custom-call | tf_op jit(solution)/shard_map/pack/pallas_call | solution.py:379
  5.5 2.9 %collective-permute-start.1 = (f32[24,128]{1,0:T(8,128)S(1)}, f32[24,128]{1,0:T(8,128)S(1)}, u32[]{:S(2)}, u32[]{:S(2)}) collective-permute-start(f32[24,128]{1,0:T(8,128)S(1)} %pack.1), channel_id=1, source_target_pairs={{0,2},{1,5},{2,0},{3,7},{4,6},{5,1},{6,4},{7,3},{8,10},{9,13},{10,... | collective-permute-start | bytes 36872 | tf_op jit(solution)/shard_map/ppermute | solution.py:45
  8.4 1.5 %collective-permute-start.3 = (f32[24,128]{1,0:T(8,128)S(1)}, f32[24,128]{1,0:T(8,128)S(1)}, u32[]{:S(2)}, u32[]{:S(2)}) collective-permute-start(f32[24,128]{1,0:T(8,128)S(1)} %pack.1), channel_id=1, source_target_pairs={{0,6},{1,7},{2,4},{3,5},{4,2},{5,3},{6,0},{7,1},{8,14},{9,15},{10,... | collective-permute-start | bytes 36872 | tf_op jit(solution)/shard_map/ppermute | solution.py:48
  9.9 0.2 collective-permute-done.1
  10.1 2.9 %collective-permute-done.3 = f32[24,128]{1,0:T(8,128)S(1)} collective-permute-done((f32[24,128]{1,0:T(8,128)S(1)}, f32[24,128]{1,0:T(8,128)S(1)}, u32[]{:S(2)}, u32[]{:S(2)}) %collective-permute-start.3) | collective-permute-done | bytes 12320 | tf_op jit(solution)/shard_map/ppermute | solution.py:48
  13.0 1.6 %collective-permute-start.4 = (f32[96,128]{1,0:T(8,128)S(1)}, f32[96,128]{1,0:T(8,128)S(1)}, u32[]{:S(2)}, u32[]{:S(2)}) collective-permute-start(f32[96,128]{1,0:T(8,128)S(1)} %pad_maximum_fusion.refs_0_), channel_id=1, source_target_pairs={{0,8},{1,17},{2,10},{3,19},{4,12},{5,21},{6,14},{7,23},{8,0},{9,25... | collective-permute-start | bytes 147464 | tf_op jit(solution)/shard_map/ppermute | solution.py:45
  14.6 2.5 %collective-permute-start.6 = (f32[96,128]{1,0:T(8,128)S(1)}, f32[96,128]{1,0:T(8,128)S(1)}, u32[]{:S(2)}, u32[]{:S(2)}) collective-permute-start(f32[96,128]{1,0:T(8,128)S(1)} %pad_maximum_fusion.refs_0_), channel_id=1, source_target_pairs={{0,24},{1,25},{2,26},{3,27},{4,28},{5,29},{6,30},{7,31},{8,16},{9,... | collective-permute-start | bytes 147464 | tf_op jit(solution)/shard_map/ppermute | solution.py:48
  17.1 0.0 collective-permute-done.4.refs_1_
  17.1 3.4 %collective-permute-done.6.refs_3_ = f32[96,128]{1,0:T(8,128)S(1)} collective-permute-done((f32[96,128]{1,0:T(8,128)S(1)}, f32[96,128]{1,0:T(8,128)S(1)}, u32[]{:S(2)}, u32[]{:S(2)}) %collective-permute-start.6) | collective-permute-done | bytes 49184 | tf_op jit(solution)/shard_map/ppermute | solution.py:48
  20.5 8.8 %forecast.1 = (f32[256,1024]{1,0:T(8,128)S(1)}, f32[72,128]{1,0:T(8,128)S(1)}) custom-call(s32[18]{0:T(128)S(1)} %pad_add_fusion.which_ref, f32[4,4]{1,0:T(4,128)S(1)} %copy-done.6, f32[32,4,1024]{2,1,0:T(4,128)S(1)} %copy-done.1, f32[32,4,1024]{2,1,0:T(4,128)S(1)} %collective-permute-done.other_head.other_tail.other_ref, f32[8,128]{1,0:T(8,128)S(1)} %bitcast.10, ...), custom_call_target="tpu_custom_call" | custom-call | tf_op jit(solution)/shard_map/forecast/pallas_call | solution.py:401
  29.3 0.8 %collective-permute-start.8 = (f32[72,128]{1,0:T(8,128)S(1)}, f32[72,128]{1,0:T(8,128)S(1)}, u32[]{:S(2)}, u32[]{:S(2)}) collective-permute-start(f32[72,128]{1,0:T(8,128)S(1)} %get-tuple-element.7), channel_id=1, source_target_pairs={{0,2},{1,5},{2,0},{3,7},{4,6},{5,1},{6,4},{7,3},{8,10},{9,13},{10,... | collective-permute-start | bytes 110600 | tf_op jit(solution)/shard_map/ppermute | solution.py:45
  30.1 2.2 %collective-permute-start.7 = (f32[72,128]{1,0:T(8,128)S(1)}, f32[72,128]{1,0:T(8,128)S(1)}, u32[]{:S(2)}, u32[]{:S(2)}) collective-permute-start(f32[72,128]{1,0:T(8,128)S(1)} %get-tuple-element.7), channel_id=1, source_target_pairs={{0,6},{1,7},{2,4},{3,5},{4,2},{5,3},{6,0},{7,1},{8,14},{9,15},{10,... | collective-permute-start | bytes 110600 | tf_op jit(solution)/shard_map/ppermute | solution.py:48
  32.3 1.0 %collective-permute-done.8 = f32[72,128]{1,0:T(8,128)S(1)} collective-permute-done((f32[72,128]{1,0:T(8,128)S(1)}, f32[72,128]{1,0:T(8,128)S(1)}, u32[]{:S(2)}, u32[]{:S(2)}) %collective-permute-start.8) | collective-permute-done | bytes 36896 | tf_op jit(solution)/shard_map/ppermute | solution.py:45
  33.3 1.7 %collective-permute-done.7 = f32[72,128]{1,0:T(8,128)S(1)} collective-permute-done((f32[72,128]{1,0:T(8,128)S(1)}, f32[72,128]{1,0:T(8,128)S(1)}, u32[]{:S(2)}, u32[]{:S(2)}) %collective-permute-start.7) | collective-permute-done | bytes 36896 | tf_op jit(solution)/shard_map/ppermute | solution.py:48
  35.0 0.7 %collective-permute-start.10 = (f32[72,128]{1,0:T(8,128)S(1)}, f32[72,128]{1,0:T(8,128)S(1)}, u32[]{:S(2)}, u32[]{:S(2)}) collective-permute-start(f32[72,128]{1,0:T(8,128)S(1)} %add_add_fusion.refs_0_), channel_id=1, source_target_pairs={{0,8},{1,17},{2,10},{3,19},{4,12},{5,21},{6,14},{7,23},{8,0},{9,25... | collective-permute-start | bytes 110600 | tf_op jit(solution)/shard_map/ppermute | solution.py:45
  35.6 1.9 %collective-permute-start.12 = (f32[72,128]{1,0:T(8,128)S(1)}, f32[72,128]{1,0:T(8,128)S(1)}, u32[]{:S(2)}, u32[]{:S(2)}) collective-permute-start(f32[72,128]{1,0:T(8,128)S(1)} %add_add_fusion.refs_0_), channel_id=1, source_target_pairs={{0,24},{1,25},{2,26},{3,27},{4,28},{5,29},{6,30},{7,31},{8,16},{9,... | collective-permute-start | bytes 110600 | tf_op jit(solution)/shard_map/ppermute | solution.py:48
  37.5 1.8 %collective-permute-done.10.refs_1_ = f32[72,128]{1,0:T(8,128)S(1)} collective-permute-done((f32[72,128]{1,0:T(8,128)S(1)}, f32[72,128]{1,0:T(8,128)S(1)}, u32[]{:S(2)}, u32[]{:S(2)}) %collective-permute-start.10) | collective-permute-done | bytes 36896 | tf_op jit(solution)/shard_map/ppermute | solution.py:45
  39.3 2.1 %collective-permute-done.12.refs_3_ = f32[72,128]{1,0:T(8,128)S(1)} collective-permute-done((f32[72,128]{1,0:T(8,128)S(1)}, f32[72,128]{1,0:T(8,128)S(1)}, u32[]{:S(2)}, u32[]{:S(2)}) %collective-permute-start.12) | collective-permute-done | bytes 36896 | tf_op jit(solution)/shard_map/ppermute | solution.py:48
  41.4 3.9 %analysis.1 = (f32[32,4,1024]{2,1,0:T(4,128)}, f32[2,128]{1,0:T(2,128)}) custom-call(s32[18]{0:T(128)S(1)} %pad_add_fusion.which_ref, f32[256,1024]{1,0:T(8,128)S(1)} %get-tuple-element.6.state_ref, f32[2,128]{1,0:T(2,128)S(1)} %bitcast.14, f32[2,128]{1,0:T(2,128)S(1)} %bitcast.16, f32[72,128]{1,0:T(8,128)S(1)} %add_add_fusion.refs_0_, ...), custom_call_target="tpu_custom_call" | custom-call | tf_op jit(solution)/shard_map/analysis/pallas_call | solution.py:434
  (29 shorter events, 0.1 us)
Async XLA Ops:
  0.6 2.3 %collective-permute-start = (f32[32,4,1024]{2,1,0:T(4,128)}, f32[32,4,1024]{2,1,0:T(4,128)S(1)}, u32[]{:S(2)}, u32[]{:S(2)}) collective-permute-start(f32[32,4,1024]{2,1,0:T(4,128)} %mine_ref.1), channel_id=1, source_target_pairs={{0,1},{1,0},{2,3},{3,2},{4,5},{5,4},{6,7},{7,6},{8,9},{9,8},{10,11... | collective-permute-start | bytes 1572872 | tf_op jit(solution)/shard_map/ppermute | solution.py:39
  1.2 1.7 %copy-start.8 = (s32[256]{0:T(256)S(1)}, s32[256]{0:T(256)}, u32[]{:S(2)}) copy-start(s32[256]{0:T(256)} %param.14) | copy-start | bytes 3076
  1.2 1.7 %copy-start.9 = (s32[1,16]{1,0:T(1,128)S(1)}, s32[1,16]{1,0:T(1,128)}, u32[]{:S(2)}) copy-start(s32[1,16]{1,0:T(1,128)} %send_ref.1) | copy-start | bytes 196
  2.9 0.7 %copy-start.5 = (f32[256]{0:T(256)S(1)}, f32[256]{0:T(256)}, u32[]{:S(2)}) copy-start(f32[256]{0:T(256)} %param.16) | copy-start | bytes 3076
  2.9 0.7 %copy-start.7 = (s32[256]{0:T(256)S(1)}, s32[256]{0:T(256)}, u32[]{:S(2)}) copy-start(s32[256]{0:T(256)} %param.13) | copy-start | bytes 3076
  2.9 0.7 %copy-start.3 = (s32[1024]{0:T(1024)S(1)}, s32[1024]{0:T(1024)}, u32[]{:S(2)}) copy-start(s32[1024]{0:T(1024)} %param.11) | copy-start | bytes 12292
  2.9 0.7 %copy-start.2 = (f32[1024]{0:T(1024)S(1)}, f32[1024]{0:T(1024)}, u32[]{:S(2)}) copy-start(f32[1024]{0:T(1024)} %param.10) | copy-start | bytes 12292
  2.9 0.7 %copy-start.4 = (f32[256]{0:T(256)S(1)}, f32[256]{0:T(256)}, u32[]{:S(2)}) copy-start(f32[256]{0:T(256)} %param.15) | copy-start | bytes 3076
  3.6 1.0 %copy-start = (f32[32,4,1024]{2,1,0:T(4,128)S(1)}, f32[32,4,1024]{2,1,0:T(4,128)}, u32[]{:S(2)}) copy-start(f32[32,4,1024]{2,1,0:T(4,128)} %mine_ref.1) | copy-start | bytes 1572868
  4.7 15.8 %copy-start.1 = (f32[32,4,1024]{2,1,0:T(4,128)S(1)}, f32[32,4,1024]{2,1,0:T(4,128)}, u32[]{:S(2)}) copy-start(f32[32,4,1024]{2,1,0:T(4,128)} %mine_ref.1) | copy-start | bytes 1572868
  5.4 15.1 %copy-start.6 = (f32[4,4]{1,0:T(4,128)S(1)}, f32[4,4]{1,0:T(4,128)}, u32[]{:S(2)}) copy-start(f32[4,4]{1,0:T(4,128)} %couple_ref.1) | copy-start | bytes 196
  5.5 4.6 %collective-permute-start.1 = (f32[24,128]{1,0:T(8,128)S(1)}, f32[24,128]{1,0:T(8,128)S(1)}, u32[]{:S(2)}, u32[]{:S(2)}) collective-permute-start(f32[24,128]{1,0:T(8,128)S(1)} %pack.1), channel_id=1, source_target_pairs={{0,2},{1,5},{2,0},{3,7},{4,6},{5,1},{6,4},{7,3},{8,10},{9,13},{10,... | collective-permute-start | bytes 36872 | tf_op jit(solution)/shard_map/ppermute | solution.py:45
  8.4 4.6 %collective-permute-start.3 = (f32[24,128]{1,0:T(8,128)S(1)}, f32[24,128]{1,0:T(8,128)S(1)}, u32[]{:S(2)}, u32[]{:S(2)}) collective-permute-start(f32[24,128]{1,0:T(8,128)S(1)} %pack.1), channel_id=1, source_target_pairs={{0,6},{1,7},{2,4},{3,5},{4,2},{5,3},{6,0},{7,1},{8,14},{9,15},{10,... | collective-permute-start | bytes 36872 | tf_op jit(solution)/shard_map/ppermute | solution.py:48
  10.1 2.9 %collective-permute-start.2 = (f32[24,128]{1,0:T(8,128)S(1)}, f32[24,128]{1,0:T(8,128)S(1)}, u32[]{:S(2)}, u32[]{:S(2)}) collective-permute-start(f32[24,128]{1,0:T(8,128)S(1)} %collective-permute-done.1), channel_id=1, source_target_pairs={{0,1},{1,0},{2,3},{3,2},{4,5},{5,4},{6,7},{7,6},{8,9},{9,8},{10,11... | collective-permute-start | bytes 36872 | tf_op jit(solution)/shard_map/ppermute | solution.py:39
  13.0 4.2 %collective-permute-start.4 = (f32[96,128]{1,0:T(8,128)S(1)}, f32[96,128]{1,0:T(8,128)S(1)}, u32[]{:S(2)}, u32[]{:S(2)}) collective-permute-start(f32[96,128]{1,0:T(8,128)S(1)} %pad_maximum_fusion.refs_0_), channel_id=1, source_target_pairs={{0,8},{1,17},{2,10},{3,19},{4,12},{5,21},{6,14},{7,23},{8,0},{9,25... | collective-permute-start | bytes 147464 | tf_op jit(solution)/shard_map/ppermute | solution.py:45
  14.6 5.9 %collective-permute-start.6 = (f32[96,128]{1,0:T(8,128)S(1)}, f32[96,128]{1,0:T(8,128)S(1)}, u32[]{:S(2)}, u32[]{:S(2)}) collective-permute-start(f32[96,128]{1,0:T(8,128)S(1)} %pad_maximum_fusion.refs_0_), channel_id=1, source_target_pairs={{0,24},{1,25},{2,26},{3,27},{4,28},{5,29},{6,30},{7,31},{8,16},{9,... | collective-permute-start | bytes 147464 | tf_op jit(solution)/shard_map/ppermute | solution.py:48
  17.1 3.4 %collective-permute-start.5 = (f32[96,128]{1,0:T(8,128)S(1)}, f32[96,128]{1,0:T(8,128)S(1)}, u32[]{:S(2)}, u32[]{:S(2)}) collective-permute-start(f32[96,128]{1,0:T(8,128)S(1)} %collective-permute-done.4.refs_1_), channel_id=1, source_target_pairs={{0,1},{1,0},{2,3},{3,2},{4,5},{5,4},{6,7},{7,6},{8,9},{9,8},{10,11... | collective-permute-start | bytes 147464 | tf_op jit(solution)/shard_map/ppermute | solution.py:39
  29.3 4.0 %collective-permute-start.8 = (f32[72,128]{1,0:T(8,128)S(1)}, f32[72,128]{1,0:T(8,128)S(1)}, u32[]{:S(2)}, u32[]{:S(2)}) collective-permute-start(f32[72,128]{1,0:T(8,128)S(1)} %get-tuple-element.7), channel_id=1, source_target_pairs={{0,2},{1,5},{2,0},{3,7},{4,6},{5,1},{6,4},{7,3},{8,10},{9,13},{10,... | collective-permute-start | bytes 110600 | tf_op jit(solution)/shard_map/ppermute | solution.py:45
  30.1 4.9 %collective-permute-start.7 = (f32[72,128]{1,0:T(8,128)S(1)}, f32[72,128]{1,0:T(8,128)S(1)}, u32[]{:S(2)}, u32[]{:S(2)}) collective-permute-start(f32[72,128]{1,0:T(8,128)S(1)} %get-tuple-element.7), channel_id=1, source_target_pairs={{0,6},{1,7},{2,4},{3,5},{4,2},{5,3},{6,0},{7,1},{8,14},{9,15},{10,... | collective-permute-start | bytes 110600 | tf_op jit(solution)/shard_map/ppermute | solution.py:48
  33.3 1.7 %collective-permute-start.9 = (f32[72,128]{1,0:T(8,128)S(1)}, f32[72,128]{1,0:T(8,128)S(1)}, u32[]{:S(2)}, u32[]{:S(2)}) collective-permute-start(f32[72,128]{1,0:T(8,128)S(1)} %collective-permute-done.8), channel_id=1, source_target_pairs={{0,1},{1,0},{2,3},{3,2},{4,5},{5,4},{6,7},{7,6},{8,9},{9,8},{10,11... | collective-permute-start | bytes 110600 | tf_op jit(solution)/shard_map/ppermute | solution.py:39
  35.0 4.4 %collective-permute-start.10 = (f32[72,128]{1,0:T(8,128)S(1)}, f32[72,128]{1,0:T(8,128)S(1)}, u32[]{:S(2)}, u32[]{:S(2)}) collective-permute-start(f32[72,128]{1,0:T(8,128)S(1)} %add_add_fusion.refs_0_), channel_id=1, source_target_pairs={{0,8},{1,17},{2,10},{3,19},{4,12},{5,21},{6,14},{7,23},{8,0},{9,25... | collective-permute-start | bytes 110600 | tf_op jit(solution)/shard_map/ppermute | solution.py:45
  35.6 5.8 %collective-permute-start.12 = (f32[72,128]{1,0:T(8,128)S(1)}, f32[72,128]{1,0:T(8,128)S(1)}, u32[]{:S(2)}, u32[]{:S(2)}) collective-permute-start(f32[72,128]{1,0:T(8,128)S(1)} %add_add_fusion.refs_0_), channel_id=1, source_target_pairs={{0,24},{1,25},{2,26},{3,27},{4,28},{5,29},{6,30},{7,31},{8,16},{9,... | collective-permute-start | bytes 110600 | tf_op jit(solution)/shard_map/ppermute | solution.py:48
  39.3 2.1 %collective-permute-start.11 = (f32[72,128]{1,0:T(8,128)S(1)}, f32[72,128]{1,0:T(8,128)S(1)}, u32[]{:S(2)}, u32[]{:S(2)}) collective-permute-start(f32[72,128]{1,0:T(8,128)S(1)} %collective-permute-done.10.refs_1_), channel_id=1, source_target_pairs={{0,1},{1,0},{2,3},{3,2},{4,5},{5,4},{6,7},{7,6},{8,9},{9,8},{10,11... | collective-permute-start | bytes 110600 | tf_op jit(solution)/shard_map/ppermute | solution.py:39

commit v2 on v1

v2 whole, which is shorter than its diff:
```python
import functools
import math

import jax
import jax.numpy as jnp
from jax import lax
from jax.experimental import pallas as pl
from jax.experimental.pallas import tpu as pltpu
from jax.sharding import PartitionSpec as P

STEPS = 4
DIFFUSION = 0.05
LANES = 128
CAP = 32
GROUPS = LANES // CAP
BOTH = ("cells", "members")
EXACT = lax.Precision.HIGHEST
VMEM_BYTES = 48 * 1024 * 1024


def core_pairs(owners, place):
    pairs = []
    for block in range(owners):
        for core in range(2):
            to_block, to_core = place(block, core)
            pairs.append((block * 2 + core, to_block * 2 + to_core))
    return pairs


def stage_units(owners):
    units = []
    unit = 1
    while unit < owners:
        units.append(unit)
        unit *= 4
    if unit != owners or len(units) < 2:
        raise ValueError("blocks not 4**n")
    return units


def swap_cores(x, owners):
    return lax.ppermute(x, BOTH, core_pairs(owners, lambda block, core: (block, 1 - core)))


def exchange(to_middle, to_third, owners, unit):
    first = lax.ppermute(
        to_middle, BOTH, core_pairs(owners, lambda block, core: (block ^ (unit * (1 + core)), core))
    )
    third = lax.ppermute(
        to_third, BOTH, core_pairs(owners, lambda block, core: (block ^ (unit * 3), core))
    )
    return first, swap_cores(first, owners), third


def digit_of(block, unit):
    return jnp.bitwise_and(lax.div(block, jnp.int32(unit)), 3)


def table_row(number, count):
    return (number % 4) * (count // 4) + number // 4


def pack_kernel(
    send_in, ensemble_ref, speed_in, flag_in, place_in, field_in, value_in, sigma_in,
    strip_ref, table_ref, send_ref, head, tail, speed_ref, flag_ref, place_ref, field_ref, value_ref,
    sigma_ref, sems, *, rows,
):
    fields, cells = ensemble_ref.shape[1:]
    small = (
        (send_in, send_ref), (speed_in, speed_ref), (flag_in, flag_ref), (place_in, place_ref),
        (field_in, field_ref), (value_in, value_ref), (sigma_in, sigma_ref),
    )
    large = (
        (ensemble_ref.at[:, :, pl.ds(0, LANES)], head),
        (ensemble_ref.at[:, :, pl.ds(cells - LANES, LANES)], tail),
    )
    copies = [
        pltpu.make_async_copy(source, target, sems.at[i])
        for i, (source, target) in enumerate(large + small)
    ]
    for copy in copies:
        copy.start()
    for copy in copies[2:]:
        copy.wait()
    tiles = speed_ref.shape[0]
    lane = lax.broadcasted_iota(jnp.int32, (1, LANES), 1)
    low = lane < LANES // 2
    toward_left = speed_ref[...] * flag_ref[...].astype(jnp.float32)
    toward_right = speed_ref[...] - toward_left
    edge_left = jnp.where(low, toward_left[:1], toward_left[tiles - 1 :])
    edge_right = jnp.where(low, toward_right[:1], toward_right[tiles - 1 :])
    ids = (field_ref[...] * cells + place_ref[...]).astype(jnp.float32)
    weight = 1.0 / (sigma_ref[...] * sigma_ref[...])
    pull = weight * value_ref[...]
    wide = rows * LANES

    def row_of(x):
        return jnp.concatenate([x[r : r + 1] for r in range(rows)], axis=1)

    listed = jnp.concatenate(
        [row_of(ids), row_of(weight), row_of(pull), jnp.zeros((5, wide), jnp.float32)], axis=0
    )
    sub = lax.broadcasted_iota(jnp.int32, (8, LANES), 0)
    lane8 = lax.broadcasted_iota(jnp.int32, (8, LANES), 1)
    empty = jnp.where(sub == 0, -1.0, 0.0)
    empty = jnp.where(sub == 3, edge_left, jnp.where(sub == 4, edge_right, empty))
    owners = send_ref.shape[1]
    count = owners // GROUPS
    for r in range(count):
        table_ref[8 * table_row(r, count) : 8 * table_row(r, count) + 8, :] = empty
    start = jnp.int32(0)
    for owner in range(owners):
        held = send_ref[0, owner]
        group, r = owner // count, owner % count
        moved = pltpu.roll(listed, lax.rem(group * CAP - start + 2 * wide, jnp.int32(wide)), 1)[:, :LANES]
        here = (lane8 >= group * CAP) & (lane8 < group * CAP + held) & (sub < 3)
        row = 8 * table_row(r, count)
        table_ref[row : row + 8, :] = jnp.where(here, moved, table_ref[row : row + 8, :])
        start = start + held
    for copy in copies[:2]:
        copy.wait()
    head_rows = jnp.concatenate([head[:, f, :] for f in range(fields)], axis=0)
    tail_rows = jnp.concatenate([tail[:, f, :] for f in range(fields)], axis=0)
    strip_ref[:STEPS, :] = jnp.transpose(head_rows)[:STEPS, :]
    strip_ref[STEPS:, :] = jnp.transpose(tail_rows)[LANES - STEPS :, :]


def incoming(digit, core, first, swapped, third):
    sub = lax.broadcasted_iota(jnp.int32, (8, LANES), 0)
    low = lax.broadcasted_iota(jnp.int32, (8, LANES), 1) < LANES // 2
    odd = jnp.bitwise_and(digit, 1) == 1
    result = []
    for part, other_part in ((0, 1), (1, 0), (2, 2)):
        near = jnp.where(
            core == 0, first[8 * part : 8 * part + 8, :], swapped[8 * other_part : 8 * other_part + 8, :]
        )
        far = third[8 * part : 8 * part + 8, :]
        from_right = jnp.where(odd, far, near)
        from_left = jnp.where(odd, near, far)
        result.append(jnp.where(sub < STEPS if part < 2 else low, from_right, from_left))
    return result


def regroup_kernel(
    which_ref, kept, first, swapped, third, _, to_middle, to_third, stay, *, unit, into_lanes,
):
    block, core = which_ref[0], which_ref[1]
    digit = digit_of(block, unit)
    after = digit_of(block, unit * 4)
    own, other, coefs = incoming(digit, core, first, swapped, third)
    sub = lax.broadcasted_iota(jnp.int32, (8, LANES), 0)
    lane_group = lax.broadcasted_iota(jnp.int32, (8, LANES), 1) // CAP
    held = (third.shape[0] - 16) // 8
    for target, partner in ((to_middle, 1 + core), (to_third, 3), (stay, 0)):
        wanted = jnp.bitwise_xor(after, partner)
        base = 0
        if target is not stay:
            target[0:8, :] = own
            target[8:16, :] = other
            base = 16

        def received(k, at):
            if k == 0:
                return kept[pl.ds(at, 8), :]
            if k == 3:
                return third[pl.ds(16 + at, 8), :]
            a, b = first[pl.ds(16 + at, 8), :], swapped[pl.ds(16 + at, 8), :]
            return jnp.where(core == k - 1, a, b)

        if into_lanes:
            for j in range(held):
                merged = coefs
                for k in range(4):
                    moved = pltpu.roll(
                        received(k, 8 * j), jnp.bitwise_and(k - wanted, 3) * CAP, 1
                    )
                    merged = jnp.where((lane_group == k) & (sub < 3), moved, merged)
                target[base + 8 * j : base + 8 * j + 8, :] = merged
        else:
            rest = held // 4
            for k in range(4):
                for r in range(rest):
                    at = pl.multiple_of((wanted * rest + r) * 8, 8)
                    row = base + 8 * (r * 4 + k)
                    target[row : row + 8, :] = jnp.where(sub < 3, received(k, at), coefs)


def power_of_coupling(couple_ref, fields):
    mix = [[couple_ref[f, g] + (1.0 if f == g else 0.0) for g in range(fields)] for f in range(fields)]
    for _ in range(2):
        mix = [
            [sum(mix[f][h] * mix[h][g] for h in range(fields)) for g in range(fields)]
            for f in range(fields)
        ]
    return mix


def transport(x, from_left, stay, from_right):
    for _ in range(STEPS):
        x = from_left * pltpu.roll(x, 1, 1) + stay * x + from_right * pltpu.roll(x, x.shape[1] - 1, 1)
    return x


def forecast_kernel(
    couple_ref, source, speed_ref, flag_ref, state, edge, sums_ref, work_ref, coef_ref,
):
    members, fields, cells = source.shape
    tiles = cells // LANES
    speed = speed_ref[...]
    toward_left = speed * flag_ref[...].astype(jnp.float32)
    toward_right = speed - toward_left

    def row_of(x):
        return jnp.concatenate([x[t : t + 1] for t in range(tiles)], axis=1)

    def shifted(x, by):
        return pltpu.roll(x, -by % cells, 1) if by else x

    step = {-1: row_of(toward_left + DIFFUSION), 0: row_of(1.0 - 2.0 * DIFFUSION - speed), 1: row_of(toward_right + DIFFUSION)}
    reach = dict(step)
    for _ in range(STEPS - 1):
        longer = {}
        for e in step:
            for d in reach:
                term = step[e] * shifted(reach[d], e)
                longer[d + e] = longer[d + e] + term if d + e in longer else term
        reach = longer
    for d in range(-STEPS, STEPS + 1):
        at = 8 * (d + STEPS)
        coef_ref[at : at + 8, :] = jnp.broadcast_to(reach[d], (8, cells))
    mix = power_of_coupling(couple_ref, fields)
    low = lax.broadcasted_iota(jnp.int32, (8, LANES), 1) < LANES // 2
    sums_ref[...] = jnp.zeros_like(sums_ref)

    def group(i, _):
        at = pl.multiple_of(i * 8, 8)
        for f in range(fields):
            x = source[pl.ds(at, 8), f, :]
            edge[pl.ds(f * members + at, 8), :] = jnp.where(
                low,
                pltpu.roll(x[:, :LANES], STEPS, 1),
                pltpu.roll(x[:, cells - LANES :], LANES // 2 + 3 * STEPS, 1),
            )
            total = None
            for d in range(-STEPS, STEPS + 1):
                term = coef_ref[8 * (d + STEPS) : 8 * (d + STEPS) + 8, :] * shifted(x, d)
                total = term if total is None else total + term
            work_ref[f * 8 : f * 8 + 8, :] = total
        for t in range(tiles):
            lanes = slice(t * LANES, (t + 1) * LANES)
            moved = [work_ref[f * 8 : (f + 1) * 8, lanes] for f in range(fields)]
            for f in range(fields):
                value = sum(mix[f][g] * moved[g] for g in range(fields))
                state[pl.ds(f * members + at, 8), lanes] = value
                place = (f * tiles + t) * 8
                sums_ref[place : place + 8, :] += value
        return 0

    lax.fori_loop(0, members // 8, group, 0)


def pieces_of(x):
    high = x.astype(jnp.bfloat16).astype(jnp.float32)
    rest = x - high
    middle = rest.astype(jnp.bfloat16).astype(jnp.float32)
    return high, middle, rest - middle


def sums_kernel(
    which_ref, couple_ref, speed_ref, flag_ref, own_state, own_edge, own_sums, other_state, other_edge, other_sums,
    kept, first, swapped, third, *refs, owners, units, fields,
):
    carried = refs[: len(units) - 1]
    (
        stay_ref, middle_ref, third_ref, edge_ref, halo_ref, onehot_ref, spread_ref, split_ref,
    ) = refs[len(units) - 1 :]
    states, raw_edges = (own_state, other_state), (own_edge, other_edge)
    block, core = which_ref[0], which_ref[1]
    members = states[0].shape[0] // fields
    cells = states[0].shape[1]
    tiles = cells // LANES
    total = 2 * members
    places = fields * tiles
    has_left = (block > 0).astype(jnp.float32)
    has_right = (block < owners - 1).astype(jnp.float32)
    sub = lax.broadcasted_iota(jnp.int32, (8, LANES), 0)
    lane = lax.broadcasted_iota(jnp.int32, (1, LANES), 1)
    lane8 = lax.broadcasted_iota(jnp.int32, (8, LANES), 1)
    half_lanes = LANES // 2
    low = lane < half_lanes

    strips = incoming(digit_of(block, units[-1]), core, first, swapped, third)
    for unit, earlier in reversed(list(zip(units, carried))):
        digit = digit_of(block, unit)
        rows = [earlier[8 * p : 8 * p + 8, :] for p in range(3)]
        picked = []
        for p in range(3):
            from_right = jnp.where(digit != 3, rows[p], strips[p])
            from_left = jnp.where(digit != 0, rows[p], strips[p])
            picked.append(jnp.where(sub < STEPS if p < 2 else lane8 < half_lanes, from_right, from_left))
        strips = picked

    right_first = half_lanes + 3 * STEPS
    strip_rows = fields * members
    for half in range(2):
        strip = strips[half]
        left = jnp.where(sub < STEPS, pltpu.roll(strip, STEPS, 0) * has_left, 0.0)
        at = right_first % 8
        right = jnp.where(
            (sub >= at) & (sub < at + STEPS), (pltpu.roll(strip, at, 0) if at else strip) * has_right, 0.0
        )
        gap = jnp.zeros((right_first - at - 8, LANES), jnp.float32)
        rest = jnp.zeros((LANES - (right_first - at) - 8, LANES), jnp.float32)
        halo_ref[half * strip_rows : (half + 1) * strip_rows, :] = jnp.transpose(
            jnp.concatenate([left, gap, right, rest], axis=0)
        )
    speed = speed_ref[...]
    toward_left = speed * flag_ref[...].astype(jnp.float32)
    toward_right = speed - toward_left
    is_left = lane < STEPS
    is_right = (lane >= right_first) & (lane < right_first + STEPS)
    inside = jnp.where(is_left, has_left, jnp.where(is_right, has_right, 1.0))
    from_outside = (lane8 < STEPS) | ((lane8 >= right_first) & (lane8 < right_first + STEPS))

    def edge_row(rows, row):
        own = jnp.where(
            low, pltpu.roll(rows[:1], STEPS, 1), pltpu.roll(rows[tiles - 1 :], half_lanes + 3 * STEPS, 1)
        )
        left = pltpu.roll(strips[2][row : row + 1], STEPS, 1)
        right = pltpu.roll(strips[2][row : row + 1], right_first, 1)
        return jnp.where(is_left, left, jnp.where(is_right, right, own))

    edge_left = edge_row(toward_left, 3)
    edge_right = edge_row(toward_right, 4)
    from_left = jnp.broadcast_to((edge_left + DIFFUSION) * inside, (8, LANES))
    from_right = jnp.broadcast_to((edge_right + DIFFUSION) * inside, (8, LANES))
    stay = jnp.broadcast_to((1.0 - 2.0 * DIFFUSION - edge_left - edge_right) * inside, (8, LANES))
    mix = power_of_coupling(couple_ref, fields)
    first_sums = [jnp.zeros((8, LANES), jnp.float32) for _ in range(fields)]
    last_sums = [jnp.zeros((8, LANES), jnp.float32) for _ in range(fields)]
    for half in range(2):
        state, edge = states[half], raw_edges[half]
        for i in range(members // 8):
            moved = []
            for f in range(fields):
                at = f * members + 8 * i
                x = edge[at : at + 8, :]
                x = jnp.where(from_outside, halo_ref[half * strip_rows + at : half * strip_rows + at + 8, :], x)
                moved.append(transport(x, from_left, stay, from_right))
            for f in range(fields):
                at = f * members + 8 * i
                value = sum(mix[f][g] * moved[g] for g in range(fields))
                first_tile = jnp.where(lane8 < STEPS, pltpu.roll(value, LANES - STEPS, 1), state[at : at + 8, :LANES])
                last_tile = jnp.where(
                    lane8 >= LANES - STEPS,
                    pltpu.roll(value, LANES - right_first, 1),
                    state[at : at + 8, cells - LANES :],
                )
                edge_ref[half * strip_rows + at : half * strip_rows + at + 8, :LANES] = first_tile
                edge_ref[half * strip_rows + at : half * strip_rows + at + 8, LANES:] = last_tile
                first_sums[f] = first_sums[f] + first_tile
                last_sums[f] = last_sums[f] + last_tile
    means = []
    for f in range(fields):
        for t in range(tiles):
            at = (f * tiles + t) * 8
            if t == 0:
                partial = first_sums[f]
            elif t == tiles - 1:
                partial = last_sums[f]
            else:
                partial = own_sums[at : at + 8, :] + other_sums[at : at + 8, :]
            means.append(jnp.sum(partial, axis=0, keepdims=True))
    mean = jnp.concatenate(means, axis=0) * (1.0 / total)

    place_ids = lax.broadcasted_iota(jnp.int32, (places, LANES), 0)
    lane_ids = lax.broadcasted_iota(jnp.int32, (LANES, LANES), 0)
    held = kept.shape[0] // 8
    sources = [(kept, 8 * j) for j in range(held)]
    for source in (first, swapped, third):
        sources += [(source, 16 + 8 * j) for j in range(held)]
    hits = []
    for n, (source, at) in enumerate(sources):
        local = source[at : at + 1, :].astype(jnp.int32)
        hit = place_ids == lax.shift_right_arithmetic(local, 7)
        hits.append(hit)
        onehot = (lane_ids == jnp.bitwise_and(local, LANES - 1)).astype(jnp.float32)
        lanes = slice(n * LANES, (n + 1) * LANES)
        onehot_ref[:, lanes] = onehot.astype(jnp.bfloat16)
        weight, pull = source[at + 1 : at + 2, :], source[at + 2 : at + 3, :]
        stack = [jnp.where(hit, piece, 0.0) for piece in pieces_of(weight) + pieces_of(pull)]
        spread_ref[:, lanes] = jnp.concatenate(stack, axis=0).astype(jnp.bfloat16)
    placed = lax.dot_general(
        spread_ref[...], onehot_ref[...], (((1,), (1,)), ((), ())), preferred_element_type=jnp.float32
    )
    placed = [placed[p * places : (p + 1) * places] for p in range(6)]
    weight = placed[0] + placed[1] + placed[2]
    pull = placed[3] + placed[4] + placed[5] - weight * mean

    root = jnp.sqrt(weight)
    pull = jnp.where(weight > 0.0, pull * lax.rsqrt(jnp.where(weight > 0.0, weight, 1.0)), 0.0)
    sub16 = lax.broadcasted_iota(jnp.int32, (16, LANES), 0)
    depth = total + 16

    def put(row, lanes, value):
        for p, piece in enumerate(pieces_of(value)):
            split_ref[pl.ds(row + p * depth, value.shape[0]), lanes] = piece.astype(jnp.bfloat16)

    for f in range(fields):
        for t in range(tiles):
            at = f * tiles + t
            lanes = slice(t * LANES, (t + 1) * LANES)
            into = slice(at * LANES, (at + 1) * LANES)
            for half in range(2):
                if t in (0, tiles - 1):
                    column = slice(0, LANES) if t == 0 else slice(LANES, 2 * LANES)
                    value = edge_ref[half * strip_rows + f * members : half * strip_rows + (f + 1) * members, column]
                else:
                    value = states[half][f * members : (f + 1) * members, lanes]
                anomaly = (value - mean[at : at + 1]) * root[at : at + 1]
                side = core if half == 0 else 1 - core
                put(pl.multiple_of(side * members, 16), into, anomaly)
            put(total, into, jnp.where(sub16 == 0, pull[at : at + 1], 0.0))
    products = lax.dot_general(
        split_ref[...], split_ref[...], (((1,), (1,)), ((), ())), preferred_element_type=jnp.float32
    )
    gram = sum(
        products[p * depth : p * depth + total + 8, q * depth : q * depth + total]
        for p, q in ((2, 0), (1, 1), (0, 2), (1, 0), (0, 1), (0, 0))
    )
    gram = jnp.concatenate([gram, jnp.zeros((total + 8, LANES - total), jnp.float32)], axis=1)
    folded = gram[:members] + pltpu.roll(gram[members:total], total, 1)
    blank = jnp.zeros((stay_ref.shape[0] - members - 1, LANES), jnp.float32)
    for out in (stay_ref, middle_ref, third_ref):
        out[:members, :] = folded
        out[members : members + 1, :] = gram[total : total + 1]
        out[members + 1 :, :] = blank

    found = lax.dot_general(
        jnp.concatenate(pieces_of(mean), axis=0).astype(jnp.bfloat16), onehot_ref[...],
        (((1,), (0,)), ((), ())), preferred_element_type=jnp.float32,
    )
    found = found[:places] + found[places : 2 * places] + found[2 * places :]
    for out, source, partner in ((stay_ref, 0, 0), (middle_ref, 1, 1 + core), (third_ref, 3, 3)):
        for j in range(held):
            n = source * held + j
            center = jnp.sum(
                jnp.where(hits[n], found[:, n * LANES : (n + 1) * LANES], 0.0), axis=0, keepdims=True
            )
            out[pl.ds(members + 1 + partner * held + j, 1), :] = center


def spread_row(row):
    return jnp.broadcast_to(row, (8, LANES))


def eliminate(rows):
    count = len(rows)
    rows = list(rows)
    sub = lax.broadcasted_iota(jnp.int32, (8, LANES), 0)
    for b in range(count):
        columns = [
            [jnp.broadcast_to(rows[i][:, 8 * b + k : 8 * b + k + 1], (8, LANES)) for k in range(8)]
            for i in range(b, count)
        ]
        for j in range(8):
            scale = lax.rsqrt(spread_row(columns[0][j][j : j + 1, :]))
            upper = spread_row(rows[b][j : j + 1, :]) * scale
            lower = columns[0][j] * scale
            factors = [spread_row(lower[k : k + 1, :]) for k in range(8)]
            for i in range(b, count):
                here = lower if i == b else columns[i - b][j] * scale
                if i == b:
                    rows[b] = jnp.where(sub == j, upper, rows[b] - jnp.where(sub > j, here, 0.0) * upper)
                else:
                    rows[i] = rows[i] - here * upper
                for k in range(j + 1, 8):
                    columns[i - b][k] = columns[i - b][k] - here * factors[k]
    return rows


def analysis_kernel(
    which_ref, send_ref, own_ref, other_ref, edge_ref, value_ref, sigma_ref, kept, first, swapped, third,
    analysis_ref, innovation_ref, mixing_ref, center_ref, *, units, obs_rows,
):
    block, core = which_ref[0], which_ref[1]
    members, fields, cells = analysis_ref.shape
    total = 2 * members
    head = members + 1
    sums = (kept[:head, :] + third[:head, :]) + (first[:head, :] + swapped[:head, :])
    returned = kept.shape[0] - head
    center_ref[:returned, :] = kept[head:, :]
    center_ref[returned : 2 * returned, :] = jnp.where(core == 0, first[head:, :], swapped[head:, :])
    center_ref[2 * returned : 3 * returned, :] = jnp.where(core == 0, swapped[head:, :], first[head:, :])
    center_ref[3 * returned :, :] = third[head:, :]
    lane = lax.broadcasted_iota(jnp.int32, (8, LANES), 1)
    sub = lax.broadcasted_iota(jnp.int32, (8, LANES), 0)
    shifted = pltpu.roll(sums[:members], LANES - total, 1)
    rows = []
    for b in range(total // 8):
        at = 8 * b
        source = sums[at : at + 8] if at < members else shifted[at - members : at - members + 8]
        own = jnp.where(lane == sub + at, total - 1.0, 0.0)
        unit = jnp.where(lane == sub + at + total, 1.0, 0.0)
        rows.append(jnp.where(lane < total, source + own, unit))
    rows = eliminate(rows)
    cross = sums[members : members + 1]
    inverse = [jnp.where(lane < total, pltpu.roll(r, LANES - total, 1), 0.0) for r in rows]
    carried = [jnp.sum(r * cross, axis=1, keepdims=True) for r in inverse]
    weights = sum(jnp.sum(r * c, axis=0, keepdims=True) for r, c in zip(inverse, carried))
    row_means = [jnp.sum(r, axis=1, keepdims=True) * (1.0 / total) for r in inverse]
    column_mean = sum(jnp.sum(r, axis=0, keepdims=True) for r in inverse) * (1.0 / total)
    grand = jnp.sum(column_mean, axis=1, keepdims=True) * (1.0 / total)
    weights = weights - jnp.sum(weights, axis=1, keepdims=True) * (1.0 / total)
    root = math.sqrt(total - 1.0)
    add = weights + 1.0 / total - root * (column_mean - grand)
    for b in range(total // 8):
        mixing_ref[8 * b : 8 * b + 8, :] = root * (inverse[b] - row_means[b]) + add
    own_rows = mixing_ref[pl.ds(pl.multiple_of(core * members, 8), members), :]
    rolled = pltpu.roll(own_rows, LANES - members, 1)
    to_own = jnp.where(core == 0, own_rows, rolled)[:, :members]
    to_other = jnp.where(core == 0, rolled, own_rows)[:, :members]
    mixing = jnp.concatenate([to_own, to_other], axis=1)
    strip_rows = fields * members
    for f in range(fields):
        rows = slice(f * members, (f + 1) * members)
        other_rows = slice(strip_rows + f * members, strip_rows + (f + 1) * members)
        states = jnp.concatenate(
            [
                jnp.concatenate([edge_ref[rows, :LANES], edge_ref[other_rows, :LANES]], axis=0),
                jnp.concatenate(
                    [own_ref[rows, LANES : cells - LANES], other_ref[rows, LANES : cells - LANES]], axis=0
                ),
                jnp.concatenate([edge_ref[rows, LANES:], edge_ref[other_rows, LANES:]], axis=0),
            ],
            axis=1,
        )
        analysis_ref[:, f, :] = jnp.dot(
            mixing, states, precision=EXACT, preferred_element_type=jnp.float32
        )
    owners = send_ref.shape[1]
    held = owners // 16
    wide = obs_rows * LANES
    slot = lax.broadcasted_iota(jnp.int32, (1, wide), 1)
    centers = jnp.zeros((1, wide), jnp.float32)
    start = jnp.int32(0)
    for owner in range(owners):
        way = [jnp.bitwise_xor(digit_of(block, unit), (owner // unit) % 4) for unit in units]
        row = way[-1] * held
        if len(units) > 2:
            row = row + sum(step * 4**s for s, step in enumerate(way[:-2]))
        size = 4 * held
        for step in reversed(way[1:-1]):
            row = row + step * size
            size = size * 4
        row = row + way[0] * returned
        line = center_ref[pl.ds(row, 1), :]
        line = jnp.concatenate([line] + [jnp.zeros((1, LANES), jnp.float32)] * (obs_rows - 1), axis=1)
        moved = pltpu.roll(line, lax.rem(start - way[-2] * CAP + 2 * wide, jnp.int32(wide)), 1)
        end = start + send_ref[0, owner]
        centers = jnp.where((slot >= start) & (slot < end), moved, centers)
        start = end
    for r in range(obs_rows):
        center = centers[:, r * LANES : (r + 1) * LANES]
        innovation_ref[r : r + 1, :] = (value_ref[r : r + 1, :] - center) / sigma_ref[r : r + 1, :]


def shards(
    ensemble, speed, direction, couple, obs_place, obs_field, obs_value, obs_sigma, send_count
):
    members, fields, cells = ensemble.shape
    owners = lax.axis_size("cells")
    total = members * lax.axis_size("members")
    obs = obs_place.shape[0]
    obs_rows = obs // LANES
    tiles = cells // LANES
    places = fields * tiles
    units = stage_units(owners)
    block = lax.axis_index("cells").astype(jnp.int32)
    core = lax.axis_index("members").astype(jnp.int32)
    which = jnp.stack([block, core])
    speed = speed.reshape(tiles, LANES)
    direction = direction.reshape(tiles, LANES)
    obs_place, obs_field, obs_value, obs_sigma = (
        x.reshape(obs_rows, LANES) for x in (obs_place, obs_field, obs_value, obs_sigma)
    )
    whole = pl.BlockSpec(memory_space=pltpu.VMEM)
    scalars = pl.BlockSpec(memory_space=pltpu.SMEM)
    params = pltpu.CompilerParams(vmem_limit_bytes=VMEM_BYTES)
    real = jnp.float32

    table_rows = 8 * (owners // GROUPS)
    strips, table = pl.pallas_call(
        functools.partial(pack_kernel, rows=obs_rows),
        out_shape=(jax.ShapeDtypeStruct((8, LANES), real), jax.ShapeDtypeStruct((table_rows, LANES), real)),
        in_specs=[pl.BlockSpec(memory_space=pltpu.HBM)] * 8,
        out_specs=(whole, whole),
        scratch_shapes=[
            pltpu.SMEM(send_count.shape, jnp.int32),
            pltpu.VMEM((members, fields, LANES), real),
            pltpu.VMEM((members, fields, LANES), real),
            pltpu.VMEM((tiles, LANES), real),
            pltpu.VMEM((tiles, LANES), jnp.int32),
            pltpu.VMEM((obs_rows, LANES), jnp.int32),
            pltpu.VMEM((obs_rows, LANES), jnp.int32),
            pltpu.VMEM((obs_rows, LANES), real),
            pltpu.VMEM((obs_rows, LANES), real),
            pltpu.SemaphoreType.DMA((9,)),
        ],
        name="pack",
    )(send_count, ensemble, speed, direction, obs_place, obs_field, obs_value, obs_sigma)

    def forecast(half):
        return pl.pallas_call(
            forecast_kernel,
            out_shape=(
                jax.ShapeDtypeStruct((strip_rows, cells), real),
                jax.ShapeDtypeStruct((strip_rows, LANES), real),
                jax.ShapeDtypeStruct((places * 8, LANES), real),
            ),
            in_specs=[scalars] + [whole] * 3,
            out_specs=(whole,) * 3,
            scratch_shapes=[
                pltpu.VMEM((fields * 8, cells), real),
                pltpu.VMEM((8 * (2 * STEPS + 1), cells), real),
            ],
            compiler_params=params,
            cost_estimate=pl.CostEstimate(
                flops=80 * strip_rows * cells, bytes_accessed=8 * strip_rows * cells, transcendentals=0
            ),
            name="forecast",
        )(couple, half, speed, direction)

    strip_rows = fields * members
    other_strips = swap_cores(strips, owners)
    other = swap_cores(ensemble, owners)
    own_forecast = forecast(ensemble)
    part = table_rows // 4
    digit = digit_of(block, 1)

    def part_of(partner):
        return lax.dynamic_slice_in_dim(table, jnp.bitwise_xor(digit, partner) * part, part, 0)

    kept = part_of(0)
    to_middle = jnp.concatenate([strips, other_strips, part_of(1 + core)], axis=0)
    to_third = jnp.concatenate([strips, other_strips, part_of(3)], axis=0)
    carried = []
    for n, unit in enumerate(units):
        arrived = exchange(to_middle, to_third, owners, unit)
        if n + 1 < len(units):
            payload = jax.ShapeDtypeStruct(to_third.shape, real)
            to_middle, to_third, kept = pl.pallas_call(
                functools.partial(regroup_kernel, unit=unit, into_lanes=n + 2 == len(units)),
                out_shape=(payload, payload, jax.ShapeDtypeStruct(kept.shape, real)),
                in_specs=[scalars] + [whole] * 4 + [pl.BlockSpec(memory_space=pl.ANY)],
                out_specs=(whole,) * 3,
                compiler_params=params,
                name="regroup",
            )(which, kept, *arrived, own_forecast[2])
            carried.append(to_third)
    other_forecast = forecast(other)

    held = kept.shape[0] // 8
    sums_rows = -(-(members + 1 + 4 * held) // 8) * 8
    all_slots = 4 * held * LANES
    sums = jax.ShapeDtypeStruct((sums_rows, LANES), real)
    stay, to_middle, to_third, edges = pl.pallas_call(
        functools.partial(sums_kernel, owners=owners, units=units, fields=fields),
        out_shape=(sums, sums, sums, jax.ShapeDtypeStruct((2 * strip_rows, 2 * LANES), real)),
        in_specs=[scalars, scalars] + [whole] * (12 + len(carried)),
        out_specs=(whole,) * 4,
        scratch_shapes=[
            pltpu.VMEM((2 * strip_rows, LANES), real),
            pltpu.VMEM((LANES, all_slots), jnp.bfloat16),
            pltpu.VMEM((6 * places, all_slots), jnp.bfloat16),
            pltpu.VMEM((3 * (total + 16), fields * cells), jnp.bfloat16),
        ],
        compiler_params=params,
        name="sums",
    )(
        which, couple, speed, direction, *own_forecast, *other_forecast, kept, *arrived, *carried,
    )

    head = members + 1
    used = head + 4 * held
    for n, unit in enumerate(reversed(units)):
        first, swapped, third = exchange(to_middle, to_third, owners, unit)
        if n + 1 < len(units):
            added = (stay + third) + (first + swapped)
            if n > 0:
                near = jnp.where(core == 0, first, swapped)
                middle = jnp.where(core == 0, swapped, first)
                added = jnp.concatenate(
                    [added[:head]] + [x[head:used] for x in (stay, near, middle, third)], axis=0
                )
                used = added.shape[0]
            stay = to_middle = to_third = added

    analysis, innovation = pl.pallas_call(
        functools.partial(analysis_kernel, units=units, obs_rows=obs_rows),
        out_shape=(
            jax.ShapeDtypeStruct((members, fields, cells), real),
            jax.ShapeDtypeStruct((obs_rows, LANES), real),
        ),
        in_specs=[scalars, scalars] + [whole] * 9,
        out_specs=(whole, whole),
        scratch_shapes=[
            pltpu.VMEM((total, LANES), real),
            pltpu.VMEM((4 * (stay.shape[0] - head), LANES), real),
        ],
        compiler_params=params,
        name="analysis",
    )(
        which, send_count, own_forecast[0], other_forecast[0], edges, obs_value, obs_sigma,
        stay, first, swapped, third,
    )
    return (analysis, innovation.reshape(obs))


def solution(mesh):
    return jax.shard_map(
        shards,
        mesh=mesh,
        in_specs=(
            P("members", None, "cells"),
            P("cells"),
            P("cells"),
            P(),
            P("cells"),
            P("cells"),
            P("cells"),
            P("cells"),
            P("cells", None),
        ),
        out_specs=(P("members", None, "cells"), P("cells")),
        check_vma=False,
    )
```

time: 45.5 us -> 40.2 us (0.88)
  waiting for transfers between devices: 14.7 us -> 8.16 us
  starting transfers between devices: 14.6 us -> 16 us
  local copies, waits for them, and re-layouts: 1.77 us -> 0.86 us
  Pallas kernels: 13.4 us -> 14.1 us
    ppermute x8, waiting for transfers between devices: 13 us -> 7.59 us  [the longest x4 6.01 us: exchange(): lax.ppermute(to_third, BOTH, core_pairs(owners, lambda block, core: (bloc...]
    ppermute x8, starting transfers between devices: 14.1 us -> 15.3 us  [the longest x4 7.93 us: exchange(): lax.ppermute(to_third, BOTH, core_pairs(owners, lambda block, core: (bloc...]
    ppermute x5 -> x6, waiting for transfers between devices: 1.63 us -> 0.57 us  [swap_cores(): lax.ppermute(x, BOTH, core_pairs(owners, lambda block, core: (block, 1 -...]
    unnamed x20 -> x18, local copies, waits for them, and re-layouts: 1.77 us -> 0.86 us
    pallas_call x3 -> x6, Pallas kernels: 13.4 us -> 14.1 us  [the longest x2 4.92 us: forecast(): pl.pallas_call(forecast_kernel, out_shape=(jax.ShapeDtypeStruct((strip_ro...]
  transfers between devices with their start and end apart: 13 -> 14, of which waited for: 8 -> 8; matrix products, arithmetic and copies ran while one was open for 0% -> 0% of each run, Pallas kernels for 0% -> 18%
where the time goes in v2:
time: 40.2 us; the launch traced here: 39.9 us
  starting transfers between devices  16 us (40%)
  Pallas kernels  14.1 us (35%)
  waiting for transfers between devices  8.16 us (20%)
  local copies, waits for them, and re-layouts  0.86 us (2%)
  between operations  0.73 us (2%)
    ppermute x4, starting transfers between devices, exchange(): lax.ppermute(to_third, BOTH, core_pairs(owners, lambda block, core: (bloc...  7.93 us
    ppermute x4, starting transfers between devices, exchange(): lax.ppermute(to_middle, BOTH, core_pairs(owners, lambda block, core: (blo...  7.34 us
    ppermute x4, waiting for transfers between devices, exchange(): lax.ppermute(to_third, BOTH, core_pairs(owners, lambda block, core: (bloc...  6.01 us
    pallas_call x2, Pallas kernels, forecast(): pl.pallas_call(forecast_kernel, out_shape=(jax.ShapeDtypeStruct((strip_ro...  4.92 us
    pallas_call x1, Pallas kernels, shards(): pl.pallas_call(functools.partial(analysis_kernel, units=units, obs_rows=o...  4.05 us
    pallas_call x1, Pallas kernels, shards(): pl.pallas_call(functools.partial(sums_kernel, owners=owners, units=units,...  2.76 us
    pallas_call x1, Pallas kernels, shards(): pl.pallas_call(functools.partial(pack_kernel, rows=obs_rows), out_shape=(...  1.72 us
    ppermute x4, waiting for transfers between devices, exchange(): lax.ppermute(to_middle, BOTH, core_pairs(owners, lambda block, core: (blo...  1.58 us
  transfers between devices with their start and end apart: 14, of which 8 were waited for; matrix products, arithmetic and copies ran while one was open for 0% of the time, Pallas kernels for 18%

profile of v2, /device:TPU:0, one launch (start us, length us, event | category | flops | bytes accessed | tf_op | source)
XLA Modules:
  0.0 39.9 jit_solution(15580716322462697581)
XLA Ops:
  0.6 0.5 %collective-permute-start = (f32[32,4,1024]{2,1,0:T(4,128)}, f32[32,4,1024]{2,1,0:T(4,128)S(1)}, u32[]{:S(2)}, u32[]{:S(2)}) collective-permute-start(f32[32,4,1024]{2,1,0:T(4,128)} %ensemble_ref.1), channel_id=1, source_target_pairs={{0,1},{1,0},{2,3},{3,2},{4,5},{5,4},{6,7},{7,6},{8,9},{9,8},{10,11... | collective-permute-start | bytes 1572872 | tf_op jit(solution)/shard_map/ppermute | solution.py:42
  1.2 1.7 %pack.1 = (f32[8,128]{1,0:T(8,128)}, f32[32,128]{1,0:T(8,128)}) custom-call(s32[1,16]{1,0:T(1,128)} %send_ref.1, f32[32,4,1024]{2,1,0:T(4,128)} %ensemble_ref.1, f32[8,128]{1,0:T(8,128)} %bitcast.9, s32[8,128]{1,0:T(8,128)} %bitcast.13, s32[2,128]{1,0:T(2,128)} %bitcast.21, s32[2,128]{1,0:T(2,128)} %bitcast.22, f32[2,128]{1,0:T(2,128)} %bitcast.17, ...), custom_call_target="tpu_custom_call" | custom-call | tf_op jit(solution)/shard_map/pack/pallas_call | solution.py:593
  3.0 0.7 %copy-done.7 = f32[32,128]{1,0:T(8,128)S(1)} copy-done((f32[32,128]{1,0:T(8,128)S(1)}, f32[32,128]{1,0:T(8,128)}, u32[]{:S(2)}) %copy-start.7) | copy-done | bytes 16408
  3.8 0.6 %collective-permute-done.1 = f32[8,128]{1,0:T(8,128)S(1)} collective-permute-done((f32[8,128]{1,0:T(8,128)}, f32[8,128]{1,0:T(8,128)S(1)}, u32[]{:S(2)}, u32[]{:S(2)}) %collective-permute-start.1) | collective-permute-done | bytes 4128 | tf_op jit(solution)/shard_map/ppermute | solution.py:42
  4.5 3.0 %collective-permute-start.2 = (f32[24,128]{1,0:T(8,128)S(1)}, f32[24,128]{1,0:T(8,128)S(1)}, u32[]{:S(2)}, u32[]{:S(2)}) collective-permute-start(f32[24,128]{1,0:T(8,128)S(1)} %get-tuple-element.40), channel_id=1, source_target_pairs={{0,2},{1,5},{2,0},{3,7},{4,6},{5,1},{6,4},{7,3},{8,10},{9,13},{10,... | collective-permute-start | bytes 36872 | tf_op jit(solution)/shard_map/ppermute | solution.py:46
  7.4 1.5 %collective-permute-start.4 = (f32[24,128]{1,0:T(8,128)S(1)}, f32[24,128]{1,0:T(8,128)S(1)}, u32[]{:S(2)}, u32[]{:S(2)}) collective-permute-start(f32[24,128]{1,0:T(8,128)S(1)} %get-tuple-element.39), channel_id=1, source_target_pairs={{0,6},{1,7},{2,4},{3,5},{4,2},{5,3},{6,0},{7,1},{8,14},{9,15},{10,... | collective-permute-start | bytes 36872 | tf_op jit(solution)/shard_map/ppermute | solution.py:49
  8.9 0.2 collective-permute-done.2.first
  9.2 2.5 %forecast.2 = (f32[128,1024]{1,0:T(8,128)S(1)}, f32[128,128]{1,0:T(8,128)S(1)}, f32[256,128]{1,0:T(8,128)S(1)}) custom-call(f32[4,4]{1,0:T(4,128)S(1)} %copy-done.3, f32[32,4,1024]{2,1,0:T(4,128)S(1)} %copy-done, f32[8,128]{1,0:T(8,128)S(1)} %bitcast.10, s32[8,128]{1,0:T(8,128)S(1)} %bitcast.14), custom_call_target="tpu_custom_call" | custom-call | flops 10485760 | bytes 1048576 | tf_op jit(solution)/shard_map/forecast/pallas_call | solution.py:614
  11.7 0.4 collective-permute-done.4.third
  12.0 0.6 %regroup.1 = (f32[24,128]{1,0:T(8,128)S(1)}, f32[24,128]{1,0:T(8,128)S(1)}, f32[8,128]{1,0:T(8,128)S(1)}) custom-call(s32[2]{0:T(128)S(1)} %pad_add_fusion.which_ref, f32[8,128]{1,0:T(8,128)S(1)} %get-tuple-element.38.kept, f32[24,128]{1,0:T(8,128)S(1)} %collective-permute-done.2.first, f32[24,128]{1,0:T(8,128)S(1)} %collective-permute-done.3.swapped, ...), custom_call_target="tpu_custom_call" | custom-call | tf_op jit(solution)/shard_map/regroup/pallas_call | solution.py:652
  12.7 1.8 %collective-permute-start.5 = (f32[24,128]{1,0:T(8,128)S(1)}, f32[24,128]{1,0:T(8,128)S(1)}, u32[]{:S(2)}, u32[]{:S(2)}) collective-permute-start(f32[24,128]{1,0:T(8,128)S(1)} %get-tuple-element.28), channel_id=1, source_target_pairs={{0,8},{1,17},{2,10},{3,19},{4,12},{5,21},{6,14},{7,23},{8,0},{9,25... | collective-permute-start | bytes 36872 | tf_op jit(solution)/shard_map/ppermute | solution.py:46
  14.5 2.5 %collective-permute-start.7 = (f32[24,128]{1,0:T(8,128)S(1)}, f32[24,128]{1,0:T(8,128)S(1)}, u32[]{:S(2)}, u32[]{:S(2)}) collective-permute-start(f32[24,128]{1,0:T(8,128)S(1)} %get-tuple-element.29.refs_0_), channel_id=1, source_target_pairs={{0,24},{1,25},{2,26},{3,27},{4,28},{5,29},{6,30},{7,31},{8,16},{9,... | collective-permute-start | bytes 36872 | tf_op jit(solution)/shard_map/ppermute | solution.py:49
  17.0 2.5 %forecast.3 = (f32[128,1024]{1,0:T(8,128)S(1)}, f32[128,128]{1,0:T(8,128)S(1)}, f32[256,128]{1,0:T(8,128)S(1)}) custom-call(f32[4,4]{1,0:T(4,128)S(1)} %copy-done.3, f32[32,4,1024]{2,1,0:T(4,128)S(1)} %collective-permute-done.source, f32[8,128]{1,0:T(8,128)S(1)} %bitcast.11, s32[8,128]{1,0:T(8,128)S(1)} %bitcast.15), custom_call_target="tpu_custom_call" | custom-call | flops 10485760 | bytes 1048576 | tf_op jit(solution)/shard_map/forecast/pallas_call | solution.py:614
  19.4 0.5 %collective-permute-done.7.third = f32[24,128]{1,0:T(8,128)S(1)} collective-permute-done((f32[24,128]{1,0:T(8,128)S(1)}, f32[24,128]{1,0:T(8,128)S(1)}, u32[]{:S(2)}, u32[]{:S(2)}) %collective-permute-start.7) | collective-permute-done | bytes 12320 | tf_op jit(solution)/shard_map/ppermute | solution.py:49
  20.0 2.8 %sums.1 = (f32[40,128]{1,0:T(8,128)S(1)}, f32[40,128]{1,0:T(8,128)S(1)}, f32[40,128]{1,0:T(8,128)S(1)}, f32[256,256]{1,0:T(8,128)S(1)}) custom-call(s32[2]{0:T(128)S(1)} %pad_add_fusion.which_ref, f32[4,4]{1,0:T(4,128)S(1)} %copy-done.3, f32[8,128]{1,0:T(8,128)S(1)} %bitcast.12, s32[8,128]{1,0:T(8,128)S(1)} %bitcast.16, ...), custom_call_target="tpu_custom_call" | custom-call | tf_op jit(solution)/shard_map/sums/pallas_call | solution.py:667
  22.7 1.0 %collective-permute-start.9 = (f32[40,128]{1,0:T(8,128)S(1)}, f32[40,128]{1,0:T(8,128)S(1)}, u32[]{:S(2)}, u32[]{:S(2)}) collective-permute-start(f32[40,128]{1,0:T(8,128)S(1)} %get-tuple-element.33), channel_id=1, source_target_pairs={{0,8},{1,17},{2,10},{3,19},{4,12},{5,21},{6,14},{7,23},{8,0},{9,25... | collective-permute-start | bytes 61448 | tf_op jit(solution)/shard_map/ppermute | solution.py:46
  23.7 2.5 %collective-permute-start.8 = (f32[40,128]{1,0:T(8,128)S(1)}, f32[40,128]{1,0:T(8,128)S(1)}, u32[]{:S(2)}, u32[]{:S(2)}) collective-permute-start(f32[40,128]{1,0:T(8,128)S(1)} %get-tuple-element.32), channel_id=1, source_target_pairs={{0,24},{1,25},{2,26},{3,27},{4,28},{5,29},{6,30},{7,31},{8,16},{9,... | collective-permute-start | bytes 61448 | tf_op jit(solution)/shard_map/ppermute | solution.py:49
  26.2 0.6 %collective-permute-done.9 = f32[40,128]{1,0:T(8,128)S(1)} collective-permute-done((f32[40,128]{1,0:T(8,128)S(1)}, f32[40,128]{1,0:T(8,128)S(1)}, u32[]{:S(2)}, u32[]{:S(2)}) %collective-permute-start.9) | collective-permute-done | bytes 20512 | tf_op jit(solution)/shard_map/ppermute | solution.py:46
  26.8 2.7 %collective-permute-done.8 = f32[40,128]{1,0:T(8,128)S(1)} collective-permute-done((f32[40,128]{1,0:T(8,128)S(1)}, f32[40,128]{1,0:T(8,128)S(1)}, u32[]{:S(2)}, u32[]{:S(2)}) %collective-permute-start.8) | collective-permute-done | bytes 20512 | tf_op jit(solution)/shard_map/ppermute | solution.py:49
  29.6 1.5 %collective-permute-start.11 = (f32[40,128]{1,0:T(8,128)S(1)}, f32[40,128]{1,0:T(8,128)S(1)}, u32[]{:S(2)}, u32[]{:S(2)}) collective-permute-start(f32[40,128]{1,0:T(8,128)S(1)} %add_add_fusion.kept), channel_id=1, source_target_pairs={{0,2},{1,5},{2,0},{3,7},{4,6},{5,1},{6,4},{7,3},{8,10},{9,13},{10,... | collective-permute-start | bytes 61448 | tf_op jit(solution)/shard_map/ppermute | solution.py:46
  31.1 1.5 %collective-permute-start.13 = (f32[40,128]{1,0:T(8,128)S(1)}, f32[40,128]{1,0:T(8,128)S(1)}, u32[]{:S(2)}, u32[]{:S(2)}) collective-permute-start(f32[40,128]{1,0:T(8,128)S(1)} %add_add_fusion.kept), channel_id=1, source_target_pairs={{0,6},{1,7},{2,4},{3,5},{4,2},{5,3},{6,0},{7,1},{8,14},{9,15},{10,... | collective-permute-start | bytes 61448 | tf_op jit(solution)/shard_map/ppermute | solution.py:49
  32.6 0.8 %collective-permute-done.11.first = f32[40,128]{1,0:T(8,128)S(1)} collective-permute-done((f32[40,128]{1,0:T(8,128)S(1)}, f32[40,128]{1,0:T(8,128)S(1)}, u32[]{:S(2)}, u32[]{:S(2)}) %collective-permute-start.11) | collective-permute-done | bytes 20512 | tf_op jit(solution)/shard_map/ppermute | solution.py:46
  33.4 2.4 %collective-permute-done.13.third = f32[40,128]{1,0:T(8,128)S(1)} collective-permute-done((f32[40,128]{1,0:T(8,128)S(1)}, f32[40,128]{1,0:T(8,128)S(1)}, u32[]{:S(2)}, u32[]{:S(2)}) %collective-permute-start.13) | collective-permute-done | bytes 20512 | tf_op jit(solution)/shard_map/ppermute | solution.py:49
  35.8 4.0 %analysis.1 = (f32[32,4,1024]{2,1,0:T(4,128)}, f32[2,128]{1,0:T(2,128)}) custom-call(s32[2]{0:T(128)S(1)} %pad_add_fusion.which_ref, s32[1,16]{1,0:T(1,128)S(1)} %copy-done.6, f32[128,1024]{1,0:T(8,128)S(1)} %get-tuple-element.19.own_state.own_ref, f32[128,1024]{1,0:T(8,128)S(1)} %get-tuple-element.20.other_state.other_ref, ...), custom_call_target="tpu_custom_call" | custom-call | tf_op jit(solution)/shard_map/analysis/pallas_call | solution.py:699
  (32 shorter events, 0.4 us)
Async XLA Ops:
  0.6 8.5 %copy-start = (f32[32,4,1024]{2,1,0:T(4,128)S(1)}, f32[32,4,1024]{2,1,0:T(4,128)}, u32[]{:S(2)}) copy-start(f32[32,4,1024]{2,1,0:T(4,128)} %ensemble_ref.1) | copy-start | bytes 1572868
  0.6 16.3 %collective-permute-start = (f32[32,4,1024]{2,1,0:T(4,128)}, f32[32,4,1024]{2,1,0:T(4,128)S(1)}, u32[]{:S(2)}, u32[]{:S(2)}) collective-permute-start(f32[32,4,1024]{2,1,0:T(4,128)} %ensemble_ref.1), channel_id=1, source_target_pairs={{0,1},{1,0},{2,3},{3,2},{4,5},{5,4},{6,7},{7,6},{8,9},{9,8},{10,11... | collective-permute-start | bytes 1572872 | tf_op jit(solution)/shard_map/ppermute | solution.py:42
  2.9 1.4 %collective-permute-start.1 = (f32[8,128]{1,0:T(8,128)}, f32[8,128]{1,0:T(8,128)S(1)}, u32[]{:S(2)}, u32[]{:S(2)}) collective-permute-start(f32[8,128]{1,0:T(8,128)} %get-tuple-element.26), channel_id=1, source_target_pairs={{0,1},{1,0},{2,3},{3,2},{4,5},{5,4},{6,7},{7,6},{8,9},{9,8},{10,11... | collective-permute-start | bytes 12296 | tf_op jit(solution)/shard_map/ppermute | solution.py:42
  3.0 0.7 %copy-start.7 = (f32[32,128]{1,0:T(8,128)S(1)}, f32[32,128]{1,0:T(8,128)}, u32[]{:S(2)}) copy-start(f32[32,128]{1,0:T(8,128)} %get-tuple-element.25) | copy-start | bytes 49156
  3.8 0.7 %copy-start.8 = (f32[8,128]{1,0:T(8,128)S(1)}, f32[8,128]{1,0:T(8,128)}, u32[]{:S(2)}) copy-start(f32[8,128]{1,0:T(8,128)} %get-tuple-element.26) | copy-start | bytes 12292
  4.4 4.7 %copy-start.3 = (f32[4,4]{1,0:T(4,128)S(1)}, f32[4,4]{1,0:T(4,128)}, u32[]{:S(2)}) copy-start(f32[4,4]{1,0:T(4,128)} %couple_ref.5) | copy-start | bytes 196
  4.4 4.7 %copy-start.2 = (s32[1024]{0:T(1024)S(1)}, s32[1024]{0:T(1024)}, u32[]{:S(2)}) copy-start(s32[1024]{0:T(1024)} %param.11) | copy-start | bytes 12292
  4.4 4.7 %copy-start.1 = (f32[1024]{0:T(1024)S(1)}, f32[1024]{0:T(1024)}, u32[]{:S(2)}) copy-start(f32[1024]{0:T(1024)} %param.10) | copy-start | bytes 12292
  4.5 4.6 %collective-permute-start.2 = (f32[24,128]{1,0:T(8,128)S(1)}, f32[24,128]{1,0:T(8,128)S(1)}, u32[]{:S(2)}, u32[]{:S(2)}) collective-permute-start(f32[24,128]{1,0:T(8,128)S(1)} %get-tuple-element.40), channel_id=1, source_target_pairs={{0,2},{1,5},{2,0},{3,7},{4,6},{5,1},{6,4},{7,3},{8,10},{9,13},{10,... | collective-permute-start | bytes 36872 | tf_op jit(solution)/shard_map/ppermute | solution.py:46
  7.4 4.6 %collective-permute-start.4 = (f32[24,128]{1,0:T(8,128)S(1)}, f32[24,128]{1,0:T(8,128)S(1)}, u32[]{:S(2)}, u32[]{:S(2)}) collective-permute-start(f32[24,128]{1,0:T(8,128)S(1)} %get-tuple-element.39), channel_id=1, source_target_pairs={{0,6},{1,7},{2,4},{3,5},{4,2},{5,3},{6,0},{7,1},{8,14},{9,15},{10,... | collective-permute-start | bytes 36872 | tf_op jit(solution)/shard_map/ppermute | solution.py:49
  9.1 2.9 %collective-permute-start.3 = (f32[24,128]{1,0:T(8,128)S(1)}, f32[24,128]{1,0:T(8,128)S(1)}, u32[]{:S(2)}, u32[]{:S(2)}) collective-permute-start(f32[24,128]{1,0:T(8,128)S(1)} %collective-permute-done.2.first), channel_id=1, source_target_pairs={{0,1},{1,0},{2,3},{3,2},{4,5},{5,4},{6,7},{7,6},{8,9},{9,8},{10,11... | collective-permute-start | bytes 36872 | tf_op jit(solution)/shard_map/ppermute | solution.py:42
  12.7 4.3 %collective-permute-start.5 = (f32[24,128]{1,0:T(8,128)S(1)}, f32[24,128]{1,0:T(8,128)S(1)}, u32[]{:S(2)}, u32[]{:S(2)}) collective-permute-start(f32[24,128]{1,0:T(8,128)S(1)} %get-tuple-element.28), channel_id=1, source_target_pairs={{0,8},{1,17},{2,10},{3,19},{4,12},{5,21},{6,14},{7,23},{8,0},{9,25... | collective-permute-start | bytes 36872 | tf_op jit(solution)/shard_map/ppermute | solution.py:46
  14.5 5.5 %collective-permute-start.7 = (f32[24,128]{1,0:T(8,128)S(1)}, f32[24,128]{1,0:T(8,128)S(1)}, u32[]{:S(2)}, u32[]{:S(2)}) collective-permute-start(f32[24,128]{1,0:T(8,128)S(1)} %get-tuple-element.29.refs_0_), channel_id=1, source_target_pairs={{0,24},{1,25},{2,26},{3,27},{4,28},{5,29},{6,30},{7,31},{8,16},{9,... | collective-permute-start | bytes 36872 | tf_op jit(solution)/shard_map/ppermute | solution.py:49
  17.0 3.0 %collective-permute-start.6 = (f32[24,128]{1,0:T(8,128)S(1)}, f32[24,128]{1,0:T(8,128)S(1)}, u32[]{:S(2)}, u32[]{:S(2)}) collective-permute-start(f32[24,128]{1,0:T(8,128)S(1)} %collective-permute-done.5.first), channel_id=1, source_target_pairs={{0,1},{1,0},{2,3},{3,2},{4,5},{5,4},{6,7},{7,6},{8,9},{9,8},{10,11... | collective-permute-start | bytes 36872 | tf_op jit(solution)/shard_map/ppermute | solution.py:42
  22.7 4.1 %collective-permute-start.9 = (f32[40,128]{1,0:T(8,128)S(1)}, f32[40,128]{1,0:T(8,128)S(1)}, u32[]{:S(2)}, u32[]{:S(2)}) collective-permute-start(f32[40,128]{1,0:T(8,128)S(1)} %get-tuple-element.33), channel_id=1, source_target_pairs={{0,8},{1,17},{2,10},{3,19},{4,12},{5,21},{6,14},{7,23},{8,0},{9,25... | collective-permute-start | bytes 61448 | tf_op jit(solution)/shard_map/ppermute | solution.py:46
  23.7 5.8 %collective-permute-start.8 = (f32[40,128]{1,0:T(8,128)S(1)}, f32[40,128]{1,0:T(8,128)S(1)}, u32[]{:S(2)}, u32[]{:S(2)}) collective-permute-start(f32[40,128]{1,0:T(8,128)S(1)} %get-tuple-element.32), channel_id=1, source_target_pairs={{0,24},{1,25},{2,26},{3,27},{4,28},{5,29},{6,30},{7,31},{8,16},{9,... | collective-permute-start | bytes 61448 | tf_op jit(solution)/shard_map/ppermute | solution.py:49
  26.8 2.8 %collective-permute-start.10 = (f32[40,128]{1,0:T(8,128)S(1)}, f32[40,128]{1,0:T(8,128)S(1)}, u32[]{:S(2)}, u32[]{:S(2)}) collective-permute-start(f32[40,128]{1,0:T(8,128)S(1)} %collective-permute-done.9), channel_id=1, source_target_pairs={{0,1},{1,0},{2,3},{3,2},{4,5},{5,4},{6,7},{7,6},{8,9},{9,8},{10,11... | collective-permute-start | bytes 61448 | tf_op jit(solution)/shard_map/ppermute | solution.py:42
  29.5 6.3 %copy-start.5 = (f32[256]{0:T(256)S(1)}, f32[256]{0:T(256)}, u32[]{:S(2)}) copy-start(f32[256]{0:T(256)} %param.16) | copy-start | bytes 3076
  29.6 6.2 %copy-start.4 = (f32[256]{0:T(256)S(1)}, f32[256]{0:T(256)}, u32[]{:S(2)}) copy-start(f32[256]{0:T(256)} %param.15) | copy-start | bytes 3076
  29.6 6.2 %copy-start.6 = (s32[1,16]{1,0:T(1,128)S(1)}, s32[1,16]{1,0:T(1,128)}, u32[]{:S(2)}) copy-start(s32[1,16]{1,0:T(1,128)} %send_ref.1) | copy-start | bytes 196
  29.6 3.8 %collective-permute-start.11 = (f32[40,128]{1,0:T(8,128)S(1)}, f32[40,128]{1,0:T(8,128)S(1)}, u32[]{:S(2)}, u32[]{:S(2)}) collective-permute-start(f32[40,128]{1,0:T(8,128)S(1)} %add_add_fusion.kept), channel_id=1, source_target_pairs={{0,2},{1,5},{2,0},{3,7},{4,6},{5,1},{6,4},{7,3},{8,10},{9,13},{10,... | collective-permute-start | bytes 61448 | tf_op jit(solution)/shard_map/ppermute | solution.py:46
  31.1 4.7 %collective-permute-start.13 = (f32[40,128]{1,0:T(8,128)S(1)}, f32[40,128]{1,0:T(8,128)S(1)}, u32[]{:S(2)}, u32[]{:S(2)}) collective-permute-start(f32[40,128]{1,0:T(8,128)S(1)} %add_add_fusion.kept), channel_id=1, source_target_pairs={{0,6},{1,7},{2,4},{3,5},{4,2},{5,3},{6,0},{7,1},{8,14},{9,15},{10,... | collective-permute-start | bytes 61448 | tf_op jit(solution)/shard_map/ppermute | solution.py:49
  33.4 2.4 %collective-permute-start.12 = (f32[40,128]{1,0:T(8,128)S(1)}, f32[40,128]{1,0:T(8,128)S(1)}, u32[]{:S(2)}, u32[]{:S(2)}) collective-permute-start(f32[40,128]{1,0:T(8,128)S(1)} %collective-permute-done.11.first), channel_id=1, source_target_pairs={{0,1},{1,0},{2,3},{3,2},{4,5},{5,4},{6,7},{7,6},{8,9},{9,8},{10,11... | collective-permute-start | bytes 61448 | tf_op jit(solution)/shard_map/ppermute | solution.py:42

commit v3 on v2

--- a/solution.py
+++ b/solution.py
@@ -42,56 +42,57 @@
     return lax.ppermute(x, BOTH, core_pairs(owners, lambda block, core: (block, 1 - core)))
 
 
-def exchange(to_middle, to_third, owners, unit):
-    first = lax.ppermute(
-        to_middle, BOTH, core_pairs(owners, lambda block, core: (block ^ (unit * (1 + core)), core))
-    )
-    third = lax.ppermute(
-        to_third, BOTH, core_pairs(owners, lambda block, core: (block ^ (unit * 3), core))
-    )
-    return first, swap_cores(first, owners), third
+def exchange(to_odd, to_even, owners, unit):
+    odd = lax.ppermute(
+        to_odd, BOTH, core_pairs(owners, lambda block, core: (block ^ (unit * (1 + 2 * core)), core))
+    )
+    even = lax.ppermute(
+        to_even, BOTH, core_pairs(owners, lambda block, core: (block ^ (unit * 2), core))
+    )
+    return odd, swap_cores(odd, owners), even
 
 
 def digit_of(block, unit):
-    return jnp.bitwise_and(lax.div(block, jnp.int32(unit)), 3)
+    return jnp.bitwise_and(lax.shift_right_logical(block, jnp.int32(unit.bit_length() - 1)), 3)
+
+
+def within(shift, wide):
+    shift = jnp.where(shift < 0, shift + wide, shift)
+    return jnp.where(shift >= wide, shift - wide, shift)
 
 
 def table_row(number, count):
     return (number % 4) * (count // 4) + number // 4
 
 
+def strips_of(head, tail):
+    fields, cells = tail.shape[1:]
+    lane = lax.broadcasted_iota(jnp.int32, (1, LANES), 1)
+    ends = [jnp.where(lane < STEPS, head[:, f, :LANES], tail[:, f, cells - LANES :]) for f in range(fields)]
+    ends = jnp.transpose(jnp.concatenate(ends, axis=0))
+    return jnp.concatenate([ends[:STEPS, :], ends[LANES - STEPS :, :]], axis=0)
+
+
 def pack_kernel(
-    send_in, ensemble_ref, speed_in, flag_in, place_in, field_in, value_in, sigma_in,
-    strip_ref, table_ref, send_ref, head, tail, speed_ref, flag_ref, place_ref, field_ref, value_ref,
-    sigma_ref, sems, *, rows,
+    which_ref, send_ref, speed_ref, flag_ref, place_ref, field_ref, value_ref, sigma_ref,
+    kept_ref, odd_ref, even_ref, small_ref, table_ref, *, rows, cells, fields,
 ):
-    fields, cells = ensemble_ref.shape[1:]
-    small = (
-        (send_in, send_ref), (speed_in, speed_ref), (flag_in, flag_ref), (place_in, place_ref),
-        (field_in, field_ref), (value_in, value_ref), (sigma_in, sigma_ref),
-    )
-    large = (
-        (ensemble_ref.at[:, :, pl.ds(0, LANES)], head),
-        (ensemble_ref.at[:, :, pl.ds(cells - LANES, LANES)], tail),
-    )
-    copies = [
-        pltpu.make_async_copy(source, target, sems.at[i])
-        for i, (source, target) in enumerate(large + small)
-    ]
-    for copy in copies:
-        copy.start()
-    for copy in copies[2:]:
-        copy.wait()
-    tiles = speed_ref.shape[0]
+    tiles = cells // LANES
+    speed, value, sigma = speed_ref[...], value_ref[...], sigma_ref[...]
+    flag, place, field = (ref[...].astype(jnp.float32) for ref in (flag_ref, place_ref, field_ref))
+    at = 0
+    for part in (speed, flag, value, sigma):
+        small_ref[at : at + part.shape[0], :] = part
+        at += part.shape[0]
     lane = lax.broadcasted_iota(jnp.int32, (1, LANES), 1)
     low = lane < LANES // 2
-    toward_left = speed_ref[...] * flag_ref[...].astype(jnp.float32)
-    toward_right = speed_ref[...] - toward_left
+    toward_left = speed * flag
+    toward_right = speed - toward_left
     edge_left = jnp.where(low, toward_left[:1], toward_left[tiles - 1 :])
     edge_right = jnp.where(low, toward_right[:1], toward_right[tiles - 1 :])
-    ids = (field_ref[...] * cells + place_ref[...]).astype(jnp.float32)
-    weight = 1.0 / (sigma_ref[...] * sigma_ref[...])
-    pull = weight * value_ref[...]
+    ids = field * float(cells) + place
+    weight = 1.0 / (sigma * sigma)
+    pull = weight * value
     wide = rows * LANES
 
     def row_of(x):
@@ -106,74 +107,77 @@
     empty = jnp.where(sub == 3, edge_left, jnp.where(sub == 4, edge_right, empty))
     owners = send_ref.shape[1]
     count = owners // GROUPS
-    for r in range(count):
-        table_ref[8 * table_row(r, count) : 8 * table_row(r, count) + 8, :] = empty
+    table = [empty] * count
     start = jnp.int32(0)
     for owner in range(owners):
         held = send_ref[0, owner]
         group, r = owner // count, owner % count
-        moved = pltpu.roll(listed, lax.rem(group * CAP - start + 2 * wide, jnp.int32(wide)), 1)[:, :LANES]
+        moved = pltpu.roll(listed, within(group * CAP - start, wide), 1)[:, :LANES]
         here = (lane8 >= group * CAP) & (lane8 < group * CAP + held) & (sub < 3)
+        table[r] = jnp.where(here, moved, table[r])
+        start = start + held
+    for r in range(count):
         row = 8 * table_row(r, count)
-        table_ref[row : row + 8, :] = jnp.where(here, moved, table_ref[row : row + 8, :])
-        start = start + held
-    for copy in copies[:2]:
-        copy.wait()
-    head_rows = jnp.concatenate([head[:, f, :] for f in range(fields)], axis=0)
-    tail_rows = jnp.concatenate([tail[:, f, :] for f in range(fields)], axis=0)
-    strip_ref[:STEPS, :] = jnp.transpose(head_rows)[:STEPS, :]
-    strip_ref[STEPS:, :] = jnp.transpose(tail_rows)[LANES - STEPS :, :]
-
-
-def incoming(digit, core, first, swapped, third):
+        table_ref[row : row + 8, :] = table[r]
+    part = kept_ref.shape[0]
+    digit = digit_of(which_ref[0], 1)
+    for out, partner in ((kept_ref, 0), (odd_ref, 1 + 2 * which_ref[1]), (even_ref, 2)):
+        out[...] = table_ref[pl.ds(pl.multiple_of(jnp.bitwise_xor(digit, partner) * part, 8), part), :]
+
+
+def strips_kernel(ensemble_ref, out_ref):
+    out_ref[...] = strips_of(ensemble_ref, ensemble_ref)
+
+
+def join_kernel(own_ref, other_ref, odd_part, even_part, odd_ref, even_ref):
+    strips = jnp.concatenate([own_ref[...], strips_of(other_ref, other_ref)], axis=0)
+    for part, out in ((odd_part, odd_ref), (even_part, even_ref)):
+        out[:16, :] = strips
+        out[16:, :] = part[...]
+
+
+def incoming(digit, core, odd, swapped):
     sub = lax.broadcasted_iota(jnp.int32, (8, LANES), 0)
     low = lax.broadcasted_iota(jnp.int32, (8, LANES), 1) < LANES // 2
-    odd = jnp.bitwise_and(digit, 1) == 1
+    direct = jnp.bitwise_xor(jnp.bitwise_and(digit, 1), core) == 0
     result = []
     for part, other_part in ((0, 1), (1, 0), (2, 2)):
-        near = jnp.where(
-            core == 0, first[8 * part : 8 * part + 8, :], swapped[8 * other_part : 8 * other_part + 8, :]
-        )
-        far = third[8 * part : 8 * part + 8, :]
-        from_right = jnp.where(odd, far, near)
-        from_left = jnp.where(odd, near, far)
+        mine = odd[8 * part : 8 * part + 8, :]
+        others = swapped[8 * other_part : 8 * other_part + 8, :]
+        from_right = jnp.where(direct, mine, others)
+        from_left = jnp.where(direct, others, mine)
         result.append(jnp.where(sub < STEPS if part < 2 else low, from_right, from_left))
     return result
 
 
 def regroup_kernel(
-    which_ref, kept, first, swapped, third, _, to_middle, to_third, stay, *, unit, into_lanes,
+    which_ref, kept, odd, swapped, even, _, to_odd, to_even, stay, *, unit, into_lanes,
 ):
     block, core = which_ref[0], which_ref[1]
-    digit = digit_of(block, unit)
     after = digit_of(block, unit * 4)
-    own, other, coefs = incoming(digit, core, first, swapped, third)
+    own, other, coefs = incoming(digit_of(block, unit), core, odd, swapped)
     sub = lax.broadcasted_iota(jnp.int32, (8, LANES), 0)
     lane_group = lax.broadcasted_iota(jnp.int32, (8, LANES), 1) // CAP
-    held = (third.shape[0] - 16) // 8
-    for target, partner in ((to_middle, 1 + core), (to_third, 3), (stay, 0)):
+    held = kept.shape[0] // 8
+
+    def received(k, at):
+        if k == 0:
+            return kept[pl.ds(at, 8), :]
+        if k == 2:
+            return even[pl.ds(16 + at, 8), :]
+        mine, others = odd[pl.ds(16 + at, 8), :], swapped[pl.ds(16 + at, 8), :]
+        return jnp.where(core == k // 2, mine, others)
+
+    for target in (to_odd, to_even):
+        target[0:8, :] = own
+        target[8:16, :] = other
+    for target, base, partner in ((to_odd, 16, 1 + 2 * core), (to_even, 16, 2), (stay, 0, 0)):
         wanted = jnp.bitwise_xor(after, partner)
-        base = 0
-        if target is not stay:
-            target[0:8, :] = own
-            target[8:16, :] = other
-            base = 16
-
-        def received(k, at):
-            if k == 0:
-                return kept[pl.ds(at, 8), :]
-            if k == 3:
-                return third[pl.ds(16 + at, 8), :]
-            a, b = first[pl.ds(16 + at, 8), :], swapped[pl.ds(16 + at, 8), :]
-            return jnp.where(core == k - 1, a, b)
-
         if into_lanes:
             for j in range(held):
                 merged = coefs
                 for k in range(4):
-                    moved = pltpu.roll(
-                        received(k, 8 * j), jnp.bitwise_and(k - wanted, 3) * CAP, 1
-                    )
+                    moved = pltpu.roll(received(k, 8 * j), jnp.bitwise_and(k - wanted, 3) * CAP, 1)
                     merged = jnp.where((lane_group == k) & (sub < 3), moved, merged)
                 target[base + 8 * j : base + 8 * j + 8, :] = merged
         else:
@@ -202,12 +206,12 @@
 
 
 def forecast_kernel(
-    couple_ref, source, speed_ref, flag_ref, state, edge, sums_ref, work_ref, coef_ref,
+    couple_ref, source, small_ref, state, edge, sums_ref, work_ref, coef_ref,
 ):
     members, fields, cells = source.shape
     tiles = cells // LANES
-    speed = speed_ref[...]
-    toward_left = speed * flag_ref[...].astype(jnp.float32)
+    speed = small_ref[:tiles, :]
+    toward_left = speed * small_ref[tiles : 2 * tiles, :]
     toward_right = speed - toward_left
 
     def row_of(x):
@@ -259,6 +263,11 @@
     lax.fori_loop(0, members // 8, group, 0)
 
 
+def halves_of(x):
+    high = x.astype(jnp.bfloat16)
+    return high, (x - high.astype(jnp.float32)).astype(jnp.bfloat16)
+
+
 def pieces_of(x):
     high = x.astype(jnp.bfloat16).astype(jnp.float32)
     rest = x - high
@@ -267,12 +276,12 @@
 
 
 def sums_kernel(
-    which_ref, couple_ref, speed_ref, flag_ref, own_state, own_edge, own_sums, other_state, other_edge, other_sums,
-    kept, first, swapped, third, *refs, owners, units, fields,
+    which_ref, couple_ref, small_ref, own_state, own_edge, own_sums, other_state, other_edge, other_sums,
+    kept, odd, swapped, even, *refs, owners, units, fields,
 ):
     carried = refs[: len(units) - 1]
     (
-        stay_ref, middle_ref, third_ref, edge_ref, halo_ref, onehot_ref, spread_ref, split_ref,
+        stay_ref, odd_ref, even_ref, edge_ref, halo_ref, onehot_ref, spread_ref, split_ref,
     ) = refs[len(units) - 1 :]
     states, raw_edges = (own_state, other_state), (own_edge, other_edge)
     block, core = which_ref[0], which_ref[1]
@@ -289,7 +298,7 @@
     half_lanes = LANES // 2
     low = lane < half_lanes
 
-    strips = incoming(digit_of(block, units[-1]), core, first, swapped, third)
+    strips = incoming(digit_of(block, units[-1]), core, odd, swapped)
     for unit, earlier in reversed(list(zip(units, carried))):
         digit = digit_of(block, unit)
         rows = [earlier[8 * p : 8 * p + 8, :] for p in range(3)]
@@ -314,8 +323,8 @@
         halo_ref[half * strip_rows : (half + 1) * strip_rows, :] = jnp.transpose(
             jnp.concatenate([left, gap, right, rest], axis=0)
         )
-    speed = speed_ref[...]
-    toward_left = speed * flag_ref[...].astype(jnp.float32)
+    speed = small_ref[:tiles, :]
+    toward_left = speed * small_ref[tiles : 2 * tiles, :]
     toward_right = speed - toward_left
     is_left = lane < STEPS
     is_right = (lane >= right_first) & (lane < right_first + STEPS)
@@ -377,8 +386,8 @@
     lane_ids = lax.broadcasted_iota(jnp.int32, (LANES, LANES), 0)
     held = kept.shape[0] // 8
     sources = [(kept, 8 * j) for j in range(held)]
-    for source in (first, swapped, third):
-        sources += [(source, 16 + 8 * j) for j in range(held)]
+    for source, base in ((odd, 16), (swapped, 16), (even, 16)):
+        sources += [(source, base + 8 * j) for j in range(held)]
     hits = []
     for n, (source, at) in enumerate(sources):
         local = source[at : at + 1, :].astype(jnp.int32)
@@ -403,8 +412,8 @@
     depth = total + 16
 
     def put(row, lanes, value):
-        for p, piece in enumerate(pieces_of(value)):
-            split_ref[pl.ds(row + p * depth, value.shape[0]), lanes] = piece.astype(jnp.bfloat16)
+        for p, piece in enumerate(halves_of(value)):
+            split_ref[pl.ds(row + p * depth, value.shape[0]), lanes] = piece
 
     for f in range(fields):
         for t in range(tiles):
@@ -426,12 +435,12 @@
     )
     gram = sum(
         products[p * depth : p * depth + total + 8, q * depth : q * depth + total]
-        for p, q in ((2, 0), (1, 1), (0, 2), (1, 0), (0, 1), (0, 0))
+        for p, q in ((1, 1), (1, 0), (0, 1), (0, 0))
     )
     gram = jnp.concatenate([gram, jnp.zeros((total + 8, LANES - total), jnp.float32)], axis=1)
     folded = gram[:members] + pltpu.roll(gram[members:total], total, 1)
     blank = jnp.zeros((stay_ref.shape[0] - members - 1, LANES), jnp.float32)
-    for out in (stay_ref, middle_ref, third_ref):
+    for out in (stay_ref, odd_ref, even_ref):
         out[:members, :] = folded
         out[members : members + 1, :] = gram[total : total + 1]
         out[members + 1 :, :] = blank
@@ -441,7 +450,7 @@
         (((1,), (0,)), ((), ())), preferred_element_type=jnp.float32,
     )
     found = found[:places] + found[places : 2 * places] + found[2 * places :]
-    for out, source, partner in ((stay_ref, 0, 0), (middle_ref, 1, 1 + core), (third_ref, 3, 3)):
+    for out, source, partner in ((stay_ref, 0, 0), (odd_ref, 1, 1 + 2 * core), (even_ref, 3, 2)):
         for j in range(held):
             n = source * held + j
             center = jnp.sum(
@@ -480,19 +489,32 @@
 
 
 def analysis_kernel(
-    which_ref, send_ref, own_ref, other_ref, edge_ref, value_ref, sigma_ref, kept, first, swapped, third,
-    analysis_ref, innovation_ref, mixing_ref, center_ref, *, units, obs_rows,
+    which_ref, send_ref, own_ref, other_ref, edge_ref, small_ref, kept, odd, swapped, even,
+    analysis_ref, innovation_ref, mixing_ref, center_ref, pieces_ref, *, units, obs_rows,
 ):
     block, core = which_ref[0], which_ref[1]
     members, fields, cells = analysis_ref.shape
     total = 2 * members
+    strip_rows = fields * members
+    for f in range(fields):
+        for half, state in enumerate((own_ref, other_ref)):
+            rows = slice(f * members, (f + 1) * members)
+            edges = slice(half * strip_rows + f * members, half * strip_rows + (f + 1) * members)
+            for lanes, value in (
+                (slice(0, LANES), edge_ref[edges, :LANES]),
+                (slice(LANES, cells - LANES), state[rows, LANES : cells - LANES]),
+                (slice(cells - LANES, cells), edge_ref[edges, LANES:]),
+            ):
+                for p, piece in enumerate(halves_of(value)):
+                    at = (f * 2 + p) * total + half * members
+                    pieces_ref[at : at + members, lanes] = piece
     head = members + 1
-    sums = (kept[:head, :] + third[:head, :]) + (first[:head, :] + swapped[:head, :])
+    sums = (kept[:head, :] + even[:head, :]) + (odd[:head, :] + swapped[:head, :])
     returned = kept.shape[0] - head
     center_ref[:returned, :] = kept[head:, :]
-    center_ref[returned : 2 * returned, :] = jnp.where(core == 0, first[head:, :], swapped[head:, :])
-    center_ref[2 * returned : 3 * returned, :] = jnp.where(core == 0, swapped[head:, :], first[head:, :])
-    center_ref[3 * returned :, :] = third[head:, :]
+    center_ref[returned : 2 * returned, :] = jnp.where(core == 0, odd[head:, :], swapped[head:, :])
+    center_ref[2 * returned : 3 * returned, :] = even[head:, :]
+    center_ref[3 * returned :, :] = jnp.where(core == 0, swapped[head:, :], odd[head:, :])
     lane = lax.broadcasted_iota(jnp.int32, (8, LANES), 1)
     sub = lax.broadcasted_iota(jnp.int32, (8, LANES), 0)
     shifted = pltpu.roll(sums[:members], LANES - total, 1)
@@ -507,11 +529,12 @@
     cross = sums[members : members + 1]
     inverse = [jnp.where(lane < total, pltpu.roll(r, LANES - total, 1), 0.0) for r in rows]
     carried = [jnp.sum(r * cross, axis=1, keepdims=True) for r in inverse]
-    weights = sum(jnp.sum(r * c, axis=0, keepdims=True) for r, c in zip(inverse, carried))
-    row_means = [jnp.sum(r, axis=1, keepdims=True) * (1.0 / total) for r in inverse]
-    column_mean = sum(jnp.sum(r, axis=0, keepdims=True) for r in inverse) * (1.0 / total)
-    grand = jnp.sum(column_mean, axis=1, keepdims=True) * (1.0 / total)
-    weights = weights - jnp.sum(weights, axis=1, keepdims=True) * (1.0 / total)
+    row_sums = [jnp.sum(r, axis=1, keepdims=True) for r in inverse]
+    row_means = [r * (1.0 / total) for r in row_sums]
+    weights = jnp.sum(sum(r * c for r, c in zip(inverse, carried)), axis=0, keepdims=True)
+    column_mean = jnp.sum(sum(inverse), axis=0, keepdims=True) * (1.0 / total)
+    grand = jnp.sum(sum(row_means), axis=0, keepdims=True) * (1.0 / total)
+    weights = weights - jnp.sum(sum(r * c for r, c in zip(row_means, carried)), axis=0, keepdims=True)
     root = math.sqrt(total - 1.0)
     add = weights + 1.0 / total - root * (column_mean - grand)
     for b in range(total // 8):
@@ -520,24 +543,16 @@
     rolled = pltpu.roll(own_rows, LANES - members, 1)
     to_own = jnp.where(core == 0, own_rows, rolled)[:, :members]
     to_other = jnp.where(core == 0, rolled, own_rows)[:, :members]
-    mixing = jnp.concatenate([to_own, to_other], axis=1)
-    strip_rows = fields * members
+    high, rest = halves_of(jnp.concatenate([to_own, to_other], axis=1))
+    mixing = jnp.concatenate(
+        [jnp.concatenate([high, high], axis=1), jnp.concatenate([rest, rest], axis=1)], axis=0
+    )
     for f in range(fields):
-        rows = slice(f * members, (f + 1) * members)
-        other_rows = slice(strip_rows + f * members, strip_rows + (f + 1) * members)
-        states = jnp.concatenate(
-            [
-                jnp.concatenate([edge_ref[rows, :LANES], edge_ref[other_rows, :LANES]], axis=0),
-                jnp.concatenate(
-                    [own_ref[rows, LANES : cells - LANES], other_ref[rows, LANES : cells - LANES]], axis=0
-                ),
-                jnp.concatenate([edge_ref[rows, LANES:], edge_ref[other_rows, LANES:]], axis=0),
-            ],
-            axis=1,
+        product = jnp.dot(
+            mixing, pieces_ref[f * 2 * total : (f + 1) * 2 * total, :], preferred_element_type=jnp.float32
         )
-        analysis_ref[:, f, :] = jnp.dot(
-            mixing, states, precision=EXACT, preferred_element_type=jnp.float32
-        )
+        analysis_ref[:, f, :] = product[:members] + product[members:]
+
     owners = send_ref.shape[1]
     held = owners // 16
     wide = obs_rows * LANES
@@ -556,13 +571,15 @@
         row = row + way[0] * returned
         line = center_ref[pl.ds(row, 1), :]
         line = jnp.concatenate([line] + [jnp.zeros((1, LANES), jnp.float32)] * (obs_rows - 1), axis=1)
-        moved = pltpu.roll(line, lax.rem(start - way[-2] * CAP + 2 * wide, jnp.int32(wide)), 1)
+        moved = pltpu.roll(line, within(start - way[-2] * CAP, wide), 1)
         end = start + send_ref[0, owner]
         centers = jnp.where((slot >= start) & (slot < end), moved, centers)
         start = end
     for r in range(obs_rows):
         center = centers[:, r * LANES : (r + 1) * LANES]
-        innovation_ref[r : r + 1, :] = (value_ref[r : r + 1, :] - center) / sigma_ref[r : r + 1, :]
+        at = small_ref.shape[0] - 2 * obs_rows + r
+        value, sigma = small_ref[at : at + 1, :], small_ref[at + obs_rows : at + obs_rows + 1, :]
+        innovation_ref[r : r + 1, :] = (value - center) / sigma
 
 
 def shards(
@@ -579,10 +596,9 @@
     block = lax.axis_index("cells").astype(jnp.int32)
     core = lax.axis_index("members").astype(jnp.int32)
     which = jnp.stack([block, core])
-    speed = speed.reshape(tiles, LANES)
-    direction = direction.reshape(tiles, LANES)
-    obs_place, obs_field, obs_value, obs_sigma = (
-        x.reshape(obs_rows, LANES) for x in (obs_place, obs_field, obs_value, obs_sigma)
+    small = (
+        speed.reshape(tiles, LANES), direction.reshape(tiles, LANES),
+        *(x.reshape(obs_rows, LANES) for x in (obs_place, obs_field, obs_value, obs_sigma)),
     )
     whole = pl.BlockSpec(memory_space=pltpu.VMEM)
     scalars = pl.BlockSpec(memory_space=pltpu.SMEM)
@@ -590,25 +606,37 @@
     real = jnp.float32
 
     table_rows = 8 * (owners // GROUPS)
-    strips, table = pl.pallas_call(
-        functools.partial(pack_kernel, rows=obs_rows),
-        out_shape=(jax.ShapeDtypeStruct((8, LANES), real), jax.ShapeDtypeStruct((table_rows, LANES), real)),
-        in_specs=[pl.BlockSpec(memory_space=pltpu.HBM)] * 8,
-        out_specs=(whole, whole),
-        scratch_shapes=[
-            pltpu.SMEM(send_count.shape, jnp.int32),
-            pltpu.VMEM((members, fields, LANES), real),
-            pltpu.VMEM((members, fields, LANES), real),
-            pltpu.VMEM((tiles, LANES), real),
-            pltpu.VMEM((tiles, LANES), jnp.int32),
-            pltpu.VMEM((obs_rows, LANES), jnp.int32),
-            pltpu.VMEM((obs_rows, LANES), jnp.int32),
-            pltpu.VMEM((obs_rows, LANES), real),
-            pltpu.VMEM((obs_rows, LANES), real),
-            pltpu.SemaphoreType.DMA((9,)),
-        ],
+    part = table_rows // 4
+    other = swap_cores(ensemble, owners)
+    rows_of = lambda count: pl.BlockSpec((count, LANES), lambda i: (0, 0))
+    small_rows = 2 * tiles + 2 * obs_rows
+    strips = pl.pallas_call(
+        strips_kernel,
+        out_shape=jax.ShapeDtypeStruct((8, LANES), real),
+        in_specs=[whole],
+        out_specs=whole,
+        compiler_params=params,
+        name="strips",
+    )(ensemble)
+    kept, to_odd, to_even, small = pl.pallas_call(
+        functools.partial(pack_kernel, rows=obs_rows, cells=cells, fields=fields),
+        out_shape=(jax.ShapeDtypeStruct((part, LANES), real),) * 3
+        + (jax.ShapeDtypeStruct((small_rows, LANES), real),),
+        grid=(1,),
+        in_specs=[scalars, scalars] + [rows_of(x.shape[0]) for x in small],
+        out_specs=(whole,) * 4,
+        scratch_shapes=[pltpu.VMEM((table_rows, LANES), real)],
+        compiler_params=params,
         name="pack",
-    )(send_count, ensemble, speed, direction, obs_place, obs_field, obs_value, obs_sigma)
+    )(which, send_count, *small)
+    to_odd, to_even = pl.pallas_call(
+        join_kernel,
+        out_shape=(jax.ShapeDtypeStruct((16 + part, LANES), real),) * 2,
+        in_specs=[whole] * 4,
+        out_specs=(whole,) * 2,
+        compiler_params=params,
+        name="join",
+    )(strips, other, to_odd, to_even)
 
     def forecast(half):
         return pl.pallas_call(
@@ -618,7 +646,7 @@
                 jax.ShapeDtypeStruct((strip_rows, LANES), real),
                 jax.ShapeDtypeStruct((places * 8, LANES), real),
             ),
-            in_specs=[scalars] + [whole] * 3,
+            in_specs=[scalars] + [whole] * 2,
             out_specs=(whole,) * 3,
             scratch_shapes=[
                 pltpu.VMEM((fields * 8, cells), real),
@@ -629,72 +657,60 @@
                 flops=80 * strip_rows * cells, bytes_accessed=8 * strip_rows * cells, transcendentals=0
             ),
             name="forecast",
-        )(couple, half, speed, direction)
+        )(couple, half, small)
 
     strip_rows = fields * members
-    other_strips = swap_cores(strips, owners)
-    other = swap_cores(ensemble, owners)
     own_forecast = forecast(ensemble)
-    part = table_rows // 4
-    digit = digit_of(block, 1)
-
-    def part_of(partner):
-        return lax.dynamic_slice_in_dim(table, jnp.bitwise_xor(digit, partner) * part, part, 0)
-
-    kept = part_of(0)
-    to_middle = jnp.concatenate([strips, other_strips, part_of(1 + core)], axis=0)
-    to_third = jnp.concatenate([strips, other_strips, part_of(3)], axis=0)
     carried = []
     for n, unit in enumerate(units):
-        arrived = exchange(to_middle, to_third, owners, unit)
+        arrived = exchange(to_odd, to_even, owners, unit)
         if n + 1 < len(units):
-            payload = jax.ShapeDtypeStruct(to_third.shape, real)
-            to_middle, to_third, kept = pl.pallas_call(
+            to_odd, to_even, kept = pl.pallas_call(
                 functools.partial(regroup_kernel, unit=unit, into_lanes=n + 2 == len(units)),
-                out_shape=(payload, payload, jax.ShapeDtypeStruct(kept.shape, real)),
+                out_shape=tuple(jax.ShapeDtypeStruct(x.shape, real) for x in (to_odd, to_even, kept)),
                 in_specs=[scalars] + [whole] * 4 + [pl.BlockSpec(memory_space=pl.ANY)],
                 out_specs=(whole,) * 3,
                 compiler_params=params,
                 name="regroup",
             )(which, kept, *arrived, own_forecast[2])
-            carried.append(to_third)
+            carried.append(to_odd)
     other_forecast = forecast(other)
 
     held = kept.shape[0] // 8
     sums_rows = -(-(members + 1 + 4 * held) // 8) * 8
     all_slots = 4 * held * LANES
     sums = jax.ShapeDtypeStruct((sums_rows, LANES), real)
-    stay, to_middle, to_third, edges = pl.pallas_call(
+    stay, to_odd, to_even, edges = pl.pallas_call(
         functools.partial(sums_kernel, owners=owners, units=units, fields=fields),
         out_shape=(sums, sums, sums, jax.ShapeDtypeStruct((2 * strip_rows, 2 * LANES), real)),
-        in_specs=[scalars, scalars] + [whole] * (12 + len(carried)),
+        in_specs=[scalars, scalars] + [whole] * (11 + len(carried)),
         out_specs=(whole,) * 4,
         scratch_shapes=[
             pltpu.VMEM((2 * strip_rows, LANES), real),
             pltpu.VMEM((LANES, all_slots), jnp.bfloat16),
             pltpu.VMEM((6 * places, all_slots), jnp.bfloat16),
-            pltpu.VMEM((3 * (total + 16), fields * cells), jnp.bfloat16),
+            pltpu.VMEM((2 * (total + 16), fields * cells), jnp.bfloat16),
         ],
         compiler_params=params,
         name="sums",
     )(
-        which, couple, speed, direction, *own_forecast, *other_forecast, kept, *arrived, *carried,
+        which, couple, small, *own_forecast, *other_forecast, kept, *arrived, *carried,
     )
 
     head = members + 1
     used = head + 4 * held
     for n, unit in enumerate(reversed(units)):
-        first, swapped, third = exchange(to_middle, to_third, owners, unit)
+        odd, swapped, even = exchange(to_odd, to_even, owners, unit)
         if n + 1 < len(units):
-            added = (stay + third) + (first + swapped)
+            added = (stay + even) + (odd + swapped)
             if n > 0:
-                near = jnp.where(core == 0, first, swapped)
-                middle = jnp.where(core == 0, swapped, first)
+                first = jnp.where(core == 0, odd, swapped)
+                third = jnp.where(core == 0, swapped, odd)
                 added = jnp.concatenate(
-                    [added[:head]] + [x[head:used] for x in (stay, near, middle, third)], axis=0
+                    [added[:head]] + [x[head:used] for x in (stay, first, even, third)], axis=0
                 )
                 used = added.shape[0]
-            stay = to_middle = to_third = added
+            stay = to_odd = to_even = added
 
     analysis, innovation = pl.pallas_call(
         functools.partial(analysis_kernel, units=units, obs_rows=obs_rows),
@@ -702,17 +718,18 @@
             jax.ShapeDtypeStruct((members, fields, cells), real),
             jax.ShapeDtypeStruct((obs_rows, LANES), real),
         ),
-        in_specs=[scalars, scalars] + [whole] * 9,
+        in_specs=[scalars, scalars] + [whole] * 8,
         out_specs=(whole, whole),
         scratch_shapes=[
             pltpu.VMEM((total, LANES), real),
             pltpu.VMEM((4 * (stay.shape[0] - head), LANES), real),
+            pltpu.VMEM((fields * 2 * total, cells), jnp.bfloat16),
         ],
         compiler_params=params,
         name="analysis",
     )(
-        which, send_count, own_forecast[0], other_forecast[0], edges, obs_value, obs_sigma,
-        stay, first, swapped, third,
+        which, send_count, own_forecast[0], other_forecast[0], edges, small,
+        stay, odd, swapped, even,
     )
     return (analysis, innovation.reshape(obs))
 

time: 40.2 us -> 37.1 us (0.923)
  waiting for transfers between devices: 8.16 us -> 3.21 us
  starting transfers between devices: 16 us -> 18.5 us
  Pallas kernels: 14.1 us -> 12.7 us
  local copies, waits for them, and re-layouts: 0.86 us -> 1.77 us
    ppermute x8, waiting for transfers between devices: 7.59 us -> 3.05 us  [the longest x4 2.12 us: exchange(): lax.ppermute(to_even, BOTH, core_pairs(owners, lambda block, core: (block...]
    ppermute x6 -> x5, starting transfers between devices: 0.68 us -> 2.74 us  [swap_cores(): lax.ppermute(x, BOTH, core_pairs(owners, lambda block, core: (block, 1 -...]
    unnamed x18 -> x20, local copies, waits for them, and re-layouts: 0.86 us -> 1.77 us
    pallas_call x1 -> x3, Pallas kernels: 1.72 us -> 0.92 us  [the longest x1 0.67 us: shards(): pl.pallas_call(functools.partial(pack_kernel, rows=obs_rows, cells=cells,...]
    ppermute x8, starting transfers between devices: 15.3 us -> 15.7 us  [the longest x4 9.12 us: exchange(): lax.ppermute(to_even, BOTH, core_pairs(owners, lambda block, core: (block...]
    ppermute x6 -> x5, waiting for transfers between devices: 0.57 us -> 0.16 us  [swap_cores(): lax.ppermute(x, BOTH, core_pairs(owners, lambda block, core: (block, 1 -...]
  transfers between devices with their start and end apart: 14 -> 13, of which waited for: 8 -> 5; matrix products, arithmetic and copies ran while one was open for 0% -> 0% of each run, Pallas kernels for 18% -> 15%
where the time goes in v3:
time: 37.1 us; the launch traced here: 37 us
  starting transfers between devices  18.5 us (50%)
  Pallas kernels  12.7 us (34%)
  waiting for transfers between devices  3.21 us (9%)
  local copies, waits for them, and re-layouts  1.77 us (5%)
  between operations  0.76 us (2%)
    ppermute x4, starting transfers between devices, exchange(): lax.ppermute(to_even, BOTH, core_pairs(owners, lambda block, core: (block...  9.12 us
    ppermute x4, starting transfers between devices, exchange(): lax.ppermute(to_odd, BOTH, core_pairs(owners, lambda block, core: (block...  6.61 us
    pallas_call x2, Pallas kernels, forecast(): pl.pallas_call(forecast_kernel, out_shape=(jax.ShapeDtypeStruct((strip_ro...  4.9 us
    pallas_call x1, Pallas kernels, shards(): pl.pallas_call(functools.partial(analysis_kernel, units=units, obs_rows=o...  3.76 us
    ppermute x5, starting transfers between devices, swap_cores(): lax.ppermute(x, BOTH, core_pairs(owners, lambda block, core: (block, 1 -...  2.74 us
    pallas_call x1, Pallas kernels, shards(): pl.pallas_call(functools.partial(sums_kernel, owners=owners, units=units,...  2.45 us
    ppermute x4, waiting for transfers between devices, exchange(): lax.ppermute(to_even, BOTH, core_pairs(owners, lambda block, core: (block...  2.12 us
    unnamed x20, local copies, waits for them, and re-layouts  1.77 us
  transfers between devices with their start and end apart: 13, of which 5 were waited for; matrix products, arithmetic and copies ran while one was open for 0% of the time, Pallas kernels for 15%

profile of v3, /device:TPU:0, one launch (start us, length us, event | category | flops | bytes accessed | tf_op | source)
XLA Modules:
  0.0 37.0 jit_solution(17962082373012552665)
XLA Ops:
  0.6 0.5 %collective-permute-start = (f32[32,4,1024]{2,1,0:T(4,128)}, f32[32,4,1024]{2,1,0:T(4,128)S(1)}, u32[]{:S(2)}, u32[]{:S(2)}) collective-permute-start(f32[32,4,1024]{2,1,0:T(4,128)} %ensemble_ref.1), channel_id=1, source_target_pairs={{0,1},{1,0},{2,3},{3,2},{4,5},{5,4},{6,7},{7,6},{8,9},{9,8},{10,11... | collective-permute-start | bytes 1572872 | tf_op jit(solution)/shard_map/ppermute | solution.py:42
  1.1 1.0 %copy-done = f32[32,4,1024]{2,1,0:T(4,128)S(1)} copy-done((f32[32,4,1024]{2,1,0:T(4,128)S(1)}, f32[32,4,1024]{2,1,0:T(4,128)}, u32[]{:S(2)}) %copy-start) | copy-done | bytes 524312
  2.5 0.6 %copy-done.6 = s32[256]{0:T(256)S(1)} copy-done((s32[256]{0:T(256)S(1)}, s32[256]{0:T(256)}, u32[]{:S(2)}) %copy-start.6) | copy-done | bytes 1048
  3.2 0.7 %pack.1 = (f32[8,128]{1,0:T(8,128)S(1)}, f32[8,128]{1,0:T(8,128)S(1)}, f32[8,128]{1,0:T(8,128)S(1)}, f32[20,128]{1,0:T(8,128)S(1)}) custom-call(s32[2]{0:T(128)S(1)} %pad_add_fusion.which_ref, s32[1,16]{1,0:T(1,128)S(1)} %copy-done.5, f32[8,128]{1,0:T(8,128)S(1)} %bitcast.9, s32[8,128]{1,0:T(8,128)S(1)} %bitcast.10, s32[2,128]{1,0:T(2,128)S(1)} %bitcast.11, ...), custom_call_target="tpu_custom_call" | custom-call | tf_op jit(solution)/shard_map/pack/pallas_call | solution.py:621
  4.0 2.6 %collective-permute-start.1 = (f32[24,128]{1,0:T(8,128)S(1)}, f32[24,128]{1,0:T(8,128)S(1)}, u32[]{:S(2)}, u32[]{:S(2)}) collective-permute-start(f32[24,128]{1,0:T(8,128)S(1)} %get-tuple-element.33), channel_id=1, source_target_pairs={{0,2},{1,7},{2,0},{3,5},{4,6},{5,3},{6,4},{7,1},{8,10},{9,15},{10,... | collective-permute-start | bytes 36872 | tf_op jit(solution)/shard_map/ppermute | solution.py:46
  6.6 1.5 %collective-permute-start.3 = (f32[24,128]{1,0:T(8,128)S(1)}, f32[24,128]{1,0:T(8,128)S(1)}, u32[]{:S(2)}, u32[]{:S(2)}) collective-permute-start(f32[24,128]{1,0:T(8,128)S(1)} %get-tuple-element.34), channel_id=1, source_target_pairs={{0,4},{1,5},{2,6},{3,7},{4,0},{5,1},{6,2},{7,3},{8,12},{9,13},{10,... | collective-permute-start | bytes 36872 | tf_op jit(solution)/shard_map/ppermute | solution.py:49
  8.2 0.6 %collective-permute-start.2 = (f32[24,128]{1,0:T(8,128)S(1)}, f32[24,128]{1,0:T(8,128)S(1)}, u32[]{:S(2)}, u32[]{:S(2)}) collective-permute-start(f32[24,128]{1,0:T(8,128)S(1)} %collective-permute-done.1.odd), channel_id=1, source_target_pairs={{0,1},{1,0},{2,3},{3,2},{4,5},{5,4},{6,7},{7,6},{8,9},{9,8},{10,11... | collective-permute-start | bytes 36872 | tf_op jit(solution)/shard_map/ppermute | solution.py:42
  8.8 2.5 %forecast.2 = (f32[128,1024]{1,0:T(8,128)S(1)}, f32[128,128]{1,0:T(8,128)S(1)}, f32[256,128]{1,0:T(8,128)S(1)}) custom-call(f32[4,4]{1,0:T(4,128)S(1)} %copy-done.2, f32[32,4,1024]{2,1,0:T(4,128)S(1)} %copy-done.1, f32[20,128]{1,0:T(8,128)S(1)} %get-tuple-element.23.small_ref), custom_call_target="tpu_custom_call" | custom-call | flops 10485760 | bytes 1048576 | tf_op jit(solution)/shard_map/forecast/pallas_call | solution.py:642
  11.3 0.6 %regroup.1 = (f32[24,128]{1,0:T(8,128)S(1)}, f32[24,128]{1,0:T(8,128)S(1)}, f32[8,128]{1,0:T(8,128)S(1)}) custom-call(s32[2]{0:T(128)S(1)} %pad_add_fusion.which_ref, f32[8,128]{1,0:T(8,128)S(1)} %get-tuple-element.30.kept, f32[24,128]{1,0:T(8,128)S(1)} %collective-permute-done.1.odd, f32[24,128]{1,0:T(8,128)S(1)} %collective-permute-done.2.swapped, ...), custom_call_target="tpu_custom_call" | custom-call | tf_op jit(solution)/shard_map/regroup/pallas_call | solution.py:668
  11.9 1.8 %collective-permute-start.4 = (f32[24,128]{1,0:T(8,128)S(1)}, f32[24,128]{1,0:T(8,128)S(1)}, u32[]{:S(2)}, u32[]{:S(2)}) collective-permute-start(f32[24,128]{1,0:T(8,128)S(1)} %get-tuple-element.36.refs_0_), channel_id=1, source_target_pairs={{0,8},{1,25},{2,10},{3,27},{4,12},{5,29},{6,14},{7,31},{8,0},{9,17... | collective-permute-start | bytes 36872 | tf_op jit(solution)/shard_map/ppermute | solution.py:46
  13.7 2.6 %collective-permute-start.6 = (f32[24,128]{1,0:T(8,128)S(1)}, f32[24,128]{1,0:T(8,128)S(1)}, u32[]{:S(2)}, u32[]{:S(2)}) collective-permute-start(f32[24,128]{1,0:T(8,128)S(1)} %get-tuple-element.37), channel_id=1, source_target_pairs={{0,16},{1,17},{2,18},{3,19},{4,20},{5,21},{6,22},{7,23},{8,24},{9,... | collective-permute-start | bytes 36872 | tf_op jit(solution)/shard_map/ppermute | solution.py:49
  16.3 0.5 %collective-permute-start.5 = (f32[24,128]{1,0:T(8,128)S(1)}, f32[24,128]{1,0:T(8,128)S(1)}, u32[]{:S(2)}, u32[]{:S(2)}) collective-permute-start(f32[24,128]{1,0:T(8,128)S(1)} %collective-permute-done.4.odd), channel_id=1, source_target_pairs={{0,1},{1,0},{2,3},{3,2},{4,5},{5,4},{6,7},{7,6},{8,9},{9,8},{10,11... | collective-permute-start | bytes 36872 | tf_op jit(solution)/shard_map/ppermute | solution.py:42
  16.8 2.5 %forecast.3 = (f32[128,1024]{1,0:T(8,128)S(1)}, f32[128,128]{1,0:T(8,128)S(1)}, f32[256,128]{1,0:T(8,128)S(1)}) custom-call(f32[4,4]{1,0:T(4,128)S(1)} %copy-done.2, f32[32,4,1024]{2,1,0:T(4,128)S(1)} %collective-permute-done.source.other_ref, f32[20,128]{1,0:T(8,128)S(1)} %get-tuple-element.23.small_ref), custom_call_target="tpu_custom_call" | custom-call | flops 10485760 | bytes 1048576 | tf_op jit(solution)/shard_map/forecast/pallas_call | solution.py:642
  19.3 2.5 %sums.1 = (f32[40,128]{1,0:T(8,128)S(1)}, f32[40,128]{1,0:T(8,128)S(1)}, f32[40,128]{1,0:T(8,128)S(1)}, f32[256,256]{1,0:T(8,128)S(1)}) custom-call(s32[2]{0:T(128)S(1)} %pad_add_fusion.which_ref, f32[4,4]{1,0:T(4,128)S(1)} %copy-done.2, f32[20,128]{1,0:T(8,128)S(1)} %get-tuple-element.23.small_ref, f32[128,1024]{1,0:T(8,128)S(1)} %get-tuple-element.24.own_state.own_ref, ...), custom_call_target="tpu_custom_call" | custom-call | tf_op jit(solution)/shard_map/sums/pallas_call | solution.py:683
  21.8 0.6 %collective-permute-start.8 = (f32[40,128]{1,0:T(8,128)S(1)}, f32[40,128]{1,0:T(8,128)S(1)}, u32[]{:S(2)}, u32[]{:S(2)}) collective-permute-start(f32[40,128]{1,0:T(8,128)S(1)} %get-tuple-element.41), channel_id=1, source_target_pairs={{0,8},{1,25},{2,10},{3,27},{4,12},{5,29},{6,14},{7,31},{8,0},{9,17... | collective-permute-start | bytes 61448 | tf_op jit(solution)/shard_map/ppermute | solution.py:46
  22.4 3.5 %collective-permute-start.7 = (f32[40,128]{1,0:T(8,128)S(1)}, f32[40,128]{1,0:T(8,128)S(1)}, u32[]{:S(2)}, u32[]{:S(2)}) collective-permute-start(f32[40,128]{1,0:T(8,128)S(1)} %get-tuple-element.40), channel_id=1, source_target_pairs={{0,16},{1,17},{2,18},{3,19},{4,20},{5,21},{6,22},{7,23},{8,24},{9,... | collective-permute-start | bytes 61448 | tf_op jit(solution)/shard_map/ppermute | solution.py:49
  25.9 0.3 collective-permute-start.9
  26.3 1.4 %collective-permute-done.7 = f32[40,128]{1,0:T(8,128)S(1)} collective-permute-done((f32[40,128]{1,0:T(8,128)S(1)}, f32[40,128]{1,0:T(8,128)S(1)}, u32[]{:S(2)}, u32[]{:S(2)}) %collective-permute-start.7) | collective-permute-done | bytes 20512 | tf_op jit(solution)/shard_map/ppermute | solution.py:49
  27.7 1.6 %collective-permute-start.10 = (f32[40,128]{1,0:T(8,128)S(1)}, f32[40,128]{1,0:T(8,128)S(1)}, u32[]{:S(2)}, u32[]{:S(2)}) collective-permute-start(f32[40,128]{1,0:T(8,128)S(1)} %add_add_fusion.kept), channel_id=1, source_target_pairs={{0,2},{1,7},{2,0},{3,5},{4,6},{5,3},{6,4},{7,1},{8,10},{9,15},{10,... | collective-permute-start | bytes 61448 | tf_op jit(solution)/shard_map/ppermute | solution.py:46
  29.3 1.5 %collective-permute-start.12 = (f32[40,128]{1,0:T(8,128)S(1)}, f32[40,128]{1,0:T(8,128)S(1)}, u32[]{:S(2)}, u32[]{:S(2)}) collective-permute-start(f32[40,128]{1,0:T(8,128)S(1)} %add_add_fusion.kept), channel_id=1, source_target_pairs={{0,4},{1,5},{2,6},{3,7},{4,0},{5,1},{6,2},{7,3},{8,12},{9,13},{10,... | collective-permute-start | bytes 61448 | tf_op jit(solution)/shard_map/ppermute | solution.py:49
  30.8 0.8 %collective-permute-done.10.odd = f32[40,128]{1,0:T(8,128)S(1)} collective-permute-done((f32[40,128]{1,0:T(8,128)S(1)}, f32[40,128]{1,0:T(8,128)S(1)}, u32[]{:S(2)}, u32[]{:S(2)}) %collective-permute-start.10) | collective-permute-done | bytes 20512 | tf_op jit(solution)/shard_map/ppermute | solution.py:46
  31.5 0.8 %collective-permute-start.11 = (f32[40,128]{1,0:T(8,128)S(1)}, f32[40,128]{1,0:T(8,128)S(1)}, u32[]{:S(2)}, u32[]{:S(2)}) collective-permute-start(f32[40,128]{1,0:T(8,128)S(1)} %collective-permute-done.10.odd), channel_id=1, source_target_pairs={{0,1},{1,0},{2,3},{3,2},{4,5},{5,4},{6,7},{7,6},{8,9},{9,8},{10,11... | collective-permute-start | bytes 61448 | tf_op jit(solution)/shard_map/ppermute | solution.py:42
  32.4 0.7 %collective-permute-done.12.even = f32[40,128]{1,0:T(8,128)S(1)} collective-permute-done((f32[40,128]{1,0:T(8,128)S(1)}, f32[40,128]{1,0:T(8,128)S(1)}, u32[]{:S(2)}, u32[]{:S(2)}) %collective-permute-start.12) | collective-permute-done | bytes 20512 | tf_op jit(solution)/shard_map/ppermute | solution.py:49
  33.2 3.8 %analysis.1 = (f32[32,4,1024]{2,1,0:T(4,128)}, f32[2,128]{1,0:T(2,128)}) custom-call(s32[2]{0:T(128)S(1)} %pad_add_fusion.which_ref, s32[1,16]{1,0:T(1,128)S(1)} %copy-done.5, f32[128,1024]{1,0:T(8,128)S(1)} %get-tuple-element.24.own_state.own_ref, f32[128,1024]{1,0:T(8,128)S(1)} %get-tuple-element.25.other_state.other_ref, ...), custom_call_target="tpu_custom_call" | custom-call | tf_op jit(solution)/shard_map/analysis/pallas_call | solution.py:715
  (32 shorter events, 0.8 us)
Async XLA Ops:
  0.6 3.2 %collective-permute-start = (f32[32,4,1024]{2,1,0:T(4,128)}, f32[32,4,1024]{2,1,0:T(4,128)S(1)}, u32[]{:S(2)}, u32[]{:S(2)}) collective-permute-start(f32[32,4,1024]{2,1,0:T(4,128)} %ensemble_ref.1), channel_id=1, source_target_pairs={{0,1},{1,0},{2,3},{3,2},{4,5},{5,4},{6,7},{7,6},{8,9},{9,8},{10,11... | collective-permute-start | bytes 1572872 | tf_op jit(solution)/shard_map/ppermute | solution.py:42
  1.1 1.0 %copy-start = (f32[32,4,1024]{2,1,0:T(4,128)S(1)}, f32[32,4,1024]{2,1,0:T(4,128)}, u32[]{:S(2)}) copy-start(f32[32,4,1024]{2,1,0:T(4,128)} %ensemble_ref.1) | copy-start | bytes 1572868
  2.2 6.6 %copy-start.1 = (f32[32,4,1024]{2,1,0:T(4,128)S(1)}, f32[32,4,1024]{2,1,0:T(4,128)}, u32[]{:S(2)}) copy-start(f32[32,4,1024]{2,1,0:T(4,128)} %ensemble_ref.1) | copy-start | bytes 1572868
  2.3 0.7 %copy-start.6 = (s32[256]{0:T(256)S(1)}, s32[256]{0:T(256)}, u32[]{:S(2)}) copy-start(s32[256]{0:T(256)} %param.13) | copy-start | bytes 3076
  2.3 0.7 %copy-start.7 = (s32[256]{0:T(256)S(1)}, s32[256]{0:T(256)}, u32[]{:S(2)}) copy-start(s32[256]{0:T(256)} %param.14) | copy-start | bytes 3076
  2.3 0.7 %copy-start.8 = (f32[256]{0:T(256)S(1)}, f32[256]{0:T(256)}, u32[]{:S(2)}) copy-start(f32[256]{0:T(256)} %param.15) | copy-start | bytes 3076
  2.4 0.7 %copy-start.9 = (f32[256]{0:T(256)S(1)}, f32[256]{0:T(256)}, u32[]{:S(2)}) copy-start(f32[256]{0:T(256)} %param.16) | copy-start | bytes 3076
  2.4 0.7 %copy-start.4 = (s32[1024]{0:T(1024)S(1)}, s32[1024]{0:T(1024)}, u32[]{:S(2)}) copy-start(s32[1024]{0:T(1024)} %param.11) | copy-start | bytes 12292
  2.5 0.7 %copy-start.3 = (f32[1024]{0:T(1024)S(1)}, f32[1024]{0:T(1024)}, u32[]{:S(2)}) copy-start(f32[1024]{0:T(1024)} %param.10) | copy-start | bytes 12292
  2.5 0.7 %copy-start.5 = (s32[1,16]{1,0:T(1,128)S(1)}, s32[1,16]{1,0:T(1,128)}, u32[]{:S(2)}) copy-start(s32[1,16]{1,0:T(1,128)} %send_ref.3) | copy-start | bytes 196
  4.0 4.8 %copy-start.2 = (f32[4,4]{1,0:T(4,128)S(1)}, f32[4,4]{1,0:T(4,128)}, u32[]{:S(2)}) copy-start(f32[4,4]{1,0:T(4,128)} %couple_ref.5) | copy-start | bytes 196
  4.0 4.2 %collective-permute-start.1 = (f32[24,128]{1,0:T(8,128)S(1)}, f32[24,128]{1,0:T(8,128)S(1)}, u32[]{:S(2)}, u32[]{:S(2)}) collective-permute-start(f32[24,128]{1,0:T(8,128)S(1)} %get-tuple-element.33), channel_id=1, source_target_pairs={{0,2},{1,7},{2,0},{3,5},{4,6},{5,3},{6,4},{7,1},{8,10},{9,15},{10,... | collective-permute-start | bytes 36872 | tf_op jit(solution)/shard_map/ppermute | solution.py:46
  6.6 4.7 %collective-permute-start.3 = (f32[24,128]{1,0:T(8,128)S(1)}, f32[24,128]{1,0:T(8,128)S(1)}, u32[]{:S(2)}, u32[]{:S(2)}) collective-permute-start(f32[24,128]{1,0:T(8,128)S(1)} %get-tuple-element.34), channel_id=1, source_target_pairs={{0,4},{1,5},{2,6},{3,7},{4,0},{5,1},{6,2},{7,3},{8,12},{9,13},{10,... | collective-permute-start | bytes 36872 | tf_op jit(solution)/shard_map/ppermute | solution.py:49
  8.2 3.1 %collective-permute-start.2 = (f32[24,128]{1,0:T(8,128)S(1)}, f32[24,128]{1,0:T(8,128)S(1)}, u32[]{:S(2)}, u32[]{:S(2)}) collective-permute-start(f32[24,128]{1,0:T(8,128)S(1)} %collective-permute-done.1.odd), channel_id=1, source_target_pairs={{0,1},{1,0},{2,3},{3,2},{4,5},{5,4},{6,7},{7,6},{8,9},{9,8},{10,11... | collective-permute-start | bytes 36872 | tf_op jit(solution)/shard_map/ppermute | solution.py:42
  11.9 4.4 %collective-permute-start.4 = (f32[24,128]{1,0:T(8,128)S(1)}, f32[24,128]{1,0:T(8,128)S(1)}, u32[]{:S(2)}, u32[]{:S(2)}) collective-permute-start(f32[24,128]{1,0:T(8,128)S(1)} %get-tuple-element.36.refs_0_), channel_id=1, source_target_pairs={{0,8},{1,25},{2,10},{3,27},{4,12},{5,29},{6,14},{7,31},{8,0},{9,17... | collective-permute-start | bytes 36872 | tf_op jit(solution)/shard_map/ppermute | solution.py:46
  13.7 5.6 %collective-permute-start.6 = (f32[24,128]{1,0:T(8,128)S(1)}, f32[24,128]{1,0:T(8,128)S(1)}, u32[]{:S(2)}, u32[]{:S(2)}) collective-permute-start(f32[24,128]{1,0:T(8,128)S(1)} %get-tuple-element.37), channel_id=1, source_target_pairs={{0,16},{1,17},{2,18},{3,19},{4,20},{5,21},{6,22},{7,23},{8,24},{9,... | collective-permute-start | bytes 36872 | tf_op jit(solution)/shard_map/ppermute | solution.py:49
  16.3 3.0 %collective-permute-start.5 = (f32[24,128]{1,0:T(8,128)S(1)}, f32[24,128]{1,0:T(8,128)S(1)}, u32[]{:S(2)}, u32[]{:S(2)}) collective-permute-start(f32[24,128]{1,0:T(8,128)S(1)} %collective-permute-done.4.odd), channel_id=1, source_target_pairs={{0,1},{1,0},{2,3},{3,2},{4,5},{5,4},{6,7},{7,6},{8,9},{9,8},{10,11... | collective-permute-start | bytes 36872 | tf_op jit(solution)/shard_map/ppermute | solution.py:42
  21.8 4.1 %collective-permute-start.8 = (f32[40,128]{1,0:T(8,128)S(1)}, f32[40,128]{1,0:T(8,128)S(1)}, u32[]{:S(2)}, u32[]{:S(2)}) collective-permute-start(f32[40,128]{1,0:T(8,128)S(1)} %get-tuple-element.41), channel_id=1, source_target_pairs={{0,8},{1,25},{2,10},{3,27},{4,12},{5,29},{6,14},{7,31},{8,0},{9,17... | collective-permute-start | bytes 61448 | tf_op jit(solution)/shard_map/ppermute | solution.py:46
  22.4 5.3 %collective-permute-start.7 = (f32[40,128]{1,0:T(8,128)S(1)}, f32[40,128]{1,0:T(8,128)S(1)}, u32[]{:S(2)}, u32[]{:S(2)}) collective-permute-start(f32[40,128]{1,0:T(8,128)S(1)} %get-tuple-element.40), channel_id=1, source_target_pairs={{0,16},{1,17},{2,18},{3,19},{4,20},{5,21},{6,22},{7,23},{8,24},{9,... | collective-permute-start | bytes 61448 | tf_op jit(solution)/shard_map/ppermute | solution.py:49
  25.9 1.8 %collective-permute-start.9 = (f32[40,128]{1,0:T(8,128)S(1)}, f32[40,128]{1,0:T(8,128)S(1)}, u32[]{:S(2)}, u32[]{:S(2)}) collective-permute-start(f32[40,128]{1,0:T(8,128)S(1)} %collective-permute-done.8), channel_id=1, source_target_pairs={{0,1},{1,0},{2,3},{3,2},{4,5},{5,4},{6,7},{7,6},{8,9},{9,8},{10,11... | collective-permute-start | bytes 61448 | tf_op jit(solution)/shard_map/ppermute | solution.py:42
  27.7 3.8 %collective-permute-start.10 = (f32[40,128]{1,0:T(8,128)S(1)}, f32[40,128]{1,0:T(8,128)S(1)}, u32[]{:S(2)}, u32[]{:S(2)}) collective-permute-start(f32[40,128]{1,0:T(8,128)S(1)} %add_add_fusion.kept), channel_id=1, source_target_pairs={{0,2},{1,7},{2,0},{3,5},{4,6},{5,3},{6,4},{7,1},{8,10},{9,15},{10,... | collective-permute-start | bytes 61448 | tf_op jit(solution)/shard_map/ppermute | solution.py:46
  29.3 3.8 %collective-permute-start.12 = (f32[40,128]{1,0:T(8,128)S(1)}, f32[40,128]{1,0:T(8,128)S(1)}, u32[]{:S(2)}, u32[]{:S(2)}) collective-permute-start(f32[40,128]{1,0:T(8,128)S(1)} %add_add_fusion.kept), channel_id=1, source_target_pairs={{0,4},{1,5},{2,6},{3,7},{4,0},{5,1},{6,2},{7,3},{8,12},{9,13},{10,... | collective-permute-start | bytes 61448 | tf_op jit(solution)/shard_map/ppermute | solution.py:49
  31.5 1.7 %collective-permute-start.11 = (f32[40,128]{1,0:T(8,128)S(1)}, f32[40,128]{1,0:T(8,128)S(1)}, u32[]{:S(2)}, u32[]{:S(2)}) collective-permute-start(f32[40,128]{1,0:T(8,128)S(1)} %collective-permute-done.10.odd), channel_id=1, source_target_pairs={{0,1},{1,0},{2,3},{3,2},{4,5},{5,4},{6,7},{7,6},{8,9},{9,8},{10,11... | collective-permute-start | bytes 61448 | tf_op jit(solution)/shard_map/ppermute | solution.py:42

commit v4 on v3

--- a/solution.py
+++ b/solution.py
@@ -56,27 +56,27 @@
     return jnp.bitwise_and(lax.shift_right_logical(block, jnp.int32(unit.bit_length() - 1)), 3)
 
 
-def within(shift, wide):
-    shift = jnp.where(shift < 0, shift + wide, shift)
-    return jnp.where(shift >= wide, shift - wide, shift)
+def here():
+    return lax.axis_index("cells"), lax.axis_index("members")
 
 
 def table_row(number, count):
     return (number % 4) * (count // 4) + number // 4
 
 
-def strips_of(head, tail):
-    fields, cells = tail.shape[1:]
+def strips_of(ref):
+    fields, cells = ref.shape[1:]
     lane = lax.broadcasted_iota(jnp.int32, (1, LANES), 1)
-    ends = [jnp.where(lane < STEPS, head[:, f, :LANES], tail[:, f, cells - LANES :]) for f in range(fields)]
+    ends = [jnp.where(lane < STEPS, ref[:, f, :LANES], ref[:, f, cells - LANES :]) for f in range(fields)]
     ends = jnp.transpose(jnp.concatenate(ends, axis=0))
     return jnp.concatenate([ends[:STEPS, :], ends[LANES - STEPS :, :]], axis=0)
 
 
 def pack_kernel(
-    which_ref, send_ref, speed_ref, flag_ref, place_ref, field_ref, value_ref, sigma_ref,
+    send_ref, speed_ref, flag_ref, place_ref, field_ref, value_ref, sigma_ref,
     kept_ref, odd_ref, even_ref, small_ref, table_ref, *, rows, cells, fields,
 ):
+    block, core = here()
     tiles = cells // LANES
     speed, value, sigma = speed_ref[...], value_ref[...], sigma_ref[...]
     flag, place, field = (ref[...].astype(jnp.float32) for ref in (flag_ref, place_ref, field_ref))
@@ -93,44 +93,49 @@
     ids = field * float(cells) + place
     weight = 1.0 / (sigma * sigma)
     pull = weight * value
-    wide = rows * LANES
-
-    def row_of(x):
-        return jnp.concatenate([x[r : r + 1] for r in range(rows)], axis=1)
-
-    listed = jnp.concatenate(
-        [row_of(ids), row_of(weight), row_of(pull), jnp.zeros((5, wide), jnp.float32)], axis=0
-    )
     sub = lax.broadcasted_iota(jnp.int32, (8, LANES), 0)
-    lane8 = lax.broadcasted_iota(jnp.int32, (8, LANES), 1)
     empty = jnp.where(sub == 0, -1.0, 0.0)
     empty = jnp.where(sub == 3, edge_left, jnp.where(sub == 4, edge_right, empty))
+    listed = [
+        jnp.where(sub == 0, ids[r : r + 1], jnp.where(sub == 1, weight[r : r + 1], pull[r : r + 1]))
+        for r in range(rows)
+    ]
     owners = send_ref.shape[1]
     count = owners // GROUPS
-    table = [empty] * count
-    start = jnp.int32(0)
-    for owner in range(owners):
-        held = send_ref[0, owner]
-        group, r = owner // count, owner % count
-        moved = pltpu.roll(listed, within(group * CAP - start, wide), 1)[:, :LANES]
-        here = (lane8 >= group * CAP) & (lane8 < group * CAP + held) & (sub < 3)
-        table[r] = jnp.where(here, moved, table[r])
-        start = start + held
+    sends = jnp.broadcast_to(send_ref[...], (8, owners)).astype(jnp.bfloat16)
+    sender = lax.broadcasted_iota(jnp.int32, (owners, LANES), 0)
+    group = lax.broadcasted_iota(jnp.int32, (owners, LANES), 1) // CAP
+    slot = lax.broadcasted_iota(jnp.int32, (8, LANES), 1) % CAP
+    one = lambda mask: jnp.where(mask, 1.0, 0.0)
+    which = jnp.concatenate(
+        [one(sender < group * count + r) for r in range(count)] + [one(sender == group * count + r) for r in range(count)],
+        axis=1,
+    )
+    found = jnp.dot(sends, which.astype(jnp.bfloat16), preferred_element_type=jnp.float32).astype(jnp.int32)
     for r in range(count):
+        index = found[:, r * LANES : (r + 1) * LANES] + slot
+        held = found[:, (count + r) * LANES : (count + r + 1) * LANES]
+        block_of = empty
+        inside = (slot < held) & (sub < 3)
+        for w in range(rows):
+            moved = jnp.take_along_axis(
+                listed[w], jnp.bitwise_and(index, LANES - 1), axis=1, mode="promise_in_bounds"
+            )
+            block_of = jnp.where(inside & (lax.shift_right_logical(index, 7) == w), moved, block_of)
         row = 8 * table_row(r, count)
-        table_ref[row : row + 8, :] = table[r]
+        table_ref[row : row + 8, :] = block_of
     part = kept_ref.shape[0]
-    digit = digit_of(which_ref[0], 1)
-    for out, partner in ((kept_ref, 0), (odd_ref, 1 + 2 * which_ref[1]), (even_ref, 2)):
+    digit = digit_of(block, 1)
+    for out, partner in ((kept_ref, 0), (odd_ref, 1 + 2 * core), (even_ref, 2)):
         out[...] = table_ref[pl.ds(pl.multiple_of(jnp.bitwise_xor(digit, partner) * part, 8), part), :]
 
 
 def strips_kernel(ensemble_ref, out_ref):
-    out_ref[...] = strips_of(ensemble_ref, ensemble_ref)
+    out_ref[...] = strips_of(ensemble_ref)
 
 
 def join_kernel(own_ref, other_ref, odd_part, even_part, odd_ref, even_ref):
-    strips = jnp.concatenate([own_ref[...], strips_of(other_ref, other_ref)], axis=0)
+    strips = jnp.concatenate([own_ref[...], strips_of(other_ref)], axis=0)
     for part, out in ((odd_part, odd_ref), (even_part, even_ref)):
         out[:16, :] = strips
         out[16:, :] = part[...]
@@ -151,9 +156,9 @@
 
 
 def regroup_kernel(
-    which_ref, kept, odd, swapped, even, _, to_odd, to_even, stay, *, unit, into_lanes,
+    kept, odd, swapped, even, _, to_odd, to_even, stay, *, unit, into_lanes,
 ):
-    block, core = which_ref[0], which_ref[1]
+    block, core = here()
     after = digit_of(block, unit * 4)
     own, other, coefs = incoming(digit_of(block, unit), core, odd, swapped)
     sub = lax.broadcasted_iota(jnp.int32, (8, LANES), 0)
@@ -189,14 +194,27 @@
                     target[row : row + 8, :] = jnp.where(sub < 3, received(k, at), coefs)
 
 
-def power_of_coupling(couple_ref, fields):
-    mix = [[couple_ref[f, g] + (1.0 if f == g else 0.0) for g in range(fields)] for f in range(fields)]
+def fill_powers(couple_ref, powers_ref):
+    fields = couple_ref.shape[0]
+    mix = [
+        [
+            jnp.broadcast_to(couple_ref[f : f + 1, g : g + 1], (1, LANES)) + (1.0 if f == g else 0.0)
+            for g in range(fields)
+        ]
+        for f in range(fields)
+    ]
     for _ in range(2):
         mix = [
             [sum(mix[f][h] * mix[h][g] for h in range(fields)) for g in range(fields)]
             for f in range(fields)
         ]
-    return mix
+    for f in range(fields):
+        for g in range(fields):
+            powers_ref[f * fields + g : f * fields + g + 1, :] = mix[f][g]
+
+
+def powers_of(powers_ref, fields):
+    return [[powers_ref[f * fields + g : f * fields + g + 1, :] for g in range(fields)] for f in range(fields)]
 
 
 def transport(x, from_left, stay, from_right):
@@ -205,10 +223,12 @@
     return x
 
 
-def forecast_kernel(
-    couple_ref, source, small_ref, state, edge, sums_ref, work_ref, coef_ref,
-):
-    members, fields, cells = source.shape
+def halves_of(x):
+    high = x.astype(jnp.bfloat16)
+    return high, (x - high.astype(jnp.float32)).astype(jnp.bfloat16)
+
+
+def fill_band(small_ref, band_ref, cells):
     tiles = cells // LANES
     speed = small_ref[:tiles, :]
     toward_left = speed * small_ref[tiles : 2 * tiles, :]
@@ -217,55 +237,110 @@
     def row_of(x):
         return jnp.concatenate([x[t : t + 1] for t in range(tiles)], axis=1)
 
-    def shifted(x, by):
-        return pltpu.roll(x, -by % cells, 1) if by else x
-
-    step = {-1: row_of(toward_left + DIFFUSION), 0: row_of(1.0 - 2.0 * DIFFUSION - speed), 1: row_of(toward_right + DIFFUSION)}
+    step = {
+        -1: row_of(toward_left + DIFFUSION),
+        0: row_of(1.0 - 2.0 * DIFFUSION - speed),
+        1: row_of(toward_right + DIFFUSION),
+    }
     reach = dict(step)
     for _ in range(STEPS - 1):
         longer = {}
         for e in step:
             for d in reach:
-                term = step[e] * shifted(reach[d], e)
+                term = step[e] * (pltpu.roll(reach[d], -e % cells, 1) if e else reach[d])
                 longer[d + e] = longer[d + e] + term if d + e in longer else term
         reach = longer
-    for d in range(-STEPS, STEPS + 1):
-        at = 8 * (d + STEPS)
-        coef_ref[at : at + 8, :] = jnp.broadcast_to(reach[d], (8, cells))
-    mix = power_of_coupling(couple_ref, fields)
-    low = lax.broadcasted_iota(jnp.int32, (8, LANES), 1) < LANES // 2
-    sums_ref[...] = jnp.zeros_like(sums_ref)
-
-    def group(i, _):
-        at = pl.multiple_of(i * 8, 8)
+    row = lax.broadcasted_iota(jnp.int32, (LANES, LANES), 0)
+    column = lax.broadcasted_iota(jnp.int32, (LANES, LANES), 1)
+    ahead = row - column
+    for t in range(tiles):
+        rule = {d: reach[d][:, t * LANES : (t + 1) * LANES] for d in reach}
+
+        def placed(distance, offsets):
+            block = jnp.zeros(distance.shape, jnp.float32)
+            for d in offsets:
+                block = jnp.where(distance == d, rule[d], block)
+            return block
+
+        block = jnp.concatenate(
+            [
+                placed(ahead, range(-STEPS, STEPS + 1)),
+                placed(ahead[:8] + LANES, range(1, STEPS + 1)),
+                jnp.zeros((LANES - 16, LANES), jnp.float32),
+                placed(ahead[LANES - 8 :] - LANES, range(-STEPS, 0)),
+            ],
+            axis=0,
+        )
+        for p, piece in enumerate(halves_of(block)):
+            band_ref[2 * t * LANES : 2 * (t + 1) * LANES, p * LANES : (p + 1) * LANES] = piece
+
+
+def fill_positions(send_ref, slots_ref):
+    owners = send_ref.shape[1]
+    count = owners // GROUPS
+    rows = slots_ref.shape[0] // 2
+    row = lax.broadcasted_iota(jnp.int32, (owners, owners), 0)
+    column = lax.broadcasted_iota(jnp.int32, (owners, owners), 1)
+    held = jnp.where(row == column, jnp.broadcast_to(send_ref[...], (owners, owners)), 0).astype(jnp.float32)
+    held = jnp.broadcast_to(jnp.sum(held, axis=1, keepdims=True), (owners, LANES))
+    ends = jnp.dot(
+        jnp.where(column <= row, 1.0, 0.0).astype(jnp.bfloat16), held.astype(jnp.bfloat16),
+        preferred_element_type=jnp.float32,
+    )
+    for r in range(rows):
+        slot = (lax.broadcasted_iota(jnp.int32, (1, LANES), 1) + r * LANES).astype(jnp.float32)
+        passed = ends <= slot
+        owner = jnp.sum(jnp.where(passed, 1.0, 0.0), axis=0, keepdims=True).astype(jnp.int32)
+        start = jnp.sum(jnp.where(passed, held, 0.0), axis=0, keepdims=True)
+        group = lax.shift_right_logical(owner, count.bit_length() - 1)
+        slots_ref[r : r + 1, :] = jnp.bitwise_and(owner, count - 1)
+        slots_ref[rows + r : rows + r + 1, :] = group * CAP + (slot - start).astype(jnp.int32)
+
+
+def forecast_kernel(extra_ref, source, from_ref, send_ref, state, edge, sums_ref, *refs, fields):
+    members, _, cells = source.shape
+    tiles = cells // LANES
+    height = fields * members
+    if len(refs) == 4:
+        band_ref, powers_ref, split_ref, raw_ref = refs
+        fill_powers(extra_ref, powers_ref)
+        fill_band(from_ref, band_ref, cells)
+    else:
+        powers_ref, slots_ref, split_ref, raw_ref = (extra_ref,) + refs
+        band_ref = from_ref
+        fill_positions(send_ref, slots_ref)
+    low = lax.broadcasted_iota(jnp.int32, (members, LANES), 1) < LANES // 2
+    for f in range(fields):
+        rows = slice(f * members, (f + 1) * members)
+        raw_ref[rows, :] = source[:, f, :]
+        x = raw_ref[rows, :]
+        edge[rows, :] = jnp.where(
+            low,
+            pltpu.roll(x[:, :LANES], STEPS, 1),
+            pltpu.roll(x[:, cells - LANES :], LANES // 2 + 3 * STEPS, 1),
+        )
+        for p, piece in enumerate(halves_of(x)):
+            split_ref[p * height + f * members : p * height + (f + 1) * members, :] = piece
+    mix = powers_of(powers_ref, fields)
+    nearer = lax.broadcasted_iota(jnp.int32, (2 * height, LANES), 1) < LANES // 2
+    for t in range(tiles):
+        lanes, after, before = (
+            slice(n % tiles * LANES, (n % tiles + 1) * LANES) for n in (t, t + 1, t - 1)
+        )
+        around = jnp.where(nearer, split_ref[:, after], split_ref[:, before])
+        product = jnp.dot(
+            jnp.concatenate([split_ref[:, lanes], around], axis=1),
+            band_ref[2 * t * LANES : 2 * (t + 1) * LANES, :],
+            preferred_element_type=jnp.float32,
+        )
+        moved = (
+            product[height:, LANES:] + (product[:height, LANES:] + product[height:, :LANES])
+        ) + product[:height, :LANES]
         for f in range(fields):
-            x = source[pl.ds(at, 8), f, :]
-            edge[pl.ds(f * members + at, 8), :] = jnp.where(
-                low,
-                pltpu.roll(x[:, :LANES], STEPS, 1),
-                pltpu.roll(x[:, cells - LANES :], LANES // 2 + 3 * STEPS, 1),
-            )
-            total = None
-            for d in range(-STEPS, STEPS + 1):
-                term = coef_ref[8 * (d + STEPS) : 8 * (d + STEPS) + 8, :] * shifted(x, d)
-                total = term if total is None else total + term
-            work_ref[f * 8 : f * 8 + 8, :] = total
-        for t in range(tiles):
-            lanes = slice(t * LANES, (t + 1) * LANES)
-            moved = [work_ref[f * 8 : (f + 1) * 8, lanes] for f in range(fields)]
-            for f in range(fields):
-                value = sum(mix[f][g] * moved[g] for g in range(fields))
-                state[pl.ds(f * members + at, 8), lanes] = value
-                place = (f * tiles + t) * 8
-                sums_ref[place : place + 8, :] += value
-        return 0
-
-    lax.fori_loop(0, members // 8, group, 0)
-
-
-def halves_of(x):
-    high = x.astype(jnp.bfloat16)
-    return high, (x - high.astype(jnp.float32)).astype(jnp.bfloat16)
+            value = sum(mix[f][g] * moved[g * members : (g + 1) * members] for g in range(fields))
+            state[f * members : (f + 1) * members, lanes] = value
+            place = (f * tiles + t) * 8
+            sums_ref[place : place + 8, :] = sum(value[8 * i : 8 * i + 8] for i in range(members // 8))
 
 
 def pieces_of(x):
@@ -276,7 +351,7 @@
 
 
 def sums_kernel(
-    which_ref, couple_ref, small_ref, own_state, own_edge, own_sums, other_state, other_edge, other_sums,
+    powers_ref, small_ref, own_state, own_edge, own_sums, other_state, other_edge, other_sums,
     kept, odd, swapped, even, *refs, owners, units, fields,
 ):
     carried = refs[: len(units) - 1]
@@ -284,7 +359,7 @@
         stay_ref, odd_ref, even_ref, edge_ref, halo_ref, onehot_ref, spread_ref, split_ref,
     ) = refs[len(units) - 1 :]
     states, raw_edges = (own_state, other_state), (own_edge, other_edge)
-    block, core = which_ref[0], which_ref[1]
+    block, core = here()
     members = states[0].shape[0] // fields
     cells = states[0].shape[1]
     tiles = cells // LANES
@@ -344,7 +419,7 @@
     from_left = jnp.broadcast_to((edge_left + DIFFUSION) * inside, (8, LANES))
     from_right = jnp.broadcast_to((edge_right + DIFFUSION) * inside, (8, LANES))
     stay = jnp.broadcast_to((1.0 - 2.0 * DIFFUSION - edge_left - edge_right) * inside, (8, LANES))
-    mix = power_of_coupling(couple_ref, fields)
+    mix = powers_of(powers_ref, fields)
     first_sums = [jnp.zeros((8, LANES), jnp.float32) for _ in range(fields)]
     last_sums = [jnp.zeros((8, LANES), jnp.float32) for _ in range(fields)]
     for half in range(2):
@@ -489,10 +564,10 @@
 
 
 def analysis_kernel(
-    which_ref, send_ref, own_ref, other_ref, edge_ref, small_ref, kept, odd, swapped, even,
-    analysis_ref, innovation_ref, mixing_ref, center_ref, pieces_ref, *, units, obs_rows,
+    own_ref, other_ref, edge_ref, small_ref, slots_ref, kept, odd, swapped, even,
+    analysis_ref, innovation_ref, mixing_ref, center_ref, pieces_ref, *, units, obs_rows, count,
 ):
-    block, core = which_ref[0], which_ref[1]
+    block, core = here()
     members, fields, cells = analysis_ref.shape
     total = 2 * members
     strip_rows = fields * members
@@ -553,30 +628,33 @@
         )
         analysis_ref[:, f, :] = product[:members] + product[members:]
 
-    owners = send_ref.shape[1]
-    held = owners // 16
-    wide = obs_rows * LANES
-    slot = lax.broadcasted_iota(jnp.int32, (1, wide), 1)
-    centers = jnp.zeros((1, wide), jnp.float32)
-    start = jnp.int32(0)
-    for owner in range(owners):
-        way = [jnp.bitwise_xor(digit_of(block, unit), (owner // unit) % 4) for unit in units]
-        row = way[-1] * held
-        if len(units) > 2:
-            row = row + sum(step * 4**s for s, step in enumerate(way[:-2]))
-        size = 4 * held
-        for step in reversed(way[1:-1]):
-            row = row + step * size
-            size = size * 4
-        row = row + way[0] * returned
-        line = center_ref[pl.ds(row, 1), :]
-        line = jnp.concatenate([line] + [jnp.zeros((1, LANES), jnp.float32)] * (obs_rows - 1), axis=1)
-        moved = pltpu.roll(line, within(start - way[-2] * CAP, wide), 1)
-        end = start + send_ref[0, owner]
-        centers = jnp.where((slot >= start) & (slot < end), moved, centers)
-        start = end
+    held = count // 4
+    lane_group = lane // CAP
+    table = []
+    for r in range(count):
+        merged = jnp.zeros((1, LANES), jnp.float32)
+        for group in range(GROUPS):
+            owner = group * count + r
+            way = [jnp.bitwise_xor(digit_of(block, unit), (owner // unit) % 4) for unit in units]
+            row = way[-1] * held
+            if len(units) > 2:
+                row = row + sum(step * 4**n for n, step in enumerate(way[:-2]))
+            size = 4 * held
+            for step in reversed(way[1:-1]):
+                row = row + step * size
+                size = size * 4
+            row = row + way[0] * returned
+            line = center_ref[pl.ds(row, 1), :]
+            moved = pltpu.roll(line, jnp.bitwise_and(group - way[-2], 3) * CAP, 1)
+            merged = jnp.where(lane_group[:1] == group, moved, merged)
+        table.append(jnp.broadcast_to(merged, (8, LANES)))
     for r in range(obs_rows):
-        center = centers[:, r * LANES : (r + 1) * LANES]
+        center = jnp.zeros((8, LANES), jnp.float32)
+        lanes = jnp.broadcast_to(slots_ref[obs_rows + r : obs_rows + r + 1, :], (8, LANES))
+        for n in range(count):
+            found = jnp.take_along_axis(table[n], lanes, axis=1, mode="promise_in_bounds")
+            center = jnp.where(slots_ref[r : r + 1, :] == n, found, center)
+        center = center[:1]
         at = small_ref.shape[0] - 2 * obs_rows + r
         value, sigma = small_ref[at : at + 1, :], small_ref[at + obs_rows : at + obs_rows + 1, :]
         innovation_ref[r : r + 1, :] = (value - center) / sigma
@@ -595,13 +673,11 @@
     units = stage_units(owners)
     block = lax.axis_index("cells").astype(jnp.int32)
     core = lax.axis_index("members").astype(jnp.int32)
-    which = jnp.stack([block, core])
     small = (
         speed.reshape(tiles, LANES), direction.reshape(tiles, LANES),
         *(x.reshape(obs_rows, LANES) for x in (obs_place, obs_field, obs_value, obs_sigma)),
     )
     whole = pl.BlockSpec(memory_space=pltpu.VMEM)
-    scalars = pl.BlockSpec(memory_space=pltpu.SMEM)
     params = pltpu.CompilerParams(vmem_limit_bytes=VMEM_BYTES)
     real = jnp.float32
 
@@ -623,12 +699,12 @@
         out_shape=(jax.ShapeDtypeStruct((part, LANES), real),) * 3
         + (jax.ShapeDtypeStruct((small_rows, LANES), real),),
         grid=(1,),
-        in_specs=[scalars, scalars] + [rows_of(x.shape[0]) for x in small],
+        in_specs=[whole] + [rows_of(x.shape[0]) for x in small],
         out_specs=(whole,) * 4,
         scratch_shapes=[pltpu.VMEM((table_rows, LANES), real)],
         compiler_params=params,
         name="pack",
-    )(which, send_count, *small)
+    )(send_count, *small)
     to_odd, to_even = pl.pallas_call(
         join_kernel,
         out_shape=(jax.ShapeDtypeStruct((16 + part, LANES), real),) * 2,
@@ -638,29 +714,32 @@
         name="join",
     )(strips, other, to_odd, to_even)
 
-    def forecast(half):
+    strip_rows = fields * members
+    band = jax.ShapeDtypeStruct((2 * cells, 2 * LANES), jnp.bfloat16)
+
+    powers = jax.ShapeDtypeStruct((fields * fields, LANES), real)
+    slots = jax.ShapeDtypeStruct((2 * obs_rows, LANES), jnp.int32)
+
+    def forecast(mixed, half, source, extra):
         return pl.pallas_call(
-            forecast_kernel,
+            functools.partial(forecast_kernel, fields=fields),
             out_shape=(
                 jax.ShapeDtypeStruct((strip_rows, cells), real),
                 jax.ShapeDtypeStruct((strip_rows, LANES), real),
                 jax.ShapeDtypeStruct((places * 8, LANES), real),
-            ),
-            in_specs=[scalars] + [whole] * 2,
-            out_specs=(whole,) * 3,
-            scratch_shapes=[
-                pltpu.VMEM((fields * 8, cells), real),
-                pltpu.VMEM((8 * (2 * STEPS + 1), cells), real),
-            ],
+            )
+            + extra,
+            in_specs=[whole] * 4,
+            out_specs=(whole,) * (3 + len(extra)),
+            scratch_shapes=[pltpu.VMEM((2 * strip_rows, cells), jnp.bfloat16), pltpu.VMEM((strip_rows, cells), real)],
             compiler_params=params,
             cost_estimate=pl.CostEstimate(
                 flops=80 * strip_rows * cells, bytes_accessed=8 * strip_rows * cells, transcendentals=0
             ),
             name="forecast",
-        )(couple, half, small)
-
-    strip_rows = fields * members
-    own_forecast = forecast(ensemble)
+        )(mixed, half, source, send_count)
+
+    *own_forecast, rule, mixed = forecast(couple, ensemble, small, (band, powers))
     carried = []
     for n, unit in enumerate(units):
         arrived = exchange(to_odd, to_even, owners, unit)
@@ -668,13 +747,13 @@
             to_odd, to_even, kept = pl.pallas_call(
                 functools.partial(regroup_kernel, unit=unit, into_lanes=n + 2 == len(units)),
                 out_shape=tuple(jax.ShapeDtypeStruct(x.shape, real) for x in (to_odd, to_even, kept)),
-                in_specs=[scalars] + [whole] * 4 + [pl.BlockSpec(memory_space=pl.ANY)],
+                in_specs=[whole] * 4 + [pl.BlockSpec(memory_space=pl.ANY)],
                 out_specs=(whole,) * 3,
                 compiler_params=params,
                 name="regroup",
-            )(which, kept, *arrived, own_forecast[2])
+            )(kept, *arrived, own_forecast[2])
             carried.append(to_odd)
-    other_forecast = forecast(other)
+    *other_forecast, slots_of = forecast(mixed, other, rule, (slots,))
 
     held = kept.shape[0] // 8
     sums_rows = -(-(members + 1 + 4 * held) // 8) * 8
@@ -683,7 +762,7 @@
     stay, to_odd, to_even, edges = pl.pallas_call(
         functools.partial(sums_kernel, owners=owners, units=units, fields=fields),
         out_shape=(sums, sums, sums, jax.ShapeDtypeStruct((2 * strip_rows, 2 * LANES), real)),
-        in_specs=[scalars, scalars] + [whole] * (11 + len(carried)),
+        in_specs=[whole] * (12 + len(carried)),
         out_specs=(whole,) * 4,
         scratch_shapes=[
             pltpu.VMEM((2 * strip_rows, LANES), real),
@@ -694,7 +773,7 @@
         compiler_params=params,
         name="sums",
     )(
-        which, couple, small, *own_forecast, *other_forecast, kept, *arrived, *carried,
+        mixed, small, *own_forecast, *other_forecast, kept, *arrived, *carried,
     )
 
     head = members + 1
@@ -713,12 +792,12 @@
             stay = to_odd = to_even = added
 
     analysis, innovation = pl.pallas_call(
-        functools.partial(analysis_kernel, units=units, obs_rows=obs_rows),
+        functools.partial(analysis_kernel, units=units, obs_rows=obs_rows, count=owners // GROUPS),
         out_shape=(
             jax.ShapeDtypeStruct((members, fields, cells), real),
             jax.ShapeDtypeStruct((obs_rows, LANES), real),
         ),
-        in_specs=[scalars, scalars] + [whole] * 8,
+        in_specs=[whole] * 9,
         out_specs=(whole, whole),
         scratch_shapes=[
             pltpu.VMEM((total, LANES), real),
@@ -728,7 +807,7 @@
         compiler_params=params,
         name="analysis",
     )(
-        which, send_count, own_forecast[0], other_forecast[0], edges, small,
+        own_forecast[0], other_forecast[0], edges, small, slots_of,
         stay, odd, swapped, even,
     )
     return (analysis, innovation.reshape(obs))

time: 37.1 us -> 33.1 us (0.89)
  Pallas kernels: 12.7 us -> 7.66 us
  waiting for transfers between devices: 3.21 us -> 4.71 us
  starting transfers between devices: 18.5 us -> 18 us
    pallas_call x2, Pallas kernels: 4.9 us -> 2.11 us  [forecast(): pl.pallas_call(functools.partial(forecast_kernel, fields=fields), out_sha...]
    ppermute x5, waiting for transfers between devices: 0.16 us -> 0.85 us  [swap_cores(): lax.ppermute(x, BOTH, core_pairs(owners, lambda block, core: (block, 1 -...]
    pallas_call x1, Pallas kernels: 2.45 us -> 1.77 us  [shards(): pl.pallas_call(functools.partial(sums_kernel, owners=owners, units=units,...]
    ppermute x4, starting transfers between devices: 6.61 us -> 6.06 us  [exchange(): lax.ppermute(to_odd, BOTH, core_pairs(owners, lambda block, core: (block...]
    pallas_call x1, Pallas kernels: 3.76 us -> 3.21 us  [shards(): pl.pallas_call(functools.partial(analysis_kernel, units=units, obs_rows=o...]
    pallas_call x1, Pallas kernels: 0.63 us -> 0.1 us  [shards(): pl.pallas_call(functools.partial(regroup_kernel, unit=unit, into_lanes=n...]
    ppermute x4, waiting for transfers between devices: 0.92 us -> 1.42 us  [exchange(): lax.ppermute(to_odd, BOTH, core_pairs(owners, lambda block, core: (block...]
    pallas_call x1, Pallas kernels: 0.67 us -> 0.21 us  [shards(): pl.pallas_call(functools.partial(pack_kernel, rows=obs_rows, cells=cells,...]
  transfers between devices with their start and end apart: 13 -> 13, of which waited for: 5 -> 6; matrix products, arithmetic and copies ran while one was open for 0% -> 0% of each run, Pallas kernels for 15% -> 7%
where the time goes in v4:
time: 33.1 us; the launch traced here: 32.9 us
  starting transfers between devices  18 us (54%)
  Pallas kernels  7.66 us (23%)
  waiting for transfers between devices  4.71 us (14%)
  local copies, waits for them, and re-layouts  1.81 us (5%)
  between operations  0.75 us (2%)
    ppermute x4, starting transfers between devices, exchange(): lax.ppermute(to_even, BOTH, core_pairs(owners, lambda block, core: (block...  8.78 us
    ppermute x4, starting transfers between devices, exchange(): lax.ppermute(to_odd, BOTH, core_pairs(owners, lambda block, core: (block...  6.06 us
    pallas_call x1, Pallas kernels, shards(): pl.pallas_call(functools.partial(analysis_kernel, units=units, obs_rows=o...  3.21 us
    ppermute x5, starting transfers between devices, swap_cores(): lax.ppermute(x, BOTH, core_pairs(owners, lambda block, core: (block, 1 -...  3.14 us
    ppermute x4, waiting for transfers between devices, exchange(): lax.ppermute(to_even, BOTH, core_pairs(owners, lambda block, core: (block...  2.44 us
    pallas_call x2, Pallas kernels, forecast(): pl.pallas_call(functools.partial(forecast_kernel, fields=fields), out_sha...  2.11 us
    unnamed x20, local copies, waits for them, and re-layouts  1.81 us
    pallas_call x1, Pallas kernels, shards(): pl.pallas_call(functools.partial(sums_kernel, owners=owners, units=units,...  1.77 us
  transfers between devices with their start and end apart: 13, of which 6 were waited for; matrix products, arithmetic and copies ran while one was open for 0% of the time, Pallas kernels for 7%

profile of v4, /device:TPU:0, one launch (start us, length us, event | category | flops | bytes accessed | tf_op | source)
XLA Modules:
  0.0 32.9 jit_solution(13771324117039382264)
XLA Ops:
  0.6 0.5 %collective-permute-start = (f32[32,4,1024]{2,1,0:T(4,128)}, f32[32,4,1024]{2,1,0:T(4,128)S(1)}, u32[]{:S(2)}, u32[]{:S(2)}) collective-permute-start(f32[32,4,1024]{2,1,0:T(4,128)} %ensemble_ref.1), channel_id=1, source_target_pairs={{0,1},{1,0},{2,3},{3,2},{4,5},{5,4},{6,7},{7,6},{8,9},{9,8},{10,11... | collective-permute-start | bytes 1572872 | tf_op jit(solution)/shard_map/ppermute | solution.py:42
  1.2 1.0 %copy-done = f32[32,4,1024]{2,1,0:T(4,128)S(1)} copy-done((f32[32,4,1024]{2,1,0:T(4,128)S(1)}, f32[32,4,1024]{2,1,0:T(4,128)}, u32[]{:S(2)}) %copy-start) | copy-done | bytes 524312
  2.4 0.5 %copy-done.6 = s32[256]{0:T(256)S(1)} copy-done((s32[256]{0:T(256)S(1)}, s32[256]{0:T(256)}, u32[]{:S(2)}) %copy-start.6) | copy-done | bytes 1048
  2.9 0.2 copy-done.4
  3.1 0.2 pack.1
  3.5 2.6 %collective-permute-start.1 = (f32[24,128]{1,0:T(8,128)S(1)}, f32[24,128]{1,0:T(8,128)S(1)}, u32[]{:S(2)}, u32[]{:S(2)}) collective-permute-start(f32[24,128]{1,0:T(8,128)S(1)} %get-tuple-element.38), channel_id=1, source_target_pairs={{0,2},{1,7},{2,0},{3,5},{4,6},{5,3},{6,4},{7,1},{8,10},{9,15},{10,... | collective-permute-start | bytes 36872 | tf_op jit(solution)/shard_map/ppermute | solution.py:46
  6.1 1.5 %collective-permute-start.3 = (f32[24,128]{1,0:T(8,128)S(1)}, f32[24,128]{1,0:T(8,128)S(1)}, u32[]{:S(2)}, u32[]{:S(2)}) collective-permute-start(f32[24,128]{1,0:T(8,128)S(1)} %get-tuple-element.39), channel_id=1, source_target_pairs={{0,4},{1,5},{2,6},{3,7},{4,0},{5,1},{6,2},{7,3},{8,12},{9,13},{10,... | collective-permute-start | bytes 36872 | tf_op jit(solution)/shard_map/ppermute | solution.py:49
  7.7 0.6 %collective-permute-start.2 = (f32[24,128]{1,0:T(8,128)S(1)}, f32[24,128]{1,0:T(8,128)S(1)}, u32[]{:S(2)}, u32[]{:S(2)}) collective-permute-start(f32[24,128]{1,0:T(8,128)S(1)} %collective-permute-done.1.odd), channel_id=1, source_target_pairs={{0,1},{1,0},{2,3},{3,2},{4,5},{5,4},{6,7},{7,6},{8,9},{9,8},{10,11... | collective-permute-start | bytes 36872 | tf_op jit(solution)/shard_map/ppermute | solution.py:42
  8.3 1.5 %forecast.2 = (f32[128,1024]{1,0:T(8,128)S(1)}, f32[128,128]{1,0:T(8,128)S(1)}, f32[256,128]{1,0:T(8,128)S(1)}, bf16[2048,256]{1,0:T(8,128)(2,1)S(1)}, f32[16,128]{1,0:T(8,128)S(1)}) custom-call(f32[4,4]{1,0:T(4,128)S(1)} %copy-done.5, f32[32,4,1024]{2,1,0:T(4,128)S(1)} %copy-done.1, f32[20,128]{1,0:T(8,128)S(1)} %get-tuple-element.26.from_ref.small_ref, ...), custom_call_target="tpu_custom_call" | custom-call | flops 10485760 | bytes 1048576 | tf_op jit(solution)/shard_map/forecast/pallas_call | solution.py:724
  9.9 1.8 %collective-permute-start.4 = (f32[24,128]{1,0:T(8,128)S(1)}, f32[24,128]{1,0:T(8,128)S(1)}, u32[]{:S(2)}, u32[]{:S(2)}) collective-permute-start(f32[24,128]{1,0:T(8,128)S(1)} %get-tuple-element.41.refs_0_), channel_id=1, source_target_pairs={{0,8},{1,25},{2,10},{3,27},{4,12},{5,29},{6,14},{7,31},{8,0},{9,17... | collective-permute-start | bytes 36872 | tf_op jit(solution)/shard_map/ppermute | solution.py:46
  11.8 2.6 %collective-permute-start.6 = (f32[24,128]{1,0:T(8,128)S(1)}, f32[24,128]{1,0:T(8,128)S(1)}, u32[]{:S(2)}, u32[]{:S(2)}) collective-permute-start(f32[24,128]{1,0:T(8,128)S(1)} %get-tuple-element.42), channel_id=1, source_target_pairs={{0,16},{1,17},{2,18},{3,19},{4,20},{5,21},{6,22},{7,23},{8,24},{9,... | collective-permute-start | bytes 36872 | tf_op jit(solution)/shard_map/ppermute | solution.py:49
  14.4 0.5 %collective-permute-start.5 = (f32[24,128]{1,0:T(8,128)S(1)}, f32[24,128]{1,0:T(8,128)S(1)}, u32[]{:S(2)}, u32[]{:S(2)}) collective-permute-start(f32[24,128]{1,0:T(8,128)S(1)} %collective-permute-done.4.odd), channel_id=1, source_target_pairs={{0,1},{1,0},{2,3},{3,2},{4,5},{5,4},{6,7},{7,6},{8,9},{9,8},{10,11... | collective-permute-start | bytes 36872 | tf_op jit(solution)/shard_map/ppermute | solution.py:42
  14.9 0.6 %forecast.3 = (f32[128,1024]{1,0:T(8,128)S(1)}, f32[128,128]{1,0:T(8,128)S(1)}, f32[256,128]{1,0:T(8,128)S(1)}, s32[4,128]{1,0:T(4,128)S(1)}) custom-call(f32[16,128]{1,0:T(8,128)S(1)} %get-tuple-element.28.extra_ref.powers_ref, f32[32,4,1024]{2,1,0:T(4,128)S(1)} %collective-permute-done.source.other_ref, bf16[2048,256]{1,0:T(8,128)(2,1)S(1)} %get-tuple-element.29.from_ref, ...), custom_call_target="tpu_custom_call" | custom-call | flops 10485760 | bytes 1048576 | tf_op jit(solution)/shard_map/forecast/pallas_call | solution.py:724
  15.5 1.0 %collective-permute-done.6.even = f32[24,128]{1,0:T(8,128)S(1)} collective-permute-done((f32[24,128]{1,0:T(8,128)S(1)}, f32[24,128]{1,0:T(8,128)S(1)}, u32[]{:S(2)}, u32[]{:S(2)}) %collective-permute-start.6) | collective-permute-done | bytes 12320 | tf_op jit(solution)/shard_map/ppermute | solution.py:49
  16.5 1.8 %sums.1 = (f32[40,128]{1,0:T(8,128)S(1)}, f32[40,128]{1,0:T(8,128)S(1)}, f32[40,128]{1,0:T(8,128)S(1)}, f32[256,256]{1,0:T(8,128)S(1)}) custom-call(f32[16,128]{1,0:T(8,128)S(1)} %get-tuple-element.28.extra_ref.powers_ref, f32[20,128]{1,0:T(8,128)S(1)} %get-tuple-element.26.from_ref.small_ref, f32[128,1024]{1,0:T(8,128)S(1)} %get-tuple-element.27.own_state.own_ref, ...), custom_call_target="tpu_custom_call" | custom-call | tf_op jit(solution)/shard_map/sums/pallas_call | solution.py:762
  18.4 3.2 %collective-permute-start.7 = (f32[40,128]{1,0:T(8,128)S(1)}, f32[40,128]{1,0:T(8,128)S(1)}, u32[]{:S(2)}, u32[]{:S(2)}) collective-permute-start(f32[40,128]{1,0:T(8,128)S(1)} %get-tuple-element.46), channel_id=1, source_target_pairs={{0,16},{1,17},{2,18},{3,19},{4,20},{5,21},{6,22},{7,23},{8,24},{9,... | collective-permute-start | bytes 61448 | tf_op jit(solution)/shard_map/ppermute | solution.py:49
  21.6 0.5 %collective-permute-done.8 = f32[40,128]{1,0:T(8,128)S(1)} collective-permute-done((f32[40,128]{1,0:T(8,128)S(1)}, f32[40,128]{1,0:T(8,128)S(1)}, u32[]{:S(2)}, u32[]{:S(2)}) %collective-permute-start.8) | collective-permute-done | bytes 20512 | tf_op jit(solution)/shard_map/ppermute | solution.py:46
  22.1 1.4 %collective-permute-start.9 = (f32[40,128]{1,0:T(8,128)S(1)}, f32[40,128]{1,0:T(8,128)S(1)}, u32[]{:S(2)}, u32[]{:S(2)}) collective-permute-start(f32[40,128]{1,0:T(8,128)S(1)} %collective-permute-done.8), channel_id=1, source_target_pairs={{0,1},{1,0},{2,3},{3,2},{4,5},{5,4},{6,7},{7,6},{8,9},{9,8},{10,11... | collective-permute-start | bytes 61448 | tf_op jit(solution)/shard_map/ppermute | solution.py:42
  23.5 0.8 %collective-permute-done.9 = f32[40,128]{1,0:T(8,128)S(1)} collective-permute-done((f32[40,128]{1,0:T(8,128)S(1)}, f32[40,128]{1,0:T(8,128)S(1)}, u32[]{:S(2)}, u32[]{:S(2)}) %collective-permute-start.9) | collective-permute-done | bytes 20512 | tf_op jit(solution)/shard_map/ppermute | solution.py:42
  24.3 1.5 %collective-permute-start.10 = (f32[40,128]{1,0:T(8,128)S(1)}, f32[40,128]{1,0:T(8,128)S(1)}, u32[]{:S(2)}, u32[]{:S(2)}) collective-permute-start(f32[40,128]{1,0:T(8,128)S(1)} %add_add_fusion.kept), channel_id=1, source_target_pairs={{0,2},{1,7},{2,0},{3,5},{4,6},{5,3},{6,4},{7,1},{8,10},{9,15},{10,... | collective-permute-start | bytes 61448 | tf_op jit(solution)/shard_map/ppermute | solution.py:46
  25.8 1.5 %collective-permute-start.12 = (f32[40,128]{1,0:T(8,128)S(1)}, f32[40,128]{1,0:T(8,128)S(1)}, u32[]{:S(2)}, u32[]{:S(2)}) collective-permute-start(f32[40,128]{1,0:T(8,128)S(1)} %add_add_fusion.kept), channel_id=1, source_target_pairs={{0,4},{1,5},{2,6},{3,7},{4,0},{5,1},{6,2},{7,3},{8,12},{9,13},{10,... | collective-permute-start | bytes 61448 | tf_op jit(solution)/shard_map/ppermute | solution.py:49
  27.3 0.8 %collective-permute-done.10.odd = f32[40,128]{1,0:T(8,128)S(1)} collective-permute-done((f32[40,128]{1,0:T(8,128)S(1)}, f32[40,128]{1,0:T(8,128)S(1)}, u32[]{:S(2)}, u32[]{:S(2)}) %collective-permute-start.10) | collective-permute-done | bytes 20512 | tf_op jit(solution)/shard_map/ppermute | solution.py:46
  28.3 1.4 %collective-permute-done.12.even = f32[40,128]{1,0:T(8,128)S(1)} collective-permute-done((f32[40,128]{1,0:T(8,128)S(1)}, f32[40,128]{1,0:T(8,128)S(1)}, u32[]{:S(2)}, u32[]{:S(2)}) %collective-permute-start.12) | collective-permute-done | bytes 20512 | tf_op jit(solution)/shard_map/ppermute | solution.py:49
  29.7 3.2 %analysis.1 = (f32[32,4,1024]{2,1,0:T(4,128)}, f32[2,128]{1,0:T(2,128)}) custom-call(f32[128,1024]{1,0:T(8,128)S(1)} %get-tuple-element.27.own_state.own_ref, f32[128,1024]{1,0:T(8,128)S(1)} %get-tuple-element.30.other_state.other_ref, f32[256,256]{1,0:T(8,128)S(1)} %get-tuple-element.43.edge_ref, f32[20,128]{1,0:T(8,128)S(1)} %get-tuple-element.26.from_ref.small_ref, ...), custom_call_target="tpu_custom_call" | custom-call | tf_op jit(solution)/shard_map/analysis/pallas_call | solution.py:794
  (31 shorter events, 0.9 us)
Async XLA Ops:
  0.6 2.7 %collective-permute-start = (f32[32,4,1024]{2,1,0:T(4,128)}, f32[32,4,1024]{2,1,0:T(4,128)S(1)}, u32[]{:S(2)}, u32[]{:S(2)}) collective-permute-start(f32[32,4,1024]{2,1,0:T(4,128)} %ensemble_ref.1), channel_id=1, source_target_pairs={{0,1},{1,0},{2,3},{3,2},{4,5},{5,4},{6,7},{7,6},{8,9},{9,8},{10,11... | collective-permute-start | bytes 1572872 | tf_op jit(solution)/shard_map/ppermute | solution.py:42
  1.1 1.0 %copy-start = (f32[32,4,1024]{2,1,0:T(4,128)S(1)}, f32[32,4,1024]{2,1,0:T(4,128)}, u32[]{:S(2)}) copy-start(f32[32,4,1024]{2,1,0:T(4,128)} %ensemble_ref.1) | copy-start | bytes 1572868
  2.2 0.7 %copy-start.6 = (s32[256]{0:T(256)S(1)}, s32[256]{0:T(256)}, u32[]{:S(2)}) copy-start(s32[256]{0:T(256)} %param.13) | copy-start | bytes 3076
  2.2 0.7 %copy-start.7 = (s32[256]{0:T(256)S(1)}, s32[256]{0:T(256)}, u32[]{:S(2)}) copy-start(s32[256]{0:T(256)} %param.14) | copy-start | bytes 3076
  2.2 0.7 %copy-start.8 = (f32[256]{0:T(256)S(1)}, f32[256]{0:T(256)}, u32[]{:S(2)}) copy-start(f32[256]{0:T(256)} %param.15) | copy-start | bytes 3076
  2.2 0.7 %copy-start.9 = (f32[256]{0:T(256)S(1)}, f32[256]{0:T(256)}, u32[]{:S(2)}) copy-start(f32[256]{0:T(256)} %param.16) | copy-start | bytes 3076
  2.2 6.1 %copy-start.1 = (f32[32,4,1024]{2,1,0:T(4,128)S(1)}, f32[32,4,1024]{2,1,0:T(4,128)}, u32[]{:S(2)}) copy-start(f32[32,4,1024]{2,1,0:T(4,128)} %ensemble_ref.1) | copy-start | bytes 1572868
  2.3 0.8 %copy-start.4 = (s32[1024]{0:T(1024)S(1)}, s32[1024]{0:T(1024)}, u32[]{:S(2)}) copy-start(s32[1024]{0:T(1024)} %param.11) | copy-start | bytes 12292
  2.4 0.8 %copy-start.3 = (f32[1024]{0:T(1024)S(1)}, f32[1024]{0:T(1024)}, u32[]{:S(2)}) copy-start(f32[1024]{0:T(1024)} %param.10) | copy-start | bytes 12292
  2.4 0.7 %copy-start.2 = (s32[1,16]{1,0:T(1,128)S(1)}, s32[1,16]{1,0:T(1,128)}, u32[]{:S(2)}) copy-start(s32[1,16]{1,0:T(1,128)} %send_ref.5) | copy-start | bytes 196
  3.5 4.8 %copy-start.5 = (f32[4,4]{1,0:T(4,128)S(1)}, f32[4,4]{1,0:T(4,128)}, u32[]{:S(2)}) copy-start(f32[4,4]{1,0:T(4,128)} %extra_ref.1) | copy-start | bytes 196
  3.5 4.2 %collective-permute-start.1 = (f32[24,128]{1,0:T(8,128)S(1)}, f32[24,128]{1,0:T(8,128)S(1)}, u32[]{:S(2)}, u32[]{:S(2)}) collective-permute-start(f32[24,128]{1,0:T(8,128)S(1)} %get-tuple-element.38), channel_id=1, source_target_pairs={{0,2},{1,7},{2,0},{3,5},{4,6},{5,3},{6,4},{7,1},{8,10},{9,15},{10,... | collective-permute-start | bytes 36872 | tf_op jit(solution)/shard_map/ppermute | solution.py:46
  6.1 3.8 %collective-permute-start.3 = (f32[24,128]{1,0:T(8,128)S(1)}, f32[24,128]{1,0:T(8,128)S(1)}, u32[]{:S(2)}, u32[]{:S(2)}) collective-permute-start(f32[24,128]{1,0:T(8,128)S(1)} %get-tuple-element.39), channel_id=1, source_target_pairs={{0,4},{1,5},{2,6},{3,7},{4,0},{5,1},{6,2},{7,3},{8,12},{9,13},{10,... | collective-permute-start | bytes 36872 | tf_op jit(solution)/shard_map/ppermute | solution.py:49
  7.7 2.1 %collective-permute-start.2 = (f32[24,128]{1,0:T(8,128)S(1)}, f32[24,128]{1,0:T(8,128)S(1)}, u32[]{:S(2)}, u32[]{:S(2)}) collective-permute-start(f32[24,128]{1,0:T(8,128)S(1)} %collective-permute-done.1.odd), channel_id=1, source_target_pairs={{0,1},{1,0},{2,3},{3,2},{4,5},{5,4},{6,7},{7,6},{8,9},{9,8},{10,11... | collective-permute-start | bytes 36872 | tf_op jit(solution)/shard_map/ppermute | solution.py:42
  9.9 4.4 %collective-permute-start.4 = (f32[24,128]{1,0:T(8,128)S(1)}, f32[24,128]{1,0:T(8,128)S(1)}, u32[]{:S(2)}, u32[]{:S(2)}) collective-permute-start(f32[24,128]{1,0:T(8,128)S(1)} %get-tuple-element.41.refs_0_), channel_id=1, source_target_pairs={{0,8},{1,25},{2,10},{3,27},{4,12},{5,29},{6,14},{7,31},{8,0},{9,17... | collective-permute-start | bytes 36872 | tf_op jit(solution)/shard_map/ppermute | solution.py:46
  11.8 4.7 %collective-permute-start.6 = (f32[24,128]{1,0:T(8,128)S(1)}, f32[24,128]{1,0:T(8,128)S(1)}, u32[]{:S(2)}, u32[]{:S(2)}) collective-permute-start(f32[24,128]{1,0:T(8,128)S(1)} %get-tuple-element.42), channel_id=1, source_target_pairs={{0,16},{1,17},{2,18},{3,19},{4,20},{5,21},{6,22},{7,23},{8,24},{9,... | collective-permute-start | bytes 36872 | tf_op jit(solution)/shard_map/ppermute | solution.py:49
  14.4 2.1 %collective-permute-start.5 = (f32[24,128]{1,0:T(8,128)S(1)}, f32[24,128]{1,0:T(8,128)S(1)}, u32[]{:S(2)}, u32[]{:S(2)}) collective-permute-start(f32[24,128]{1,0:T(8,128)S(1)} %collective-permute-done.4.odd), channel_id=1, source_target_pairs={{0,1},{1,0},{2,3},{3,2},{4,5},{5,4},{6,7},{7,6},{8,9},{9,8},{10,11... | collective-permute-start | bytes 36872 | tf_op jit(solution)/shard_map/ppermute | solution.py:42
  18.3 3.8 %collective-permute-start.8 = (f32[40,128]{1,0:T(8,128)S(1)}, f32[40,128]{1,0:T(8,128)S(1)}, u32[]{:S(2)}, u32[]{:S(2)}) collective-permute-start(f32[40,128]{1,0:T(8,128)S(1)} %get-tuple-element.47), channel_id=1, source_target_pairs={{0,8},{1,25},{2,10},{3,27},{4,12},{5,29},{6,14},{7,31},{8,0},{9,17... | collective-permute-start | bytes 61448 | tf_op jit(solution)/shard_map/ppermute | solution.py:46
  18.4 5.0 %collective-permute-start.7 = (f32[40,128]{1,0:T(8,128)S(1)}, f32[40,128]{1,0:T(8,128)S(1)}, u32[]{:S(2)}, u32[]{:S(2)}) collective-permute-start(f32[40,128]{1,0:T(8,128)S(1)} %get-tuple-element.46), channel_id=1, source_target_pairs={{0,16},{1,17},{2,18},{3,19},{4,20},{5,21},{6,22},{7,23},{8,24},{9,... | collective-permute-start | bytes 61448 | tf_op jit(solution)/shard_map/ppermute | solution.py:49
  22.1 2.2 %collective-permute-start.9 = (f32[40,128]{1,0:T(8,128)S(1)}, f32[40,128]{1,0:T(8,128)S(1)}, u32[]{:S(2)}, u32[]{:S(2)}) collective-permute-start(f32[40,128]{1,0:T(8,128)S(1)} %collective-permute-done.8), channel_id=1, source_target_pairs={{0,1},{1,0},{2,3},{3,2},{4,5},{5,4},{6,7},{7,6},{8,9},{9,8},{10,11... | collective-permute-start | bytes 61448 | tf_op jit(solution)/shard_map/ppermute | solution.py:42
  24.3 3.8 %collective-permute-start.10 = (f32[40,128]{1,0:T(8,128)S(1)}, f32[40,128]{1,0:T(8,128)S(1)}, u32[]{:S(2)}, u32[]{:S(2)}) collective-permute-start(f32[40,128]{1,0:T(8,128)S(1)} %add_add_fusion.kept), channel_id=1, source_target_pairs={{0,2},{1,7},{2,0},{3,5},{4,6},{5,3},{6,4},{7,1},{8,10},{9,15},{10,... | collective-permute-start | bytes 61448 | tf_op jit(solution)/shard_map/ppermute | solution.py:46
  25.8 3.9 %collective-permute-start.12 = (f32[40,128]{1,0:T(8,128)S(1)}, f32[40,128]{1,0:T(8,128)S(1)}, u32[]{:S(2)}, u32[]{:S(2)}) collective-permute-start(f32[40,128]{1,0:T(8,128)S(1)} %add_add_fusion.kept), channel_id=1, source_target_pairs={{0,4},{1,5},{2,6},{3,7},{4,0},{5,1},{6,2},{7,3},{8,12},{9,13},{10,... | collective-permute-start | bytes 61448 | tf_op jit(solution)/shard_map/ppermute | solution.py:49
  28.1 1.6 %collective-permute-start.11 = (f32[40,128]{1,0:T(8,128)S(1)}, f32[40,128]{1,0:T(8,128)S(1)}, u32[]{:S(2)}, u32[]{:S(2)}) collective-permute-start(f32[40,128]{1,0:T(8,128)S(1)} %collective-permute-done.10.odd), channel_id=1, source_target_pairs={{0,1},{1,0},{2,3},{3,2},{4,5},{5,4},{6,7},{7,6},{8,9},{9,8},{10,11... | collective-permute-start | bytes 61448 | tf_op jit(solution)/shard_map/ppermute | solution.py:42

commit v5 on v4

--- a/solution.py
+++ b/solution.py
@@ -297,18 +297,27 @@
         slots_ref[rows + r : rows + r + 1, :] = group * CAP + (slot - start).astype(jnp.int32)
 
 
-def forecast_kernel(extra_ref, source, from_ref, send_ref, state, edge, sums_ref, *refs, fields):
+def forecast_kernel(extra_ref, source, from_ref, *refs, fields, own):
     members, _, cells = source.shape
     tiles = cells // LANES
     height = fields * members
-    if len(refs) == 4:
-        band_ref, powers_ref, split_ref, raw_ref = refs
+    if own:
+        state, edge, sums_ref, band_ref, powers_ref, split_ref, raw_ref = refs
         fill_powers(extra_ref, powers_ref)
         fill_band(from_ref, band_ref, cells)
     else:
-        powers_ref, slots_ref, split_ref, raw_ref = (extra_ref,) + refs
-        band_ref = from_ref
+        send_ref, own_state, state, edge, sums_ref, slots_ref, pieces_ref, split_ref, raw_ref = refs
+        powers_ref, band_ref = extra_ref, from_ref
         fill_positions(send_ref, slots_ref)
+        core = here()[1]
+
+        def put_pieces(side, f, lanes, value):
+            for p, piece in enumerate(halves_of(value)):
+                at = pl.multiple_of((f * 2 + p) * 2 * members + side * members, 16)
+                pieces_ref[pl.ds(at, members), lanes] = piece
+
+        for f in range(fields):
+            put_pieces(core, f, slice(0, cells), own_state[f * members : (f + 1) * members, :])
     low = lax.broadcasted_iota(jnp.int32, (members, LANES), 1) < LANES // 2
     for f in range(fields):
         rows = slice(f * members, (f + 1) * members)
@@ -339,6 +348,8 @@
         for f in range(fields):
             value = sum(mix[f][g] * moved[g * members : (g + 1) * members] for g in range(fields))
             state[f * members : (f + 1) * members, lanes] = value
+            if not own:
+                put_pieces(1 - core, f, lanes, value)
             place = (f * tiles + t) * 8
             sums_ref[place : place + 8, :] = sum(value[8 * i : 8 * i + 8] for i in range(members // 8))
 
@@ -383,6 +394,67 @@
             from_left = jnp.where(digit != 0, rows[p], strips[p])
             picked.append(jnp.where(sub < STEPS if p < 2 else lane8 < half_lanes, from_right, from_left))
         strips = picked
+
+    place_ids = lax.broadcasted_iota(jnp.int32, (places, LANES), 0)
+    lane_ids = lax.broadcasted_iota(jnp.int32, (LANES, LANES), 0)
+    held = kept.shape[0] // 8
+    sources = [(kept, 8 * j) for j in range(held)]
+    for source, base in ((odd, 16), (swapped, 16), (even, 16)):
+        sources += [(source, base + 8 * j) for j in range(held)]
+    hits = []
+    for n, (source, at) in enumerate(sources):
+        local = source[at : at + 1, :].astype(jnp.int32)
+        hit = place_ids == lax.shift_right_arithmetic(local, 7)
+        hits.append(hit)
+        onehot = (lane_ids == jnp.bitwise_and(local, LANES - 1)).astype(jnp.float32)
+        lanes = slice(n * LANES, (n + 1) * LANES)
+        onehot_ref[:, lanes] = onehot.astype(jnp.bfloat16)
+        weight, pull = source[at + 1 : at + 2, :], source[at + 2 : at + 3, :]
+        stack = [jnp.where(hit, piece, 0.0) for piece in pieces_of(weight) + pieces_of(pull)]
+        spread_ref[:, lanes] = jnp.concatenate(stack, axis=0).astype(jnp.bfloat16)
+    placed = lax.dot_general(
+        spread_ref[...], onehot_ref[...], (((1,), (1,)), ((), ())), preferred_element_type=jnp.float32
+    )
+    placed = [placed[p * places : (p + 1) * places] for p in range(6)]
+    weight = placed[0] + placed[1] + placed[2]
+    pull = placed[3] + placed[4] + placed[5]
+
+    root = jnp.sqrt(weight)
+    scale = jnp.where(weight > 0.0, lax.rsqrt(jnp.where(weight > 0.0, weight, 1.0)), 0.0)
+    sub16 = lax.broadcasted_iota(jnp.int32, (16, LANES), 0)
+    depth = total + 16
+    means = {}
+
+    def put(row, lanes, value):
+        for p, piece in enumerate(halves_of(value)):
+            split_ref[pl.ds(row + p * depth, value.shape[0]), lanes] = piece
+
+    def put_tile(at, sums, halves, into):
+        means[at] = jnp.sum(sums, axis=0, keepdims=True) * (1.0 / total)
+        lanes = slice(into * LANES, (into + 1) * LANES)
+        for half, value in enumerate(halves):
+            side = core if half == 0 else 1 - core
+            anomaly = (value - means[at]) * root[at : at + 1]
+            put(pl.multiple_of(side * members, 16), lanes, anomaly)
+        drawn = (pull[at : at + 1] - weight[at : at + 1] * means[at]) * scale[at : at + 1]
+        put(total, lanes, jnp.where(sub16 == 0, drawn, 0.0))
+
+    def product_of(first, last):
+        lanes = slice(first * LANES, last * LANES)
+        return lax.dot_general(
+            split_ref[:, lanes], split_ref[:, lanes], (((1,), (1,)), ((), ())), preferred_element_type=jnp.float32
+        )
+
+    inner = tiles - 2
+    products = []
+    for f in range(fields):
+        rows = slice(f * members, (f + 1) * members)
+        for t in range(1, tiles - 1):
+            at = f * tiles + t
+            lanes = slice(t * LANES, (t + 1) * LANES)
+            sums = own_sums[8 * at : 8 * at + 8, :] + other_sums[8 * at : 8 * at + 8, :]
+            put_tile(at, sums, [state[rows, lanes] for state in states], f * inner + t - 1)
+        products.append(product_of(f * inner, (f + 1) * inner))
 
     right_first = half_lanes + 3 * STEPS
     strip_rows = fields * members
@@ -444,76 +516,24 @@
                 edge_ref[half * strip_rows + at : half * strip_rows + at + 8, LANES:] = last_tile
                 first_sums[f] = first_sums[f] + first_tile
                 last_sums[f] = last_sums[f] + last_tile
-    means = []
+    edge_at = fields * inner
     for f in range(fields):
-        for t in range(tiles):
-            at = (f * tiles + t) * 8
-            if t == 0:
-                partial = first_sums[f]
-            elif t == tiles - 1:
-                partial = last_sums[f]
-            else:
-                partial = own_sums[at : at + 8, :] + other_sums[at : at + 8, :]
-            means.append(jnp.sum(partial, axis=0, keepdims=True))
-    mean = jnp.concatenate(means, axis=0) * (1.0 / total)
-
-    place_ids = lax.broadcasted_iota(jnp.int32, (places, LANES), 0)
-    lane_ids = lax.broadcasted_iota(jnp.int32, (LANES, LANES), 0)
-    held = kept.shape[0] // 8
-    sources = [(kept, 8 * j) for j in range(held)]
-    for source, base in ((odd, 16), (swapped, 16), (even, 16)):
-        sources += [(source, base + 8 * j) for j in range(held)]
-    hits = []
-    for n, (source, at) in enumerate(sources):
-        local = source[at : at + 1, :].astype(jnp.int32)
-        hit = place_ids == lax.shift_right_arithmetic(local, 7)
-        hits.append(hit)
-        onehot = (lane_ids == jnp.bitwise_and(local, LANES - 1)).astype(jnp.float32)
-        lanes = slice(n * LANES, (n + 1) * LANES)
-        onehot_ref[:, lanes] = onehot.astype(jnp.bfloat16)
-        weight, pull = source[at + 1 : at + 2, :], source[at + 2 : at + 3, :]
-        stack = [jnp.where(hit, piece, 0.0) for piece in pieces_of(weight) + pieces_of(pull)]
-        spread_ref[:, lanes] = jnp.concatenate(stack, axis=0).astype(jnp.bfloat16)
-    placed = lax.dot_general(
-        spread_ref[...], onehot_ref[...], (((1,), (1,)), ((), ())), preferred_element_type=jnp.float32
-    )
-    placed = [placed[p * places : (p + 1) * places] for p in range(6)]
-    weight = placed[0] + placed[1] + placed[2]
-    pull = placed[3] + placed[4] + placed[5] - weight * mean
-
-    root = jnp.sqrt(weight)
-    pull = jnp.where(weight > 0.0, pull * lax.rsqrt(jnp.where(weight > 0.0, weight, 1.0)), 0.0)
-    sub16 = lax.broadcasted_iota(jnp.int32, (16, LANES), 0)
-    depth = total + 16
-
-    def put(row, lanes, value):
-        for p, piece in enumerate(halves_of(value)):
-            split_ref[pl.ds(row + p * depth, value.shape[0]), lanes] = piece
-
-    for f in range(fields):
-        for t in range(tiles):
-            at = f * tiles + t
-            lanes = slice(t * LANES, (t + 1) * LANES)
-            into = slice(at * LANES, (at + 1) * LANES)
-            for half in range(2):
-                if t in (0, tiles - 1):
-                    column = slice(0, LANES) if t == 0 else slice(LANES, 2 * LANES)
-                    value = edge_ref[half * strip_rows + f * members : half * strip_rows + (f + 1) * members, column]
-                else:
-                    value = states[half][f * members : (f + 1) * members, lanes]
-                anomaly = (value - mean[at : at + 1]) * root[at : at + 1]
-                side = core if half == 0 else 1 - core
-                put(pl.multiple_of(side * members, 16), into, anomaly)
-            put(total, into, jnp.where(sub16 == 0, pull[at : at + 1], 0.0))
-    products = lax.dot_general(
-        split_ref[...], split_ref[...], (((1,), (1,)), ((), ())), preferred_element_type=jnp.float32
-    )
+        for n, (t, sums) in enumerate(((0, first_sums[f]), (tiles - 1, last_sums[f]))):
+            column = slice(n * LANES, (n + 1) * LANES)
+            halves = [
+                edge_ref[half * strip_rows + f * members : half * strip_rows + (f + 1) * members, column]
+                for half in range(2)
+            ]
+            put_tile(f * tiles + t, sums, halves, edge_at + 2 * f + n)
+    products.append(product_of(edge_at, edge_at + 2 * fields))
+    products = sum(products)
+    mean = jnp.concatenate([means[at] for at in range(places)], axis=0)
     gram = sum(
         products[p * depth : p * depth + total + 8, q * depth : q * depth + total]
         for p, q in ((1, 1), (1, 0), (0, 1), (0, 0))
     )
     gram = jnp.concatenate([gram, jnp.zeros((total + 8, LANES - total), jnp.float32)], axis=1)
-    folded = gram[:members] + pltpu.roll(gram[members:total], total, 1)
+    folded = pltpu.roll(gram[:members], total, 1) + gram[members:total]
     blank = jnp.zeros((stay_ref.shape[0] - members - 1, LANES), jnp.float32)
     for out in (stay_ref, odd_ref, even_ref):
         out[:members, :] = folded
@@ -542,47 +562,51 @@
     count = len(rows)
     rows = list(rows)
     sub = lax.broadcasted_iota(jnp.int32, (8, LANES), 0)
+
+    def columns_of(row, b):
+        first = 8 * (count + b)
+        return [jnp.broadcast_to(row[:, first + k : first + k + 1], (8, LANES)) for k in range(8)]
+
+    upcoming = columns_of(rows[0], 0)
     for b in range(count):
-        columns = [
-            [jnp.broadcast_to(rows[i][:, 8 * b + k : 8 * b + k + 1], (8, LANES)) for k in range(8)]
-            for i in range(b, count)
-        ]
+        own = upcoming
+        below = {i: columns_of(rows[i], b) for i in range(b + 1, count)}
+        if b + 1 < count:
+            upcoming = columns_of(rows[b + 1], b + 1)
         for j in range(8):
-            scale = lax.rsqrt(spread_row(columns[0][j][j : j + 1, :]))
+            scale = lax.rsqrt(spread_row(own[j][j : j + 1, :]))
             upper = spread_row(rows[b][j : j + 1, :]) * scale
-            lower = columns[0][j] * scale
-            factors = [spread_row(lower[k : k + 1, :]) for k in range(8)]
-            for i in range(b, count):
-                here = lower if i == b else columns[i - b][j] * scale
-                if i == b:
-                    rows[b] = jnp.where(sub == j, upper, rows[b] - jnp.where(sub > j, here, 0.0) * upper)
-                else:
-                    rows[i] = rows[i] - here * upper
+            lower = own[j] * scale
+            factors = {k: spread_row(lower[k : k + 1, :]) for k in range(j + 1, 8)}
+            for k in range(j + 1, 8):
+                own[k] = own[k] - lower * factors[k]
+            rows[b] = jnp.where(sub == j, upper, rows[b] - jnp.where(sub > j, lower, 0.0) * upper)
+            for i in range(b + 1, count):
+                here = below[i][j] * scale
+                if i == b + 1:
+                    for k in range(8):
+                        upcoming[k] = upcoming[k] - here * spread_row(here[k : k + 1, :])
                 for k in range(j + 1, 8):
-                    columns[i - b][k] = columns[i - b][k] - here * factors[k]
+                    below[i][k] = below[i][k] - here * factors[k]
+                rows[i] = rows[i] - here * upper
     return rows
 
 
 def analysis_kernel(
-    own_ref, other_ref, edge_ref, small_ref, slots_ref, kept, odd, swapped, even,
-    analysis_ref, innovation_ref, mixing_ref, center_ref, pieces_ref, *, units, obs_rows, count,
+    split_ref, edge_ref, small_ref, slots_ref, kept, odd, swapped, even,
+    analysis_ref, innovation_ref, center_ref, pieces_ref, result_ref, sems, *, units, obs_rows, count,
 ):
     block, core = here()
     members, fields, cells = analysis_ref.shape
     total = 2 * members
     strip_rows = fields * members
     for f in range(fields):
-        for half, state in enumerate((own_ref, other_ref)):
-            rows = slice(f * members, (f + 1) * members)
-            edges = slice(half * strip_rows + f * members, half * strip_rows + (f + 1) * members)
-            for lanes, value in (
-                (slice(0, LANES), edge_ref[edges, :LANES]),
-                (slice(LANES, cells - LANES), state[rows, LANES : cells - LANES]),
-                (slice(cells - LANES, cells), edge_ref[edges, LANES:]),
-            ):
-                for p, piece in enumerate(halves_of(value)):
-                    at = (f * 2 + p) * total + half * members
-                    pieces_ref[at : at + members, lanes] = piece
+        for half in range(2):
+            rows = slice(half * strip_rows + f * members, half * strip_rows + (f + 1) * members)
+            side = core if half == 0 else 1 - core
+            for p, piece in enumerate(halves_of(edge_ref[rows, :])):
+                at = pl.multiple_of((f * 2 + p) * total + side * members, 16)
+                pieces_ref[pl.ds(at, members), :] = piece
     head = members + 1
     sums = (kept[:head, :] + even[:head, :]) + (odd[:head, :] + swapped[:head, :])
     returned = kept.shape[0] - head
@@ -592,17 +616,17 @@
     center_ref[3 * returned :, :] = jnp.where(core == 0, swapped[head:, :], odd[head:, :])
     lane = lax.broadcasted_iota(jnp.int32, (8, LANES), 1)
     sub = lax.broadcasted_iota(jnp.int32, (8, LANES), 0)
-    shifted = pltpu.roll(sums[:members], LANES - total, 1)
+    shifted = pltpu.roll(sums[:members], total, 1)
     rows = []
     for b in range(total // 8):
         at = 8 * b
         source = sums[at : at + 8] if at < members else shifted[at - members : at - members + 8]
-        own = jnp.where(lane == sub + at, total - 1.0, 0.0)
-        unit = jnp.where(lane == sub + at + total, 1.0, 0.0)
-        rows.append(jnp.where(lane < total, source + own, unit))
+        own = jnp.where(lane == sub + at + total, total - 1.0, 0.0)
+        unit = jnp.where(lane == sub + at, 1.0, 0.0)
+        rows.append(jnp.where(lane >= total, source + own, unit))
     rows = eliminate(rows)
     cross = sums[members : members + 1]
-    inverse = [jnp.where(lane < total, pltpu.roll(r, LANES - total, 1), 0.0) for r in rows]
+    inverse = [jnp.where(lane < total, r, 0.0) for r in rows]
     carried = [jnp.sum(r * cross, axis=1, keepdims=True) for r in inverse]
     row_sums = [jnp.sum(r, axis=1, keepdims=True) for r in inverse]
     row_means = [r * (1.0 / total) for r in row_sums]
@@ -612,21 +636,35 @@
     weights = weights - jnp.sum(sum(r * c for r, c in zip(row_means, carried)), axis=0, keepdims=True)
     root = math.sqrt(total - 1.0)
     add = weights + 1.0 / total - root * (column_mean - grand)
-    for b in range(total // 8):
-        mixing_ref[8 * b : 8 * b + 8, :] = root * (inverse[b] - row_means[b]) + add
-    own_rows = mixing_ref[pl.ds(pl.multiple_of(core * members, 8), members), :]
-    rolled = pltpu.roll(own_rows, LANES - members, 1)
-    to_own = jnp.where(core == 0, own_rows, rolled)[:, :members]
-    to_other = jnp.where(core == 0, rolled, own_rows)[:, :members]
-    high, rest = halves_of(jnp.concatenate([to_own, to_other], axis=1))
+    count_here = members // 8
+    mixing = [
+        root * jnp.where(core == 0, inverse[b] - row_means[b], inverse[b + count_here] - row_means[b + count_here]) + add
+        for b in range(count_here)
+    ]
+    high, rest = halves_of(jnp.concatenate(mixing, axis=0)[:, :total])
     mixing = jnp.concatenate(
         [jnp.concatenate([high, high], axis=1), jnp.concatenate([rest, rest], axis=1)], axis=0
     )
-    for f in range(fields):
-        product = jnp.dot(
-            mixing, pieces_ref[f * 2 * total : (f + 1) * 2 * total, :], preferred_element_type=jnp.float32
+    copies = []
+    width = cells // 2
+    for n in range(2):
+        lanes = slice(n * width, (n + 1) * width)
+        for f in range(fields):
+            rows = slice(f * 2 * total, (f + 1) * 2 * total)
+            if n == 0:
+                states = [pieces_ref[rows, :LANES], split_ref[rows, LANES:width]]
+            else:
+                states = [split_ref[rows, width : cells - LANES], pieces_ref[rows, LANES:]]
+            product = jnp.dot(mixing, jnp.concatenate(states, axis=1), preferred_element_type=jnp.float32)
+            result_ref[:, f, lanes] = product[:members] + product[members:]
+        copies.append(
+            pltpu.make_async_copy(
+                result_ref.at[:, :, pl.ds(n * width, width)],
+                analysis_ref.at[:, :, pl.ds(n * width, width)],
+                sems.at[n],
+            )
         )
-        analysis_ref[:, f, :] = product[:members] + product[members:]
+        copies[-1].start()
 
     held = count // 4
     lane_group = lane // CAP
@@ -658,6 +696,8 @@
         at = small_ref.shape[0] - 2 * obs_rows + r
         value, sigma = small_ref[at : at + 1, :], small_ref[at + obs_rows : at + obs_rows + 1, :]
         innovation_ref[r : r + 1, :] = (value - center) / sigma
+    for copy in copies:
+        copy.wait()
 
 
 def shards(
@@ -720,16 +760,18 @@
     powers = jax.ShapeDtypeStruct((fields * fields, LANES), real)
     slots = jax.ShapeDtypeStruct((2 * obs_rows, LANES), jnp.int32)
 
-    def forecast(mixed, half, source, extra):
+    pieces = jax.ShapeDtypeStruct((fields * 2 * total, cells), jnp.bfloat16)
+
+    def forecast(operands, extra, own):
         return pl.pallas_call(
-            functools.partial(forecast_kernel, fields=fields),
+            functools.partial(forecast_kernel, fields=fields, own=own),
             out_shape=(
                 jax.ShapeDtypeStruct((strip_rows, cells), real),
                 jax.ShapeDtypeStruct((strip_rows, LANES), real),
                 jax.ShapeDtypeStruct((places * 8, LANES), real),
             )
             + extra,
-            in_specs=[whole] * 4,
+            in_specs=[whole] * len(operands),
             out_specs=(whole,) * (3 + len(extra)),
             scratch_shapes=[pltpu.VMEM((2 * strip_rows, cells), jnp.bfloat16), pltpu.VMEM((strip_rows, cells), real)],
             compiler_params=params,
@@ -737,9 +779,9 @@
                 flops=80 * strip_rows * cells, bytes_accessed=8 * strip_rows * cells, transcendentals=0
             ),
             name="forecast",
-        )(mixed, half, source, send_count)
-
-    *own_forecast, rule, mixed = forecast(couple, ensemble, small, (band, powers))
+        )(*operands)
+
+    *own_forecast, rule, mixed = forecast((couple, ensemble, small), (band, powers), True)
     carried = []
     for n, unit in enumerate(units):
         arrived = exchange(to_odd, to_even, owners, unit)
@@ -753,7 +795,9 @@
                 name="regroup",
             )(kept, *arrived, own_forecast[2])
             carried.append(to_odd)
-    *other_forecast, slots_of = forecast(mixed, other, rule, (slots,))
+    *other_forecast, slots_of, split = forecast(
+        (mixed, other, rule, send_count, own_forecast[0]), (slots, pieces), False
+    )
 
     held = kept.shape[0] // 8
     sums_rows = -(-(members + 1 + 4 * held) // 8) * 8
@@ -797,17 +841,18 @@
             jax.ShapeDtypeStruct((members, fields, cells), real),
             jax.ShapeDtypeStruct((obs_rows, LANES), real),
         ),
-        in_specs=[whole] * 9,
-        out_specs=(whole, whole),
+        in_specs=[whole] * 8,
+        out_specs=(pl.BlockSpec(memory_space=pl.ANY), whole),
         scratch_shapes=[
-            pltpu.VMEM((total, LANES), real),
             pltpu.VMEM((4 * (stay.shape[0] - head), LANES), real),
-            pltpu.VMEM((fields * 2 * total, cells), jnp.bfloat16),
+            pltpu.VMEM((fields * 2 * total, 2 * LANES), jnp.bfloat16),
+            pltpu.VMEM((members, fields, cells), real),
+            pltpu.SemaphoreType.DMA((2,)),
         ],
         compiler_params=params,
         name="analysis",
     )(
-        own_forecast[0], other_forecast[0], edges, small, slots_of,
+        split, edges, small, slots_of,
         stay, odd, swapped, even,
     )
     return (analysis, innovation.reshape(obs))

time: 33.1 us -> 32.6 us (0.985)
  transfers between devices with their start and end apart: 13 -> 13, of which waited for: 6 -> 6; matrix products, arithmetic and copies ran while one was open for 0% -> 0% of each run, Pallas kernels for 7% -> 8%
where the time goes in v5:
time: 32.6 us; the launch traced here: 32.5 us
  starting transfers between devices  18 us (55%)
  Pallas kernels  7.39 us (23%)
  waiting for transfers between devices  4.52 us (14%)
  local copies, waits for them, and re-layouts  1.81 us (6%)
  between operations  0.75 us (2%)
    ppermute x4, starting transfers between devices, exchange(): lax.ppermute(to_even, BOTH, core_pairs(owners, lambda block, core: (block...  8.79 us
    ppermute x4, starting transfers between devices, exchange(): lax.ppermute(to_odd, BOTH, core_pairs(owners, lambda block, core: (block...  6.06 us
    ppermute x5, starting transfers between devices, swap_cores(): lax.ppermute(x, BOTH, core_pairs(owners, lambda block, core: (block, 1 -...  3.13 us
    pallas_call x1, Pallas kernels, shards(): pl.pallas_call(functools.partial(analysis_kernel, units=units, obs_rows=o...  2.91 us
    pallas_call x2, Pallas kernels, forecast(): pl.pallas_call(functools.partial(forecast_kernel, fields=fields, own=own)...  2.3 us
    ppermute x4, waiting for transfers between devices, exchange(): lax.ppermute(to_even, BOTH, core_pairs(owners, lambda block, core: (block...  2.27 us
    unnamed x20, local copies, waits for them, and re-layouts  1.81 us
    pallas_call x1, Pallas kernels, shards(): pl.pallas_call(functools.partial(sums_kernel, owners=owners, units=units,...  1.61 us
  transfers between devices with their start and end apart: 13, of which 6 were waited for; matrix products, arithmetic and copies ran while one was open for 0% of the time, Pallas kernels for 8%

profile of v5, /device:TPU:0, one launch (start us, length us, event | category | flops | bytes accessed | tf_op | source)
XLA Modules:
  0.0 32.5 jit_solution(12165129947320957109)
XLA Ops:
  0.6 0.5 %collective-permute-start = (f32[32,4,1024]{2,1,0:T(4,128)}, f32[32,4,1024]{2,1,0:T(4,128)S(1)}, u32[]{:S(2)}, u32[]{:S(2)}) collective-permute-start(f32[32,4,1024]{2,1,0:T(4,128)} %ensemble_ref.1), channel_id=1, source_target_pairs={{0,1},{1,0},{2,3},{3,2},{4,5},{5,4},{6,7},{7,6},{8,9},{9,8},{10,11... | collective-permute-start | bytes 1572872 | tf_op jit(solution)/shard_map/ppermute | solution.py:42
  1.2 1.0 %copy-done = f32[32,4,1024]{2,1,0:T(4,128)S(1)} copy-done((f32[32,4,1024]{2,1,0:T(4,128)S(1)}, f32[32,4,1024]{2,1,0:T(4,128)}, u32[]{:S(2)}) %copy-start) | copy-done | bytes 524312
  2.4 0.5 %copy-done.6 = s32[256]{0:T(256)S(1)} copy-done((s32[256]{0:T(256)S(1)}, s32[256]{0:T(256)}, u32[]{:S(2)}) %copy-start.6) | copy-done | bytes 1048
  2.9 0.2 copy-done.3
  3.1 0.2 pack.1
  3.5 2.6 %collective-permute-start.1 = (f32[24,128]{1,0:T(8,128)S(1)}, f32[24,128]{1,0:T(8,128)S(1)}, u32[]{:S(2)}, u32[]{:S(2)}) collective-permute-start(f32[24,128]{1,0:T(8,128)S(1)} %get-tuple-element.40), channel_id=1, source_target_pairs={{0,2},{1,7},{2,0},{3,5},{4,6},{5,3},{6,4},{7,1},{8,10},{9,15},{10,... | collective-permute-start | bytes 36872 | tf_op jit(solution)/shard_map/ppermute | solution.py:46
  6.1 1.5 %collective-permute-start.3 = (f32[24,128]{1,0:T(8,128)S(1)}, f32[24,128]{1,0:T(8,128)S(1)}, u32[]{:S(2)}, u32[]{:S(2)}) collective-permute-start(f32[24,128]{1,0:T(8,128)S(1)} %get-tuple-element.41), channel_id=1, source_target_pairs={{0,4},{1,5},{2,6},{3,7},{4,0},{5,1},{6,2},{7,3},{8,12},{9,13},{10,... | collective-permute-start | bytes 36872 | tf_op jit(solution)/shard_map/ppermute | solution.py:49
  7.7 0.6 %collective-permute-start.2 = (f32[24,128]{1,0:T(8,128)S(1)}, f32[24,128]{1,0:T(8,128)S(1)}, u32[]{:S(2)}, u32[]{:S(2)}) collective-permute-start(f32[24,128]{1,0:T(8,128)S(1)} %collective-permute-done.1.odd), channel_id=1, source_target_pairs={{0,1},{1,0},{2,3},{3,2},{4,5},{5,4},{6,7},{7,6},{8,9},{9,8},{10,11... | collective-permute-start | bytes 36872 | tf_op jit(solution)/shard_map/ppermute | solution.py:42
  8.3 1.5 %forecast.2 = (f32[128,1024]{1,0:T(8,128)S(1)}, f32[128,128]{1,0:T(8,128)S(1)}, f32[256,128]{1,0:T(8,128)S(1)}, bf16[2048,256]{1,0:T(8,128)(2,1)S(1)}, f32[16,128]{1,0:T(8,128)S(1)}) custom-call(f32[4,4]{1,0:T(4,128)S(1)} %copy-done.4, f32[32,4,1024]{2,1,0:T(4,128)S(1)} %copy-done.1, f32[20,128]{1,0:T(8,128)S(1)} %get-tuple-element.27.from_ref.small_ref), custom_call_target="tpu_custom_call" | custom-call | flops 10485760 | bytes 1048576 | tf_op jit(solution)/shard_map/forecast/pallas_call | solution.py:766
  9.9 1.8 %collective-permute-start.4 = (f32[24,128]{1,0:T(8,128)S(1)}, f32[24,128]{1,0:T(8,128)S(1)}, u32[]{:S(2)}, u32[]{:S(2)}) collective-permute-start(f32[24,128]{1,0:T(8,128)S(1)} %get-tuple-element.43.refs_0_), channel_id=1, source_target_pairs={{0,8},{1,25},{2,10},{3,27},{4,12},{5,29},{6,14},{7,31},{8,0},{9,17... | collective-permute-start | bytes 36872 | tf_op jit(solution)/shard_map/ppermute | solution.py:46
  11.8 2.6 %collective-permute-start.6 = (f32[24,128]{1,0:T(8,128)S(1)}, f32[24,128]{1,0:T(8,128)S(1)}, u32[]{:S(2)}, u32[]{:S(2)}) collective-permute-start(f32[24,128]{1,0:T(8,128)S(1)} %get-tuple-element.44), channel_id=1, source_target_pairs={{0,16},{1,17},{2,18},{3,19},{4,20},{5,21},{6,22},{7,23},{8,24},{9,... | collective-permute-start | bytes 36872 | tf_op jit(solution)/shard_map/ppermute | solution.py:49
  14.4 0.5 %collective-permute-start.5 = (f32[24,128]{1,0:T(8,128)S(1)}, f32[24,128]{1,0:T(8,128)S(1)}, u32[]{:S(2)}, u32[]{:S(2)}) collective-permute-start(f32[24,128]{1,0:T(8,128)S(1)} %collective-permute-done.4.odd), channel_id=1, source_target_pairs={{0,1},{1,0},{2,3},{3,2},{4,5},{5,4},{6,7},{7,6},{8,9},{9,8},{10,11... | collective-permute-start | bytes 36872 | tf_op jit(solution)/shard_map/ppermute | solution.py:42
  14.9 0.8 %forecast.3 = (f32[128,1024]{1,0:T(8,128)S(1)}, f32[128,128]{1,0:T(8,128)S(1)}, f32[256,128]{1,0:T(8,128)S(1)}, s32[4,128]{1,0:T(4,128)S(1)}, bf16[512,1024]{1,0:T(8,128)(2,1)S(1)}) custom-call(f32[16,128]{1,0:T(8,128)S(1)} %get-tuple-element.28.extra_ref.powers_ref, f32[32,4,1024]{2,1,0:T(4,128)S(1)} %collective-permute-done.source.other_ref, ...), custom_call_target="tpu_custom_call" | custom-call | flops 10485760 | bytes 1048576 | tf_op jit(solution)/shard_map/forecast/pallas_call | solution.py:766
  15.7 0.8 %collective-permute-done.6.even = f32[24,128]{1,0:T(8,128)S(1)} collective-permute-done((f32[24,128]{1,0:T(8,128)S(1)}, f32[24,128]{1,0:T(8,128)S(1)}, u32[]{:S(2)}, u32[]{:S(2)}) %collective-permute-start.6) | collective-permute-done | bytes 12320 | tf_op jit(solution)/shard_map/ppermute | solution.py:49
  16.5 1.6 %sums.1 = (f32[40,128]{1,0:T(8,128)S(1)}, f32[40,128]{1,0:T(8,128)S(1)}, f32[40,128]{1,0:T(8,128)S(1)}, f32[256,256]{1,0:T(8,128)S(1)}) custom-call(f32[16,128]{1,0:T(8,128)S(1)} %get-tuple-element.28.extra_ref.powers_ref, f32[20,128]{1,0:T(8,128)S(1)} %get-tuple-element.27.from_ref.small_ref, f32[128,1024]{1,0:T(8,128)S(1)} %get-tuple-element.30.refs_1_.own_state, ...), custom_call_target="tpu_custom_call" | custom-call | tf_op jit(solution)/shard_map/sums/pallas_call | solution.py:806
  18.3 3.2 %collective-permute-start.7 = (f32[40,128]{1,0:T(8,128)S(1)}, f32[40,128]{1,0:T(8,128)S(1)}, u32[]{:S(2)}, u32[]{:S(2)}) collective-permute-start(f32[40,128]{1,0:T(8,128)S(1)} %get-tuple-element.48), channel_id=1, source_target_pairs={{0,16},{1,17},{2,18},{3,19},{4,20},{5,21},{6,22},{7,23},{8,24},{9,... | collective-permute-start | bytes 61448 | tf_op jit(solution)/shard_map/ppermute | solution.py:49
  21.5 0.5 %collective-permute-done.8 = f32[40,128]{1,0:T(8,128)S(1)} collective-permute-done((f32[40,128]{1,0:T(8,128)S(1)}, f32[40,128]{1,0:T(8,128)S(1)}, u32[]{:S(2)}, u32[]{:S(2)}) %collective-permute-start.8) | collective-permute-done | bytes 20512 | tf_op jit(solution)/shard_map/ppermute | solution.py:46
  21.9 1.4 %collective-permute-start.9 = (f32[40,128]{1,0:T(8,128)S(1)}, f32[40,128]{1,0:T(8,128)S(1)}, u32[]{:S(2)}, u32[]{:S(2)}) collective-permute-start(f32[40,128]{1,0:T(8,128)S(1)} %collective-permute-done.8), channel_id=1, source_target_pairs={{0,1},{1,0},{2,3},{3,2},{4,5},{5,4},{6,7},{7,6},{8,9},{9,8},{10,11... | collective-permute-start | bytes 61448 | tf_op jit(solution)/shard_map/ppermute | solution.py:42
  23.3 0.8 %collective-permute-done.9 = f32[40,128]{1,0:T(8,128)S(1)} collective-permute-done((f32[40,128]{1,0:T(8,128)S(1)}, f32[40,128]{1,0:T(8,128)S(1)}, u32[]{:S(2)}, u32[]{:S(2)}) %collective-permute-start.9) | collective-permute-done | bytes 20512 | tf_op jit(solution)/shard_map/ppermute | solution.py:42
  24.2 1.5 %collective-permute-start.10 = (f32[40,128]{1,0:T(8,128)S(1)}, f32[40,128]{1,0:T(8,128)S(1)}, u32[]{:S(2)}, u32[]{:S(2)}) collective-permute-start(f32[40,128]{1,0:T(8,128)S(1)} %add_add_fusion.kept), channel_id=1, source_target_pairs={{0,2},{1,7},{2,0},{3,5},{4,6},{5,3},{6,4},{7,1},{8,10},{9,15},{10,... | collective-permute-start | bytes 61448 | tf_op jit(solution)/shard_map/ppermute | solution.py:46
  25.7 1.5 %collective-permute-start.12 = (f32[40,128]{1,0:T(8,128)S(1)}, f32[40,128]{1,0:T(8,128)S(1)}, u32[]{:S(2)}, u32[]{:S(2)}) collective-permute-start(f32[40,128]{1,0:T(8,128)S(1)} %add_add_fusion.kept), channel_id=1, source_target_pairs={{0,4},{1,5},{2,6},{3,7},{4,0},{5,1},{6,2},{7,3},{8,12},{9,13},{10,... | collective-permute-start | bytes 61448 | tf_op jit(solution)/shard_map/ppermute | solution.py:49
  27.2 0.8 %collective-permute-done.10.odd = f32[40,128]{1,0:T(8,128)S(1)} collective-permute-done((f32[40,128]{1,0:T(8,128)S(1)}, f32[40,128]{1,0:T(8,128)S(1)}, u32[]{:S(2)}, u32[]{:S(2)}) %collective-permute-start.10) | collective-permute-done | bytes 20512 | tf_op jit(solution)/shard_map/ppermute | solution.py:46
  28.1 1.4 %collective-permute-done.12.even = f32[40,128]{1,0:T(8,128)S(1)} collective-permute-done((f32[40,128]{1,0:T(8,128)S(1)}, f32[40,128]{1,0:T(8,128)S(1)}, u32[]{:S(2)}, u32[]{:S(2)}) %collective-permute-start.12) | collective-permute-done | bytes 20512 | tf_op jit(solution)/shard_map/ppermute | solution.py:49
  29.5 2.9 %analysis.1 = (f32[32,4,1024]{2,1,0:T(4,128)}, f32[2,128]{1,0:T(2,128)}) custom-call(bf16[512,1024]{1,0:T(8,128)(2,1)S(1)} %get-tuple-element.31.split_ref, f32[256,256]{1,0:T(8,128)S(1)} %get-tuple-element.45.edge_ref, f32[20,128]{1,0:T(8,128)S(1)} %get-tuple-element.27.from_ref.small_ref, s32[4,128]{1,0:T(4,128)S(1)} %get-tuple-element.46.slots_ref, ...), custom_call_target="tpu_custom_call" | custom-call | tf_op jit(solution)/shard_map/analysis/pallas_call | solution.py:838
  (31 shorter events, 1.0 us)
Async XLA Ops:
  0.6 2.7 %collective-permute-start = (f32[32,4,1024]{2,1,0:T(4,128)}, f32[32,4,1024]{2,1,0:T(4,128)S(1)}, u32[]{:S(2)}, u32[]{:S(2)}) collective-permute-start(f32[32,4,1024]{2,1,0:T(4,128)} %ensemble_ref.1), channel_id=1, source_target_pairs={{0,1},{1,0},{2,3},{3,2},{4,5},{5,4},{6,7},{7,6},{8,9},{9,8},{10,11... | collective-permute-start | bytes 1572872 | tf_op jit(solution)/shard_map/ppermute | solution.py:42
  1.1 1.0 %copy-start = (f32[32,4,1024]{2,1,0:T(4,128)S(1)}, f32[32,4,1024]{2,1,0:T(4,128)}, u32[]{:S(2)}) copy-start(f32[32,4,1024]{2,1,0:T(4,128)} %ensemble_ref.1) | copy-start | bytes 1572868
  2.2 0.7 %copy-start.6 = (s32[256]{0:T(256)S(1)}, s32[256]{0:T(256)}, u32[]{:S(2)}) copy-start(s32[256]{0:T(256)} %param.13) | copy-start | bytes 3076
  2.2 0.7 %copy-start.7 = (s32[256]{0:T(256)S(1)}, s32[256]{0:T(256)}, u32[]{:S(2)}) copy-start(s32[256]{0:T(256)} %param.14) | copy-start | bytes 3076
  2.2 0.7 %copy-start.8 = (f32[256]{0:T(256)S(1)}, f32[256]{0:T(256)}, u32[]{:S(2)}) copy-start(f32[256]{0:T(256)} %param.15) | copy-start | bytes 3076
  2.2 0.7 %copy-start.9 = (f32[256]{0:T(256)S(1)}, f32[256]{0:T(256)}, u32[]{:S(2)}) copy-start(f32[256]{0:T(256)} %param.16) | copy-start | bytes 3076
  2.2 6.1 %copy-start.1 = (f32[32,4,1024]{2,1,0:T(4,128)S(1)}, f32[32,4,1024]{2,1,0:T(4,128)}, u32[]{:S(2)}) copy-start(f32[32,4,1024]{2,1,0:T(4,128)} %ensemble_ref.1) | copy-start | bytes 1572868
  2.3 0.8 %copy-start.3 = (s32[1024]{0:T(1024)S(1)}, s32[1024]{0:T(1024)}, u32[]{:S(2)}) copy-start(s32[1024]{0:T(1024)} %param.11) | copy-start | bytes 12292
  2.4 0.8 %copy-start.2 = (f32[1024]{0:T(1024)S(1)}, f32[1024]{0:T(1024)}, u32[]{:S(2)}) copy-start(f32[1024]{0:T(1024)} %param.10) | copy-start | bytes 12292
  2.4 0.7 %copy-start.5 = (s32[1,16]{1,0:T(1,128)S(1)}, s32[1,16]{1,0:T(1,128)}, u32[]{:S(2)}) copy-start(s32[1,16]{1,0:T(1,128)} %refs_0_.1) | copy-start | bytes 196
  3.5 4.8 %copy-start.4 = (f32[4,4]{1,0:T(4,128)S(1)}, f32[4,4]{1,0:T(4,128)}, u32[]{:S(2)}) copy-start(f32[4,4]{1,0:T(4,128)} %extra_ref.1) | copy-start | bytes 196
  3.5 4.2 %collective-permute-start.1 = (f32[24,128]{1,0:T(8,128)S(1)}, f32[24,128]{1,0:T(8,128)S(1)}, u32[]{:S(2)}, u32[]{:S(2)}) collective-permute-start(f32[24,128]{1,0:T(8,128)S(1)} %get-tuple-element.40), channel_id=1, source_target_pairs={{0,2},{1,7},{2,0},{3,5},{4,6},{5,3},{6,4},{7,1},{8,10},{9,15},{10,... | collective-permute-start | bytes 36872 | tf_op jit(solution)/shard_map/ppermute | solution.py:46
  6.1 3.8 %collective-permute-start.3 = (f32[24,128]{1,0:T(8,128)S(1)}, f32[24,128]{1,0:T(8,128)S(1)}, u32[]{:S(2)}, u32[]{:S(2)}) collective-permute-start(f32[24,128]{1,0:T(8,128)S(1)} %get-tuple-element.41), channel_id=1, source_target_pairs={{0,4},{1,5},{2,6},{3,7},{4,0},{5,1},{6,2},{7,3},{8,12},{9,13},{10,... | collective-permute-start | bytes 36872 | tf_op jit(solution)/shard_map/ppermute | solution.py:49
  7.7 2.1 %collective-permute-start.2 = (f32[24,128]{1,0:T(8,128)S(1)}, f32[24,128]{1,0:T(8,128)S(1)}, u32[]{:S(2)}, u32[]{:S(2)}) collective-permute-start(f32[24,128]{1,0:T(8,128)S(1)} %collective-permute-done.1.odd), channel_id=1, source_target_pairs={{0,1},{1,0},{2,3},{3,2},{4,5},{5,4},{6,7},{7,6},{8,9},{9,8},{10,11... | collective-permute-start | bytes 36872 | tf_op jit(solution)/shard_map/ppermute | solution.py:42
  9.9 4.4 %collective-permute-start.4 = (f32[24,128]{1,0:T(8,128)S(1)}, f32[24,128]{1,0:T(8,128)S(1)}, u32[]{:S(2)}, u32[]{:S(2)}) collective-permute-start(f32[24,128]{1,0:T(8,128)S(1)} %get-tuple-element.43.refs_0_), channel_id=1, source_target_pairs={{0,8},{1,25},{2,10},{3,27},{4,12},{5,29},{6,14},{7,31},{8,0},{9,17... | collective-permute-start | bytes 36872 | tf_op jit(solution)/shard_map/ppermute | solution.py:46
  11.8 4.7 %collective-permute-start.6 = (f32[24,128]{1,0:T(8,128)S(1)}, f32[24,128]{1,0:T(8,128)S(1)}, u32[]{:S(2)}, u32[]{:S(2)}) collective-permute-start(f32[24,128]{1,0:T(8,128)S(1)} %get-tuple-element.44), channel_id=1, source_target_pairs={{0,16},{1,17},{2,18},{3,19},{4,20},{5,21},{6,22},{7,23},{8,24},{9,... | collective-permute-start | bytes 36872 | tf_op jit(solution)/shard_map/ppermute | solution.py:49
  14.4 2.1 %collective-permute-start.5 = (f32[24,128]{1,0:T(8,128)S(1)}, f32[24,128]{1,0:T(8,128)S(1)}, u32[]{:S(2)}, u32[]{:S(2)}) collective-permute-start(f32[24,128]{1,0:T(8,128)S(1)} %collective-permute-done.4.odd), channel_id=1, source_target_pairs={{0,1},{1,0},{2,3},{3,2},{4,5},{5,4},{6,7},{7,6},{8,9},{9,8},{10,11... | collective-permute-start | bytes 36872 | tf_op jit(solution)/shard_map/ppermute | solution.py:42
  18.1 3.8 %collective-permute-start.8 = (f32[40,128]{1,0:T(8,128)S(1)}, f32[40,128]{1,0:T(8,128)S(1)}, u32[]{:S(2)}, u32[]{:S(2)}) collective-permute-start(f32[40,128]{1,0:T(8,128)S(1)} %get-tuple-element.49), channel_id=1, source_target_pairs={{0,8},{1,25},{2,10},{3,27},{4,12},{5,29},{6,14},{7,31},{8,0},{9,17... | collective-permute-start | bytes 61448 | tf_op jit(solution)/shard_map/ppermute | solution.py:46
  18.3 5.0 %collective-permute-start.7 = (f32[40,128]{1,0:T(8,128)S(1)}, f32[40,128]{1,0:T(8,128)S(1)}, u32[]{:S(2)}, u32[]{:S(2)}) collective-permute-start(f32[40,128]{1,0:T(8,128)S(1)} %get-tuple-element.48), channel_id=1, source_target_pairs={{0,16},{1,17},{2,18},{3,19},{4,20},{5,21},{6,22},{7,23},{8,24},{9,... | collective-permute-start | bytes 61448 | tf_op jit(solution)/shard_map/ppermute | solution.py:49
  21.9 2.2 %collective-permute-start.9 = (f32[40,128]{1,0:T(8,128)S(1)}, f32[40,128]{1,0:T(8,128)S(1)}, u32[]{:S(2)}, u32[]{:S(2)}) collective-permute-start(f32[40,128]{1,0:T(8,128)S(1)} %collective-permute-done.8), channel_id=1, source_target_pairs={{0,1},{1,0},{2,3},{3,2},{4,5},{5,4},{6,7},{7,6},{8,9},{9,8},{10,11... | collective-permute-start | bytes 61448 | tf_op jit(solution)/shard_map/ppermute | solution.py:42
  24.2 3.8 %collective-permute-start.10 = (f32[40,128]{1,0:T(8,128)S(1)}, f32[40,128]{1,0:T(8,128)S(1)}, u32[]{:S(2)}, u32[]{:S(2)}) collective-permute-start(f32[40,128]{1,0:T(8,128)S(1)} %add_add_fusion.kept), channel_id=1, source_target_pairs={{0,2},{1,7},{2,0},{3,5},{4,6},{5,3},{6,4},{7,1},{8,10},{9,15},{10,... | collective-permute-start | bytes 61448 | tf_op jit(solution)/shard_map/ppermute | solution.py:46
  25.7 3.9 %collective-permute-start.12 = (f32[40,128]{1,0:T(8,128)S(1)}, f32[40,128]{1,0:T(8,128)S(1)}, u32[]{:S(2)}, u32[]{:S(2)}) collective-permute-start(f32[40,128]{1,0:T(8,128)S(1)} %add_add_fusion.kept), channel_id=1, source_target_pairs={{0,4},{1,5},{2,6},{3,7},{4,0},{5,1},{6,2},{7,3},{8,12},{9,13},{10,... | collective-permute-start | bytes 61448 | tf_op jit(solution)/shard_map/ppermute | solution.py:49
  27.9 1.6 %collective-permute-start.11 = (f32[40,128]{1,0:T(8,128)S(1)}, f32[40,128]{1,0:T(8,128)S(1)}, u32[]{:S(2)}, u32[]{:S(2)}) collective-permute-start(f32[40,128]{1,0:T(8,128)S(1)} %collective-permute-done.10.odd), channel_id=1, source_target_pairs={{0,1},{1,0},{2,3},{3,2},{4,5},{5,4},{6,7},{7,6},{8,9},{9,8},{10,11... | collective-permute-start | bytes 61448 | tf_op jit(solution)/shard_map/ppermute | solution.py:42

commit v6 on v5

--- a/solution.py
+++ b/solution.py
@@ -228,33 +228,36 @@
     return high, (x - high.astype(jnp.float32)).astype(jnp.bfloat16)
 
 
-def fill_band(small_ref, band_ref, cells):
+def band_maker(small_ref, band_ref, cells):
     tiles = cells // LANES
     speed = small_ref[:tiles, :]
     toward_left = speed * small_ref[tiles : 2 * tiles, :]
     toward_right = speed - toward_left
 
-    def row_of(x):
-        return jnp.concatenate([x[t : t + 1] for t in range(tiles)], axis=1)
-
-    step = {
-        -1: row_of(toward_left + DIFFUSION),
-        0: row_of(1.0 - 2.0 * DIFFUSION - speed),
-        1: row_of(toward_right + DIFFUSION),
-    }
+    lane = lax.broadcasted_iota(jnp.int32, (tiles, LANES), 1)
+
+    def shifted(x, by):
+        if by == 0:
+            return x
+        turned = pltpu.roll(x, 1 if by < 0 else LANES - 1, 1)
+        carried = pltpu.roll(turned, 1 if by < 0 else tiles - 1, 0)
+        return jnp.where(lane == (0 if by < 0 else LANES - 1), carried, turned)
+
+    step = {-1: toward_left + DIFFUSION, 0: 1.0 - 2.0 * DIFFUSION - speed, 1: toward_right + DIFFUSION}
     reach = dict(step)
     for _ in range(STEPS - 1):
         longer = {}
         for e in step:
             for d in reach:
-                term = step[e] * (pltpu.roll(reach[d], -e % cells, 1) if e else reach[d])
+                term = step[e] * shifted(reach[d], e)
                 longer[d + e] = longer[d + e] + term if d + e in longer else term
         reach = longer
     row = lax.broadcasted_iota(jnp.int32, (LANES, LANES), 0)
     column = lax.broadcasted_iota(jnp.int32, (LANES, LANES), 1)
     ahead = row - column
-    for t in range(tiles):
-        rule = {d: reach[d][:, t * LANES : (t + 1) * LANES] for d in reach}
+
+    def make(t):
+        rule = {d: reach[d][t : t + 1, :] for d in reach}
 
         def placed(distance, offsets):
             block = jnp.zeros(distance.shape, jnp.float32)
@@ -274,6 +277,8 @@
         for p, piece in enumerate(halves_of(block)):
             band_ref[2 * t * LANES : 2 * (t + 1) * LANES, p * LANES : (p + 1) * LANES] = piece
 
+    return make
+
 
 def fill_positions(send_ref, slots_ref):
     owners = send_ref.shape[1]
@@ -304,7 +309,7 @@
     if own:
         state, edge, sums_ref, band_ref, powers_ref, split_ref, raw_ref = refs
         fill_powers(extra_ref, powers_ref)
-        fill_band(from_ref, band_ref, cells)
+        make_band = band_maker(from_ref, band_ref, cells)
     else:
         send_ref, own_state, state, edge, sums_ref, slots_ref, pieces_ref, split_ref, raw_ref = refs
         powers_ref, band_ref = extra_ref, from_ref
@@ -336,6 +341,8 @@
         lanes, after, before = (
             slice(n % tiles * LANES, (n % tiles + 1) * LANES) for n in (t, t + 1, t - 1)
         )
+        if own:
+            make_band(t)
         around = jnp.where(nearer, split_ref[:, after], split_ref[:, before])
         product = jnp.dot(
             jnp.concatenate([split_ref[:, lanes], around], axis=1),
@@ -441,8 +448,9 @@
 
     def product_of(first, last):
         lanes = slice(first * LANES, last * LANES)
+        anomalies = jnp.concatenate([split_ref[:total, lanes], split_ref[depth : depth + total, lanes]], axis=0)
         return lax.dot_general(
-            split_ref[:, lanes], split_ref[:, lanes], (((1,), (1,)), ((), ())), preferred_element_type=jnp.float32
+            split_ref[:, lanes], anomalies, (((1,), (1,)), ((), ())), preferred_element_type=jnp.float32
         )
 
     inner = tiles - 2
@@ -492,8 +500,8 @@
     from_right = jnp.broadcast_to((edge_right + DIFFUSION) * inside, (8, LANES))
     stay = jnp.broadcast_to((1.0 - 2.0 * DIFFUSION - edge_left - edge_right) * inside, (8, LANES))
     mix = powers_of(powers_ref, fields)
-    first_sums = [jnp.zeros((8, LANES), jnp.float32) for _ in range(fields)]
-    last_sums = [jnp.zeros((8, LANES), jnp.float32) for _ in range(fields)]
+    first_sums = [[jnp.zeros((8, LANES), jnp.float32)] * fields for _ in range(2)]
+    last_sums = [[jnp.zeros((8, LANES), jnp.float32)] * fields for _ in range(2)]
     for half in range(2):
         state, edge = states[half], raw_edges[half]
         for i in range(members // 8):
@@ -514,26 +522,24 @@
                 )
                 edge_ref[half * strip_rows + at : half * strip_rows + at + 8, :LANES] = first_tile
                 edge_ref[half * strip_rows + at : half * strip_rows + at + 8, LANES:] = last_tile
-                first_sums[f] = first_sums[f] + first_tile
-                last_sums[f] = last_sums[f] + last_tile
+                first_sums[half][f] = first_sums[half][f] + first_tile
+                last_sums[half][f] = last_sums[half][f] + last_tile
     edge_at = fields * inner
     for f in range(fields):
-        for n, (t, sums) in enumerate(((0, first_sums[f]), (tiles - 1, last_sums[f]))):
+        for n, (t, sums) in enumerate(((0, first_sums), (tiles - 1, last_sums))):
             column = slice(n * LANES, (n + 1) * LANES)
             halves = [
                 edge_ref[half * strip_rows + f * members : half * strip_rows + (f + 1) * members, column]
                 for half in range(2)
             ]
-            put_tile(f * tiles + t, sums, halves, edge_at + 2 * f + n)
+            put_tile(f * tiles + t, sums[0][f] + sums[1][f], halves, edge_at + 2 * f + n)
     products.append(product_of(edge_at, edge_at + 2 * fields))
     products = sum(products)
     mean = jnp.concatenate([means[at] for at in range(places)], axis=0)
-    gram = sum(
-        products[p * depth : p * depth + total + 8, q * depth : q * depth + total]
-        for p, q in ((1, 1), (1, 0), (0, 1), (0, 0))
-    )
-    gram = jnp.concatenate([gram, jnp.zeros((total + 8, LANES - total), jnp.float32)], axis=1)
-    folded = pltpu.roll(gram[:members], total, 1) + gram[members:total]
+    gram = products[: total + 8] + products[depth : depth + total + 8]
+    gram = gram + pltpu.roll(gram, total, 1)
+    in_low = lax.broadcasted_iota(jnp.int32, (members, LANES), 1) < total
+    folded = jnp.where(in_low, gram[members:total], gram[:members])
     blank = jnp.zeros((stay_ref.shape[0] - members - 1, LANES), jnp.float32)
     for out in (stay_ref, odd_ref, even_ref):
         out[:members, :] = folded

time: 32.6 us -> 32.4 us (level)
  transfers between devices with their start and end apart: 13 -> 13, of which waited for: 6 -> 7; matrix products, arithmetic and copies ran while one was open for 0% -> 0% of each run, Pallas kernels for 8% -> 8%
where the time goes in v6:
time: 32.4 us; the launch traced here: 32.3 us
  starting transfers between devices  18 us (56%)
  Pallas kernels  7.14 us (22%)
  waiting for transfers between devices  4.6 us (14%)
  local copies, waits for them, and re-layouts  1.81 us (6%)
  between operations  0.74 us (2%)
    ppermute x4, starting transfers between devices, exchange(): lax.ppermute(to_even, BOTH, core_pairs(owners, lambda block, core: (block...  8.75 us
    ppermute x4, starting transfers between devices, exchange(): lax.ppermute(to_odd, BOTH, core_pairs(owners, lambda block, core: (block...  6.08 us
    ppermute x5, starting transfers between devices, swap_cores(): lax.ppermute(x, BOTH, core_pairs(owners, lambda block, core: (block, 1 -...  3.14 us
    pallas_call x1, Pallas kernels, shards(): pl.pallas_call(functools.partial(analysis_kernel, units=units, obs_rows=o...  2.91 us
    ppermute x4, waiting for transfers between devices, exchange(): lax.ppermute(to_even, BOTH, core_pairs(owners, lambda block, core: (block...  2.34 us
    pallas_call x2, Pallas kernels, forecast(): pl.pallas_call(functools.partial(forecast_kernel, fields=fields, own=own)...  2.14 us
    unnamed x20, local copies, waits for them, and re-layouts  1.81 us
    pallas_call x1, Pallas kernels, shards(): pl.pallas_call(functools.partial(sums_kernel, owners=owners, units=units,...  1.53 us
  transfers between devices with their start and end apart: 13, of which 7 were waited for; matrix products, arithmetic and copies ran while one was open for 0% of the time, Pallas kernels for 8%

profile of v6, /device:TPU:0, one launch (start us, length us, event | category | flops | bytes accessed | tf_op | source)
XLA Modules:
  0.0 32.3 jit_solution(11118881486699407532)
XLA Ops:
  0.6 0.5 %collective-permute-start = (f32[32,4,1024]{2,1,0:T(4,128)}, f32[32,4,1024]{2,1,0:T(4,128)S(1)}, u32[]{:S(2)}, u32[]{:S(2)}) collective-permute-start(f32[32,4,1024]{2,1,0:T(4,128)} %ensemble_ref.1), channel_id=1, source_target_pairs={{0,1},{1,0},{2,3},{3,2},{4,5},{5,4},{6,7},{7,6},{8,9},{9,8},{10,11... | collective-permute-start | bytes 1572872 | tf_op jit(solution)/shard_map/ppermute | solution.py:42
  1.2 1.0 %copy-done = f32[32,4,1024]{2,1,0:T(4,128)S(1)} copy-done((f32[32,4,1024]{2,1,0:T(4,128)S(1)}, f32[32,4,1024]{2,1,0:T(4,128)}, u32[]{:S(2)}) %copy-start) | copy-done | bytes 524312
  2.4 0.5 %copy-done.6 = s32[256]{0:T(256)S(1)} copy-done((s32[256]{0:T(256)S(1)}, s32[256]{0:T(256)}, u32[]{:S(2)}) %copy-start.6) | copy-done | bytes 1048
  3.1 0.2 pack.1
  3.5 2.6 %collective-permute-start.1 = (f32[24,128]{1,0:T(8,128)S(1)}, f32[24,128]{1,0:T(8,128)S(1)}, u32[]{:S(2)}, u32[]{:S(2)}) collective-permute-start(f32[24,128]{1,0:T(8,128)S(1)} %get-tuple-element.40), channel_id=1, source_target_pairs={{0,2},{1,7},{2,0},{3,5},{4,6},{5,3},{6,4},{7,1},{8,10},{9,15},{10,... | collective-permute-start | bytes 36872 | tf_op jit(solution)/shard_map/ppermute | solution.py:46
  6.1 1.5 %collective-permute-start.3 = (f32[24,128]{1,0:T(8,128)S(1)}, f32[24,128]{1,0:T(8,128)S(1)}, u32[]{:S(2)}, u32[]{:S(2)}) collective-permute-start(f32[24,128]{1,0:T(8,128)S(1)} %get-tuple-element.41), channel_id=1, source_target_pairs={{0,4},{1,5},{2,6},{3,7},{4,0},{5,1},{6,2},{7,3},{8,12},{9,13},{10,... | collective-permute-start | bytes 36872 | tf_op jit(solution)/shard_map/ppermute | solution.py:49
  7.7 0.6 %collective-permute-start.2 = (f32[24,128]{1,0:T(8,128)S(1)}, f32[24,128]{1,0:T(8,128)S(1)}, u32[]{:S(2)}, u32[]{:S(2)}) collective-permute-start(f32[24,128]{1,0:T(8,128)S(1)} %collective-permute-done.1.odd), channel_id=1, source_target_pairs={{0,1},{1,0},{2,3},{3,2},{4,5},{5,4},{6,7},{7,6},{8,9},{9,8},{10,11... | collective-permute-start | bytes 36872 | tf_op jit(solution)/shard_map/ppermute | solution.py:42
  8.3 1.3 %forecast.2 = (f32[128,1024]{1,0:T(8,128)S(1)}, f32[128,128]{1,0:T(8,128)S(1)}, f32[256,128]{1,0:T(8,128)S(1)}, bf16[2048,256]{1,0:T(8,128)(2,1)S(1)}, f32[16,128]{1,0:T(8,128)S(1)}) custom-call(f32[4,4]{1,0:T(4,128)S(1)} %copy-done.4, f32[32,4,1024]{2,1,0:T(4,128)S(1)} %copy-done.1, f32[20,128]{1,0:T(8,128)S(1)} %get-tuple-element.27.from_ref.small_ref), custom_call_target="tpu_custom_call" | custom-call | flops 10485760 | bytes 1048576 | tf_op jit(solution)/shard_map/forecast/pallas_call | solution.py:772
  9.8 1.8 %collective-permute-start.4 = (f32[24,128]{1,0:T(8,128)S(1)}, f32[24,128]{1,0:T(8,128)S(1)}, u32[]{:S(2)}, u32[]{:S(2)}) collective-permute-start(f32[24,128]{1,0:T(8,128)S(1)} %get-tuple-element.43.refs_0_), channel_id=1, source_target_pairs={{0,8},{1,25},{2,10},{3,27},{4,12},{5,29},{6,14},{7,31},{8,0},{9,17... | collective-permute-start | bytes 36872 | tf_op jit(solution)/shard_map/ppermute | solution.py:46
  11.6 2.6 %collective-permute-start.6 = (f32[24,128]{1,0:T(8,128)S(1)}, f32[24,128]{1,0:T(8,128)S(1)}, u32[]{:S(2)}, u32[]{:S(2)}) collective-permute-start(f32[24,128]{1,0:T(8,128)S(1)} %get-tuple-element.44), channel_id=1, source_target_pairs={{0,16},{1,17},{2,18},{3,19},{4,20},{5,21},{6,22},{7,23},{8,24},{9,... | collective-permute-start | bytes 36872 | tf_op jit(solution)/shard_map/ppermute | solution.py:49
  14.2 0.5 %collective-permute-start.5 = (f32[24,128]{1,0:T(8,128)S(1)}, f32[24,128]{1,0:T(8,128)S(1)}, u32[]{:S(2)}, u32[]{:S(2)}) collective-permute-start(f32[24,128]{1,0:T(8,128)S(1)} %collective-permute-done.4.odd), channel_id=1, source_target_pairs={{0,1},{1,0},{2,3},{3,2},{4,5},{5,4},{6,7},{7,6},{8,9},{9,8},{10,11... | collective-permute-start | bytes 36872 | tf_op jit(solution)/shard_map/ppermute | solution.py:42
  14.7 0.8 %forecast.3 = (f32[128,1024]{1,0:T(8,128)S(1)}, f32[128,128]{1,0:T(8,128)S(1)}, f32[256,128]{1,0:T(8,128)S(1)}, s32[4,128]{1,0:T(4,128)S(1)}, bf16[512,1024]{1,0:T(8,128)(2,1)S(1)}) custom-call(f32[16,128]{1,0:T(8,128)S(1)} %get-tuple-element.28.extra_ref.powers_ref, f32[32,4,1024]{2,1,0:T(4,128)S(1)} %collective-permute-done.source.other_ref, ...), custom_call_target="tpu_custom_call" | custom-call | flops 10485760 | bytes 1048576 | tf_op jit(solution)/shard_map/forecast/pallas_call | solution.py:772
  15.5 0.8 %collective-permute-done.6.even = f32[24,128]{1,0:T(8,128)S(1)} collective-permute-done((f32[24,128]{1,0:T(8,128)S(1)}, f32[24,128]{1,0:T(8,128)S(1)}, u32[]{:S(2)}, u32[]{:S(2)}) %collective-permute-start.6) | collective-permute-done | bytes 12320 | tf_op jit(solution)/shard_map/ppermute | solution.py:49
  16.3 1.5 %sums.1 = (f32[40,128]{1,0:T(8,128)S(1)}, f32[40,128]{1,0:T(8,128)S(1)}, f32[40,128]{1,0:T(8,128)S(1)}, f32[256,256]{1,0:T(8,128)S(1)}) custom-call(f32[16,128]{1,0:T(8,128)S(1)} %get-tuple-element.28.extra_ref.powers_ref, f32[20,128]{1,0:T(8,128)S(1)} %get-tuple-element.27.from_ref.small_ref, f32[128,1024]{1,0:T(8,128)S(1)} %get-tuple-element.30.refs_1_.own_state, ...), custom_call_target="tpu_custom_call" | custom-call | tf_op jit(solution)/shard_map/sums/pallas_call | solution.py:812
  17.9 0.3 collective-permute-start.8
  18.1 3.1 %collective-permute-start.7 = (f32[40,128]{1,0:T(8,128)S(1)}, f32[40,128]{1,0:T(8,128)S(1)}, u32[]{:S(2)}, u32[]{:S(2)}) collective-permute-start(f32[40,128]{1,0:T(8,128)S(1)} %get-tuple-element.48), channel_id=1, source_target_pairs={{0,16},{1,17},{2,18},{3,19},{4,20},{5,21},{6,22},{7,23},{8,24},{9,... | collective-permute-start | bytes 61448 | tf_op jit(solution)/shard_map/ppermute | solution.py:49
  21.3 0.5 %collective-permute-done.8 = f32[40,128]{1,0:T(8,128)S(1)} collective-permute-done((f32[40,128]{1,0:T(8,128)S(1)}, f32[40,128]{1,0:T(8,128)S(1)}, u32[]{:S(2)}, u32[]{:S(2)}) %collective-permute-start.8) | collective-permute-done | bytes 20512 | tf_op jit(solution)/shard_map/ppermute | solution.py:46
  21.7 1.4 %collective-permute-start.9 = (f32[40,128]{1,0:T(8,128)S(1)}, f32[40,128]{1,0:T(8,128)S(1)}, u32[]{:S(2)}, u32[]{:S(2)}) collective-permute-start(f32[40,128]{1,0:T(8,128)S(1)} %collective-permute-done.8), channel_id=1, source_target_pairs={{0,1},{1,0},{2,3},{3,2},{4,5},{5,4},{6,7},{7,6},{8,9},{9,8},{10,11... | collective-permute-start | bytes 61448 | tf_op jit(solution)/shard_map/ppermute | solution.py:42
  23.1 0.8 %collective-permute-done.9 = f32[40,128]{1,0:T(8,128)S(1)} collective-permute-done((f32[40,128]{1,0:T(8,128)S(1)}, f32[40,128]{1,0:T(8,128)S(1)}, u32[]{:S(2)}, u32[]{:S(2)}) %collective-permute-start.9) | collective-permute-done | bytes 20512 | tf_op jit(solution)/shard_map/ppermute | solution.py:42
  24.0 1.5 %collective-permute-start.10 = (f32[40,128]{1,0:T(8,128)S(1)}, f32[40,128]{1,0:T(8,128)S(1)}, u32[]{:S(2)}, u32[]{:S(2)}) collective-permute-start(f32[40,128]{1,0:T(8,128)S(1)} %add_add_fusion.kept), channel_id=1, source_target_pairs={{0,2},{1,7},{2,0},{3,5},{4,6},{5,3},{6,4},{7,1},{8,10},{9,15},{10,... | collective-permute-start | bytes 61448 | tf_op jit(solution)/shard_map/ppermute | solution.py:46
  25.5 1.5 %collective-permute-start.12 = (f32[40,128]{1,0:T(8,128)S(1)}, f32[40,128]{1,0:T(8,128)S(1)}, u32[]{:S(2)}, u32[]{:S(2)}) collective-permute-start(f32[40,128]{1,0:T(8,128)S(1)} %add_add_fusion.kept), channel_id=1, source_target_pairs={{0,4},{1,5},{2,6},{3,7},{4,0},{5,1},{6,2},{7,3},{8,12},{9,13},{10,... | collective-permute-start | bytes 61448 | tf_op jit(solution)/shard_map/ppermute | solution.py:49
  27.0 0.8 %collective-permute-done.10.odd = f32[40,128]{1,0:T(8,128)S(1)} collective-permute-done((f32[40,128]{1,0:T(8,128)S(1)}, f32[40,128]{1,0:T(8,128)S(1)}, u32[]{:S(2)}, u32[]{:S(2)}) %collective-permute-start.10) | collective-permute-done | bytes 20512 | tf_op jit(solution)/shard_map/ppermute | solution.py:46
  27.9 1.4 %collective-permute-done.12.even = f32[40,128]{1,0:T(8,128)S(1)} collective-permute-done((f32[40,128]{1,0:T(8,128)S(1)}, f32[40,128]{1,0:T(8,128)S(1)}, u32[]{:S(2)}, u32[]{:S(2)}) %collective-permute-start.12) | collective-permute-done | bytes 20512 | tf_op jit(solution)/shard_map/ppermute | solution.py:49
  29.4 2.9 %analysis.1 = (f32[32,4,1024]{2,1,0:T(4,128)}, f32[2,128]{1,0:T(2,128)}) custom-call(bf16[512,1024]{1,0:T(8,128)(2,1)S(1)} %get-tuple-element.31.split_ref, f32[256,256]{1,0:T(8,128)S(1)} %get-tuple-element.45.edge_ref, f32[20,128]{1,0:T(8,128)S(1)} %get-tuple-element.27.from_ref.small_ref, s32[4,128]{1,0:T(4,128)S(1)} %get-tuple-element.46.slots_ref, ...), custom_call_target="tpu_custom_call" | custom-call | tf_op jit(solution)/shard_map/analysis/pallas_call | solution.py:844
  (31 shorter events, 1.0 us)
Async XLA Ops:
  0.6 2.7 %collective-permute-start = (f32[32,4,1024]{2,1,0:T(4,128)}, f32[32,4,1024]{2,1,0:T(4,128)S(1)}, u32[]{:S(2)}, u32[]{:S(2)}) collective-permute-start(f32[32,4,1024]{2,1,0:T(4,128)} %ensemble_ref.1), channel_id=1, source_target_pairs={{0,1},{1,0},{2,3},{3,2},{4,5},{5,4},{6,7},{7,6},{8,9},{9,8},{10,11... | collective-permute-start | bytes 1572872 | tf_op jit(solution)/shard_map/ppermute | solution.py:42
  1.1 1.0 %copy-start = (f32[32,4,1024]{2,1,0:T(4,128)S(1)}, f32[32,4,1024]{2,1,0:T(4,128)}, u32[]{:S(2)}) copy-start(f32[32,4,1024]{2,1,0:T(4,128)} %ensemble_ref.1) | copy-start | bytes 1572868
  2.2 0.7 %copy-start.6 = (s32[256]{0:T(256)S(1)}, s32[256]{0:T(256)}, u32[]{:S(2)}) copy-start(s32[256]{0:T(256)} %param.13) | copy-start | bytes 3076
  2.2 0.7 %copy-start.7 = (s32[256]{0:T(256)S(1)}, s32[256]{0:T(256)}, u32[]{:S(2)}) copy-start(s32[256]{0:T(256)} %param.14) | copy-start | bytes 3076
  2.2 0.7 %copy-start.8 = (f32[256]{0:T(256)S(1)}, f32[256]{0:T(256)}, u32[]{:S(2)}) copy-start(f32[256]{0:T(256)} %param.15) | copy-start | bytes 3076
  2.2 0.7 %copy-start.9 = (f32[256]{0:T(256)S(1)}, f32[256]{0:T(256)}, u32[]{:S(2)}) copy-start(f32[256]{0:T(256)} %param.16) | copy-start | bytes 3076
  2.2 6.1 %copy-start.1 = (f32[32,4,1024]{2,1,0:T(4,128)S(1)}, f32[32,4,1024]{2,1,0:T(4,128)}, u32[]{:S(2)}) copy-start(f32[32,4,1024]{2,1,0:T(4,128)} %ensemble_ref.1) | copy-start | bytes 1572868
  2.3 0.8 %copy-start.3 = (s32[1024]{0:T(1024)S(1)}, s32[1024]{0:T(1024)}, u32[]{:S(2)}) copy-start(s32[1024]{0:T(1024)} %param.11) | copy-start | bytes 12292
  2.4 0.8 %copy-start.2 = (f32[1024]{0:T(1024)S(1)}, f32[1024]{0:T(1024)}, u32[]{:S(2)}) copy-start(f32[1024]{0:T(1024)} %param.10) | copy-start | bytes 12292
  2.4 0.7 %copy-start.5 = (s32[1,16]{1,0:T(1,128)S(1)}, s32[1,16]{1,0:T(1,128)}, u32[]{:S(2)}) copy-start(s32[1,16]{1,0:T(1,128)} %refs_0_.1) | copy-start | bytes 196
  3.5 4.8 %copy-start.4 = (f32[4,4]{1,0:T(4,128)S(1)}, f32[4,4]{1,0:T(4,128)}, u32[]{:S(2)}) copy-start(f32[4,4]{1,0:T(4,128)} %extra_ref.1) | copy-start | bytes 196
  3.5 4.2 %collective-permute-start.1 = (f32[24,128]{1,0:T(8,128)S(1)}, f32[24,128]{1,0:T(8,128)S(1)}, u32[]{:S(2)}, u32[]{:S(2)}) collective-permute-start(f32[24,128]{1,0:T(8,128)S(1)} %get-tuple-element.40), channel_id=1, source_target_pairs={{0,2},{1,7},{2,0},{3,5},{4,6},{5,3},{6,4},{7,1},{8,10},{9,15},{10,... | collective-permute-start | bytes 36872 | tf_op jit(solution)/shard_map/ppermute | solution.py:46
  6.1 3.7 %collective-permute-start.3 = (f32[24,128]{1,0:T(8,128)S(1)}, f32[24,128]{1,0:T(8,128)S(1)}, u32[]{:S(2)}, u32[]{:S(2)}) collective-permute-start(f32[24,128]{1,0:T(8,128)S(1)} %get-tuple-element.41), channel_id=1, source_target_pairs={{0,4},{1,5},{2,6},{3,7},{4,0},{5,1},{6,2},{7,3},{8,12},{9,13},{10,... | collective-permute-start | bytes 36872 | tf_op jit(solution)/shard_map/ppermute | solution.py:49
  7.7 2.0 %collective-permute-start.2 = (f32[24,128]{1,0:T(8,128)S(1)}, f32[24,128]{1,0:T(8,128)S(1)}, u32[]{:S(2)}, u32[]{:S(2)}) collective-permute-start(f32[24,128]{1,0:T(8,128)S(1)} %collective-permute-done.1.odd), channel_id=1, source_target_pairs={{0,1},{1,0},{2,3},{3,2},{4,5},{5,4},{6,7},{7,6},{8,9},{9,8},{10,11... | collective-permute-start | bytes 36872 | tf_op jit(solution)/shard_map/ppermute | solution.py:42
  9.8 4.4 %collective-permute-start.4 = (f32[24,128]{1,0:T(8,128)S(1)}, f32[24,128]{1,0:T(8,128)S(1)}, u32[]{:S(2)}, u32[]{:S(2)}) collective-permute-start(f32[24,128]{1,0:T(8,128)S(1)} %get-tuple-element.43.refs_0_), channel_id=1, source_target_pairs={{0,8},{1,25},{2,10},{3,27},{4,12},{5,29},{6,14},{7,31},{8,0},{9,17... | collective-permute-start | bytes 36872 | tf_op jit(solution)/shard_map/ppermute | solution.py:46
  11.6 4.7 %collective-permute-start.6 = (f32[24,128]{1,0:T(8,128)S(1)}, f32[24,128]{1,0:T(8,128)S(1)}, u32[]{:S(2)}, u32[]{:S(2)}) collective-permute-start(f32[24,128]{1,0:T(8,128)S(1)} %get-tuple-element.44), channel_id=1, source_target_pairs={{0,16},{1,17},{2,18},{3,19},{4,20},{5,21},{6,22},{7,23},{8,24},{9,... | collective-permute-start | bytes 36872 | tf_op jit(solution)/shard_map/ppermute | solution.py:49
  14.2 2.1 %collective-permute-start.5 = (f32[24,128]{1,0:T(8,128)S(1)}, f32[24,128]{1,0:T(8,128)S(1)}, u32[]{:S(2)}, u32[]{:S(2)}) collective-permute-start(f32[24,128]{1,0:T(8,128)S(1)} %collective-permute-done.4.odd), channel_id=1, source_target_pairs={{0,1},{1,0},{2,3},{3,2},{4,5},{5,4},{6,7},{7,6},{8,9},{9,8},{10,11... | collective-permute-start | bytes 36872 | tf_op jit(solution)/shard_map/ppermute | solution.py:42
  17.9 3.8 %collective-permute-start.8 = (f32[40,128]{1,0:T(8,128)S(1)}, f32[40,128]{1,0:T(8,128)S(1)}, u32[]{:S(2)}, u32[]{:S(2)}) collective-permute-start(f32[40,128]{1,0:T(8,128)S(1)} %get-tuple-element.49), channel_id=1, source_target_pairs={{0,8},{1,25},{2,10},{3,27},{4,12},{5,29},{6,14},{7,31},{8,0},{9,17... | collective-permute-start | bytes 61448 | tf_op jit(solution)/shard_map/ppermute | solution.py:46
  18.1 5.0 %collective-permute-start.7 = (f32[40,128]{1,0:T(8,128)S(1)}, f32[40,128]{1,0:T(8,128)S(1)}, u32[]{:S(2)}, u32[]{:S(2)}) collective-permute-start(f32[40,128]{1,0:T(8,128)S(1)} %get-tuple-element.48), channel_id=1, source_target_pairs={{0,16},{1,17},{2,18},{3,19},{4,20},{5,21},{6,22},{7,23},{8,24},{9,... | collective-permute-start | bytes 61448 | tf_op jit(solution)/shard_map/ppermute | solution.py:49
  21.7 2.2 %collective-permute-start.9 = (f32[40,128]{1,0:T(8,128)S(1)}, f32[40,128]{1,0:T(8,128)S(1)}, u32[]{:S(2)}, u32[]{:S(2)}) collective-permute-start(f32[40,128]{1,0:T(8,128)S(1)} %collective-permute-done.8), channel_id=1, source_target_pairs={{0,1},{1,0},{2,3},{3,2},{4,5},{5,4},{6,7},{7,6},{8,9},{9,8},{10,11... | collective-permute-start | bytes 61448 | tf_op jit(solution)/shard_map/ppermute | solution.py:42
  24.0 3.8 %collective-permute-start.10 = (f32[40,128]{1,0:T(8,128)S(1)}, f32[40,128]{1,0:T(8,128)S(1)}, u32[]{:S(2)}, u32[]{:S(2)}) collective-permute-start(f32[40,128]{1,0:T(8,128)S(1)} %add_add_fusion.kept), channel_id=1, source_target_pairs={{0,2},{1,7},{2,0},{3,5},{4,6},{5,3},{6,4},{7,1},{8,10},{9,15},{10,... | collective-permute-start | bytes 61448 | tf_op jit(solution)/shard_map/ppermute | solution.py:46
  25.5 3.9 %collective-permute-start.12 = (f32[40,128]{1,0:T(8,128)S(1)}, f32[40,128]{1,0:T(8,128)S(1)}, u32[]{:S(2)}, u32[]{:S(2)}) collective-permute-start(f32[40,128]{1,0:T(8,128)S(1)} %add_add_fusion.kept), channel_id=1, source_target_pairs={{0,4},{1,5},{2,6},{3,7},{4,0},{5,1},{6,2},{7,3},{8,12},{9,13},{10,... | collective-permute-start | bytes 61448 | tf_op jit(solution)/shard_map/ppermute | solution.py:49
  27.8 1.6 %collective-permute-start.11 = (f32[40,128]{1,0:T(8,128)S(1)}, f32[40,128]{1,0:T(8,128)S(1)}, u32[]{:S(2)}, u32[]{:S(2)}) collective-permute-start(f32[40,128]{1,0:T(8,128)S(1)} %collective-permute-done.10.odd), channel_id=1, source_target_pairs={{0,1},{1,0},{2,3},{3,2},{4,5},{5,4},{6,7},{7,6},{8,9},{9,8},{10,11... | collective-permute-start | bytes 61448 | tf_op jit(solution)/shard_map/ppermute | solution.py:42

commit v7 on v6

--- a/solution.py
+++ b/solution.py
@@ -600,7 +600,7 @@
 
 def analysis_kernel(
     split_ref, edge_ref, small_ref, slots_ref, kept, odd, swapped, even,
-    analysis_ref, innovation_ref, center_ref, pieces_ref, result_ref, sems, *, units, obs_rows, count,
+    analysis_ref, innovation_ref, center_ref, pieces_ref, result_ref, departure_ref, sems, *, units, obs_rows, count,
 ):
     block, core = here()
     members, fields, cells = analysis_ref.shape
@@ -701,7 +701,9 @@
         center = center[:1]
         at = small_ref.shape[0] - 2 * obs_rows + r
         value, sigma = small_ref[at : at + 1, :], small_ref[at + obs_rows : at + obs_rows + 1, :]
-        innovation_ref[r : r + 1, :] = (value - center) / sigma
+        departure_ref[r : r + 1, :] = (value - center) / sigma
+    copies.append(pltpu.make_async_copy(departure_ref, innovation_ref, sems.at[2]))
+    copies[-1].start()
     for copy in copies:
         copy.wait()
 
@@ -848,12 +850,13 @@
             jax.ShapeDtypeStruct((obs_rows, LANES), real),
         ),
         in_specs=[whole] * 8,
-        out_specs=(pl.BlockSpec(memory_space=pl.ANY), whole),
+        out_specs=(pl.BlockSpec(memory_space=pl.ANY),) * 2,
         scratch_shapes=[
             pltpu.VMEM((4 * (stay.shape[0] - head), LANES), real),
             pltpu.VMEM((fields * 2 * total, 2 * LANES), jnp.bfloat16),
             pltpu.VMEM((members, fields, cells), real),
-            pltpu.SemaphoreType.DMA((2,)),
+            pltpu.VMEM((obs_rows, LANES), real),
+            pltpu.SemaphoreType.DMA((3,)),
         ],
         compiler_params=params,
         name="analysis",

time: 32.4 us -> 31.9 us (0.985)
  Pallas kernels: 7.14 us -> 6.6 us
    pallas_call x1, Pallas kernels: 2.91 us -> 2.37 us  [shards(): pl.pallas_call(functools.partial(analysis_kernel, units=units, obs_rows=o...]
where the time goes in v7:
time: 31.9 us; the launch traced here: 31.7 us
  starting transfers between devices  18 us (56%)
  Pallas kernels  6.6 us (21%)
  waiting for transfers between devices  4.6 us (14%)
  local copies, waits for them, and re-layouts  1.81 us (6%)
  between operations  0.74 us (2%)
    ppermute x4, starting transfers between devices, exchange(): lax.ppermute(to_even, BOTH, core_pairs(owners, lambda block, core: (block...  8.75 us
    ppermute x4, starting transfers between devices, exchange(): lax.ppermute(to_odd, BOTH, core_pairs(owners, lambda block, core: (block...  6.08 us
    ppermute x5, starting transfers between devices, swap_cores(): lax.ppermute(x, BOTH, core_pairs(owners, lambda block, core: (block, 1 -...  3.14 us
    pallas_call x1, Pallas kernels, shards(): pl.pallas_call(functools.partial(analysis_kernel, units=units, obs_rows=o...  2.37 us
    ppermute x4, waiting for transfers between devices, exchange(): lax.ppermute(to_even, BOTH, core_pairs(owners, lambda block, core: (block...  2.34 us
    pallas_call x2, Pallas kernels, forecast(): pl.pallas_call(functools.partial(forecast_kernel, fields=fields, own=own)...  2.14 us
    unnamed x20, local copies, waits for them, and re-layouts  1.81 us
    pallas_call x1, Pallas kernels, shards(): pl.pallas_call(functools.partial(sums_kernel, owners=owners, units=units,...  1.53 us
  transfers between devices with their start and end apart: 13, of which 7 were waited for; matrix products, arithmetic and copies ran while one was open for 0% of the time, Pallas kernels for 8%

profile of v7, /device:TPU:0, one launch (start us, length us, event | category | flops | bytes accessed | tf_op | source)
XLA Modules:
  0.0 31.7 jit_solution(15133159160780887427)
XLA Ops:
  0.6 0.5 %collective-permute-start = (f32[32,4,1024]{2,1,0:T(4,128)}, f32[32,4,1024]{2,1,0:T(4,128)S(1)}, u32[]{:S(2)}, u32[]{:S(2)}) collective-permute-start(f32[32,4,1024]{2,1,0:T(4,128)} %ensemble_ref.1), channel_id=1, source_target_pairs={{0,1},{1,0},{2,3},{3,2},{4,5},{5,4},{6,7},{7,6},{8,9},{9,8},{10,11... | collective-permute-start | bytes 1572872 | tf_op jit(solution)/shard_map/ppermute | solution.py:42
  1.2 1.0 %copy-done = f32[32,4,1024]{2,1,0:T(4,128)S(1)} copy-done((f32[32,4,1024]{2,1,0:T(4,128)S(1)}, f32[32,4,1024]{2,1,0:T(4,128)}, u32[]{:S(2)}) %copy-start) | copy-done | bytes 524312
  2.4 0.5 %copy-done.6 = s32[256]{0:T(256)S(1)} copy-done((s32[256]{0:T(256)S(1)}, s32[256]{0:T(256)}, u32[]{:S(2)}) %copy-start.6) | copy-done | bytes 1048
  3.1 0.2 pack.1
  3.5 2.6 %collective-permute-start.1 = (f32[24,128]{1,0:T(8,128)S(1)}, f32[24,128]{1,0:T(8,128)S(1)}, u32[]{:S(2)}, u32[]{:S(2)}) collective-permute-start(f32[24,128]{1,0:T(8,128)S(1)} %get-tuple-element.40), channel_id=1, source_target_pairs={{0,2},{1,7},{2,0},{3,5},{4,6},{5,3},{6,4},{7,1},{8,10},{9,15},{10,... | collective-permute-start | bytes 36872 | tf_op jit(solution)/shard_map/ppermute | solution.py:46
  6.1 1.5 %collective-permute-start.3 = (f32[24,128]{1,0:T(8,128)S(1)}, f32[24,128]{1,0:T(8,128)S(1)}, u32[]{:S(2)}, u32[]{:S(2)}) collective-permute-start(f32[24,128]{1,0:T(8,128)S(1)} %get-tuple-element.41), channel_id=1, source_target_pairs={{0,4},{1,5},{2,6},{3,7},{4,0},{5,1},{6,2},{7,3},{8,12},{9,13},{10,... | collective-permute-start | bytes 36872 | tf_op jit(solution)/shard_map/ppermute | solution.py:49
  7.7 0.6 %collective-permute-start.2 = (f32[24,128]{1,0:T(8,128)S(1)}, f32[24,128]{1,0:T(8,128)S(1)}, u32[]{:S(2)}, u32[]{:S(2)}) collective-permute-start(f32[24,128]{1,0:T(8,128)S(1)} %collective-permute-done.1.odd), channel_id=1, source_target_pairs={{0,1},{1,0},{2,3},{3,2},{4,5},{5,4},{6,7},{7,6},{8,9},{9,8},{10,11... | collective-permute-start | bytes 36872 | tf_op jit(solution)/shard_map/ppermute | solution.py:42
  8.3 1.3 %forecast.2 = (f32[128,1024]{1,0:T(8,128)S(1)}, f32[128,128]{1,0:T(8,128)S(1)}, f32[256,128]{1,0:T(8,128)S(1)}, bf16[2048,256]{1,0:T(8,128)(2,1)S(1)}, f32[16,128]{1,0:T(8,128)S(1)}) custom-call(f32[4,4]{1,0:T(4,128)S(1)} %copy-done.4, f32[32,4,1024]{2,1,0:T(4,128)S(1)} %copy-done.1, f32[20,128]{1,0:T(8,128)S(1)} %get-tuple-element.27.from_ref.small_ref), custom_call_target="tpu_custom_call" | custom-call | flops 10485760 | bytes 1048576 | tf_op jit(solution)/shard_map/forecast/pallas_call | solution.py:774
  9.8 1.8 %collective-permute-start.4 = (f32[24,128]{1,0:T(8,128)S(1)}, f32[24,128]{1,0:T(8,128)S(1)}, u32[]{:S(2)}, u32[]{:S(2)}) collective-permute-start(f32[24,128]{1,0:T(8,128)S(1)} %get-tuple-element.43.refs_0_), channel_id=1, source_target_pairs={{0,8},{1,25},{2,10},{3,27},{4,12},{5,29},{6,14},{7,31},{8,0},{9,17... | collective-permute-start | bytes 36872 | tf_op jit(solution)/shard_map/ppermute | solution.py:46
  11.6 2.6 %collective-permute-start.6 = (f32[24,128]{1,0:T(8,128)S(1)}, f32[24,128]{1,0:T(8,128)S(1)}, u32[]{:S(2)}, u32[]{:S(2)}) collective-permute-start(f32[24,128]{1,0:T(8,128)S(1)} %get-tuple-element.44), channel_id=1, source_target_pairs={{0,16},{1,17},{2,18},{3,19},{4,20},{5,21},{6,22},{7,23},{8,24},{9,... | collective-permute-start | bytes 36872 | tf_op jit(solution)/shard_map/ppermute | solution.py:49
  14.2 0.5 %collective-permute-start.5 = (f32[24,128]{1,0:T(8,128)S(1)}, f32[24,128]{1,0:T(8,128)S(1)}, u32[]{:S(2)}, u32[]{:S(2)}) collective-permute-start(f32[24,128]{1,0:T(8,128)S(1)} %collective-permute-done.4.odd), channel_id=1, source_target_pairs={{0,1},{1,0},{2,3},{3,2},{4,5},{5,4},{6,7},{7,6},{8,9},{9,8},{10,11... | collective-permute-start | bytes 36872 | tf_op jit(solution)/shard_map/ppermute | solution.py:42
  14.7 0.8 %forecast.3 = (f32[128,1024]{1,0:T(8,128)S(1)}, f32[128,128]{1,0:T(8,128)S(1)}, f32[256,128]{1,0:T(8,128)S(1)}, s32[4,128]{1,0:T(4,128)S(1)}, bf16[512,1024]{1,0:T(8,128)(2,1)S(1)}) custom-call(f32[16,128]{1,0:T(8,128)S(1)} %get-tuple-element.28.extra_ref.powers_ref, f32[32,4,1024]{2,1,0:T(4,128)S(1)} %collective-permute-done.source.other_ref, ...), custom_call_target="tpu_custom_call" | custom-call | flops 10485760 | bytes 1048576 | tf_op jit(solution)/shard_map/forecast/pallas_call | solution.py:774
  15.5 0.8 %collective-permute-done.6.even = f32[24,128]{1,0:T(8,128)S(1)} collective-permute-done((f32[24,128]{1,0:T(8,128)S(1)}, f32[24,128]{1,0:T(8,128)S(1)}, u32[]{:S(2)}, u32[]{:S(2)}) %collective-permute-start.6) | collective-permute-done | bytes 12320 | tf_op jit(solution)/shard_map/ppermute | solution.py:49
  16.3 1.5 %sums.1 = (f32[40,128]{1,0:T(8,128)S(1)}, f32[40,128]{1,0:T(8,128)S(1)}, f32[40,128]{1,0:T(8,128)S(1)}, f32[256,256]{1,0:T(8,128)S(1)}) custom-call(f32[16,128]{1,0:T(8,128)S(1)} %get-tuple-element.28.extra_ref.powers_ref, f32[20,128]{1,0:T(8,128)S(1)} %get-tuple-element.27.from_ref.small_ref, f32[128,1024]{1,0:T(8,128)S(1)} %get-tuple-element.30.refs_1_.own_state, ...), custom_call_target="tpu_custom_call" | custom-call | tf_op jit(solution)/shard_map/sums/pallas_call | solution.py:814
  17.9 0.3 collective-permute-start.8
  18.1 3.1 %collective-permute-start.7 = (f32[40,128]{1,0:T(8,128)S(1)}, f32[40,128]{1,0:T(8,128)S(1)}, u32[]{:S(2)}, u32[]{:S(2)}) collective-permute-start(f32[40,128]{1,0:T(8,128)S(1)} %get-tuple-element.48), channel_id=1, source_target_pairs={{0,16},{1,17},{2,18},{3,19},{4,20},{5,21},{6,22},{7,23},{8,24},{9,... | collective-permute-start | bytes 61448 | tf_op jit(solution)/shard_map/ppermute | solution.py:49
  21.3 0.5 %collective-permute-done.8 = f32[40,128]{1,0:T(8,128)S(1)} collective-permute-done((f32[40,128]{1,0:T(8,128)S(1)}, f32[40,128]{1,0:T(8,128)S(1)}, u32[]{:S(2)}, u32[]{:S(2)}) %collective-permute-start.8) | collective-permute-done | bytes 20512 | tf_op jit(solution)/shard_map/ppermute | solution.py:46
  21.7 1.4 %collective-permute-start.9 = (f32[40,128]{1,0:T(8,128)S(1)}, f32[40,128]{1,0:T(8,128)S(1)}, u32[]{:S(2)}, u32[]{:S(2)}) collective-permute-start(f32[40,128]{1,0:T(8,128)S(1)} %collective-permute-done.8), channel_id=1, source_target_pairs={{0,1},{1,0},{2,3},{3,2},{4,5},{5,4},{6,7},{7,6},{8,9},{9,8},{10,11... | collective-permute-start | bytes 61448 | tf_op jit(solution)/shard_map/ppermute | solution.py:42
  23.1 0.8 %collective-permute-done.9 = f32[40,128]{1,0:T(8,128)S(1)} collective-permute-done((f32[40,128]{1,0:T(8,128)S(1)}, f32[40,128]{1,0:T(8,128)S(1)}, u32[]{:S(2)}, u32[]{:S(2)}) %collective-permute-start.9) | collective-permute-done | bytes 20512 | tf_op jit(solution)/shard_map/ppermute | solution.py:42
  24.0 1.5 %collective-permute-start.10 = (f32[40,128]{1,0:T(8,128)S(1)}, f32[40,128]{1,0:T(8,128)S(1)}, u32[]{:S(2)}, u32[]{:S(2)}) collective-permute-start(f32[40,128]{1,0:T(8,128)S(1)} %add_add_fusion.kept), channel_id=1, source_target_pairs={{0,2},{1,7},{2,0},{3,5},{4,6},{5,3},{6,4},{7,1},{8,10},{9,15},{10,... | collective-permute-start | bytes 61448 | tf_op jit(solution)/shard_map/ppermute | solution.py:46
  25.5 1.5 %collective-permute-start.12 = (f32[40,128]{1,0:T(8,128)S(1)}, f32[40,128]{1,0:T(8,128)S(1)}, u32[]{:S(2)}, u32[]{:S(2)}) collective-permute-start(f32[40,128]{1,0:T(8,128)S(1)} %add_add_fusion.kept), channel_id=1, source_target_pairs={{0,4},{1,5},{2,6},{3,7},{4,0},{5,1},{6,2},{7,3},{8,12},{9,13},{10,... | collective-permute-start | bytes 61448 | tf_op jit(solution)/shard_map/ppermute | solution.py:49
  27.0 0.8 %collective-permute-done.10.odd = f32[40,128]{1,0:T(8,128)S(1)} collective-permute-done((f32[40,128]{1,0:T(8,128)S(1)}, f32[40,128]{1,0:T(8,128)S(1)}, u32[]{:S(2)}, u32[]{:S(2)}) %collective-permute-start.10) | collective-permute-done | bytes 20512 | tf_op jit(solution)/shard_map/ppermute | solution.py:46
  27.9 1.4 %collective-permute-done.12.even = f32[40,128]{1,0:T(8,128)S(1)} collective-permute-done((f32[40,128]{1,0:T(8,128)S(1)}, f32[40,128]{1,0:T(8,128)S(1)}, u32[]{:S(2)}, u32[]{:S(2)}) %collective-permute-start.12) | collective-permute-done | bytes 20512 | tf_op jit(solution)/shard_map/ppermute | solution.py:49
  29.4 2.4 %analysis.1 = (f32[32,4,1024]{2,1,0:T(4,128)}, f32[2,128]{1,0:T(2,128)}) custom-call(bf16[512,1024]{1,0:T(8,128)(2,1)S(1)} %get-tuple-element.31.split_ref, f32[256,256]{1,0:T(8,128)S(1)} %get-tuple-element.45.edge_ref, f32[20,128]{1,0:T(8,128)S(1)} %get-tuple-element.27.from_ref.small_ref, s32[4,128]{1,0:T(4,128)S(1)} %get-tuple-element.46.slots_ref, ...), custom_call_target="tpu_custom_call" | custom-call | tf_op jit(solution)/shard_map/analysis/pallas_call | solution.py:846
  (31 shorter events, 1.0 us)
Async XLA Ops:
  0.6 2.7 %collective-permute-start = (f32[32,4,1024]{2,1,0:T(4,128)}, f32[32,4,1024]{2,1,0:T(4,128)S(1)}, u32[]{:S(2)}, u32[]{:S(2)}) collective-permute-start(f32[32,4,1024]{2,1,0:T(4,128)} %ensemble_ref.1), channel_id=1, source_target_pairs={{0,1},{1,0},{2,3},{3,2},{4,5},{5,4},{6,7},{7,6},{8,9},{9,8},{10,11... | collective-permute-start | bytes 1572872 | tf_op jit(solution)/shard_map/ppermute | solution.py:42
  1.1 1.0 %copy-start = (f32[32,4,1024]{2,1,0:T(4,128)S(1)}, f32[32,4,1024]{2,1,0:T(4,128)}, u32[]{:S(2)}) copy-start(f32[32,4,1024]{2,1,0:T(4,128)} %ensemble_ref.1) | copy-start | bytes 1572868
  2.2 0.7 %copy-start.6 = (s32[256]{0:T(256)S(1)}, s32[256]{0:T(256)}, u32[]{:S(2)}) copy-start(s32[256]{0:T(256)} %param.13) | copy-start | bytes 3076
  2.2 0.7 %copy-start.7 = (s32[256]{0:T(256)S(1)}, s32[256]{0:T(256)}, u32[]{:S(2)}) copy-start(s32[256]{0:T(256)} %param.14) | copy-start | bytes 3076
  2.2 0.7 %copy-start.8 = (f32[256]{0:T(256)S(1)}, f32[256]{0:T(256)}, u32[]{:S(2)}) copy-start(f32[256]{0:T(256)} %param.15) | copy-start | bytes 3076
  2.2 0.7 %copy-start.9 = (f32[256]{0:T(256)S(1)}, f32[256]{0:T(256)}, u32[]{:S(2)}) copy-start(f32[256]{0:T(256)} %param.16) | copy-start | bytes 3076
  2.2 6.1 %copy-start.1 = (f32[32,4,1024]{2,1,0:T(4,128)S(1)}, f32[32,4,1024]{2,1,0:T(4,128)}, u32[]{:S(2)}) copy-start(f32[32,4,1024]{2,1,0:T(4,128)} %ensemble_ref.1) | copy-start | bytes 1572868
  2.3 0.8 %copy-start.3 = (s32[1024]{0:T(1024)S(1)}, s32[1024]{0:T(1024)}, u32[]{:S(2)}) copy-start(s32[1024]{0:T(1024)} %param.11) | copy-start | bytes 12292
  2.4 0.8 %copy-start.2 = (f32[1024]{0:T(1024)S(1)}, f32[1024]{0:T(1024)}, u32[]{:S(2)}) copy-start(f32[1024]{0:T(1024)} %param.10) | copy-start | bytes 12292
  2.4 0.7 %copy-start.5 = (s32[1,16]{1,0:T(1,128)S(1)}, s32[1,16]{1,0:T(1,128)}, u32[]{:S(2)}) copy-start(s32[1,16]{1,0:T(1,128)} %refs_0_.1) | copy-start | bytes 196
  3.5 4.8 %copy-start.4 = (f32[4,4]{1,0:T(4,128)S(1)}, f32[4,4]{1,0:T(4,128)}, u32[]{:S(2)}) copy-start(f32[4,4]{1,0:T(4,128)} %extra_ref.1) | copy-start | bytes 196
  3.5 4.2 %collective-permute-start.1 = (f32[24,128]{1,0:T(8,128)S(1)}, f32[24,128]{1,0:T(8,128)S(1)}, u32[]{:S(2)}, u32[]{:S(2)}) collective-permute-start(f32[24,128]{1,0:T(8,128)S(1)} %get-tuple-element.40), channel_id=1, source_target_pairs={{0,2},{1,7},{2,0},{3,5},{4,6},{5,3},{6,4},{7,1},{8,10},{9,15},{10,... | collective-permute-start | bytes 36872 | tf_op jit(solution)/shard_map/ppermute | solution.py:46
  6.1 3.7 %collective-permute-start.3 = (f32[24,128]{1,0:T(8,128)S(1)}, f32[24,128]{1,0:T(8,128)S(1)}, u32[]{:S(2)}, u32[]{:S(2)}) collective-permute-start(f32[24,128]{1,0:T(8,128)S(1)} %get-tuple-element.41), channel_id=1, source_target_pairs={{0,4},{1,5},{2,6},{3,7},{4,0},{5,1},{6,2},{7,3},{8,12},{9,13},{10,... | collective-permute-start | bytes 36872 | tf_op jit(solution)/shard_map/ppermute | solution.py:49
  7.7 2.0 %collective-permute-start.2 = (f32[24,128]{1,0:T(8,128)S(1)}, f32[24,128]{1,0:T(8,128)S(1)}, u32[]{:S(2)}, u32[]{:S(2)}) collective-permute-start(f32[24,128]{1,0:T(8,128)S(1)} %collective-permute-done.1.odd), channel_id=1, source_target_pairs={{0,1},{1,0},{2,3},{3,2},{4,5},{5,4},{6,7},{7,6},{8,9},{9,8},{10,11... | collective-permute-start | bytes 36872 | tf_op jit(solution)/shard_map/ppermute | solution.py:42
  9.8 4.4 %collective-permute-start.4 = (f32[24,128]{1,0:T(8,128)S(1)}, f32[24,128]{1,0:T(8,128)S(1)}, u32[]{:S(2)}, u32[]{:S(2)}) collective-permute-start(f32[24,128]{1,0:T(8,128)S(1)} %get-tuple-element.43.refs_0_), channel_id=1, source_target_pairs={{0,8},{1,25},{2,10},{3,27},{4,12},{5,29},{6,14},{7,31},{8,0},{9,17... | collective-permute-start | bytes 36872 | tf_op jit(solution)/shard_map/ppermute | solution.py:46
  11.6 4.7 %collective-permute-start.6 = (f32[24,128]{1,0:T(8,128)S(1)}, f32[24,128]{1,0:T(8,128)S(1)}, u32[]{:S(2)}, u32[]{:S(2)}) collective-permute-start(f32[24,128]{1,0:T(8,128)S(1)} %get-tuple-element.44), channel_id=1, source_target_pairs={{0,16},{1,17},{2,18},{3,19},{4,20},{5,21},{6,22},{7,23},{8,24},{9,... | collective-permute-start | bytes 36872 | tf_op jit(solution)/shard_map/ppermute | solution.py:49
  14.2 2.1 %collective-permute-start.5 = (f32[24,128]{1,0:T(8,128)S(1)}, f32[24,128]{1,0:T(8,128)S(1)}, u32[]{:S(2)}, u32[]{:S(2)}) collective-permute-start(f32[24,128]{1,0:T(8,128)S(1)} %collective-permute-done.4.odd), channel_id=1, source_target_pairs={{0,1},{1,0},{2,3},{3,2},{4,5},{5,4},{6,7},{7,6},{8,9},{9,8},{10,11... | collective-permute-start | bytes 36872 | tf_op jit(solution)/shard_map/ppermute | solution.py:42
  17.9 3.8 %collective-permute-start.8 = (f32[40,128]{1,0:T(8,128)S(1)}, f32[40,128]{1,0:T(8,128)S(1)}, u32[]{:S(2)}, u32[]{:S(2)}) collective-permute-start(f32[40,128]{1,0:T(8,128)S(1)} %get-tuple-element.49), channel_id=1, source_target_pairs={{0,8},{1,25},{2,10},{3,27},{4,12},{5,29},{6,14},{7,31},{8,0},{9,17... | collective-permute-start | bytes 61448 | tf_op jit(solution)/shard_map/ppermute | solution.py:46
  18.1 5.0 %collective-permute-start.7 = (f32[40,128]{1,0:T(8,128)S(1)}, f32[40,128]{1,0:T(8,128)S(1)}, u32[]{:S(2)}, u32[]{:S(2)}) collective-permute-start(f32[40,128]{1,0:T(8,128)S(1)} %get-tuple-element.48), channel_id=1, source_target_pairs={{0,16},{1,17},{2,18},{3,19},{4,20},{5,21},{6,22},{7,23},{8,24},{9,... | collective-permute-start | bytes 61448 | tf_op jit(solution)/shard_map/ppermute | solution.py:49
  21.7 2.2 %collective-permute-start.9 = (f32[40,128]{1,0:T(8,128)S(1)}, f32[40,128]{1,0:T(8,128)S(1)}, u32[]{:S(2)}, u32[]{:S(2)}) collective-permute-start(f32[40,128]{1,0:T(8,128)S(1)} %collective-permute-done.8), channel_id=1, source_target_pairs={{0,1},{1,0},{2,3},{3,2},{4,5},{5,4},{6,7},{7,6},{8,9},{9,8},{10,11... | collective-permute-start | bytes 61448 | tf_op jit(solution)/shard_map/ppermute | solution.py:42
  24.0 3.8 %collective-permute-start.10 = (f32[40,128]{1,0:T(8,128)S(1)}, f32[40,128]{1,0:T(8,128)S(1)}, u32[]{:S(2)}, u32[]{:S(2)}) collective-permute-start(f32[40,128]{1,0:T(8,128)S(1)} %add_add_fusion.kept), channel_id=1, source_target_pairs={{0,2},{1,7},{2,0},{3,5},{4,6},{5,3},{6,4},{7,1},{8,10},{9,15},{10,... | collective-permute-start | bytes 61448 | tf_op jit(solution)/shard_map/ppermute | solution.py:46
  25.5 3.9 %collective-permute-start.12 = (f32[40,128]{1,0:T(8,128)S(1)}, f32[40,128]{1,0:T(8,128)S(1)}, u32[]{:S(2)}, u32[]{:S(2)}) collective-permute-start(f32[40,128]{1,0:T(8,128)S(1)} %add_add_fusion.kept), channel_id=1, source_target_pairs={{0,4},{1,5},{2,6},{3,7},{4,0},{5,1},{6,2},{7,3},{8,12},{9,13},{10,... | collective-permute-start | bytes 61448 | tf_op jit(solution)/shard_map/ppermute | solution.py:49
  27.8 1.6 %collective-permute-start.11 = (f32[40,128]{1,0:T(8,128)S(1)}, f32[40,128]{1,0:T(8,128)S(1)}, u32[]{:S(2)}, u32[]{:S(2)}) collective-permute-start(f32[40,128]{1,0:T(8,128)S(1)} %collective-permute-done.10.odd), channel_id=1, source_target_pairs={{0,1},{1,0},{2,3},{3,2},{4,5},{5,4},{6,7},{7,6},{8,9},{9,8},{10,11... | collective-permute-start | bytes 61448 | tf_op jit(solution)/shard_map/ppermute | solution.py:42

commit v8 on v7

--- a/solution.py
+++ b/solution.py
@@ -302,17 +302,21 @@
         slots_ref[rows + r : rows + r + 1, :] = group * CAP + (slot - start).astype(jnp.int32)
 
 
-def forecast_kernel(extra_ref, source, from_ref, *refs, fields, own):
+def rule_kernel(couple_ref, small_ref, band_ref, powers_ref, *, tiles):
+    fill_powers(couple_ref, powers_ref)
+    make_band = band_maker(small_ref, band_ref, tiles * LANES)
+    for t in range(tiles):
+        make_band(t)
+
+
+def forecast_kernel(powers_ref, source, band_ref, *refs, fields, own):
     members, _, cells = source.shape
     tiles = cells // LANES
     height = fields * members
     if own:
-        state, edge, sums_ref, band_ref, powers_ref, split_ref, raw_ref = refs
-        fill_powers(extra_ref, powers_ref)
-        make_band = band_maker(from_ref, band_ref, cells)
+        state, edge, sums_ref, split_ref, raw_ref = refs
     else:
         send_ref, own_state, state, edge, sums_ref, slots_ref, pieces_ref, split_ref, raw_ref = refs
-        powers_ref, band_ref = extra_ref, from_ref
         fill_positions(send_ref, slots_ref)
         core = here()[1]
 
@@ -341,8 +345,6 @@
         lanes, after, before = (
             slice(n % tiles * LANES, (n % tiles + 1) * LANES) for n in (t, t + 1, t - 1)
         )
-        if own:
-            make_band(t)
         around = jnp.where(nearer, split_ref[:, after], split_ref[:, before])
         product = jnp.dot(
             jnp.concatenate([split_ref[:, lanes], around], axis=1),
@@ -789,7 +791,18 @@
             name="forecast",
         )(*operands)
 
-    *own_forecast, rule, mixed = forecast((couple, ensemble, small), (band, powers), True)
+    rule, mixed = pl.pallas_call(
+        functools.partial(rule_kernel, tiles=tiles),
+        out_shape=(band, powers),
+        in_specs=[whole] * 2,
+        out_specs=(whole,) * 2,
+        compiler_params=params,
+        cost_estimate=pl.CostEstimate(
+            flops=40 * strip_rows * cells, bytes_accessed=4 * strip_rows * cells, transcendentals=0
+        ),
+        name="rule",
+    )(couple, small)
+    own_forecast = forecast((mixed, ensemble, rule), (), True)
     carried = []
     for n, unit in enumerate(units):
         arrived = exchange(to_odd, to_even, owners, unit)
@@ -801,7 +814,7 @@
                 out_specs=(whole,) * 3,
                 compiler_params=params,
                 name="regroup",
-            )(kept, *arrived, own_forecast[2])
+            )(kept, *arrived, mixed)
             carried.append(to_odd)
     *other_forecast, slots_of, split = forecast(
         (mixed, other, rule, send_count, own_forecast[0]), (slots, pieces), False

time: 31.9 us -> 31.4 us (0.984)
  waiting for transfers between devices: 4.6 us -> 3.85 us
    pallas_call x0 -> x1, Pallas kernels: none -> 0.72 us  [shards(): pl.pallas_call(functools.partial(rule_kernel, tiles=tiles), out_shape=(ba...]
    pallas_call x2, Pallas kernels: 2.14 us -> 1.43 us  [forecast(): pl.pallas_call(functools.partial(forecast_kernel, fields=fields, own=own)...]
    ppermute x5, waiting for transfers between devices: 0.85 us -> 0.27 us  [swap_cores(): lax.ppermute(x, BOTH, core_pairs(owners, lambda block, core: (block, 1 -...]
where the time goes in v8:
time: 31.4 us; the launch traced here: 31.2 us
  starting transfers between devices  18.2 us (58%)
  Pallas kernels  6.6 us (21%)
  waiting for transfers between devices  3.85 us (12%)
  local copies, waits for them, and re-layouts  1.81 us (6%)
  between operations  0.75 us (2%)
    ppermute x4, starting transfers between devices, exchange(): lax.ppermute(to_even, BOTH, core_pairs(owners, lambda block, core: (block...  8.98 us
    ppermute x4, starting transfers between devices, exchange(): lax.ppermute(to_odd, BOTH, core_pairs(owners, lambda block, core: (block...  6.02 us
    ppermute x5, starting transfers between devices, swap_cores(): lax.ppermute(x, BOTH, core_pairs(owners, lambda block, core: (block, 1 -...  3.18 us
    ppermute x4, waiting for transfers between devices, exchange(): lax.ppermute(to_even, BOTH, core_pairs(owners, lambda block, core: (block...  2.47 us
    pallas_call x1, Pallas kernels, shards(): pl.pallas_call(functools.partial(analysis_kernel, units=units, obs_rows=o...  2.37 us
    unnamed x20, local copies, waits for them, and re-layouts  1.81 us
    pallas_call x1, Pallas kernels, shards(): pl.pallas_call(functools.partial(sums_kernel, owners=owners, units=units,...  1.52 us
    pallas_call x2, Pallas kernels, forecast(): pl.pallas_call(functools.partial(forecast_kernel, fields=fields, own=own)...  1.43 us
  transfers between devices with their start and end apart: 13, of which 7 were waited for; matrix products, arithmetic and copies ran while one was open for 0% of the time, Pallas kernels for 8%

profile of v8, /device:TPU:0, one launch (start us, length us, event | category | flops | bytes accessed | tf_op | source)
XLA Modules:
  0.0 31.2 jit_solution(13568067748233328273)
XLA Ops:
  0.6 0.5 %collective-permute-start = (f32[32,4,1024]{2,1,0:T(4,128)}, f32[32,4,1024]{2,1,0:T(4,128)S(1)}, u32[]{:S(2)}, u32[]{:S(2)}) collective-permute-start(f32[32,4,1024]{2,1,0:T(4,128)} %ensemble_ref.1), channel_id=1, source_target_pairs={{0,1},{1,0},{2,3},{3,2},{4,5},{5,4},{6,7},{7,6},{8,9},{9,8},{10,11... | collective-permute-start | bytes 1572872 | tf_op jit(solution)/shard_map/ppermute | solution.py:42
  1.2 1.0 %copy-done = f32[32,4,1024]{2,1,0:T(4,128)S(1)} copy-done((f32[32,4,1024]{2,1,0:T(4,128)S(1)}, f32[32,4,1024]{2,1,0:T(4,128)}, u32[]{:S(2)}) %copy-start) | copy-done | bytes 524312
  2.4 0.5 %copy-done.5 = s32[256]{0:T(256)S(1)} copy-done((s32[256]{0:T(256)S(1)}, s32[256]{0:T(256)}, u32[]{:S(2)}) %copy-start.5) | copy-done | bytes 1048
  3.5 2.6 %collective-permute-start.1 = (f32[24,128]{1,0:T(8,128)S(1)}, f32[24,128]{1,0:T(8,128)S(1)}, u32[]{:S(2)}, u32[]{:S(2)}) collective-permute-start(f32[24,128]{1,0:T(8,128)S(1)} %get-tuple-element.40), channel_id=1, source_target_pairs={{0,2},{1,7},{2,0},{3,5},{4,6},{5,3},{6,4},{7,1},{8,10},{9,15},{10,... | collective-permute-start | bytes 36872 | tf_op jit(solution)/shard_map/ppermute | solution.py:46
  6.1 1.5 %collective-permute-start.3 = (f32[24,128]{1,0:T(8,128)S(1)}, f32[24,128]{1,0:T(8,128)S(1)}, u32[]{:S(2)}, u32[]{:S(2)}) collective-permute-start(f32[24,128]{1,0:T(8,128)S(1)} %get-tuple-element.41), channel_id=1, source_target_pairs={{0,4},{1,5},{2,6},{3,7},{4,0},{5,1},{6,2},{7,3},{8,12},{9,13},{10,... | collective-permute-start | bytes 36872 | tf_op jit(solution)/shard_map/ppermute | solution.py:49
  7.7 0.6 %collective-permute-start.2 = (f32[24,128]{1,0:T(8,128)S(1)}, f32[24,128]{1,0:T(8,128)S(1)}, u32[]{:S(2)}, u32[]{:S(2)}) collective-permute-start(f32[24,128]{1,0:T(8,128)S(1)} %collective-permute-done.1.odd), channel_id=1, source_target_pairs={{0,1},{1,0},{2,3},{3,2},{4,5},{5,4},{6,7},{7,6},{8,9},{9,8},{10,11... | collective-permute-start | bytes 36872 | tf_op jit(solution)/shard_map/ppermute | solution.py:42
  8.3 0.7 %rule.1 = (bf16[2048,256]{1,0:T(8,128)(2,1)S(1)}, f32[16,128]{1,0:T(8,128)S(1)}) custom-call(f32[4,4]{1,0:T(4,128)S(1)} %copy-done.9, f32[20,128]{1,0:T(8,128)S(1)} %get-tuple-element.27.small_ref), custom_call_target="tpu_custom_call" | custom-call | flops 5242880 | bytes 524288 | tf_op jit(solution)/shard_map/rule/pallas_call | solution.py:794
  9.0 0.7 %collective-permute-done.3.even = f32[24,128]{1,0:T(8,128)S(1)} collective-permute-done((f32[24,128]{1,0:T(8,128)S(1)}, f32[24,128]{1,0:T(8,128)S(1)}, u32[]{:S(2)}, u32[]{:S(2)}) %collective-permute-start.3) | collective-permute-done | bytes 12320 | tf_op jit(solution)/shard_map/ppermute | solution.py:49
  9.8 1.6 %collective-permute-start.4 = (f32[24,128]{1,0:T(8,128)S(1)}, f32[24,128]{1,0:T(8,128)S(1)}, u32[]{:S(2)}, u32[]{:S(2)}) collective-permute-start(f32[24,128]{1,0:T(8,128)S(1)} %get-tuple-element.43.refs_0_), channel_id=1, source_target_pairs={{0,8},{1,25},{2,10},{3,27},{4,12},{5,29},{6,14},{7,31},{8,0},{9,17... | collective-permute-start | bytes 36872 | tf_op jit(solution)/shard_map/ppermute | solution.py:46
  11.5 2.6 %collective-permute-start.6 = (f32[24,128]{1,0:T(8,128)S(1)}, f32[24,128]{1,0:T(8,128)S(1)}, u32[]{:S(2)}, u32[]{:S(2)}) collective-permute-start(f32[24,128]{1,0:T(8,128)S(1)} %get-tuple-element.44), channel_id=1, source_target_pairs={{0,16},{1,17},{2,18},{3,19},{4,20},{5,21},{6,22},{7,23},{8,24},{9,... | collective-permute-start | bytes 36872 | tf_op jit(solution)/shard_map/ppermute | solution.py:49
  14.1 0.4 %collective-permute-start.5 = (f32[24,128]{1,0:T(8,128)S(1)}, f32[24,128]{1,0:T(8,128)S(1)}, u32[]{:S(2)}, u32[]{:S(2)}) collective-permute-start(f32[24,128]{1,0:T(8,128)S(1)} %collective-permute-done.4.odd), channel_id=1, source_target_pairs={{0,1},{1,0},{2,3},{3,2},{4,5},{5,4},{6,7},{7,6},{8,9},{9,8},{10,11... | collective-permute-start | bytes 36872 | tf_op jit(solution)/shard_map/ppermute | solution.py:42
  14.4 0.6 %forecast.2 = (f32[128,1024]{1,0:T(8,128)S(1)}, f32[128,128]{1,0:T(8,128)S(1)}, f32[256,128]{1,0:T(8,128)S(1)}) custom-call(f32[16,128]{1,0:T(8,128)S(1)} %get-tuple-element.28.powers_ref._, f32[32,4,1024]{2,1,0:T(4,128)S(1)} %copy-done.1, bf16[2048,256]{1,0:T(8,128)(2,1)S(1)} %get-tuple-element.29.band_ref), custom_call_target="tpu_custom_call" | custom-call | flops 10485760 | bytes 1048576 | tf_op jit(solution)/shard_map/forecast/pallas_call | solution.py:776
  15.1 0.8 %forecast.3 = (f32[128,1024]{1,0:T(8,128)S(1)}, f32[128,128]{1,0:T(8,128)S(1)}, f32[256,128]{1,0:T(8,128)S(1)}, s32[4,128]{1,0:T(4,128)S(1)}, bf16[512,1024]{1,0:T(8,128)(2,1)S(1)}) custom-call(f32[16,128]{1,0:T(8,128)S(1)} %get-tuple-element.28.powers_ref._, f32[32,4,1024]{2,1,0:T(4,128)S(1)} %collective-permute-done.source.other_ref, ...), custom_call_target="tpu_custom_call" | custom-call | flops 10485760 | bytes 1048576 | tf_op jit(solution)/shard_map/forecast/pallas_call | solution.py:776
  16.2 1.5 %sums.1 = (f32[40,128]{1,0:T(8,128)S(1)}, f32[40,128]{1,0:T(8,128)S(1)}, f32[40,128]{1,0:T(8,128)S(1)}, f32[256,256]{1,0:T(8,128)S(1)}) custom-call(f32[16,128]{1,0:T(8,128)S(1)} %get-tuple-element.28.powers_ref._, f32[20,128]{1,0:T(8,128)S(1)} %get-tuple-element.27.small_ref, f32[128,1024]{1,0:T(8,128)S(1)} %get-tuple-element.30.refs_1_.own_state, ...), custom_call_target="tpu_custom_call" | custom-call | tf_op jit(solution)/shard_map/sums/pallas_call | solution.py:827
  17.8 0.5 %collective-permute-start.8 = (f32[40,128]{1,0:T(8,128)S(1)}, f32[40,128]{1,0:T(8,128)S(1)}, u32[]{:S(2)}, u32[]{:S(2)}) collective-permute-start(f32[40,128]{1,0:T(8,128)S(1)} %get-tuple-element.49), channel_id=1, source_target_pairs={{0,8},{1,25},{2,10},{3,27},{4,12},{5,29},{6,14},{7,31},{8,0},{9,17... | collective-permute-start | bytes 61448 | tf_op jit(solution)/shard_map/ppermute | solution.py:46
  18.3 3.3 %collective-permute-start.7 = (f32[40,128]{1,0:T(8,128)S(1)}, f32[40,128]{1,0:T(8,128)S(1)}, u32[]{:S(2)}, u32[]{:S(2)}) collective-permute-start(f32[40,128]{1,0:T(8,128)S(1)} %get-tuple-element.48), channel_id=1, source_target_pairs={{0,16},{1,17},{2,18},{3,19},{4,20},{5,21},{6,22},{7,23},{8,24},{9,... | collective-permute-start | bytes 61448 | tf_op jit(solution)/shard_map/ppermute | solution.py:49
  21.6 1.2 %collective-permute-start.9 = (f32[40,128]{1,0:T(8,128)S(1)}, f32[40,128]{1,0:T(8,128)S(1)}, u32[]{:S(2)}, u32[]{:S(2)}) collective-permute-start(f32[40,128]{1,0:T(8,128)S(1)} %collective-permute-done.8), channel_id=1, source_target_pairs={{0,1},{1,0},{2,3},{3,2},{4,5},{5,4},{6,7},{7,6},{8,9},{9,8},{10,11... | collective-permute-start | bytes 61448 | tf_op jit(solution)/shard_map/ppermute | solution.py:42
  22.8 0.6 %collective-permute-done.7 = f32[40,128]{1,0:T(8,128)S(1)} collective-permute-done((f32[40,128]{1,0:T(8,128)S(1)}, f32[40,128]{1,0:T(8,128)S(1)}, u32[]{:S(2)}, u32[]{:S(2)}) %collective-permute-start.7) | collective-permute-done | bytes 20512 | tf_op jit(solution)/shard_map/ppermute | solution.py:49
  23.7 1.3 %collective-permute-start.10 = (f32[40,128]{1,0:T(8,128)S(1)}, f32[40,128]{1,0:T(8,128)S(1)}, u32[]{:S(2)}, u32[]{:S(2)}) collective-permute-start(f32[40,128]{1,0:T(8,128)S(1)} %add_add_fusion.kept), channel_id=1, source_target_pairs={{0,2},{1,7},{2,0},{3,5},{4,6},{5,3},{6,4},{7,1},{8,10},{9,15},{10,... | collective-permute-start | bytes 61448 | tf_op jit(solution)/shard_map/ppermute | solution.py:46
  25.0 1.5 %collective-permute-start.12 = (f32[40,128]{1,0:T(8,128)S(1)}, f32[40,128]{1,0:T(8,128)S(1)}, u32[]{:S(2)}, u32[]{:S(2)}) collective-permute-start(f32[40,128]{1,0:T(8,128)S(1)} %add_add_fusion.kept), channel_id=1, source_target_pairs={{0,4},{1,5},{2,6},{3,7},{4,0},{5,1},{6,2},{7,3},{8,12},{9,13},{10,... | collective-permute-start | bytes 61448 | tf_op jit(solution)/shard_map/ppermute | solution.py:49
  26.5 0.9 %collective-permute-done.10.odd = f32[40,128]{1,0:T(8,128)S(1)} collective-permute-done((f32[40,128]{1,0:T(8,128)S(1)}, f32[40,128]{1,0:T(8,128)S(1)}, u32[]{:S(2)}, u32[]{:S(2)}) %collective-permute-start.10) | collective-permute-done | bytes 20512 | tf_op jit(solution)/shard_map/ppermute | solution.py:46
  27.5 0.5 %collective-permute-start.11 = (f32[40,128]{1,0:T(8,128)S(1)}, f32[40,128]{1,0:T(8,128)S(1)}, u32[]{:S(2)}, u32[]{:S(2)}) collective-permute-start(f32[40,128]{1,0:T(8,128)S(1)} %collective-permute-done.10.odd), channel_id=1, source_target_pairs={{0,1},{1,0},{2,3},{3,2},{4,5},{5,4},{6,7},{7,6},{8,9},{9,8},{10,11... | collective-permute-start | bytes 61448 | tf_op jit(solution)/shard_map/ppermute | solution.py:42
  28.0 0.8 %collective-permute-done.12.even = f32[40,128]{1,0:T(8,128)S(1)} collective-permute-done((f32[40,128]{1,0:T(8,128)S(1)}, f32[40,128]{1,0:T(8,128)S(1)}, u32[]{:S(2)}, u32[]{:S(2)}) %collective-permute-start.12) | collective-permute-done | bytes 20512 | tf_op jit(solution)/shard_map/ppermute | solution.py:49
  28.8 2.4 %analysis.1 = (f32[32,4,1024]{2,1,0:T(4,128)}, f32[2,128]{1,0:T(2,128)}) custom-call(bf16[512,1024]{1,0:T(8,128)(2,1)S(1)} %get-tuple-element.31.split_ref, f32[256,256]{1,0:T(8,128)S(1)} %get-tuple-element.45.edge_ref, f32[20,128]{1,0:T(8,128)S(1)} %get-tuple-element.27.small_ref, s32[4,128]{1,0:T(4,128)S(1)} %get-tuple-element.46.slots_ref, ...), custom_call_target="tpu_custom_call" | custom-call | tf_op jit(solution)/shard_map/analysis/pallas_call | solution.py:859
  (32 shorter events, 1.6 us)
Async XLA Ops:
  0.6 2.7 %collective-permute-start = (f32[32,4,1024]{2,1,0:T(4,128)}, f32[32,4,1024]{2,1,0:T(4,128)S(1)}, u32[]{:S(2)}, u32[]{:S(2)}) collective-permute-start(f32[32,4,1024]{2,1,0:T(4,128)} %ensemble_ref.1), channel_id=1, source_target_pairs={{0,1},{1,0},{2,3},{3,2},{4,5},{5,4},{6,7},{7,6},{8,9},{9,8},{10,11... | collective-permute-start | bytes 1572872 | tf_op jit(solution)/shard_map/ppermute | solution.py:42
  1.1 1.0 %copy-start = (f32[32,4,1024]{2,1,0:T(4,128)S(1)}, f32[32,4,1024]{2,1,0:T(4,128)}, u32[]{:S(2)}) copy-start(f32[32,4,1024]{2,1,0:T(4,128)} %ensemble_ref.1) | copy-start | bytes 1572868
  2.2 0.7 %copy-start.5 = (s32[256]{0:T(256)S(1)}, s32[256]{0:T(256)}, u32[]{:S(2)}) copy-start(s32[256]{0:T(256)} %param.13) | copy-start | bytes 3076
  2.2 0.7 %copy-start.6 = (s32[256]{0:T(256)S(1)}, s32[256]{0:T(256)}, u32[]{:S(2)}) copy-start(s32[256]{0:T(256)} %param.14) | copy-start | bytes 3076
  2.2 0.7 %copy-start.7 = (f32[256]{0:T(256)S(1)}, f32[256]{0:T(256)}, u32[]{:S(2)}) copy-start(f32[256]{0:T(256)} %param.15) | copy-start | bytes 3076
  2.2 0.7 %copy-start.8 = (f32[256]{0:T(256)S(1)}, f32[256]{0:T(256)}, u32[]{:S(2)}) copy-start(f32[256]{0:T(256)} %param.16) | copy-start | bytes 3076
  2.2 12.2 %copy-start.1 = (f32[32,4,1024]{2,1,0:T(4,128)S(1)}, f32[32,4,1024]{2,1,0:T(4,128)}, u32[]{:S(2)}) copy-start(f32[32,4,1024]{2,1,0:T(4,128)} %ensemble_ref.1) | copy-start | bytes 1572868
  2.3 0.8 %copy-start.3 = (s32[1024]{0:T(1024)S(1)}, s32[1024]{0:T(1024)}, u32[]{:S(2)}) copy-start(s32[1024]{0:T(1024)} %param.11) | copy-start | bytes 12292
  2.4 0.8 %copy-start.2 = (f32[1024]{0:T(1024)S(1)}, f32[1024]{0:T(1024)}, u32[]{:S(2)}) copy-start(f32[1024]{0:T(1024)} %param.10) | copy-start | bytes 12292
  2.4 0.7 %copy-start.4 = (s32[1,16]{1,0:T(1,128)S(1)}, s32[1,16]{1,0:T(1,128)}, u32[]{:S(2)}) copy-start(s32[1,16]{1,0:T(1,128)} %refs_0_.1) | copy-start | bytes 196
  3.5 4.8 %copy-start.9 = (f32[4,4]{1,0:T(4,128)S(1)}, f32[4,4]{1,0:T(4,128)}, u32[]{:S(2)}) copy-start(f32[4,4]{1,0:T(4,128)} %couple_ref.1) | copy-start | bytes 196
  3.5 4.2 %collective-permute-start.1 = (f32[24,128]{1,0:T(8,128)S(1)}, f32[24,128]{1,0:T(8,128)S(1)}, u32[]{:S(2)}, u32[]{:S(2)}) collective-permute-start(f32[24,128]{1,0:T(8,128)S(1)} %get-tuple-element.40), channel_id=1, source_target_pairs={{0,2},{1,7},{2,0},{3,5},{4,6},{5,3},{6,4},{7,1},{8,10},{9,15},{10,... | collective-permute-start | bytes 36872 | tf_op jit(solution)/shard_map/ppermute | solution.py:46
  6.1 3.7 %collective-permute-start.3 = (f32[24,128]{1,0:T(8,128)S(1)}, f32[24,128]{1,0:T(8,128)S(1)}, u32[]{:S(2)}, u32[]{:S(2)}) collective-permute-start(f32[24,128]{1,0:T(8,128)S(1)} %get-tuple-element.41), channel_id=1, source_target_pairs={{0,4},{1,5},{2,6},{3,7},{4,0},{5,1},{6,2},{7,3},{8,12},{9,13},{10,... | collective-permute-start | bytes 36872 | tf_op jit(solution)/shard_map/ppermute | solution.py:49
  7.7 2.0 %collective-permute-start.2 = (f32[24,128]{1,0:T(8,128)S(1)}, f32[24,128]{1,0:T(8,128)S(1)}, u32[]{:S(2)}, u32[]{:S(2)}) collective-permute-start(f32[24,128]{1,0:T(8,128)S(1)} %collective-permute-done.1.odd), channel_id=1, source_target_pairs={{0,1},{1,0},{2,3},{3,2},{4,5},{5,4},{6,7},{7,6},{8,9},{9,8},{10,11... | collective-permute-start | bytes 36872 | tf_op jit(solution)/shard_map/ppermute | solution.py:42
  9.8 4.2 %collective-permute-start.4 = (f32[24,128]{1,0:T(8,128)S(1)}, f32[24,128]{1,0:T(8,128)S(1)}, u32[]{:S(2)}, u32[]{:S(2)}) collective-permute-start(f32[24,128]{1,0:T(8,128)S(1)} %get-tuple-element.43.refs_0_), channel_id=1, source_target_pairs={{0,8},{1,25},{2,10},{3,27},{4,12},{5,29},{6,14},{7,31},{8,0},{9,17... | collective-permute-start | bytes 36872 | tf_op jit(solution)/shard_map/ppermute | solution.py:46
  11.5 4.7 %collective-permute-start.6 = (f32[24,128]{1,0:T(8,128)S(1)}, f32[24,128]{1,0:T(8,128)S(1)}, u32[]{:S(2)}, u32[]{:S(2)}) collective-permute-start(f32[24,128]{1,0:T(8,128)S(1)} %get-tuple-element.44), channel_id=1, source_target_pairs={{0,16},{1,17},{2,18},{3,19},{4,20},{5,21},{6,22},{7,23},{8,24},{9,... | collective-permute-start | bytes 36872 | tf_op jit(solution)/shard_map/ppermute | solution.py:49
  14.1 2.1 %collective-permute-start.5 = (f32[24,128]{1,0:T(8,128)S(1)}, f32[24,128]{1,0:T(8,128)S(1)}, u32[]{:S(2)}, u32[]{:S(2)}) collective-permute-start(f32[24,128]{1,0:T(8,128)S(1)} %collective-permute-done.4.odd), channel_id=1, source_target_pairs={{0,1},{1,0},{2,3},{3,2},{4,5},{5,4},{6,7},{7,6},{8,9},{9,8},{10,11... | collective-permute-start | bytes 36872 | tf_op jit(solution)/shard_map/ppermute | solution.py:42
  17.8 3.9 %collective-permute-start.8 = (f32[40,128]{1,0:T(8,128)S(1)}, f32[40,128]{1,0:T(8,128)S(1)}, u32[]{:S(2)}, u32[]{:S(2)}) collective-permute-start(f32[40,128]{1,0:T(8,128)S(1)} %get-tuple-element.49), channel_id=1, source_target_pairs={{0,8},{1,25},{2,10},{3,27},{4,12},{5,29},{6,14},{7,31},{8,0},{9,17... | collective-permute-start | bytes 61448 | tf_op jit(solution)/shard_map/ppermute | solution.py:46
  18.3 5.2 %collective-permute-start.7 = (f32[40,128]{1,0:T(8,128)S(1)}, f32[40,128]{1,0:T(8,128)S(1)}, u32[]{:S(2)}, u32[]{:S(2)}) collective-permute-start(f32[40,128]{1,0:T(8,128)S(1)} %get-tuple-element.48), channel_id=1, source_target_pairs={{0,16},{1,17},{2,18},{3,19},{4,20},{5,21},{6,22},{7,23},{8,24},{9,... | collective-permute-start | bytes 61448 | tf_op jit(solution)/shard_map/ppermute | solution.py:49
  21.6 2.1 %collective-permute-start.9 = (f32[40,128]{1,0:T(8,128)S(1)}, f32[40,128]{1,0:T(8,128)S(1)}, u32[]{:S(2)}, u32[]{:S(2)}) collective-permute-start(f32[40,128]{1,0:T(8,128)S(1)} %collective-permute-done.8), channel_id=1, source_target_pairs={{0,1},{1,0},{2,3},{3,2},{4,5},{5,4},{6,7},{7,6},{8,9},{9,8},{10,11... | collective-permute-start | bytes 61448 | tf_op jit(solution)/shard_map/ppermute | solution.py:42
  23.7 3.8 %collective-permute-start.10 = (f32[40,128]{1,0:T(8,128)S(1)}, f32[40,128]{1,0:T(8,128)S(1)}, u32[]{:S(2)}, u32[]{:S(2)}) collective-permute-start(f32[40,128]{1,0:T(8,128)S(1)} %add_add_fusion.kept), channel_id=1, source_target_pairs={{0,2},{1,7},{2,0},{3,5},{4,6},{5,3},{6,4},{7,1},{8,10},{9,15},{10,... | collective-permute-start | bytes 61448 | tf_op jit(solution)/shard_map/ppermute | solution.py:46
  25.0 3.8 %collective-permute-start.12 = (f32[40,128]{1,0:T(8,128)S(1)}, f32[40,128]{1,0:T(8,128)S(1)}, u32[]{:S(2)}, u32[]{:S(2)}) collective-permute-start(f32[40,128]{1,0:T(8,128)S(1)} %add_add_fusion.kept), channel_id=1, source_target_pairs={{0,4},{1,5},{2,6},{3,7},{4,0},{5,1},{6,2},{7,3},{8,12},{9,13},{10,... | collective-permute-start | bytes 61448 | tf_op jit(solution)/shard_map/ppermute | solution.py:49
  27.5 1.3 %collective-permute-start.11 = (f32[40,128]{1,0:T(8,128)S(1)}, f32[40,128]{1,0:T(8,128)S(1)}, u32[]{:S(2)}, u32[]{:S(2)}) collective-permute-start(f32[40,128]{1,0:T(8,128)S(1)} %collective-permute-done.10.odd), channel_id=1, source_target_pairs={{0,1},{1,0},{2,3},{3,2},{4,5},{5,4},{6,7},{7,6},{8,9},{9,8},{10,11... | collective-permute-start | bytes 61448 | tf_op jit(solution)/shard_map/ppermute | solution.py:42

commit v9 on v8

--- a/solution.py
+++ b/solution.py
@@ -302,31 +302,9 @@
         slots_ref[rows + r : rows + r + 1, :] = group * CAP + (slot - start).astype(jnp.int32)
 
 
-def rule_kernel(couple_ref, small_ref, band_ref, powers_ref, *, tiles):
-    fill_powers(couple_ref, powers_ref)
-    make_band = band_maker(small_ref, band_ref, tiles * LANES)
-    for t in range(tiles):
-        make_band(t)
-
-
-def forecast_kernel(powers_ref, source, band_ref, *refs, fields, own):
-    members, _, cells = source.shape
-    tiles = cells // LANES
+def fill_split(source, edge, split_ref, raw_ref):
+    members, fields, cells = source.shape
     height = fields * members
-    if own:
-        state, edge, sums_ref, split_ref, raw_ref = refs
-    else:
-        send_ref, own_state, state, edge, sums_ref, slots_ref, pieces_ref, split_ref, raw_ref = refs
-        fill_positions(send_ref, slots_ref)
-        core = here()[1]
-
-        def put_pieces(side, f, lanes, value):
-            for p, piece in enumerate(halves_of(value)):
-                at = pl.multiple_of((f * 2 + p) * 2 * members + side * members, 16)
-                pieces_ref[pl.ds(at, members), lanes] = piece
-
-        for f in range(fields):
-            put_pieces(core, f, slice(0, cells), own_state[f * members : (f + 1) * members, :])
     low = lax.broadcasted_iota(jnp.int32, (members, LANES), 1) < LANES // 2
     for f in range(fields):
         rows = slice(f * members, (f + 1) * members)
@@ -339,6 +317,39 @@
         )
         for p, piece in enumerate(halves_of(x)):
             split_ref[p * height + f * members : p * height + (f + 1) * members, :] = piece
+
+
+def rule_kernel(
+    couple_ref, small_ref, send_ref, source, band_ref, powers_ref, slots_ref, split_ref, edge, raw_ref, *, tiles,
+):
+    fill_split(source, edge, split_ref, raw_ref)
+    fill_powers(couple_ref, powers_ref)
+    fill_positions(send_ref, slots_ref)
+    make_band = band_maker(small_ref, band_ref, tiles * LANES)
+    for t in range(tiles):
+        make_band(t)
+
+
+def forecast_kernel(powers_ref, source, band_ref, *refs, fields, own):
+    cells = source.shape[-1]
+    members = source.shape[0] // (2 * fields) if own else source.shape[0]
+    tiles = cells // LANES
+    height = fields * members
+    if own:
+        split_ref, (state, sums_ref) = source, refs
+    else:
+        own_state, state, edge, sums_ref, pieces_ref, split_ref, raw_ref = refs
+        core = here()[1]
+
+        def put_pieces(side, f, lanes, value):
+            for p, piece in enumerate(halves_of(value)):
+                at = pl.multiple_of((f * 2 + p) * 2 * members + side * members, 16)
+                pieces_ref[pl.ds(at, members), lanes] = piece
+
+        for f in range(fields):
+            put_pieces(core, f, slice(0, cells), own_state[f * members : (f + 1) * members, :])
+    if not own:
+        fill_split(source, edge, split_ref, raw_ref)
     mix = powers_of(powers_ref, fields)
     nearer = lax.broadcasted_iota(jnp.int32, (2 * height, LANES), 1) < LANES // 2
     for t in range(tiles):
@@ -773,17 +784,17 @@
     pieces = jax.ShapeDtypeStruct((fields * 2 * total, cells), jnp.bfloat16)
 
     def forecast(operands, extra, own):
+        states = jax.ShapeDtypeStruct((strip_rows, cells), real)
+        edges = () if own else (jax.ShapeDtypeStruct((strip_rows, LANES), real),)
+        outs = (states,) + edges + (jax.ShapeDtypeStruct((places * 8, LANES), real),) + extra
         return pl.pallas_call(
             functools.partial(forecast_kernel, fields=fields, own=own),
-            out_shape=(
-                jax.ShapeDtypeStruct((strip_rows, cells), real),
-                jax.ShapeDtypeStruct((strip_rows, LANES), real),
-                jax.ShapeDtypeStruct((places * 8, LANES), real),
-            )
-            + extra,
+            out_shape=outs,
             in_specs=[whole] * len(operands),
-            out_specs=(whole,) * (3 + len(extra)),
-            scratch_shapes=[pltpu.VMEM((2 * strip_rows, cells), jnp.bfloat16), pltpu.VMEM((strip_rows, cells), real)],
+            out_specs=(whole,) * len(outs),
+            scratch_shapes=[]
+            if own
+            else [pltpu.VMEM((2 * strip_rows, cells), jnp.bfloat16), pltpu.VMEM((strip_rows, cells), real)],
             compiler_params=params,
             cost_estimate=pl.CostEstimate(
                 flops=80 * strip_rows * cells, bytes_accessed=8 * strip_rows * cells, transcendentals=0
@@ -791,18 +802,22 @@
             name="forecast",
         )(*operands)
 
-    rule, mixed = pl.pallas_call(
+    split_shape = jax.ShapeDtypeStruct((2 * strip_rows, cells), jnp.bfloat16)
+    edge_shape = jax.ShapeDtypeStruct((strip_rows, LANES), real)
+    rule, mixed, slots_of, own_split, own_edge = pl.pallas_call(
         functools.partial(rule_kernel, tiles=tiles),
-        out_shape=(band, powers),
-        in_specs=[whole] * 2,
-        out_specs=(whole,) * 2,
+        out_shape=(band, powers, slots, split_shape, edge_shape),
+        in_specs=[whole] * 4,
+        out_specs=(whole,) * 5,
+        scratch_shapes=[pltpu.VMEM((strip_rows, cells), real)],
         compiler_params=params,
         cost_estimate=pl.CostEstimate(
             flops=40 * strip_rows * cells, bytes_accessed=4 * strip_rows * cells, transcendentals=0
         ),
         name="rule",
-    )(couple, small)
-    own_forecast = forecast((mixed, ensemble, rule), (), True)
+    )(couple, small, send_count, ensemble)
+    own_state, own_sums = forecast((mixed, own_split, rule), (), True)
+    own_forecast = (own_state, own_edge, own_sums)
     carried = []
     for n, unit in enumerate(units):
         arrived = exchange(to_odd, to_even, owners, unit)
@@ -816,9 +831,7 @@
                 name="regroup",
             )(kept, *arrived, mixed)
             carried.append(to_odd)
-    *other_forecast, slots_of, split = forecast(
-        (mixed, other, rule, send_count, own_forecast[0]), (slots, pieces), False
-    )
+    *other_forecast, split = forecast((mixed, other, rule, own_forecast[0]), (pieces,), False)
 
     held = kept.shape[0] // 8
     sums_rows = -(-(members + 1 + 4 * held) // 8) * 8

time: 31.4 us -> 31.3 us (level)
  waiting for transfers between devices: 3.85 us -> 4.23 us
  transfers between devices with their start and end apart: 13 -> 13, of which waited for: 7 -> 8; matrix products, arithmetic and copies ran while one was open for 0% -> 0% of each run, Pallas kernels for 8% -> 8%
where the time goes in v9:
time: 31.3 us; the launch traced here: 31.2 us
  starting transfers between devices  17.9 us (57%)
  Pallas kernels  6.5 us (21%)
  waiting for transfers between devices  4.23 us (14%)
  local copies, waits for them, and re-layouts  1.81 us (6%)
  between operations  0.75 us (2%)
    ppermute x4, starting transfers between devices, exchange(): lax.ppermute(to_even, BOTH, core_pairs(owners, lambda block, core: (block...  8.84 us
    ppermute x4, starting transfers between devices, exchange(): lax.ppermute(to_odd, BOTH, core_pairs(owners, lambda block, core: (block...  6.02 us
    ppermute x5, starting transfers between devices, swap_cores(): lax.ppermute(x, BOTH, core_pairs(owners, lambda block, core: (block, 1 -...  3 us
    ppermute x4, waiting for transfers between devices, exchange(): lax.ppermute(to_even, BOTH, core_pairs(owners, lambda block, core: (block...  2.76 us
    pallas_call x1, Pallas kernels, shards(): pl.pallas_call(functools.partial(analysis_kernel, units=units, obs_rows=o...  2.37 us
    unnamed x20, local copies, waits for them, and re-layouts  1.81 us
    pallas_call x1, Pallas kernels, shards(): pl.pallas_call(functools.partial(sums_kernel, owners=owners, units=units,...  1.53 us
    pallas_call x2, Pallas kernels, forecast(): pl.pallas_call(functools.partial(forecast_kernel, fields=fields, own=own)...  1.31 us
  transfers between devices with their start and end apart: 13, of which 8 were waited for; matrix products, arithmetic and copies ran while one was open for 0% of the time, Pallas kernels for 8%

profile of v9, /device:TPU:0, one launch (start us, length us, event | category | flops | bytes accessed | tf_op | source)
XLA Modules:
  0.0 31.2 jit_solution(6944195299034214486)
XLA Ops:
  0.6 0.5 %collective-permute-start = (f32[32,4,1024]{2,1,0:T(4,128)}, f32[32,4,1024]{2,1,0:T(4,128)S(1)}, u32[]{:S(2)}, u32[]{:S(2)}) collective-permute-start(f32[32,4,1024]{2,1,0:T(4,128)} %ensemble_ref.1), channel_id=1, source_target_pairs={{0,1},{1,0},{2,3},{3,2},{4,5},{5,4},{6,7},{7,6},{8,9},{9,8},{10,11... | collective-permute-start | bytes 1572872 | tf_op jit(solution)/shard_map/ppermute | solution.py:42
  1.2 1.0 %copy-done = f32[32,4,1024]{2,1,0:T(4,128)S(1)} copy-done((f32[32,4,1024]{2,1,0:T(4,128)S(1)}, f32[32,4,1024]{2,1,0:T(4,128)}, u32[]{:S(2)}) %copy-start) | copy-done | bytes 524312
  2.4 0.5 %copy-done.6 = s32[256]{0:T(256)S(1)} copy-done((s32[256]{0:T(256)S(1)}, s32[256]{0:T(256)}, u32[]{:S(2)}) %copy-start.6) | copy-done | bytes 1048
  3.5 2.6 %collective-permute-start.1 = (f32[24,128]{1,0:T(8,128)S(1)}, f32[24,128]{1,0:T(8,128)S(1)}, u32[]{:S(2)}, u32[]{:S(2)}) collective-permute-start(f32[24,128]{1,0:T(8,128)S(1)} %get-tuple-element.42), channel_id=1, source_target_pairs={{0,2},{1,7},{2,0},{3,5},{4,6},{5,3},{6,4},{7,1},{8,10},{9,15},{10,... | collective-permute-start | bytes 36872 | tf_op jit(solution)/shard_map/ppermute | solution.py:46
  6.1 1.5 %collective-permute-start.3 = (f32[24,128]{1,0:T(8,128)S(1)}, f32[24,128]{1,0:T(8,128)S(1)}, u32[]{:S(2)}, u32[]{:S(2)}) collective-permute-start(f32[24,128]{1,0:T(8,128)S(1)} %get-tuple-element.43), channel_id=1, source_target_pairs={{0,4},{1,5},{2,6},{3,7},{4,0},{5,1},{6,2},{7,3},{8,12},{9,13},{10,... | collective-permute-start | bytes 36872 | tf_op jit(solution)/shard_map/ppermute | solution.py:49
  7.7 0.6 %collective-permute-start.2 = (f32[24,128]{1,0:T(8,128)S(1)}, f32[24,128]{1,0:T(8,128)S(1)}, u32[]{:S(2)}, u32[]{:S(2)}) collective-permute-start(f32[24,128]{1,0:T(8,128)S(1)} %collective-permute-done.1.odd), channel_id=1, source_target_pairs={{0,1},{1,0},{2,3},{3,2},{4,5},{5,4},{6,7},{7,6},{8,9},{9,8},{10,11... | collective-permute-start | bytes 36872 | tf_op jit(solution)/shard_map/ppermute | solution.py:42
  8.3 0.7 %rule.1 = (bf16[2048,256]{1,0:T(8,128)(2,1)S(1)}, f32[16,128]{1,0:T(8,128)S(1)}, s32[4,128]{1,0:T(4,128)S(1)}, bf16[256,1024]{1,0:T(8,128)(2,1)S(1)}, f32[128,128]{1,0:T(8,128)S(1)}) custom-call(f32[4,4]{1,0:T(4,128)S(1)} %copy-done.4, f32[20,128]{1,0:T(8,128)S(1)} %get-tuple-element.28.small_ref, s32[1,16]{1,0:T(1,128)S(1)} %copy-done.5, ...), custom_call_target="tpu_custom_call" | custom-call | flops 5242880 | bytes 524288 | tf_op jit(solution)/shard_map/rule/pallas_call | solution.py:807
  9.1 0.7 %collective-permute-done.3.even = f32[24,128]{1,0:T(8,128)S(1)} collective-permute-done((f32[24,128]{1,0:T(8,128)S(1)}, f32[24,128]{1,0:T(8,128)S(1)}, u32[]{:S(2)}, u32[]{:S(2)}) %collective-permute-start.3) | collective-permute-done | bytes 12320 | tf_op jit(solution)/shard_map/ppermute | solution.py:49
  9.8 1.6 %collective-permute-start.4 = (f32[24,128]{1,0:T(8,128)S(1)}, f32[24,128]{1,0:T(8,128)S(1)}, u32[]{:S(2)}, u32[]{:S(2)}) collective-permute-start(f32[24,128]{1,0:T(8,128)S(1)} %get-tuple-element.45.refs_0_), channel_id=1, source_target_pairs={{0,8},{1,25},{2,10},{3,27},{4,12},{5,29},{6,14},{7,31},{8,0},{9,17... | collective-permute-start | bytes 36872 | tf_op jit(solution)/shard_map/ppermute | solution.py:46
  11.5 2.6 %collective-permute-start.6 = (f32[24,128]{1,0:T(8,128)S(1)}, f32[24,128]{1,0:T(8,128)S(1)}, u32[]{:S(2)}, u32[]{:S(2)}) collective-permute-start(f32[24,128]{1,0:T(8,128)S(1)} %get-tuple-element.46), channel_id=1, source_target_pairs={{0,16},{1,17},{2,18},{3,19},{4,20},{5,21},{6,22},{7,23},{8,24},{9,... | collective-permute-start | bytes 36872 | tf_op jit(solution)/shard_map/ppermute | solution.py:49
  14.1 0.4 %collective-permute-start.5 = (f32[24,128]{1,0:T(8,128)S(1)}, f32[24,128]{1,0:T(8,128)S(1)}, u32[]{:S(2)}, u32[]{:S(2)}) collective-permute-start(f32[24,128]{1,0:T(8,128)S(1)} %collective-permute-done.4.odd), channel_id=1, source_target_pairs={{0,1},{1,0},{2,3},{3,2},{4,5},{5,4},{6,7},{7,6},{8,9},{9,8},{10,11... | collective-permute-start | bytes 36872 | tf_op jit(solution)/shard_map/ppermute | solution.py:42
  14.4 0.5 %forecast.2 = (f32[128,1024]{1,0:T(8,128)S(1)}, f32[256,128]{1,0:T(8,128)S(1)}) custom-call(f32[16,128]{1,0:T(8,128)S(1)} %get-tuple-element.29.powers_ref._, bf16[256,1024]{1,0:T(8,128)(2,1)S(1)} %get-tuple-element.31.source, bf16[2048,256]{1,0:T(8,128)(2,1)S(1)} %get-tuple-element.30.band_ref), custom_call_target="tpu_custom_call" | custom-call | flops 10485760 | bytes 1048576 | tf_op jit(solution)/shard_map/forecast/pallas_call | solution.py:790
  15.0 0.8 %forecast.3 = (f32[128,1024]{1,0:T(8,128)S(1)}, f32[128,128]{1,0:T(8,128)S(1)}, f32[256,128]{1,0:T(8,128)S(1)}, bf16[512,1024]{1,0:T(8,128)(2,1)S(1)}) custom-call(f32[16,128]{1,0:T(8,128)S(1)} %get-tuple-element.29.powers_ref._, f32[32,4,1024]{2,1,0:T(4,128)S(1)} %collective-permute-done.source.other_ref, bf16[2048,256]{1,0:T(8,128)(2,1)S(1)} %get-tuple-element.30.band_ref, ...), custom_call_target="tpu_custom_call" | custom-call | flops 10485760 | bytes 1048576 | tf_op jit(solution)/shard_map/forecast/pallas_call | solution.py:790
  15.8 0.5 %collective-permute-done.6.even = f32[24,128]{1,0:T(8,128)S(1)} collective-permute-done((f32[24,128]{1,0:T(8,128)S(1)}, f32[24,128]{1,0:T(8,128)S(1)}, u32[]{:S(2)}, u32[]{:S(2)}) %collective-permute-start.6) | collective-permute-done | bytes 12320 | tf_op jit(solution)/shard_map/ppermute | solution.py:49
  16.2 1.5 %sums.1 = (f32[40,128]{1,0:T(8,128)S(1)}, f32[40,128]{1,0:T(8,128)S(1)}, f32[40,128]{1,0:T(8,128)S(1)}, f32[256,256]{1,0:T(8,128)S(1)}) custom-call(f32[16,128]{1,0:T(8,128)S(1)} %get-tuple-element.29.powers_ref._, f32[20,128]{1,0:T(8,128)S(1)} %get-tuple-element.28.small_ref, f32[128,1024]{1,0:T(8,128)S(1)} %get-tuple-element.32.refs_0_.own_state, ...), custom_call_target="tpu_custom_call" | custom-call | tf_op jit(solution)/shard_map/sums/pallas_call | solution.py:840
  17.8 0.5 %collective-permute-start.8 = (f32[40,128]{1,0:T(8,128)S(1)}, f32[40,128]{1,0:T(8,128)S(1)}, u32[]{:S(2)}, u32[]{:S(2)}) collective-permute-start(f32[40,128]{1,0:T(8,128)S(1)} %get-tuple-element.51), channel_id=1, source_target_pairs={{0,8},{1,25},{2,10},{3,27},{4,12},{5,29},{6,14},{7,31},{8,0},{9,17... | collective-permute-start | bytes 61448 | tf_op jit(solution)/shard_map/ppermute | solution.py:46
  18.3 3.2 %collective-permute-start.7 = (f32[40,128]{1,0:T(8,128)S(1)}, f32[40,128]{1,0:T(8,128)S(1)}, u32[]{:S(2)}, u32[]{:S(2)}) collective-permute-start(f32[40,128]{1,0:T(8,128)S(1)} %get-tuple-element.50), channel_id=1, source_target_pairs={{0,16},{1,17},{2,18},{3,19},{4,20},{5,21},{6,22},{7,23},{8,24},{9,... | collective-permute-start | bytes 61448 | tf_op jit(solution)/shard_map/ppermute | solution.py:49
  21.6 1.2 %collective-permute-start.9 = (f32[40,128]{1,0:T(8,128)S(1)}, f32[40,128]{1,0:T(8,128)S(1)}, u32[]{:S(2)}, u32[]{:S(2)}) collective-permute-start(f32[40,128]{1,0:T(8,128)S(1)} %collective-permute-done.8), channel_id=1, source_target_pairs={{0,1},{1,0},{2,3},{3,2},{4,5},{5,4},{6,7},{7,6},{8,9},{9,8},{10,11... | collective-permute-start | bytes 61448 | tf_op jit(solution)/shard_map/ppermute | solution.py:42
  22.8 0.6 %collective-permute-done.7 = f32[40,128]{1,0:T(8,128)S(1)} collective-permute-done((f32[40,128]{1,0:T(8,128)S(1)}, f32[40,128]{1,0:T(8,128)S(1)}, u32[]{:S(2)}, u32[]{:S(2)}) %collective-permute-start.7) | collective-permute-done | bytes 20512 | tf_op jit(solution)/shard_map/ppermute | solution.py:49
  23.7 1.3 %collective-permute-start.10 = (f32[40,128]{1,0:T(8,128)S(1)}, f32[40,128]{1,0:T(8,128)S(1)}, u32[]{:S(2)}, u32[]{:S(2)}) collective-permute-start(f32[40,128]{1,0:T(8,128)S(1)} %add_add_fusion.kept), channel_id=1, source_target_pairs={{0,2},{1,7},{2,0},{3,5},{4,6},{5,3},{6,4},{7,1},{8,10},{9,15},{10,... | collective-permute-start | bytes 61448 | tf_op jit(solution)/shard_map/ppermute | solution.py:46
  25.0 1.5 %collective-permute-start.12 = (f32[40,128]{1,0:T(8,128)S(1)}, f32[40,128]{1,0:T(8,128)S(1)}, u32[]{:S(2)}, u32[]{:S(2)}) collective-permute-start(f32[40,128]{1,0:T(8,128)S(1)} %add_add_fusion.kept), channel_id=1, source_target_pairs={{0,4},{1,5},{2,6},{3,7},{4,0},{5,1},{6,2},{7,3},{8,12},{9,13},{10,... | collective-permute-start | bytes 61448 | tf_op jit(solution)/shard_map/ppermute | solution.py:49
  26.5 1.0 %collective-permute-done.10.odd = f32[40,128]{1,0:T(8,128)S(1)} collective-permute-done((f32[40,128]{1,0:T(8,128)S(1)}, f32[40,128]{1,0:T(8,128)S(1)}, u32[]{:S(2)}, u32[]{:S(2)}) %collective-permute-start.10) | collective-permute-done | bytes 20512 | tf_op jit(solution)/shard_map/ppermute | solution.py:46
  27.8 1.0 %collective-permute-done.12.even = f32[40,128]{1,0:T(8,128)S(1)} collective-permute-done((f32[40,128]{1,0:T(8,128)S(1)}, f32[40,128]{1,0:T(8,128)S(1)}, u32[]{:S(2)}, u32[]{:S(2)}) %collective-permute-start.12) | collective-permute-done | bytes 20512 | tf_op jit(solution)/shard_map/ppermute | solution.py:49
  28.8 2.4 %analysis.1 = (f32[32,4,1024]{2,1,0:T(4,128)}, f32[2,128]{1,0:T(2,128)}) custom-call(bf16[512,1024]{1,0:T(8,128)(2,1)S(1)} %get-tuple-element.33.split_ref, f32[256,256]{1,0:T(8,128)S(1)} %get-tuple-element.47.edge_ref, f32[20,128]{1,0:T(8,128)S(1)} %get-tuple-element.28.small_ref, s32[4,128]{1,0:T(4,128)S(1)} %get-tuple-element.48.slots_ref, ...), custom_call_target="tpu_custom_call" | custom-call | tf_op jit(solution)/shard_map/analysis/pallas_call | solution.py:872
  (32 shorter events, 1.7 us)
Async XLA Ops:
  0.6 2.7 %collective-permute-start = (f32[32,4,1024]{2,1,0:T(4,128)}, f32[32,4,1024]{2,1,0:T(4,128)S(1)}, u32[]{:S(2)}, u32[]{:S(2)}) collective-permute-start(f32[32,4,1024]{2,1,0:T(4,128)} %ensemble_ref.1), channel_id=1, source_target_pairs={{0,1},{1,0},{2,3},{3,2},{4,5},{5,4},{6,7},{7,6},{8,9},{9,8},{10,11... | collective-permute-start | bytes 1572872 | tf_op jit(solution)/shard_map/ppermute | solution.py:42
  1.1 1.0 %copy-start = (f32[32,4,1024]{2,1,0:T(4,128)S(1)}, f32[32,4,1024]{2,1,0:T(4,128)}, u32[]{:S(2)}) copy-start(f32[32,4,1024]{2,1,0:T(4,128)} %ensemble_ref.1) | copy-start | bytes 1572868
  2.2 0.7 %copy-start.6 = (s32[256]{0:T(256)S(1)}, s32[256]{0:T(256)}, u32[]{:S(2)}) copy-start(s32[256]{0:T(256)} %param.13) | copy-start | bytes 3076
  2.2 0.7 %copy-start.7 = (s32[256]{0:T(256)S(1)}, s32[256]{0:T(256)}, u32[]{:S(2)}) copy-start(s32[256]{0:T(256)} %param.14) | copy-start | bytes 3076
  2.2 0.7 %copy-start.8 = (f32[256]{0:T(256)S(1)}, f32[256]{0:T(256)}, u32[]{:S(2)}) copy-start(f32[256]{0:T(256)} %param.15) | copy-start | bytes 3076
  2.2 0.7 %copy-start.9 = (f32[256]{0:T(256)S(1)}, f32[256]{0:T(256)}, u32[]{:S(2)}) copy-start(f32[256]{0:T(256)} %param.16) | copy-start | bytes 3076
  2.2 6.1 %copy-start.1 = (f32[32,4,1024]{2,1,0:T(4,128)S(1)}, f32[32,4,1024]{2,1,0:T(4,128)}, u32[]{:S(2)}) copy-start(f32[32,4,1024]{2,1,0:T(4,128)} %ensemble_ref.1) | copy-start | bytes 1572868
  2.3 0.8 %copy-start.3 = (s32[1024]{0:T(1024)S(1)}, s32[1024]{0:T(1024)}, u32[]{:S(2)}) copy-start(s32[1024]{0:T(1024)} %param.11) | copy-start | bytes 12292
  2.4 0.8 %copy-start.2 = (f32[1024]{0:T(1024)S(1)}, f32[1024]{0:T(1024)}, u32[]{:S(2)}) copy-start(f32[1024]{0:T(1024)} %param.10) | copy-start | bytes 12292
  2.4 0.7 %copy-start.5 = (s32[1,16]{1,0:T(1,128)S(1)}, s32[1,16]{1,0:T(1,128)}, u32[]{:S(2)}) copy-start(s32[1,16]{1,0:T(1,128)} %send_ref.3) | copy-start | bytes 196
  3.5 4.8 %copy-start.4 = (f32[4,4]{1,0:T(4,128)S(1)}, f32[4,4]{1,0:T(4,128)}, u32[]{:S(2)}) copy-start(f32[4,4]{1,0:T(4,128)} %couple_ref.1) | copy-start | bytes 196
  3.5 4.2 %collective-permute-start.1 = (f32[24,128]{1,0:T(8,128)S(1)}, f32[24,128]{1,0:T(8,128)S(1)}, u32[]{:S(2)}, u32[]{:S(2)}) collective-permute-start(f32[24,128]{1,0:T(8,128)S(1)} %get-tuple-element.42), channel_id=1, source_target_pairs={{0,2},{1,7},{2,0},{3,5},{4,6},{5,3},{6,4},{7,1},{8,10},{9,15},{10,... | collective-permute-start | bytes 36872 | tf_op jit(solution)/shard_map/ppermute | solution.py:46
  6.1 3.7 %collective-permute-start.3 = (f32[24,128]{1,0:T(8,128)S(1)}, f32[24,128]{1,0:T(8,128)S(1)}, u32[]{:S(2)}, u32[]{:S(2)}) collective-permute-start(f32[24,128]{1,0:T(8,128)S(1)} %get-tuple-element.43), channel_id=1, source_target_pairs={{0,4},{1,5},{2,6},{3,7},{4,0},{5,1},{6,2},{7,3},{8,12},{9,13},{10,... | collective-permute-start | bytes 36872 | tf_op jit(solution)/shard_map/ppermute | solution.py:49
  7.7 2.0 %collective-permute-start.2 = (f32[24,128]{1,0:T(8,128)S(1)}, f32[24,128]{1,0:T(8,128)S(1)}, u32[]{:S(2)}, u32[]{:S(2)}) collective-permute-start(f32[24,128]{1,0:T(8,128)S(1)} %collective-permute-done.1.odd), channel_id=1, source_target_pairs={{0,1},{1,0},{2,3},{3,2},{4,5},{5,4},{6,7},{7,6},{8,9},{9,8},{10,11... | collective-permute-start | bytes 36872 | tf_op jit(solution)/shard_map/ppermute | solution.py:42
  9.8 4.2 %collective-permute-start.4 = (f32[24,128]{1,0:T(8,128)S(1)}, f32[24,128]{1,0:T(8,128)S(1)}, u32[]{:S(2)}, u32[]{:S(2)}) collective-permute-start(f32[24,128]{1,0:T(8,128)S(1)} %get-tuple-element.45.refs_0_), channel_id=1, source_target_pairs={{0,8},{1,25},{2,10},{3,27},{4,12},{5,29},{6,14},{7,31},{8,0},{9,17... | collective-permute-start | bytes 36872 | tf_op jit(solution)/shard_map/ppermute | solution.py:46
  11.5 4.7 %collective-permute-start.6 = (f32[24,128]{1,0:T(8,128)S(1)}, f32[24,128]{1,0:T(8,128)S(1)}, u32[]{:S(2)}, u32[]{:S(2)}) collective-permute-start(f32[24,128]{1,0:T(8,128)S(1)} %get-tuple-element.46), channel_id=1, source_target_pairs={{0,16},{1,17},{2,18},{3,19},{4,20},{5,21},{6,22},{7,23},{8,24},{9,... | collective-permute-start | bytes 36872 | tf_op jit(solution)/shard_map/ppermute | solution.py:49
  14.1 2.1 %collective-permute-start.5 = (f32[24,128]{1,0:T(8,128)S(1)}, f32[24,128]{1,0:T(8,128)S(1)}, u32[]{:S(2)}, u32[]{:S(2)}) collective-permute-start(f32[24,128]{1,0:T(8,128)S(1)} %collective-permute-done.4.odd), channel_id=1, source_target_pairs={{0,1},{1,0},{2,3},{3,2},{4,5},{5,4},{6,7},{7,6},{8,9},{9,8},{10,11... | collective-permute-start | bytes 36872 | tf_op jit(solution)/shard_map/ppermute | solution.py:42
  17.8 3.8 %collective-permute-start.8 = (f32[40,128]{1,0:T(8,128)S(1)}, f32[40,128]{1,0:T(8,128)S(1)}, u32[]{:S(2)}, u32[]{:S(2)}) collective-permute-start(f32[40,128]{1,0:T(8,128)S(1)} %get-tuple-element.51), channel_id=1, source_target_pairs={{0,8},{1,25},{2,10},{3,27},{4,12},{5,29},{6,14},{7,31},{8,0},{9,17... | collective-permute-start | bytes 61448 | tf_op jit(solution)/shard_map/ppermute | solution.py:46
  18.3 5.2 %collective-permute-start.7 = (f32[40,128]{1,0:T(8,128)S(1)}, f32[40,128]{1,0:T(8,128)S(1)}, u32[]{:S(2)}, u32[]{:S(2)}) collective-permute-start(f32[40,128]{1,0:T(8,128)S(1)} %get-tuple-element.50), channel_id=1, source_target_pairs={{0,16},{1,17},{2,18},{3,19},{4,20},{5,21},{6,22},{7,23},{8,24},{9,... | collective-permute-start | bytes 61448 | tf_op jit(solution)/shard_map/ppermute | solution.py:49
  21.6 2.1 %collective-permute-start.9 = (f32[40,128]{1,0:T(8,128)S(1)}, f32[40,128]{1,0:T(8,128)S(1)}, u32[]{:S(2)}, u32[]{:S(2)}) collective-permute-start(f32[40,128]{1,0:T(8,128)S(1)} %collective-permute-done.8), channel_id=1, source_target_pairs={{0,1},{1,0},{2,3},{3,2},{4,5},{5,4},{6,7},{7,6},{8,9},{9,8},{10,11... | collective-permute-start | bytes 61448 | tf_op jit(solution)/shard_map/ppermute | solution.py:42
  23.7 3.8 %collective-permute-start.10 = (f32[40,128]{1,0:T(8,128)S(1)}, f32[40,128]{1,0:T(8,128)S(1)}, u32[]{:S(2)}, u32[]{:S(2)}) collective-permute-start(f32[40,128]{1,0:T(8,128)S(1)} %add_add_fusion.kept), channel_id=1, source_target_pairs={{0,2},{1,7},{2,0},{3,5},{4,6},{5,3},{6,4},{7,1},{8,10},{9,15},{10,... | collective-permute-start | bytes 61448 | tf_op jit(solution)/shard_map/ppermute | solution.py:46
  25.0 3.8 %collective-permute-start.12 = (f32[40,128]{1,0:T(8,128)S(1)}, f32[40,128]{1,0:T(8,128)S(1)}, u32[]{:S(2)}, u32[]{:S(2)}) collective-permute-start(f32[40,128]{1,0:T(8,128)S(1)} %add_add_fusion.kept), channel_id=1, source_target_pairs={{0,4},{1,5},{2,6},{3,7},{4,0},{5,1},{6,2},{7,3},{8,12},{9,13},{10,... | collective-permute-start | bytes 61448 | tf_op jit(solution)/shard_map/ppermute | solution.py:49
  27.5 1.3 %collective-permute-start.11 = (f32[40,128]{1,0:T(8,128)S(1)}, f32[40,128]{1,0:T(8,128)S(1)}, u32[]{:S(2)}, u32[]{:S(2)}) collective-permute-start(f32[40,128]{1,0:T(8,128)S(1)} %collective-permute-done.10.odd), channel_id=1, source_target_pairs={{0,1},{1,0},{2,3},{3,2},{4,5},{5,4},{6,7},{7,6},{8,9},{9,8},{10,11... | collective-permute-start | bytes 61448 | tf_op jit(solution)/shard_map/ppermute | solution.py:42

commit v10 on v9

--- a/solution.py
+++ b/solution.py
@@ -596,7 +596,7 @@
             scale = lax.rsqrt(spread_row(own[j][j : j + 1, :]))
             upper = spread_row(rows[b][j : j + 1, :]) * scale
             lower = own[j] * scale
-            factors = {k: spread_row(lower[k : k + 1, :]) for k in range(j + 1, 8)}
+            factors = {k: spread_row(own[j][k : k + 1, :]) * scale for k in range(j + 1, 8)}
             for k in range(j + 1, 8):
                 own[k] = own[k] - lower * factors[k]
             rows[b] = jnp.where(sub == j, upper, rows[b] - jnp.where(sub > j, lower, 0.0) * upper)

time: 31.3 us -> 31.2 us (level)
  no operation moved by 1% of the time
where the time goes in v10:
time: 31.2 us; the launch traced here: 31.1 us
  starting transfers between devices  17.9 us (57%)
  Pallas kernels  6.41 us (21%)
  waiting for transfers between devices  4.23 us (14%)
  local copies, waits for them, and re-layouts  1.81 us (6%)
  between operations  0.75 us (2%)
    ppermute x4, starting transfers between devices, exchange(): lax.ppermute(to_even, BOTH, core_pairs(owners, lambda block, core: (block...  8.84 us
    ppermute x4, starting transfers between devices, exchange(): lax.ppermute(to_odd, BOTH, core_pairs(owners, lambda block, core: (block...  6.02 us
    ppermute x5, starting transfers between devices, swap_cores(): lax.ppermute(x, BOTH, core_pairs(owners, lambda block, core: (block, 1 -...  3 us
    ppermute x4, waiting for transfers between devices, exchange(): lax.ppermute(to_even, BOTH, core_pairs(owners, lambda block, core: (block...  2.76 us
    pallas_call x1, Pallas kernels, shards(): pl.pallas_call(functools.partial(analysis_kernel, units=units, obs_rows=o...  2.28 us
    unnamed x20, local copies, waits for them, and re-layouts  1.81 us
    pallas_call x1, Pallas kernels, shards(): pl.pallas_call(functools.partial(sums_kernel, owners=owners, units=units,...  1.53 us
    pallas_call x2, Pallas kernels, forecast(): pl.pallas_call(functools.partial(forecast_kernel, fields=fields, own=own)...  1.31 us
  transfers between devices with their start and end apart: 13, of which 8 were waited for; matrix products, arithmetic and copies ran while one was open for 0% of the time, Pallas kernels for 8%

profile of v10, /device:TPU:0, one launch (start us, length us, event | category | flops | bytes accessed | tf_op | source)
XLA Modules:
  0.0 31.1 jit_solution(15597000024014115056)
XLA Ops:
  0.6 0.5 %collective-permute-start = (f32[32,4,1024]{2,1,0:T(4,128)}, f32[32,4,1024]{2,1,0:T(4,128)S(1)}, u32[]{:S(2)}, u32[]{:S(2)}) collective-permute-start(f32[32,4,1024]{2,1,0:T(4,128)} %ensemble_ref.1), channel_id=1, source_target_pairs={{0,1},{1,0},{2,3},{3,2},{4,5},{5,4},{6,7},{7,6},{8,9},{9,8},{10,11... | collective-permute-start | bytes 1572872 | tf_op jit(solution)/shard_map/ppermute | solution.py:42
  1.2 1.0 %copy-done = f32[32,4,1024]{2,1,0:T(4,128)S(1)} copy-done((f32[32,4,1024]{2,1,0:T(4,128)S(1)}, f32[32,4,1024]{2,1,0:T(4,128)}, u32[]{:S(2)}) %copy-start) | copy-done | bytes 524312
  2.4 0.5 %copy-done.6 = s32[256]{0:T(256)S(1)} copy-done((s32[256]{0:T(256)S(1)}, s32[256]{0:T(256)}, u32[]{:S(2)}) %copy-start.6) | copy-done | bytes 1048
  3.5 2.6 %collective-permute-start.1 = (f32[24,128]{1,0:T(8,128)S(1)}, f32[24,128]{1,0:T(8,128)S(1)}, u32[]{:S(2)}, u32[]{:S(2)}) collective-permute-start(f32[24,128]{1,0:T(8,128)S(1)} %get-tuple-element.42), channel_id=1, source_target_pairs={{0,2},{1,7},{2,0},{3,5},{4,6},{5,3},{6,4},{7,1},{8,10},{9,15},{10,... | collective-permute-start | bytes 36872 | tf_op jit(solution)/shard_map/ppermute | solution.py:46
  6.1 1.5 %collective-permute-start.3 = (f32[24,128]{1,0:T(8,128)S(1)}, f32[24,128]{1,0:T(8,128)S(1)}, u32[]{:S(2)}, u32[]{:S(2)}) collective-permute-start(f32[24,128]{1,0:T(8,128)S(1)} %get-tuple-element.43), channel_id=1, source_target_pairs={{0,4},{1,5},{2,6},{3,7},{4,0},{5,1},{6,2},{7,3},{8,12},{9,13},{10,... | collective-permute-start | bytes 36872 | tf_op jit(solution)/shard_map/ppermute | solution.py:49
  7.7 0.6 %collective-permute-start.2 = (f32[24,128]{1,0:T(8,128)S(1)}, f32[24,128]{1,0:T(8,128)S(1)}, u32[]{:S(2)}, u32[]{:S(2)}) collective-permute-start(f32[24,128]{1,0:T(8,128)S(1)} %collective-permute-done.1.odd), channel_id=1, source_target_pairs={{0,1},{1,0},{2,3},{3,2},{4,5},{5,4},{6,7},{7,6},{8,9},{9,8},{10,11... | collective-permute-start | bytes 36872 | tf_op jit(solution)/shard_map/ppermute | solution.py:42
  8.3 0.7 %rule.1 = (bf16[2048,256]{1,0:T(8,128)(2,1)S(1)}, f32[16,128]{1,0:T(8,128)S(1)}, s32[4,128]{1,0:T(4,128)S(1)}, bf16[256,1024]{1,0:T(8,128)(2,1)S(1)}, f32[128,128]{1,0:T(8,128)S(1)}) custom-call(f32[4,4]{1,0:T(4,128)S(1)} %copy-done.4, f32[20,128]{1,0:T(8,128)S(1)} %get-tuple-element.28.small_ref, s32[1,16]{1,0:T(1,128)S(1)} %copy-done.5, ...), custom_call_target="tpu_custom_call" | custom-call | flops 5242880 | bytes 524288 | tf_op jit(solution)/shard_map/rule/pallas_call | solution.py:807
  9.1 0.7 %collective-permute-done.3.even = f32[24,128]{1,0:T(8,128)S(1)} collective-permute-done((f32[24,128]{1,0:T(8,128)S(1)}, f32[24,128]{1,0:T(8,128)S(1)}, u32[]{:S(2)}, u32[]{:S(2)}) %collective-permute-start.3) | collective-permute-done | bytes 12320 | tf_op jit(solution)/shard_map/ppermute | solution.py:49
  9.8 1.6 %collective-permute-start.4 = (f32[24,128]{1,0:T(8,128)S(1)}, f32[24,128]{1,0:T(8,128)S(1)}, u32[]{:S(2)}, u32[]{:S(2)}) collective-permute-start(f32[24,128]{1,0:T(8,128)S(1)} %get-tuple-element.45.refs_0_), channel_id=1, source_target_pairs={{0,8},{1,25},{2,10},{3,27},{4,12},{5,29},{6,14},{7,31},{8,0},{9,17... | collective-permute-start | bytes 36872 | tf_op jit(solution)/shard_map/ppermute | solution.py:46
  11.5 2.6 %collective-permute-start.6 = (f32[24,128]{1,0:T(8,128)S(1)}, f32[24,128]{1,0:T(8,128)S(1)}, u32[]{:S(2)}, u32[]{:S(2)}) collective-permute-start(f32[24,128]{1,0:T(8,128)S(1)} %get-tuple-element.46), channel_id=1, source_target_pairs={{0,16},{1,17},{2,18},{3,19},{4,20},{5,21},{6,22},{7,23},{8,24},{9,... | collective-permute-start | bytes 36872 | tf_op jit(solution)/shard_map/ppermute | solution.py:49
  14.1 0.4 %collective-permute-start.5 = (f32[24,128]{1,0:T(8,128)S(1)}, f32[24,128]{1,0:T(8,128)S(1)}, u32[]{:S(2)}, u32[]{:S(2)}) collective-permute-start(f32[24,128]{1,0:T(8,128)S(1)} %collective-permute-done.4.odd), channel_id=1, source_target_pairs={{0,1},{1,0},{2,3},{3,2},{4,5},{5,4},{6,7},{7,6},{8,9},{9,8},{10,11... | collective-permute-start | bytes 36872 | tf_op jit(solution)/shard_map/ppermute | solution.py:42
  14.4 0.5 %forecast.2 = (f32[128,1024]{1,0:T(8,128)S(1)}, f32[256,128]{1,0:T(8,128)S(1)}) custom-call(f32[16,128]{1,0:T(8,128)S(1)} %get-tuple-element.29.powers_ref._, bf16[256,1024]{1,0:T(8,128)(2,1)S(1)} %get-tuple-element.31.source, bf16[2048,256]{1,0:T(8,128)(2,1)S(1)} %get-tuple-element.30.band_ref), custom_call_target="tpu_custom_call" | custom-call | flops 10485760 | bytes 1048576 | tf_op jit(solution)/shard_map/forecast/pallas_call | solution.py:790
  15.0 0.8 %forecast.3 = (f32[128,1024]{1,0:T(8,128)S(1)}, f32[128,128]{1,0:T(8,128)S(1)}, f32[256,128]{1,0:T(8,128)S(1)}, bf16[512,1024]{1,0:T(8,128)(2,1)S(1)}) custom-call(f32[16,128]{1,0:T(8,128)S(1)} %get-tuple-element.29.powers_ref._, f32[32,4,1024]{2,1,0:T(4,128)S(1)} %collective-permute-done.source.other_ref, bf16[2048,256]{1,0:T(8,128)(2,1)S(1)} %get-tuple-element.30.band_ref, ...), custom_call_target="tpu_custom_call" | custom-call | flops 10485760 | bytes 1048576 | tf_op jit(solution)/shard_map/forecast/pallas_call | solution.py:790
  15.8 0.5 %collective-permute-done.6.even = f32[24,128]{1,0:T(8,128)S(1)} collective-permute-done((f32[24,128]{1,0:T(8,128)S(1)}, f32[24,128]{1,0:T(8,128)S(1)}, u32[]{:S(2)}, u32[]{:S(2)}) %collective-permute-start.6) | collective-permute-done | bytes 12320 | tf_op jit(solution)/shard_map/ppermute | solution.py:49
  16.2 1.5 %sums.1 = (f32[40,128]{1,0:T(8,128)S(1)}, f32[40,128]{1,0:T(8,128)S(1)}, f32[40,128]{1,0:T(8,128)S(1)}, f32[256,256]{1,0:T(8,128)S(1)}) custom-call(f32[16,128]{1,0:T(8,128)S(1)} %get-tuple-element.29.powers_ref._, f32[20,128]{1,0:T(8,128)S(1)} %get-tuple-element.28.small_ref, f32[128,1024]{1,0:T(8,128)S(1)} %get-tuple-element.32.refs_0_.own_state, ...), custom_call_target="tpu_custom_call" | custom-call | tf_op jit(solution)/shard_map/sums/pallas_call | solution.py:840
  17.8 0.5 %collective-permute-start.8 = (f32[40,128]{1,0:T(8,128)S(1)}, f32[40,128]{1,0:T(8,128)S(1)}, u32[]{:S(2)}, u32[]{:S(2)}) collective-permute-start(f32[40,128]{1,0:T(8,128)S(1)} %get-tuple-element.51), channel_id=1, source_target_pairs={{0,8},{1,25},{2,10},{3,27},{4,12},{5,29},{6,14},{7,31},{8,0},{9,17... | collective-permute-start | bytes 61448 | tf_op jit(solution)/shard_map/ppermute | solution.py:46
  18.3 3.2 %collective-permute-start.7 = (f32[40,128]{1,0:T(8,128)S(1)}, f32[40,128]{1,0:T(8,128)S(1)}, u32[]{:S(2)}, u32[]{:S(2)}) collective-permute-start(f32[40,128]{1,0:T(8,128)S(1)} %get-tuple-element.50), channel_id=1, source_target_pairs={{0,16},{1,17},{2,18},{3,19},{4,20},{5,21},{6,22},{7,23},{8,24},{9,... | collective-permute-start | bytes 61448 | tf_op jit(solution)/shard_map/ppermute | solution.py:49
  21.6 1.2 %collective-permute-start.9 = (f32[40,128]{1,0:T(8,128)S(1)}, f32[40,128]{1,0:T(8,128)S(1)}, u32[]{:S(2)}, u32[]{:S(2)}) collective-permute-start(f32[40,128]{1,0:T(8,128)S(1)} %collective-permute-done.8), channel_id=1, source_target_pairs={{0,1},{1,0},{2,3},{3,2},{4,5},{5,4},{6,7},{7,6},{8,9},{9,8},{10,11... | collective-permute-start | bytes 61448 | tf_op jit(solution)/shard_map/ppermute | solution.py:42
  22.8 0.6 %collective-permute-done.7 = f32[40,128]{1,0:T(8,128)S(1)} collective-permute-done((f32[40,128]{1,0:T(8,128)S(1)}, f32[40,128]{1,0:T(8,128)S(1)}, u32[]{:S(2)}, u32[]{:S(2)}) %collective-permute-start.7) | collective-permute-done | bytes 20512 | tf_op jit(solution)/shard_map/ppermute | solution.py:49
  23.7 1.3 %collective-permute-start.10 = (f32[40,128]{1,0:T(8,128)S(1)}, f32[40,128]{1,0:T(8,128)S(1)}, u32[]{:S(2)}, u32[]{:S(2)}) collective-permute-start(f32[40,128]{1,0:T(8,128)S(1)} %add_add_fusion.kept), channel_id=1, source_target_pairs={{0,2},{1,7},{2,0},{3,5},{4,6},{5,3},{6,4},{7,1},{8,10},{9,15},{10,... | collective-permute-start | bytes 61448 | tf_op jit(solution)/shard_map/ppermute | solution.py:46
  25.0 1.5 %collective-permute-start.12 = (f32[40,128]{1,0:T(8,128)S(1)}, f32[40,128]{1,0:T(8,128)S(1)}, u32[]{:S(2)}, u32[]{:S(2)}) collective-permute-start(f32[40,128]{1,0:T(8,128)S(1)} %add_add_fusion.kept), channel_id=1, source_target_pairs={{0,4},{1,5},{2,6},{3,7},{4,0},{5,1},{6,2},{7,3},{8,12},{9,13},{10,... | collective-permute-start | bytes 61448 | tf_op jit(solution)/shard_map/ppermute | solution.py:49
  26.5 1.0 %collective-permute-done.10.odd = f32[40,128]{1,0:T(8,128)S(1)} collective-permute-done((f32[40,128]{1,0:T(8,128)S(1)}, f32[40,128]{1,0:T(8,128)S(1)}, u32[]{:S(2)}, u32[]{:S(2)}) %collective-permute-start.10) | collective-permute-done | bytes 20512 | tf_op jit(solution)/shard_map/ppermute | solution.py:46
  27.8 1.0 %collective-permute-done.12.even = f32[40,128]{1,0:T(8,128)S(1)} collective-permute-done((f32[40,128]{1,0:T(8,128)S(1)}, f32[40,128]{1,0:T(8,128)S(1)}, u32[]{:S(2)}, u32[]{:S(2)}) %collective-permute-start.12) | collective-permute-done | bytes 20512 | tf_op jit(solution)/shard_map/ppermute | solution.py:49
  28.8 2.3 %analysis.1 = (f32[32,4,1024]{2,1,0:T(4,128)}, f32[2,128]{1,0:T(2,128)}) custom-call(bf16[512,1024]{1,0:T(8,128)(2,1)S(1)} %get-tuple-element.33.split_ref, f32[256,256]{1,0:T(8,128)S(1)} %get-tuple-element.47.edge_ref, f32[20,128]{1,0:T(8,128)S(1)} %get-tuple-element.28.small_ref, s32[4,128]{1,0:T(4,128)S(1)} %get-tuple-element.48.slots_ref, ...), custom_call_target="tpu_custom_call" | custom-call | tf_op jit(solution)/shard_map/analysis/pallas_call | solution.py:872
  (32 shorter events, 1.7 us)
Async XLA Ops:
  0.6 2.7 %collective-permute-start = (f32[32,4,1024]{2,1,0:T(4,128)}, f32[32,4,1024]{2,1,0:T(4,128)S(1)}, u32[]{:S(2)}, u32[]{:S(2)}) collective-permute-start(f32[32,4,1024]{2,1,0:T(4,128)} %ensemble_ref.1), channel_id=1, source_target_pairs={{0,1},{1,0},{2,3},{3,2},{4,5},{5,4},{6,7},{7,6},{8,9},{9,8},{10,11... | collective-permute-start | bytes 1572872 | tf_op jit(solution)/shard_map/ppermute | solution.py:42
  1.1 1.0 %copy-start = (f32[32,4,1024]{2,1,0:T(4,128)S(1)}, f32[32,4,1024]{2,1,0:T(4,128)}, u32[]{:S(2)}) copy-start(f32[32,4,1024]{2,1,0:T(4,128)} %ensemble_ref.1) | copy-start | bytes 1572868
  2.2 0.7 %copy-start.6 = (s32[256]{0:T(256)S(1)}, s32[256]{0:T(256)}, u32[]{:S(2)}) copy-start(s32[256]{0:T(256)} %param.13) | copy-start | bytes 3076
  2.2 0.7 %copy-start.7 = (s32[256]{0:T(256)S(1)}, s32[256]{0:T(256)}, u32[]{:S(2)}) copy-start(s32[256]{0:T(256)} %param.14) | copy-start | bytes 3076
  2.2 0.7 %copy-start.8 = (f32[256]{0:T(256)S(1)}, f32[256]{0:T(256)}, u32[]{:S(2)}) copy-start(f32[256]{0:T(256)} %param.15) | copy-start | bytes 3076
  2.2 0.7 %copy-start.9 = (f32[256]{0:T(256)S(1)}, f32[256]{0:T(256)}, u32[]{:S(2)}) copy-start(f32[256]{0:T(256)} %param.16) | copy-start | bytes 3076
  2.2 6.1 %copy-start.1 = (f32[32,4,1024]{2,1,0:T(4,128)S(1)}, f32[32,4,1024]{2,1,0:T(4,128)}, u32[]{:S(2)}) copy-start(f32[32,4,1024]{2,1,0:T(4,128)} %ensemble_ref.1) | copy-start | bytes 1572868
  2.3 0.8 %copy-start.3 = (s32[1024]{0:T(1024)S(1)}, s32[1024]{0:T(1024)}, u32[]{:S(2)}) copy-start(s32[1024]{0:T(1024)} %param.11) | copy-start | bytes 12292
  2.4 0.8 %copy-start.2 = (f32[1024]{0:T(1024)S(1)}, f32[1024]{0:T(1024)}, u32[]{:S(2)}) copy-start(f32[1024]{0:T(1024)} %param.10) | copy-start | bytes 12292
  2.4 0.7 %copy-start.5 = (s32[1,16]{1,0:T(1,128)S(1)}, s32[1,16]{1,0:T(1,128)}, u32[]{:S(2)}) copy-start(s32[1,16]{1,0:T(1,128)} %send_ref.3) | copy-start | bytes 196
  3.5 4.8 %copy-start.4 = (f32[4,4]{1,0:T(4,128)S(1)}, f32[4,4]{1,0:T(4,128)}, u32[]{:S(2)}) copy-start(f32[4,4]{1,0:T(4,128)} %couple_ref.1) | copy-start | bytes 196
  3.5 4.2 %collective-permute-start.1 = (f32[24,128]{1,0:T(8,128)S(1)}, f32[24,128]{1,0:T(8,128)S(1)}, u32[]{:S(2)}, u32[]{:S(2)}) collective-permute-start(f32[24,128]{1,0:T(8,128)S(1)} %get-tuple-element.42), channel_id=1, source_target_pairs={{0,2},{1,7},{2,0},{3,5},{4,6},{5,3},{6,4},{7,1},{8,10},{9,15},{10,... | collective-permute-start | bytes 36872 | tf_op jit(solution)/shard_map/ppermute | solution.py:46
  6.1 3.7 %collective-permute-start.3 = (f32[24,128]{1,0:T(8,128)S(1)}, f32[24,128]{1,0:T(8,128)S(1)}, u32[]{:S(2)}, u32[]{:S(2)}) collective-permute-start(f32[24,128]{1,0:T(8,128)S(1)} %get-tuple-element.43), channel_id=1, source_target_pairs={{0,4},{1,5},{2,6},{3,7},{4,0},{5,1},{6,2},{7,3},{8,12},{9,13},{10,... | collective-permute-start | bytes 36872 | tf_op jit(solution)/shard_map/ppermute | solution.py:49
  7.7 2.0 %collective-permute-start.2 = (f32[24,128]{1,0:T(8,128)S(1)}, f32[24,128]{1,0:T(8,128)S(1)}, u32[]{:S(2)}, u32[]{:S(2)}) collective-permute-start(f32[24,128]{1,0:T(8,128)S(1)} %collective-permute-done.1.odd), channel_id=1, source_target_pairs={{0,1},{1,0},{2,3},{3,2},{4,5},{5,4},{6,7},{7,6},{8,9},{9,8},{10,11... | collective-permute-start | bytes 36872 | tf_op jit(solution)/shard_map/ppermute | solution.py:42
  9.8 4.2 %collective-permute-start.4 = (f32[24,128]{1,0:T(8,128)S(1)}, f32[24,128]{1,0:T(8,128)S(1)}, u32[]{:S(2)}, u32[]{:S(2)}) collective-permute-start(f32[24,128]{1,0:T(8,128)S(1)} %get-tuple-element.45.refs_0_), channel_id=1, source_target_pairs={{0,8},{1,25},{2,10},{3,27},{4,12},{5,29},{6,14},{7,31},{8,0},{9,17... | collective-permute-start | bytes 36872 | tf_op jit(solution)/shard_map/ppermute | solution.py:46
  11.5 4.7 %collective-permute-start.6 = (f32[24,128]{1,0:T(8,128)S(1)}, f32[24,128]{1,0:T(8,128)S(1)}, u32[]{:S(2)}, u32[]{:S(2)}) collective-permute-start(f32[24,128]{1,0:T(8,128)S(1)} %get-tuple-element.46), channel_id=1, source_target_pairs={{0,16},{1,17},{2,18},{3,19},{4,20},{5,21},{6,22},{7,23},{8,24},{9,... | collective-permute-start | bytes 36872 | tf_op jit(solution)/shard_map/ppermute | solution.py:49
  14.1 2.1 %collective-permute-start.5 = (f32[24,128]{1,0:T(8,128)S(1)}, f32[24,128]{1,0:T(8,128)S(1)}, u32[]{:S(2)}, u32[]{:S(2)}) collective-permute-start(f32[24,128]{1,0:T(8,128)S(1)} %collective-permute-done.4.odd), channel_id=1, source_target_pairs={{0,1},{1,0},{2,3},{3,2},{4,5},{5,4},{6,7},{7,6},{8,9},{9,8},{10,11... | collective-permute-start | bytes 36872 | tf_op jit(solution)/shard_map/ppermute | solution.py:42
  17.8 3.8 %collective-permute-start.8 = (f32[40,128]{1,0:T(8,128)S(1)}, f32[40,128]{1,0:T(8,128)S(1)}, u32[]{:S(2)}, u32[]{:S(2)}) collective-permute-start(f32[40,128]{1,0:T(8,128)S(1)} %get-tuple-element.51), channel_id=1, source_target_pairs={{0,8},{1,25},{2,10},{3,27},{4,12},{5,29},{6,14},{7,31},{8,0},{9,17... | collective-permute-start | bytes 61448 | tf_op jit(solution)/shard_map/ppermute | solution.py:46
  18.3 5.2 %collective-permute-start.7 = (f32[40,128]{1,0:T(8,128)S(1)}, f32[40,128]{1,0:T(8,128)S(1)}, u32[]{:S(2)}, u32[]{:S(2)}) collective-permute-start(f32[40,128]{1,0:T(8,128)S(1)} %get-tuple-element.50), channel_id=1, source_target_pairs={{0,16},{1,17},{2,18},{3,19},{4,20},{5,21},{6,22},{7,23},{8,24},{9,... | collective-permute-start | bytes 61448 | tf_op jit(solution)/shard_map/ppermute | solution.py:49
  21.6 2.1 %collective-permute-start.9 = (f32[40,128]{1,0:T(8,128)S(1)}, f32[40,128]{1,0:T(8,128)S(1)}, u32[]{:S(2)}, u32[]{:S(2)}) collective-permute-start(f32[40,128]{1,0:T(8,128)S(1)} %collective-permute-done.8), channel_id=1, source_target_pairs={{0,1},{1,0},{2,3},{3,2},{4,5},{5,4},{6,7},{7,6},{8,9},{9,8},{10,11... | collective-permute-start | bytes 61448 | tf_op jit(solution)/shard_map/ppermute | solution.py:42
  23.7 3.8 %collective-permute-start.10 = (f32[40,128]{1,0:T(8,128)S(1)}, f32[40,128]{1,0:T(8,128)S(1)}, u32[]{:S(2)}, u32[]{:S(2)}) collective-permute-start(f32[40,128]{1,0:T(8,128)S(1)} %add_add_fusion.kept), channel_id=1, source_target_pairs={{0,2},{1,7},{2,0},{3,5},{4,6},{5,3},{6,4},{7,1},{8,10},{9,15},{10,... | collective-permute-start | bytes 61448 | tf_op jit(solution)/shard_map/ppermute | solution.py:46
  25.0 3.8 %collective-permute-start.12 = (f32[40,128]{1,0:T(8,128)S(1)}, f32[40,128]{1,0:T(8,128)S(1)}, u32[]{:S(2)}, u32[]{:S(2)}) collective-permute-start(f32[40,128]{1,0:T(8,128)S(1)} %add_add_fusion.kept), channel_id=1, source_target_pairs={{0,4},{1,5},{2,6},{3,7},{4,0},{5,1},{6,2},{7,3},{8,12},{9,13},{10,... | collective-permute-start | bytes 61448 | tf_op jit(solution)/shard_map/ppermute | solution.py:49
  27.5 1.3 %collective-permute-start.11 = (f32[40,128]{1,0:T(8,128)S(1)}, f32[40,128]{1,0:T(8,128)S(1)}, u32[]{:S(2)}, u32[]{:S(2)}) collective-permute-start(f32[40,128]{1,0:T(8,128)S(1)} %collective-permute-done.10.odd), channel_id=1, source_target_pairs={{0,1},{1,0},{2,3},{3,2},{4,5},{5,4},{6,7},{7,6},{8,9},{9,8},{10,11... | collective-permute-start | bytes 61448 | tf_op jit(solution)/shard_map/ppermute | solution.py:42
